TPU v7x, 32 devices: a whole 2x2x4 slice. The times are simulated.
32 devices in a mesh: tm: 4 (over y, core), space: 8 (over z, x).
Axes of the slice: x: 2, y: 2, z: 4, core: 2. Of those that a mesh axis runs over, the one named last changes fastest.
Arguments:
- snapshots: float32 [512, 128, 512], P('space', None, 'tm'), may hold values from -6 to 6
- land_mask: int32 [512, 128], P('space'), may hold values 0 or 1
- taps_rows: float32 [6], replicated, may hold values from -2.5 to 2.5
- taps_cols: float32 [6], replicated, may hold values from -2.5 to 2.5
- probes: float32 [256, 64, 128], P('space'), may hold values from -6 to 6
Outputs:
- basis: float32 [256, 64, 128], P('space', None, 'tm')
- coefficients: float32 [128, 128], P('tm')
All inputs are finite; a program needn't handle non-finite values. No bound on the sum of `land_mask` on one device may be relied on, other than what follows from the above.
Results may differ from a plain program's by a relative error of at most 0.00028.
Values sent between devices are 32-bit elements; how exact they have to be, the bound alone decides.
No kernel may reach another device: no remote copies, remote signals or barrier semaphores. Data moves between devices by JAX's collectives and lax.ppermute only.
A program may use at most 64 MiB of HBM per device.

v0:
```python
import jax
import jax.numpy as jnp
from jax import lax
from jax.sharding import PartitionSpec as P

SIGN_STEPS = 8


exact_dot = lax.Precision.HIGHEST


def padded_2(x, sides, width):
    for axis, dim in sides:
        size, length = (lax.axis_size(axis), x.shape[dim])
        up = [(i, (i + 1) % size) for i in range(size - 1)]
        down = [(j, i) for i, j in up]
        last = lax.slice_in_dim(x, length - width, length, axis=dim)
        initial = lax.slice_in_dim(x, 0, width, axis=dim)
        before = lax.ppermute(last, axis, up)
        after = lax.ppermute(initial, axis, down)
        x = jnp.concatenate([before, x, after], axis=dim)
    return x


def partner(block, axis, distance):
    count = lax.axis_size(axis)
    route = []
    for low in range(count):
        high = low | 1 << distance
        if high != low and high < count:
            route += [(low, high), (high, low)]
    return lax.ppermute(block, axis, route)


def band_matrix(tap_values, out_count, in_width, shift_by):
    row_ids = lax.broadcasted_iota(jnp.int32, (out_count, in_width), 0)
    col_ids = lax.broadcasted_iota(jnp.int32, (out_count, in_width), 1)
    tap_offset = col_ids - 2 * row_ids - shift_by
    band_table = jnp.zeros((out_count, in_width), jnp.float32)
    for tap_index in range(6):
        band_table = band_table + jnp.where(tap_offset == tap_index, tap_values[tap_index], 0.0)
    return band_table


def merge_level(paired):
    partial_gram = jnp.einsum("gra,grb->gab", paired, paired, precision=exact_dot)
    gram_total = lax.psum(partial_gram, "space")
    order_size = gram_total.shape[-1]
    identity = jnp.eye(order_size, dtype=jnp.float32)
    mean_eig = jnp.sum(gram_total * identity, axis=(1, 2)) / order_size
    shifted = gram_total - mean_eig[:, None, None] * identity
    norm_scale = jnp.sqrt(jnp.sum(shifted * shifted, axis=(1, 2)) + 1e-06)
    sign_iter = shifted / norm_scale[:, None, None]
    for sweep_index in range(SIGN_STEPS):
        square = jnp.einsum("gab,gbc->gac", sign_iter, sign_iter, precision=exact_dot)
        sign_iter = 1.5 * sign_iter - 0.5 * jnp.einsum(
            "gab,gbc->gac", sign_iter, square, precision=exact_dot
        )
    projector = 0.5 * (identity + sign_iter)
    half_order = order_size // 2
    combine = projector[:, :, :half_order] + projector[:, :, half_order:]
    return jnp.einsum("gra,gab->grb", paired, combine, precision=exact_dot)


def local(snapshots, land_mask, taps_rows, taps_cols, probes):
    rows_dev, cell_cols, columns = snapshots.shape
    ocean_field = snapshots * land_mask.astype(jnp.float32)[:, :, None]
    across = band_matrix(taps_cols, cell_cols // 2, cell_cols, -2)
    narrowed = jnp.einsum("jy,xys->xjs", across, ocean_field, precision=exact_dot)
    padded = padded_2(narrowed, (("space", 0),), 3)
    row_filter = band_matrix(taps_rows, rows_dev // 2, rows_dev + 6, 1)
    filtered = jnp.einsum("ip,pjs->ijs", row_filter, padded, precision=exact_dot)
    cell_rows = rows_dev // 2 * (cell_cols // 2)
    factor = filtered.reshape(cell_rows, columns)
    flat_probes = probes.reshape(cell_rows, probes.shape[2])
    levels = lax.axis_size("tm").bit_length() - 1
    position = lax.axis_index("tm")
    merged = factor
    for level_index in range(levels):
        partner_fac = partner(merged, "tm", level_index)
        is_upper = position >> level_index & 1 == 1
        lower_part = jnp.where(is_upper, partner_fac, merged)
        upper_part = jnp.where(is_upper, merged, partner_fac)
        merged = merge_level(jnp.concatenate([lower_part, upper_part], axis=1)[None])[0]
    width_dev = columns // lax.axis_size("tm")
    col_start = position * width_dev
    partial_coef = jnp.einsum("rs,rp->sp", merged, flat_probes, precision=exact_dot)
    coefficients = lax.psum(partial_coef, "space")
    basis_own = lax.dynamic_slice_in_dim(merged, col_start, width_dev, 1)
    coef_own = lax.dynamic_slice_in_dim(coefficients, col_start, width_dev, 0)
    return (basis_own.reshape(rows_dev // 2, cell_cols // 2, width_dev), coef_own)


def solution(mesh):
    placed = (P("space", None, "tm"), P("space", None), P(), P(), P("space", None, None))
    return jax.shard_map(
        local,
        mesh=mesh,
        in_specs=placed,
        out_specs=(P("space", None, "tm"), P("tm", None)),
        check_vma=False,
    )
```

profile of v0, /device:TPU:0, one launch (start us, length us, event | category | flops | bytes accessed | tf_op | source)
XLA Modules:
  0.0 323.3 jit_solution(6129101247048303545)
XLA Ops:
  7.2 1.5 fusion.212
  9.5 8.9 %fusion.9 = f32[64,64,128]{2,1,0:T(8,128)S(1)} fusion(f32[64,128,128]{2,1,0:T(8,128)} %param.5, f32[64,128]{1,0:T(8,128)S(1)} %convert_element_type.18, f32[]{:T(128)} %bitcast.12, f32[]{:T(128)} %bitcast.11, f32[]{:T(128)} %bitcast.10, f32[]{:T(128)} %bitcast.9, f32[]{:T(128)} %bitcast.8, f32[]{:T(128)} %bitcast.7, s32[64]{0:T(128)S(1)} %iota_multiply_fusion), kind=kOutput, calls=%fused_computation.12 | convolution fusion | flops 806510592 | bytes 6324504 | tf_op jit(solution)/shard_map/jy,xys->xjs/dot_general | solution.py:69
  18.5 4.8 %collective-permute-start = (f32[3,64,128]{2,1,0:T(8,128)S(1)}, f32[3,64,128]{2,1,0:T(8,128)S(1)}, u32[]{:S(2)}, u32[]{:S(2)}) collective-permute-start(f32[3,64,128]{2,1,0:T(8,128)S(1)} %get-tuple-element.8), channel_id=1, source_target_pairs={{0,1},{1,2},{2,3},{3,4},{4,5},{5,6},{6,7},{8,9},{9,10},{10,11},{11... | collective-permute-start | bytes 294920 | tf_op jit(solution)/shard_map/ppermute | solution.py:19
  25.5 4.3 %collective-permute-done.1 = f32[3,64,128]{2,1,0:T(8,128)S(1)} collective-permute-done((f32[3,64,128]{2,1,0:T(8,128)S(1)}, f32[3,64,128]{2,1,0:T(8,128)S(1)}, u32[]{:S(2)}, u32[]{:S(2)}) %collective-permute-start.1) | collective-permute-done | bytes 98336 | tf_op jit(solution)/shard_map/ppermute | solution.py:20
  30.1 6.4 %fusion.2 = f32[32,64,128]{2,0,1:T(8,128)S(1)} fusion(f32[70,64,128]{2,1,0:T(8,128)S(1)} %pad_maximum_fusion, f32[]{:T(128)} %bitcast.5, f32[]{:T(128)} %bitcast.4, f32[]{:T(128)} %bitcast.3, f32[]{:T(128)} %bitcast.2, f32[]{:T(128)} %bitcast.1, f32[]{:T(128)} %bitcast, s32[32]{0:T(128)S(1)} %iota_multiply_fusion.1), kind=kOutput, calls=%fused_computation.2 | convolution fusion | flops 220243520 | bytes 3342488 | tf_op jit(solution)/shard_map/ip,pjs->ijs/dot_general | solution.py:72
  38.2 1.8 collective-permute-done.2
  40.0 1.7 broadcast_select_fusion.1
  41.7 4.2 %fusion.12 = f32[1,256,256]{2,1,0:T(8,128)} fusion(f32[2048,128]{1,0:T(8,128)S(1)} %get-tuple-element.7, f32[2048,128]{1,0:T(8,128)S(1)} %get-tuple-element.6), kind=kOutput, calls=%fused_computation.13 | convolution fusion | flops 1611137024 | bytes 2359296 | tf_op jit(solution)/shard_map/gra,grb->gab/dot_general | solution.py:46
  46.1 71.7 %all-reduce.4.cloned.1.call-done = f32[1,256,256]{2,1,0:T(8,128)} async-done(((f32[1,256,256]{2,1,0:T(8,128)}), f32[1,256,256]{2,1,0:T(8,128)}) %all-reduce.4.cloned.1.call-update) | async-done | bytes 262160 | tf_op jit(solution)/shard_map/psum | solution.py:47
  117.8 1.6 select_reduce_fusion.1
  120.1 1.6 multiply_reduce_fusion.1
  122.4 1.4 fusion.96
  123.8 1.4 fusion.30
  130.7 3.3 %fusion.7 = f32[2048,128]{0,1:T(8,128)} fusion(f32[2048,128]{1,0:T(8,128)S(1)} %get-tuple-element.7, f32[2048,128]{1,0:T(8,128)S(1)} %get-tuple-element.6, f32[1,256,256]{2,1,0:T(8,128)S(1)} %fusion.39), kind=kOutput, calls=%fused_computation.10 | convolution fusion | flops 805863424 | bytes 3407872 | tf_op jit(solution)/shard_map/gra,gab->grb/dot_general | solution.py:62
  134.0 1.5 collective-permute-start.3
  135.5 21.9 %collective-permute-done.3 = f32[2048,128]{0,1:T(8,128)} collective-permute-done((f32[2048,128]{0,1:T(8,128)}, f32[2048,128]{0,1:T(8,128)}, u32[]{:S(2)}, u32[]{:S(2)}) %collective-permute-start.3) | collective-permute-done | bytes 1048608 | tf_op jit(solution)/shard_map/ppermute | solution.py:32
  157.4 1.7 broadcast_select_fusion.3
  159.1 2.6 fusion.13
  162.0 69.5 %all-reduce.6.cloned.1.call-done = f32[1,256,256]{2,1,0:T(8,128)} async-done(((f32[1,256,256]{2,1,0:T(8,128)}), f32[1,256,256]{2,1,0:T(8,128)}) %all-reduce.6.cloned.1.call-update) | async-done | bytes 262160 | tf_op jit(solution)/shard_map/psum | solution.py:47
  231.5 1.6 select_reduce_fusion
  233.7 1.6 multiply_reduce_fusion
  236.0 1.4 fusion.72
  245.8 1.8 fusion.213
  248.9 66.5 %all-reduce.8.cloned.1.call-done = f32[128,128]{1,0:T(8,128)} async-done(((f32[128,128]{1,0:T(8,128)}), f32[128,128]{1,0:T(8,128)}) %all-reduce.8.cloned.1.call-update) | async-done | bytes 65552 | tf_op jit(solution)/shard_map/psum | solution.py:88
  (60 shorter events, 21.5 us)
Async XLA Ops:
  7.2 238.6 %copy-start = (f32[32,64,128]{2,1,0:T(8,128)S(1)}, f32[32,64,128]{2,1,0:T(8,128)}, u32[]{:S(2)}) copy-start(f32[32,64,128]{2,1,0:T(8,128)} %param.9) | copy-start | bytes 3145732
  7.2 110.6 %all-reduce.4.cloned.1.call-start = ((), (), s32[]{:S(2)}) async-start(), calls=%async_computation | async-start | bytes 524288 | tf_op jit(solution)/shard_map/psum | solution.py:47
  9.5 15.1 %copy-start.4 = (f32[6]{0:T(128)S(1)}, f32[6]{0:T(128)}, u32[]{:S(2)}) copy-start(f32[6]{0:T(128)} %param.7) | copy-start | bytes 76
  18.5 7.0 %collective-permute-start = (f32[3,64,128]{2,1,0:T(8,128)S(1)}, f32[3,64,128]{2,1,0:T(8,128)S(1)}, u32[]{:S(2)}, u32[]{:S(2)}) collective-permute-start(f32[3,64,128]{2,1,0:T(8,128)S(1)} %get-tuple-element.8), channel_id=1, source_target_pairs={{0,1},{1,2},{2,3},{3,4},{4,5},{5,6},{6,7},{8,9},{9,10},{10,11},{11... | collective-permute-start | bytes 294920 | tf_op jit(solution)/shard_map/ppermute | solution.py:19
  23.4 6.5 %collective-permute-start.1 = (f32[3,64,128]{2,1,0:T(8,128)S(1)}, f32[3,64,128]{2,1,0:T(8,128)S(1)}, u32[]{:S(2)}, u32[]{:S(2)}) collective-permute-start(f32[3,64,128]{2,1,0:T(8,128)S(1)} %get-tuple-element.9), channel_id=1, source_target_pairs={{1,0},{2,1},{3,2},{4,3},{5,4},{6,5},{7,6},{9,8},{10,9},{11,10},{12... | collective-permute-start | bytes 294920 | tf_op jit(solution)/shard_map/ppermute | solution.py:20
  37.1 1.0 copy-start.3
  37.1 2.9 collective-permute-start.2
  45.9 185.6 %all-reduce.6.cloned.1.call-start = ((), (), s32[]{:S(2)}) async-start(), calls=%async_computation.1 | async-start | bytes 524288 | tf_op jit(solution)/shard_map/psum | solution.py:47
  134.0 23.4 %collective-permute-start.3 = (f32[2048,128]{0,1:T(8,128)}, f32[2048,128]{0,1:T(8,128)}, u32[]{:S(2)}, u32[]{:S(2)}) collective-permute-start(f32[2048,128]{0,1:T(8,128)} %fusion.7), channel_id=1, source_target_pairs={{0,16},{16,0},{8,24},{24,8},{1,17},{17,1},{9,25},{25,9},{2,18},{18... | collective-permute-start | bytes 3145736 | tf_op jit(solution)/shard_map/ppermute | solution.py:32
  159.1 78.4 %copy-start.1 = (f32[2048,128]{0,1:T(8,128)}, f32[2048,128]{0,1:T(8,128)S(1)}, u32[]{:S(2)}) copy-start(f32[2048,128]{0,1:T(8,128)S(1)} %get-tuple-element.5) | copy-start | bytes 3145732
  161.7 153.7 %all-reduce.8.cloned.1.call-start = ((), (), s32[]{:S(2)}) async-start(), calls=%async_computation.2 | async-start | bytes 131072 | tf_op jit(solution)/shard_map/psum | solution.py:88
  242.0 2.3 copy-start.2
Sparse Core Ops, SparseCore 0:
  46.0 71.7 all-reduce.3
  161.9 69.5 all-reduce.5
  247.7 67.7 all-reduce.7
where the time goes:
time: 324 us; the launch traced here: 323 us
  waiting for transfers between devices  236 us (73%)
  matrix products  44.9 us (14%)
  between operations  16.9 us (5%)
  other arithmetic  10.8 us (3%)
  starting transfers between devices  8.2 us (3%)
  local copies, waits for them, and re-layouts  6.43 us (2%)
    psum x2, waiting for transfers between devices, merge_level(): gram_total = lax.psum(partial_gram, 'space')  141 us
    psum x1, waiting for transfers between devices, local(): coefficients = lax.psum(partial_coef, 'space')  66.5 us
    ppermute x2, waiting for transfers between devices, partner(): return lax.ppermute(block, axis, route)  23.8 us
    dot_general x1, matrix products, local(): jnp.einsum('jy,xys->xjs', across, ocean_field, precision=exact_dot)  8.93 us
    dot_general x16, matrix products, merge_level(): jnp.einsum('gab,gbc->gac', sign_iter, square, precision=exact_dot)  8.23 us
    dot_general x16, matrix products, merge_level(): jnp.einsum('gab,gbc->gac', sign_iter, sign_iter, precision=exact_dot)  8.17 us
    dot_general x2, matrix products, merge_level(): jnp.einsum('gra,grb->gab', paired, paired, precision=exact_dot)  6.76 us
  transfers between devices with their start and end apart: 7, of which 7 were waited for; matrix products, arithmetic and copies ran while one was open for 1% of the time, Pallas kernels for 0%

commit v1 on v0

v1 whole, which is shorter than its diff:
```python
import functools

import jax
import jax.numpy as jnp
from jax import lax
from jax.experimental import pallas as pl
from jax.experimental.pallas import tpu as pltpu
from jax.sharding import PartitionSpec as P

SIGN_STEPS = 8
TAPS = 6
ROW_BLOCK = 16
exact = lax.Precision.HIGHEST
F32 = jnp.float32
VMEM_LIMIT = 48 * 1024 * 1024


def params():
    return pltpu.CompilerParams(vmem_limit_bytes=VMEM_LIMIT)


def whole():
    return pl.BlockSpec(memory_space=pltpu.VMEM)


def scalars():
    return pl.BlockSpec(memory_space=pltpu.SMEM)


def swap(x, axis, mask):
    count = lax.axis_size(axis)
    return lax.ppermute(x, axis, [(i, i ^ mask) for i in range(count)])


def shift_rows(x, by):
    edge = jnp.zeros((1, x.shape[1]), x.dtype)
    if by > 0:
        return jnp.concatenate([edge, x[:-1]], axis=0)
    return jnp.concatenate([x[1:], edge], axis=0)


def narrow_row(snap_ref, x, mask_even, mask_odd, taps):
    half = snap_ref.shape[1] // 2
    even = snap_ref[x, pl.ds(0, half, stride=2), :] * mask_even
    odd = snap_ref[x, pl.ds(1, half, stride=2), :] * mask_odd
    before = taps[0] * even + taps[1] * odd
    here = taps[2] * even + taps[3] * odd
    after = taps[4] * even + taps[5] * odd
    return shift_rows(before, 1) + here + shift_rows(after, -1)


def masks_of(mask_ref, mask_t):
    half = mask_ref.shape[1] // 2
    mask_t[...] = mask_ref[...].astype(F32).T
    return mask_t[pl.ds(0, half, stride=2), :], mask_t[pl.ds(1, half, stride=2), :]


def edge_kernel(taps_ref, first_ref, last_ref, mask_ref, top_ref, end_ref, mask_t):
    taps = [taps_ref[k] for k in range(TAPS)]
    even, odd = masks_of(mask_ref, mask_t)
    rows = mask_ref.shape[0]
    for x in range(2):
        top_ref[x] = narrow_row(first_ref, x, even[:, x:x + 1], odd[:, x:x + 1], taps)
        y = rows - 2 + x
        end_ref[x] = narrow_row(last_ref, x, even[:, y:y + 1], odd[:, y:y + 1], taps)


def filter_kernel(parts, me_ref, rtaps_ref, ctaps_ref, snap_ref, mask_ref, above_ref, below_ref, *rest):
    outs, (mask_t, narrowed, filtered) = rest[:parts], rest[parts:]
    step = pl.program_id(0)
    taps = [ctaps_ref[k] for k in range(TAPS)]
    even, odd = masks_of(mask_ref, mask_t)
    block = snap_ref.shape[0]
    for x in range(block):
        narrowed[2 + step * block + x] = narrow_row(snap_ref, x, even[:, x:x + 1], odd[:, x:x + 1], taps)

    @pl.when(step == pl.num_programs(0) - 1)
    def _():
        size = narrowed.shape[0]
        narrowed[0:2] = above_ref[...]
        narrowed[size - 2:size] = below_ref[...]
        rtaps = [rtaps_ref[k] for k in range(TAPS)]
        cells = narrowed.shape[1]
        for i in range((size - 4) // 2):
            total = rtaps[0] * narrowed[2 * i]
            for k in range(1, TAPS):
                total = total + rtaps[k] * narrowed[2 * i + k]
            filtered[i * cells:(i + 1) * cells, :] = total
        me = me_ref[0]
        piece = filtered.shape[0] // parts
        for k in range(parts):
            outs[k][...] = filtered[pl.ds(pl.multiple_of((me ^ k) * piece, 8), piece), :]


def probe_kernel(parts, me_ref, *refs):
    pieces, probes_ref, out_ref = refs[:parts], refs[parts], refs[parts + 1]
    me = me_ref[0]
    size = pieces[0].shape[0]
    total = None
    for k in range(parts):
        there = probes_ref[pl.ds(pl.multiple_of((me ^ k) * size, 8), size), :]
        term = lax.dot_general(pieces[k][...], there, (((0,), (0,)), ((), ())), precision=exact, preferred_element_type=F32)
        total = term if total is None else total + term
    out_ref[...] = total


def block_order(parts):
    return [(a, b) for a in range(parts) for b in range(a, parts)]


def send_groups(parts):
    groups, bit = [], 1
    while bit < parts:
        groups.append([k for k in range(parts) if k & (2 * bit - 1) == bit])
        bit *= 2
    return groups + [[0]]


def gram_kernel(parts, me_ref, *refs):
    pieces = refs[:parts]
    groups = send_groups(parts)
    outs = refs[parts:parts + len(groups)]
    wide, flat = refs[parts + len(groups):]
    me = me_ref[0]
    cols = pieces[0].shape[1]
    for k in range(parts):
        wide[:, pl.ds(pl.multiple_of((me ^ k) * cols, cols), cols)] = pieces[k][...]
    where = {ab: j for j, ab in enumerate(block_order(parts))}
    for a in range(0, parts, 2):
        left = wide[:, a * cols:(a + 2) * cols]
        for b in range(a, parts, 2):
            right = wide[:, b * cols:(b + 2) * cols]
            prod = lax.dot_general(left, right, (((0,), (0,)), ((), ())), precision=exact, preferred_element_type=F32)
            for i in range(2):
                for j in range(2):
                    if (a + i, b + j) in where:
                        at = where[a + i, b + j] * cols
                        flat[at:at + cols, :] = prod[i * cols:(i + 1) * cols, j * cols:(j + 1) * cols]
    size = flat.shape[0] // parts
    for group, out in zip(groups, outs):
        for at, k in enumerate(group):
            out[at] = flat[pl.ds(pl.multiple_of((me ^ k) * size, 8), size), :]


def split(x):
    high = x.astype(jnp.bfloat16)
    return high, (x - high.astype(F32)).astype(jnp.bfloat16)


def dot(a, b, dims):
    return lax.dot_general(a, b, (dims, ((), ())), preferred_element_type=F32)


def dot_parts(a, b, dims=((1,), (0,))):
    (ah, al), (bh, bl) = a, b
    return dot(ah, bh, dims) + (dot(ah, bl, dims) + dot(al, bh, dims))


def exact_dot(a, b, dims=((1,), (0,))):
    return lax.dot_general(a, b, (dims, ((), ())), precision=exact, preferred_element_type=F32)


def combine_of(grams):
    order = grams[0].shape[0]
    diagonal = lax.broadcasted_iota(jnp.int32, (order, order), 0) == lax.broadcasted_iota(jnp.int32, (order, order), 1)
    signs = []
    for gram in grams:
        mean = jnp.sum(jnp.where(diagonal, gram, 0.0)) / order
        shifted = jnp.where(diagonal, gram - mean, gram)
        signs.append(shifted / jnp.sqrt(jnp.sum(shifted * shifted, keepdims=True) + 1e-6))
    for _ in range(SIGN_STEPS):
        halves = [split(y) for y in signs]
        squares = [split(dot_parts(y, y)) for y in halves]
        cubes = [dot_parts(y, s) for y, s in zip(halves, squares)]
        signs = [1.5 * y - 0.5 * c for y, c in zip(signs, cubes)]
    half = order // 2
    combines = []
    for y in signs:
        projector = 0.5 * (jnp.where(diagonal, 1.0, 0.0) + y)
        combines.append(projector[:, :half] + projector[:, half:])
    return combines


def merge_kernel(parts, me_ref, *refs):
    gram_in, factors = refs[:parts], refs[parts:2 * parts]
    probe_ref = refs[2 * parts]
    outs = refs[2 * parts + 1:3 * parts + 1]
    flat, weight, turned = refs[3 * parts + 1:]
    me = me_ref[0]
    size, cols = gram_in[0].shape
    for k in range(parts):
        flat[pl.ds(pl.multiple_of((me ^ k) * size, 8), size), :] = gram_in[k][...]
    blocks = {ab: flat[j * cols:(j + 1) * cols, :] for j, ab in enumerate(block_order(parts))}
    weights, count = None, parts
    while count > 1:
        grams = []
        for p in range(0, count, 2):
            low = jnp.concatenate([blocks[p, p], blocks[p, p + 1]], axis=1)
            high = jnp.concatenate([blocks[p, p + 1].T, blocks[p + 1, p + 1]], axis=1)
            grams.append(jnp.concatenate([low, high], axis=0))
        combines = combine_of(grams)
        if weights is None:
            weights = combines
        else:
            per = len(weights) // len(combines)
            weights = [
                exact_dot(w, combines[i // per][(i % per) * cols:(i % per + 1) * cols, :])
                for i, w in enumerate(weights)
            ]
            weights = [jnp.concatenate(weights[i:i + per], axis=0) for i in range(0, len(weights), per)]
        merged = {}
        if count > 2:
            for p in range(count // 2):
                for q in range(p, count // 2):
                    if p == q:
                        cross = grams[p]
                    else:
                        cross = jnp.concatenate([
                            jnp.concatenate([blocks[2 * p + i, 2 * q], blocks[2 * p + i, 2 * q + 1]], axis=1)
                            for i in range(2)
                        ], axis=0)
                    right = exact_dot(cross, combines[q])
                    merged[p, q] = exact_dot(combines[p], right, ((0,), (0,)))
        blocks, count = merged, count // 2
    weight[...] = weights[0]
    total = None
    for k in range(parts):
        there = weight[pl.ds(pl.multiple_of((me ^ k) * cols, cols), cols), :]
        term = dot_parts(split(factors[k][...]), split(there))
        total = term if total is None else total + term
    rows = total.shape[0]
    turned[:, :rows] = total.T
    mine = weight[pl.ds(pl.multiple_of(me * cols, cols), cols), :]
    turned[:, rows:] = exact_dot(mine, probe_ref[...], ((0,), (0,)))
    width = cols // parts
    for k in range(parts):
        outs[k][...] = turned[pl.ds(pl.multiple_of((me ^ k) * width, 8), width), :]


def final_kernel(parts, me_ref, *refs):
    pieces, (basis_ref, coef_ref) = refs[:parts], refs[parts:]
    me = me_ref[0]
    rows = basis_ref.shape[0] // parts
    total = None
    for k in range(parts):
        basis_ref[pl.ds(pl.multiple_of((me ^ k) * rows, 8), rows), :] = pieces[k][:, :rows].T
        tail = pieces[k][:, rows:]
        total = tail if total is None else total + tail
    coef_ref[...] = total


def shape(*dims):
    return jax.ShapeDtypeStruct(dims, F32)


def local(snapshots, land_mask, taps_rows, taps_cols, probes):
    rows, grid_cols, cols = snapshots.shape
    half_rows, half_cols = rows // 2, grid_cols // 2
    parts, patches = lax.axis_size("tm"), lax.axis_size("space")
    cells = half_rows * half_cols
    piece = cells // parts
    me = lax.axis_index("tm").astype(jnp.int32).reshape(1)

    top, end = pl.pallas_call(
        edge_kernel,
        out_shape=(shape(2, half_cols, cols), shape(2, half_cols, cols)),
        grid=(1,),
        in_specs=[
            scalars(),
            pl.BlockSpec((2, grid_cols, cols), lambda i: (0, 0, 0)),
            pl.BlockSpec((2, grid_cols, cols), lambda i: (rows // 2 - 1, 0, 0)),
            pl.BlockSpec((rows, grid_cols), lambda i: (0, 0)),
        ],
        out_specs=(
            pl.BlockSpec((2, half_cols, cols), lambda i: (0, 0, 0)),
            pl.BlockSpec((2, half_cols, cols), lambda i: (0, 0, 0)),
        ),
        scratch_shapes=[pltpu.VMEM((grid_cols, rows), F32)],
        compiler_params=params(),
        name="edge",
    )(taps_cols, snapshots, snapshots, land_mask)
    up = [(i, i + 1) for i in range(patches - 1)]
    above = lax.ppermute(end, "space", up)
    below = lax.ppermute(top, "space", [(j, i) for i, j in up])

    same = pl.BlockSpec((2, half_cols, cols), lambda i: (0, 0, 0))
    pieces = pl.pallas_call(
        functools.partial(filter_kernel, parts),
        out_shape=[shape(piece, cols)] * parts,
        grid=(rows // ROW_BLOCK,),
        in_specs=[
            scalars(), scalars(), scalars(),
            pl.BlockSpec((ROW_BLOCK, grid_cols, cols), lambda i: (i, 0, 0)),
            pl.BlockSpec((ROW_BLOCK, grid_cols), lambda i: (i, 0)),
            same, same,
        ],
        out_specs=[pl.BlockSpec((piece, cols), lambda i: (0, 0))] * parts,
        scratch_shapes=[
            pltpu.VMEM((grid_cols, ROW_BLOCK), F32),
            pltpu.VMEM((rows + 4, half_cols, cols), F32),
            pltpu.VMEM((cells, cols), F32),
        ],
        compiler_params=params(),
        name="filter",
    )(me, taps_rows, taps_cols, snapshots, land_mask, above, below)

    factors = [pieces[0]] + [swap(pieces[k], "tm", k) for k in range(1, parts)]

    probe_sum = pl.pallas_call(
        functools.partial(probe_kernel, parts),
        out_shape=shape(cols, cols),
        in_specs=[scalars()] + [whole()] * (parts + 1),
        out_specs=whole(),
        compiler_params=params(),
        cost_estimate=pl.CostEstimate(flops=12 * cells * cols * cols, bytes_accessed=8 * cells * cols, transcendentals=0),
        name="probe",
    )(me, *pieces, probes.reshape(cells, cols))

    def over_space(x):
        bit = 1
        while bit < patches:
            x = x + swap(x, "space", bit)
            bit *= 2
        return x

    probe_sum = over_space(probe_sum)

    blocks = parts * (parts + 1) // 2
    size = blocks * cols // parts
    groups = send_groups(parts)
    sends = pl.pallas_call(
        functools.partial(gram_kernel, parts),
        out_shape=[shape(len(g), size, cols) for g in groups],
        in_specs=[scalars()] + [whole()] * parts,
        out_specs=[whole()] * len(groups),
        scratch_shapes=[pltpu.VMEM((piece, parts * cols), F32), pltpu.VMEM((blocks * cols, cols), F32)],
        compiler_params=params(),
        name="gram",
    )(me, *factors)
    sends = list(sends)
    for step in range(len(groups) - 1):
        got = swap(sends[step], "tm", 1 << step)
        order = [k ^ (1 << step) for k in groups[step]]
        for later in range(step + 1, len(groups)):
            pick = [order.index(k) for k in groups[later]]
            sends[later] = sends[later] + jnp.stack([got[i] for i in pick])
    gram_piece = over_space(sends[-1][0])

    have, bit = {0: gram_piece}, parts // 2
    while bit:
        have.update({k ^ bit: swap(x, "tm", bit) for k, x in list(have.items())})
        bit //= 2

    width = cols // parts
    sent = pl.pallas_call(
        functools.partial(merge_kernel, parts),
        out_shape=[shape(width, piece + cols)] * parts,
        in_specs=[scalars()] + [whole()] * (2 * parts + 1),
        out_specs=[whole()] * parts,
        scratch_shapes=[
            pltpu.VMEM((blocks * cols, cols), F32),
            pltpu.VMEM((parts * cols, cols), F32),
            pltpu.VMEM((cols, piece + cols), F32),
        ],
        compiler_params=params(),
        name="merge",
    )(me, *[have[k] for k in range(parts)], *factors, probe_sum)
    last = [sent[0]] + [swap(sent[k], "tm", k) for k in range(1, parts)]

    basis, coefficients = pl.pallas_call(
        functools.partial(final_kernel, parts),
        out_shape=(shape(cells, width), shape(width, cols)),
        in_specs=[scalars()] + [whole()] * parts,
        out_specs=(whole(), whole()),
        compiler_params=params(),
        name="final",
    )(me, *last)
    return basis.reshape(half_rows, half_cols, width), coefficients


def solution(mesh):
    placed = (P("space", None, "tm"), P("space", None), P(), P(), P("space", None, None))
    return jax.shard_map(
        local,
        mesh=mesh,
        in_specs=placed,
        out_specs=(P("space", None, "tm"), P("tm", None)),
        check_vma=False,
    )
```

time: 324 us -> 106 us (0.33)
  waiting for transfers between devices: 236 us -> 52 us
  matrix products: 44.9 us -> 0 us
  Pallas kernels: 0 us -> 22.5 us
  between operations: 16.9 us -> 0.8 us
  starting transfers between devices: 8.2 us -> 23.2 us
  other arithmetic: 10.8 us -> 0.13 us
    psum x3 -> x0, waiting for transfers between devices: 208 us -> none  [the longest x2 141 us: merge_level(): gram_total = lax.psum(partial_gram, 'space')]
    dot_general x39 -> x0, matrix products: 44.9 us -> none  [the longest x1 8.93 us: local(): jnp.einsum('jy,xys->xjs', across, ocean_field, precision=exact_dot)]
    ppermute x4 -> x19, waiting for transfers between devices: 28.3 us -> 52 us  [the longest x17 47.2 us: swap(): return lax.ppermute(x, axis, [(i, i ^ mask) for i in range(count)])]
    pallas_call x0 -> x6, Pallas kernels: none -> 22.5 us  [the longest x1 14.9 us: local(): pl.pallas_call(functools.partial(merge_kernel, parts), out_shape=[shape(w...]
    ppermute x4 -> x19, starting transfers between devices: 7.68 us -> 23.2 us  [the longest x17 17.1 us: swap(): return lax.ppermute(x, axis, [(i, i ^ mask) for i in range(count)])]
    reduce_sum x4 -> x0, other arithmetic: 6.43 us -> none  [the longest x2 3.25 us: merge_level(): norm_scale = jnp.sqrt(jnp.sum(shifted * shifted, axis=(1, 2)) + 1e-06)]
    unnamed x11 -> x17, local copies, waits for them, and re-layouts: 2.05 us -> 6.91 us
    select_n x2 -> x0, other arithmetic: 3.36 us -> none  [local(): lower_part = jnp.where(is_upper, partner_fac, merged)]
  transfers between devices with their start and end apart: 7 -> 19, of which waited for: 7 -> 15; matrix products, arithmetic and copies ran while one was open for 1% -> 0% of each run, Pallas kernels for 0% -> 1%
where the time goes in v1:
time: 106 us
  waiting for transfers between devices  52 us (49%)
  starting transfers between devices  23.2 us (22%)
  Pallas kernels  22.5 us (21%)
  local copies, waits for them, and re-layouts  6.91 us (7%)
    ppermute x17, waiting for transfers between devices, swap(): return lax.ppermute(x, axis, [(i, i ^ mask) for i in range(count)])  47.2 us
    ppermute x17, starting transfers between devices, swap(): return lax.ppermute(x, axis, [(i, i ^ mask) for i in range(count)])  17.1 us
    pallas_call x1, Pallas kernels, local(): pl.pallas_call(functools.partial(merge_kernel, parts), out_shape=[shape(w...  14.9 us
    unnamed x17, local copies, waits for them, and re-layouts  6.91 us
    ppermute x1, starting transfers between devices, local(): above = lax.ppermute(end, 'space', up)  4.85 us
    ppermute x1, waiting for transfers between devices, local(): below = lax.ppermute(top, 'space', [(j, i) for i, j in up])  4.27 us
    pallas_call x1, Pallas kernels, local(): pl.pallas_call(functools.partial(filter_kernel, parts), out_shape=[shape(...  3.07 us
  transfers between devices with their start and end apart: 19, of which 15 were waited for; matrix products, arithmetic and copies ran while one was open for 0% of the time, Pallas kernels for 1%

profile of v1, /device:TPU:0, one launch (start us, length us, event | category | flops | bytes accessed | tf_op | source)
XLA Modules:
  0.0 105.5 jit_solution(4077536899060087907)
XLA Ops:
  0.6 2.2 %copy-done = f32[64,128,128]{2,1,0:T(8,128)S(1)} copy-done((f32[64,128,128]{2,1,0:T(8,128)S(1)}, f32[64,128,128]{2,1,0:T(8,128)}, u32[]{:S(2)}) %copy-start) | copy-done | bytes 4194328
  5.1 4.8 %collective-permute-start = (f32[2,64,128]{2,1,0:T(8,128)S(1)}, f32[2,64,128]{2,1,0:T(8,128)S(1)}, u32[]{:S(2)}, u32[]{:S(2)}) collective-permute-start(f32[2,64,128]{2,1,0:T(8,128)S(1)} %get-tuple-element.17), channel_id=1, source_target_pairs={{0,1},{1,2},{2,3},{3,4},{4,5},{5,6},{6,7},{8,9},{9,10},{10,11},{11... | collective-permute-start | bytes 196616 | tf_op jit(solution)/shard_map/ppermute | solution.py:283
  11.8 4.3 %collective-permute-done.1.below_ref = f32[2,64,128]{2,1,0:T(8,128)S(1)} collective-permute-done((f32[2,64,128]{2,1,0:T(8,128)S(1)}, f32[2,64,128]{2,1,0:T(8,128)S(1)}, u32[]{:S(2)}, u32[]{:S(2)}) %collective-permute-start.1) | collective-permute-done | bytes 65568 | tf_op jit(solution)/shard_map/ppermute | solution.py:284
  16.1 2.2 %copy-done.1 = f32[64,128,128]{2,1,0:T(8,128)S(1)} copy-done((f32[64,128,128]{2,1,0:T(8,128)S(1)}, f32[64,128,128]{2,1,0:T(8,128)}, u32[]{:S(2)}) %copy-start.1) | copy-done | bytes 4194328
  18.3 3.1 %filter.1 = (f32[512,128]{1,0:T(8,128)S(1)}, f32[512,128]{1,0:T(8,128)S(1)}, f32[512,128]{1,0:T(8,128)S(1)}, f32[512,128]{1,0:T(8,128)S(1)}) custom-call(s32[1]{0:T(128)} %bitcast.me_ref, f32[6]{0:T(128)S(1)} %copy-done.7, f32[6]{0:T(128)S(1)} %copy-done.6, f32[64,128,128]{2,1,0:T(8,128)S(1)} %copy-done.1, s32[64,128]{1,0:T(8,128)S(1)} %copy-done.4, ...), custom_call_target="tpu_custom_call" | custom-call | tf_op jit(solution)/shard_map/filter/pallas_call | solution.py:287
  21.4 1.6 %collective-permute-start.3 = (f32[512,128]{1,0:T(8,128)S(1)}, f32[512,128]{1,0:T(8,128)S(1)}, u32[]{:S(2)}, u32[]{:S(2)}) collective-permute-start(f32[512,128]{1,0:T(8,128)S(1)} %get-tuple-element.21.refs_2_), channel_id=1, source_target_pairs={{0,16},{8,24},{16,0},{24,8},{1,17},{9,25},{17,1},{25,9},{2,18},{10... | collective-permute-start | bytes 786440 | tf_op jit(solution)/shard_map/ppermute | solution.py:32
  23.3 7.3 %collective-permute-done.3.refs_2_.refs_6_ = f32[512,128]{1,0:T(8,128)S(1)} collective-permute-done((f32[512,128]{1,0:T(8,128)S(1)}, f32[512,128]{1,0:T(8,128)S(1)}, u32[]{:S(2)}, u32[]{:S(2)}) %collective-permute-start.3) | collective-permute-done | bytes 262176 | tf_op jit(solution)/shard_map/ppermute | solution.py:32
  30.6 4.7 %collective-permute-done.4.refs_3_.refs_7_ = f32[512,128]{1,0:T(8,128)S(1)} collective-permute-done((f32[512,128]{1,0:T(8,128)S(1)}, f32[512,128]{1,0:T(8,128)S(1)}, u32[]{:S(2)}, u32[]{:S(2)}) %collective-permute-start.4) | collective-permute-done | bytes 262176 | tf_op jit(solution)/shard_map/ppermute | solution.py:32
  35.3 1.8 %gram.1 = (f32[2,320,128]{2,1,0:T(8,128)S(1)}, f32[1,320,128]{2,1,0:T(8,128)S(1)}, f32[1,320,128]{2,1,0:T(8,128)S(1)}) custom-call(s32[1]{0:T(128)} %bitcast.me_ref, f32[512,128]{1,0:T(8,128)S(1)} %get-tuple-element.19.refs_0_.refs_4_, f32[512,128]{1,0:T(8,128)S(1)} %collective-permute-done.2.refs_1_.refs_5_, ...), custom_call_target="tpu_custom_call" | custom-call | tf_op jit(solution)/shard_map/gram/pallas_call | solution.py:331
  38.8 1.6 %collective-permute-start.6 = (f32[1,320,128]{2,1,0:T(8,128)S(1)}, f32[1,320,128]{2,1,0:T(8,128)S(1)}, u32[]{:S(2)}, u32[]{:S(2)}) collective-permute-start(f32[1,320,128]{2,1,0:T(8,128)S(1)} %slice_add_fusion), channel_id=1, source_target_pairs={{0,16},{8,24},{16,0},{24,8},{1,17},{9,25},{17,1},{25,9},{2,18},{10... | collective-permute-start | bytes 491528 | tf_op jit(solution)/shard_map/ppermute | solution.py:32
  40.4 4.9 %collective-permute-done.6 = f32[1,320,128]{2,1,0:T(8,128)S(1)} collective-permute-done((f32[1,320,128]{2,1,0:T(8,128)S(1)}, f32[1,320,128]{2,1,0:T(8,128)S(1)}, u32[]{:S(2)}, u32[]{:S(2)}) %collective-permute-start.6) | collective-permute-done | bytes 163872 | tf_op jit(solution)/shard_map/ppermute | solution.py:32
  45.3 2.5 %collective-permute-start.7 = (f32[320,128]{1,0:T(8,128)S(1)}, f32[320,128]{1,0:T(8,128)S(1)}, u32[]{:S(2)}, u32[]{:S(2)}) collective-permute-start(f32[320,128]{1,0:T(8,128)S(1)} %fusion.1), channel_id=1, source_target_pairs={{0,1},{1,0},{2,3},{3,2},{4,5},{5,4},{6,7},{7,6},{8,9},{9,8},{10,11... | collective-permute-start | bytes 491528 | tf_op jit(solution)/shard_map/ppermute | solution.py:32
  47.8 3.8 %collective-permute-done.7 = f32[320,128]{1,0:T(8,128)S(1)} collective-permute-done((f32[320,128]{1,0:T(8,128)S(1)}, f32[320,128]{1,0:T(8,128)S(1)}, u32[]{:S(2)}, u32[]{:S(2)}) %collective-permute-start.7) | collective-permute-done | bytes 163872 | tf_op jit(solution)/shard_map/ppermute | solution.py:32
  51.7 1.6 %collective-permute-start.8 = (f32[320,128]{1,0:T(8,128)S(1)}, f32[320,128]{1,0:T(8,128)S(1)}, u32[]{:S(2)}, u32[]{:S(2)}) collective-permute-start(f32[320,128]{1,0:T(8,128)S(1)} %add.30), channel_id=1, source_target_pairs={{0,2},{1,3},{2,0},{3,1},{4,6},{5,7},{6,4},{7,5},{8,10},{9,11},{10,... | collective-permute-start | bytes 491528 | tf_op jit(solution)/shard_map/ppermute | solution.py:32
  53.3 3.7 %collective-permute-done.8 = f32[320,128]{1,0:T(8,128)S(1)} collective-permute-done((f32[320,128]{1,0:T(8,128)S(1)}, f32[320,128]{1,0:T(8,128)S(1)}, u32[]{:S(2)}, u32[]{:S(2)}) %collective-permute-start.8) | collective-permute-done | bytes 163872 | tf_op jit(solution)/shard_map/ppermute | solution.py:32
  57.1 2.7 %collective-permute-start.9 = (f32[320,128]{1,0:T(8,128)S(1)}, f32[320,128]{1,0:T(8,128)S(1)}, u32[]{:S(2)}, u32[]{:S(2)}) collective-permute-start(f32[320,128]{1,0:T(8,128)S(1)} %add.31), channel_id=1, source_target_pairs={{0,4},{1,5},{2,6},{3,7},{4,0},{5,1},{6,2},{7,3},{8,12},{9,13},{10,... | collective-permute-start | bytes 491528 | tf_op jit(solution)/shard_map/ppermute | solution.py:32
  59.7 5.6 %collective-permute-done.9 = f32[320,128]{1,0:T(8,128)S(1)} collective-permute-done((f32[320,128]{1,0:T(8,128)S(1)}, f32[320,128]{1,0:T(8,128)S(1)}, u32[]{:S(2)}, u32[]{:S(2)}) %collective-permute-start.9) | collective-permute-done | bytes 163872 | tf_op jit(solution)/shard_map/ppermute | solution.py:32
  65.4 1.6 %collective-permute-start.11 = (f32[320,128]{1,0:T(8,128)S(1)}, f32[320,128]{1,0:T(8,128)S(1)}, u32[]{:S(2)}, u32[]{:S(2)}) collective-permute-start(f32[320,128]{1,0:T(8,128)S(1)} %add.32.refs_0_), channel_id=1, source_target_pairs={{0,16},{8,24},{16,0},{24,8},{1,17},{9,25},{17,1},{25,9},{2,18},{10... | collective-permute-start | bytes 491528 | tf_op jit(solution)/shard_map/ppermute | solution.py:32
  68.1 1.6 %collective-permute-start.13 = (f32[128,128]{1,0:T(8,128)S(1)}, f32[128,128]{1,0:T(8,128)S(1)}, u32[]{:S(2)}, u32[]{:S(2)}) collective-permute-start(f32[128,128]{1,0:T(8,128)S(1)} %probe.1), channel_id=1, source_target_pairs={{0,1},{1,0},{2,3},{3,2},{4,5},{5,4},{6,7},{7,6},{8,9},{9,8},{10,11... | collective-permute-start | bytes 196616 | tf_op jit(solution)/shard_map/ppermute | solution.py:32
  70.8 1.6 %collective-permute-done.13 = f32[128,128]{1,0:T(8,128)S(1)} collective-permute-done((f32[128,128]{1,0:T(8,128)S(1)}, f32[128,128]{1,0:T(8,128)S(1)}, u32[]{:S(2)}, u32[]{:S(2)}) %collective-permute-start.13) | collective-permute-done | bytes 65568 | tf_op jit(solution)/shard_map/ppermute | solution.py:32
  72.5 4.3 %collective-permute-done.14 = f32[128,128]{1,0:T(8,128)S(1)} collective-permute-done((f32[128,128]{1,0:T(8,128)S(1)}, f32[128,128]{1,0:T(8,128)S(1)}, u32[]{:S(2)}, u32[]{:S(2)}) %collective-permute-start.14) | collective-permute-done | bytes 65568 | tf_op jit(solution)/shard_map/ppermute | solution.py:32
  78.0 4.4 %collective-permute-done.15 = f32[128,128]{1,0:T(8,128)S(1)} collective-permute-done((f32[128,128]{1,0:T(8,128)S(1)}, f32[128,128]{1,0:T(8,128)S(1)}, u32[]{:S(2)}, u32[]{:S(2)}) %collective-permute-start.15) | collective-permute-done | bytes 65568 | tf_op jit(solution)/shard_map/ppermute | solution.py:32
  82.4 14.9 %merge.1 = (f32[32,640]{1,0:T(8,128)S(1)}, f32[32,640]{1,0:T(8,128)S(1)}, f32[32,640]{1,0:T(8,128)S(1)}, f32[32,640]{1,0:T(8,128)S(1)}) custom-call(s32[1]{0:T(128)} %bitcast.me_ref, f32[320,128]{1,0:T(8,128)S(1)} %add.32.refs_0_, f32[320,128]{1,0:T(8,128)S(1)} %collective-permute-done.10.refs_1_, f32[320,128]{1,0:T(8,128)S(1)} %collective-permute-done.11.refs_2_, ...), custom_call_target="tpu_custom_call" | custom-call | tf_op jit(solution)/shard_map/merge/pallas_call | solution.py:355
  99.3 3.4 %collective-permute-done.17.refs_2_ = f32[32,640]{1,0:T(8,128)S(1)} collective-permute-done((f32[32,640]{1,0:T(8,128)S(1)}, f32[32,640]{1,0:T(8,128)S(1)}, u32[]{:S(2)}, u32[]{:S(2)}) %collective-permute-start.17) | collective-permute-done | bytes 81952 | tf_op jit(solution)/shard_map/ppermute | solution.py:32
  (45 shorter events, 14.6 us)
Async XLA Ops:
  0.6 2.2 %copy-start = (f32[64,128,128]{2,1,0:T(8,128)S(1)}, f32[64,128,128]{2,1,0:T(8,128)}, u32[]{:S(2)}) copy-start(f32[64,128,128]{2,1,0:T(8,128)} %snap_ref.1) | copy-start | bytes 12582916
  4.2 11.8 %copy-start.4 = (s32[64,128]{1,0:T(8,128)S(1)}, s32[64,128]{1,0:T(8,128)}, u32[]{:S(2)}) copy-start(s32[64,128]{1,0:T(8,128)} %mask_ref.3) | copy-start | bytes 98308
  4.2 11.8 %copy-start.6 = (f32[6]{0:T(128)S(1)}, f32[6]{0:T(128)}, u32[]{:S(2)}) copy-start(f32[6]{0:T(128)} %ctaps_ref.1) | copy-start | bytes 76
  4.2 11.8 %copy-start.7 = (f32[6]{0:T(128)S(1)}, f32[6]{0:T(128)}, u32[]{:S(2)}) copy-start(f32[6]{0:T(128)} %rtaps_ref.1) | copy-start | bytes 76
  4.2 62.7 %copy-start.2 = (f32[32,64,128]{2,1,0:T(8,128)S(1)}, f32[32,64,128]{2,1,0:T(8,128)}, u32[]{:S(2)}) copy-start(f32[32,64,128]{2,1,0:T(8,128)} %param.9) | copy-start | bytes 3145732
  5.1 6.7 %collective-permute-start = (f32[2,64,128]{2,1,0:T(8,128)S(1)}, f32[2,64,128]{2,1,0:T(8,128)S(1)}, u32[]{:S(2)}, u32[]{:S(2)}) collective-permute-start(f32[2,64,128]{2,1,0:T(8,128)S(1)} %get-tuple-element.17), channel_id=1, source_target_pairs={{0,1},{1,2},{2,3},{3,4},{4,5},{5,6},{6,7},{8,9},{9,10},{10,11},{11... | collective-permute-start | bytes 196616 | tf_op jit(solution)/shard_map/ppermute | solution.py:283
  9.9 6.2 %collective-permute-start.1 = (f32[2,64,128]{2,1,0:T(8,128)S(1)}, f32[2,64,128]{2,1,0:T(8,128)S(1)}, u32[]{:S(2)}, u32[]{:S(2)}) collective-permute-start(f32[2,64,128]{2,1,0:T(8,128)S(1)} %get-tuple-element.18), channel_id=1, source_target_pairs={{1,0},{2,1},{3,2},{4,3},{5,4},{6,5},{7,6},{9,8},{10,9},{11,10},{12... | collective-permute-start | bytes 196616 | tf_op jit(solution)/shard_map/ppermute | solution.py:284
  21.4 1.9 %collective-permute-start.2 = (f32[512,128]{1,0:T(8,128)S(1)}, f32[512,128]{1,0:T(8,128)S(1)}, u32[]{:S(2)}, u32[]{:S(2)}) collective-permute-start(f32[512,128]{1,0:T(8,128)S(1)} %get-tuple-element.20.refs_1_), channel_id=1, source_target_pairs={{0,8},{8,0},{16,24},{24,16},{1,9},{9,1},{17,25},{25,17},{2,10},{10... | collective-permute-start | bytes 786440 | tf_op jit(solution)/shard_map/ppermute | solution.py:32
  21.4 9.2 %collective-permute-start.3 = (f32[512,128]{1,0:T(8,128)S(1)}, f32[512,128]{1,0:T(8,128)S(1)}, u32[]{:S(2)}, u32[]{:S(2)}) collective-permute-start(f32[512,128]{1,0:T(8,128)S(1)} %get-tuple-element.21.refs_2_), channel_id=1, source_target_pairs={{0,16},{8,24},{16,0},{24,8},{1,17},{9,25},{17,1},{25,9},{2,18},{10... | collective-permute-start | bytes 786440 | tf_op jit(solution)/shard_map/ppermute | solution.py:32
  23.0 12.3 %collective-permute-start.4 = (f32[512,128]{1,0:T(8,128)S(1)}, f32[512,128]{1,0:T(8,128)S(1)}, u32[]{:S(2)}, u32[]{:S(2)}) collective-permute-start(f32[512,128]{1,0:T(8,128)S(1)} %get-tuple-element.22.refs_3_), channel_id=1, source_target_pairs={{0,24},{8,16},{16,8},{24,0},{1,25},{9,17},{17,9},{25,1},{2,26},{10... | collective-permute-start | bytes 786440 | tf_op jit(solution)/shard_map/ppermute | solution.py:32
  37.1 1.7 %collective-permute-start.5 = (f32[2,320,128]{2,1,0:T(8,128)S(1)}, f32[2,320,128]{2,1,0:T(8,128)S(1)}, u32[]{:S(2)}, u32[]{:S(2)}) collective-permute-start(f32[2,320,128]{2,1,0:T(8,128)S(1)} %get-tuple-element.24), channel_id=1, source_target_pairs={{0,8},{8,0},{16,24},{24,16},{1,9},{9,1},{17,25},{25,17},{2,10},{10... | collective-permute-start | bytes 983048 | tf_op jit(solution)/shard_map/ppermute | solution.py:32
  38.8 6.4 %collective-permute-start.6 = (f32[1,320,128]{2,1,0:T(8,128)S(1)}, f32[1,320,128]{2,1,0:T(8,128)S(1)}, u32[]{:S(2)}, u32[]{:S(2)}) collective-permute-start(f32[1,320,128]{2,1,0:T(8,128)S(1)} %slice_add_fusion), channel_id=1, source_target_pairs={{0,16},{8,24},{16,0},{24,8},{1,17},{9,25},{17,1},{25,9},{2,18},{10... | collective-permute-start | bytes 491528 | tf_op jit(solution)/shard_map/ppermute | solution.py:32
  45.3 6.3 %collective-permute-start.7 = (f32[320,128]{1,0:T(8,128)S(1)}, f32[320,128]{1,0:T(8,128)S(1)}, u32[]{:S(2)}, u32[]{:S(2)}) collective-permute-start(f32[320,128]{1,0:T(8,128)S(1)} %fusion.1), channel_id=1, source_target_pairs={{0,1},{1,0},{2,3},{3,2},{4,5},{5,4},{6,7},{7,6},{8,9},{9,8},{10,11... | collective-permute-start | bytes 491528 | tf_op jit(solution)/shard_map/ppermute | solution.py:32
  51.7 5.4 %collective-permute-start.8 = (f32[320,128]{1,0:T(8,128)S(1)}, f32[320,128]{1,0:T(8,128)S(1)}, u32[]{:S(2)}, u32[]{:S(2)}) collective-permute-start(f32[320,128]{1,0:T(8,128)S(1)} %add.30), channel_id=1, source_target_pairs={{0,2},{1,3},{2,0},{3,1},{4,6},{5,7},{6,4},{7,5},{8,10},{9,11},{10,... | collective-permute-start | bytes 491528 | tf_op jit(solution)/shard_map/ppermute | solution.py:32
  57.1 8.3 %collective-permute-start.9 = (f32[320,128]{1,0:T(8,128)S(1)}, f32[320,128]{1,0:T(8,128)S(1)}, u32[]{:S(2)}, u32[]{:S(2)}) collective-permute-start(f32[320,128]{1,0:T(8,128)S(1)} %add.31), channel_id=1, source_target_pairs={{0,4},{1,5},{2,6},{3,7},{4,0},{5,1},{6,2},{7,3},{8,12},{9,13},{10,... | collective-permute-start | bytes 491528 | tf_op jit(solution)/shard_map/ppermute | solution.py:32
  65.4 5.4 %collective-permute-start.11 = (f32[320,128]{1,0:T(8,128)S(1)}, f32[320,128]{1,0:T(8,128)S(1)}, u32[]{:S(2)}, u32[]{:S(2)}) collective-permute-start(f32[320,128]{1,0:T(8,128)S(1)} %add.32.refs_0_), channel_id=1, source_target_pairs={{0,16},{8,24},{16,0},{24,8},{1,17},{9,25},{17,1},{25,9},{2,18},{10... | collective-permute-start | bytes 491528 | tf_op jit(solution)/shard_map/ppermute | solution.py:32
  68.1 4.3 %collective-permute-start.13 = (f32[128,128]{1,0:T(8,128)S(1)}, f32[128,128]{1,0:T(8,128)S(1)}, u32[]{:S(2)}, u32[]{:S(2)}) collective-permute-start(f32[128,128]{1,0:T(8,128)S(1)} %probe.1), channel_id=1, source_target_pairs={{0,1},{1,0},{2,3},{3,2},{4,5},{5,4},{6,7},{7,6},{8,9},{9,8},{10,11... | collective-permute-start | bytes 196616 | tf_op jit(solution)/shard_map/ppermute | solution.py:32
  69.6 12.8 %collective-permute-start.10 = (f32[320,128]{1,0:T(8,128)S(1)}, f32[320,128]{1,0:T(8,128)S(1)}, u32[]{:S(2)}, u32[]{:S(2)}) collective-permute-start(f32[320,128]{1,0:T(8,128)S(1)} %add.32.refs_0_), channel_id=1, source_target_pairs={{0,8},{8,0},{16,24},{24,16},{1,9},{9,1},{17,25},{25,17},{2,10},{10... | collective-permute-start | bytes 491528 | tf_op jit(solution)/shard_map/ppermute | solution.py:32
  70.8 11.7 %collective-permute-start.12 = (f32[320,128]{1,0:T(8,128)S(1)}, f32[320,128]{1,0:T(8,128)S(1)}, u32[]{:S(2)}, u32[]{:S(2)}) collective-permute-start(f32[320,128]{1,0:T(8,128)S(1)} %collective-permute-done.11.refs_2_), channel_id=1, source_target_pairs={{0,8},{8,0},{16,24},{24,16},{1,9},{9,1},{17,25},{25,17},{2,10},{10... | collective-permute-start | bytes 491528 | tf_op jit(solution)/shard_map/ppermute | solution.py:32
  72.4 4.3 %collective-permute-start.14 = (f32[128,128]{1,0:T(8,128)S(1)}, f32[128,128]{1,0:T(8,128)S(1)}, u32[]{:S(2)}, u32[]{:S(2)}) collective-permute-start(f32[128,128]{1,0:T(8,128)S(1)} %add.33), channel_id=1, source_target_pairs={{0,2},{1,3},{2,0},{3,1},{4,6},{5,7},{6,4},{7,5},{8,10},{9,11},{10,... | collective-permute-start | bytes 196616 | tf_op jit(solution)/shard_map/ppermute | solution.py:32
  76.7 5.7 %collective-permute-start.15 = (f32[128,128]{1,0:T(8,128)S(1)}, f32[128,128]{1,0:T(8,128)S(1)}, u32[]{:S(2)}, u32[]{:S(2)}) collective-permute-start(f32[128,128]{1,0:T(8,128)S(1)} %add.34), channel_id=1, source_target_pairs={{0,4},{1,5},{2,6},{3,7},{4,0},{5,1},{6,2},{7,3},{8,12},{9,13},{10,... | collective-permute-start | bytes 196616 | tf_op jit(solution)/shard_map/ppermute | solution.py:32
  97.3 1.9 %collective-permute-start.16 = (f32[32,640]{1,0:T(8,128)S(1)}, f32[32,640]{1,0:T(8,128)S(1)}, u32[]{:S(2)}, u32[]{:S(2)}) collective-permute-start(f32[32,640]{1,0:T(8,128)S(1)} %get-tuple-element.27), channel_id=1, source_target_pairs={{0,8},{8,0},{16,24},{24,16},{1,9},{9,1},{17,25},{25,17},{2,10},{10... | collective-permute-start | bytes 245768 | tf_op jit(solution)/shard_map/ppermute | solution.py:32
  97.4 5.3 %collective-permute-start.17 = (f32[32,640]{1,0:T(8,128)S(1)}, f32[32,640]{1,0:T(8,128)S(1)}, u32[]{:S(2)}, u32[]{:S(2)}) collective-permute-start(f32[32,640]{1,0:T(8,128)S(1)} %get-tuple-element.28), channel_id=1, source_target_pairs={{0,16},{8,24},{16,0},{24,8},{1,17},{9,25},{17,1},{25,9},{2,18},{10... | collective-permute-start | bytes 245768 | tf_op jit(solution)/shard_map/ppermute | solution.py:32
  98.0 5.6 %collective-permute-start.18 = (f32[32,640]{1,0:T(8,128)S(1)}, f32[32,640]{1,0:T(8,128)S(1)}, u32[]{:S(2)}, u32[]{:S(2)}) collective-permute-start(f32[32,640]{1,0:T(8,128)S(1)} %get-tuple-element.29), channel_id=1, source_target_pairs={{0,24},{8,16},{16,8},{24,0},{1,25},{9,17},{17,9},{25,1},{2,26},{10... | collective-permute-start | bytes 245768 | tf_op jit(solution)/shard_map/ppermute | solution.py:32
  (3 other events, 3.6 us)

commit v2 on v1

v2 whole, which is shorter than its diff:
```python
import functools

import jax
import jax.numpy as jnp
from jax import lax
from jax.experimental import pallas as pl
from jax.experimental.pallas import tpu as pltpu
from jax.sharding import PartitionSpec as P

SIGN_STEPS = 8
TAPS = 6
CHUNK = 8
exact = lax.Precision.HIGHEST
F32 = jnp.float32
VMEM_LIMIT = 48 * 1024 * 1024


def params():
    return pltpu.CompilerParams(vmem_limit_bytes=VMEM_LIMIT)


def whole():
    return pl.BlockSpec(memory_space=pltpu.VMEM)


def scalars():
    return pl.BlockSpec(memory_space=pltpu.SMEM)


def swap(x, axis, mask):
    count = lax.axis_size(axis)
    return lax.ppermute(x, axis, [(i, i ^ mask) for i in range(count)])


def swap_both(x, mask):
    parts, patches = lax.axis_size("tm"), lax.axis_size("space")
    route = []
    for t in range(parts):
        for s in range(patches):
            there = (t ^ (mask % parts)) * patches + (s ^ (mask // parts))
            route.append((t * patches + s, there))
    return lax.ppermute(x, ("tm", "space"), route)


def shift_rows(x, by):
    edge = jnp.zeros((1, x.shape[1]), x.dtype)
    if by > 0:
        return jnp.concatenate([edge, x[:-1]], axis=0)
    return jnp.concatenate([x[1:], edge], axis=0)


def narrow_row(snap_ref, x, mask_even, mask_odd, taps):
    half = snap_ref.shape[1] // 2
    even = snap_ref[x, pl.ds(0, half, stride=2), :] * mask_even
    odd = snap_ref[x, pl.ds(1, half, stride=2), :] * mask_odd
    before = taps[0] * even + taps[1] * odd
    here = taps[2] * even + taps[3] * odd
    after = taps[4] * even + taps[5] * odd
    return shift_rows(before, 1) + here + shift_rows(after, -1)


def filter_kernel(parts, me_ref, rtaps_ref, ctaps_ref, snap_hbm, mask_ref, *rest):
    bigs, (small_ref, up_ref, down_ref) = rest[:parts], rest[parts:parts + 3]
    snaps, sems, mask_t, narrowed, filtered = rest[parts + 3:]
    rows, cells = snaps.shape[0], narrowed.shape[1]
    chunks = rows // CHUNK

    def fetch(c):
        at = pl.ds(c * CHUNK, CHUNK)
        return pltpu.make_async_copy(snap_hbm.at[at], snaps.at[at], sems.at[c])

    for c in range(chunks):
        fetch(c).start()
    ctaps = [ctaps_ref[k] for k in range(TAPS)]
    rtaps = [rtaps_ref[k] for k in range(TAPS)]
    edge = jnp.zeros((2,) + narrowed.shape[1:], F32)
    narrowed[0:2] = edge
    narrowed[rows + 2:rows + 4] = edge

    def narrow(c, carry):
        fetch(c).wait()
        base = pl.multiple_of(c * CHUNK, CHUNK)
        mask_t[...] = mask_ref[pl.ds(base, CHUNK), :].astype(F32).T
        even = mask_t[pl.ds(0, cells, stride=2), :]
        odd = mask_t[pl.ds(1, cells, stride=2), :]
        for x in range(CHUNK):
            row = narrow_row(snaps, base + x, even[:, x:x + 1], odd[:, x:x + 1], ctaps)
            narrowed[2 + base + x] = row
        return carry

    lax.fori_loop(0, chunks, narrow, 0)
    for i in range(rows // 2):
        total = rtaps[0] * narrowed[2 * i]
        for k in range(1, TAPS):
            total = total + rtaps[k] * narrowed[2 * i + k]
        filtered[i * cells:(i + 1) * cells, :] = total
    up_ref[...] = rtaps[4] * narrowed[2] + rtaps[5] * narrowed[3]
    down_ref[...] = rtaps[0] * narrowed[rows] + rtaps[1] * narrowed[rows + 1]
    me = me_ref[0]
    piece = filtered.shape[0] // parts
    for k in range(parts):
        inner = pl.multiple_of((me ^ k) * piece + cells, 8)
        bigs[k][...] = filtered[pl.ds(inner, piece - 2 * cells), :]
    for d in range(parts):
        small_ref[2 * d * cells:(2 * d + 1) * cells, :] = filtered[d * piece:d * piece + cells, :]
        small_ref[(2 * d + 1) * cells:(2 * d + 2) * cells, :] = filtered[(d + 1) * piece - cells:(d + 1) * piece, :]


def edge_kernel(parts, me_ref, small_ref, above_ref, below_ref, *rest):
    outs, (held,) = rest[:parts], rest[parts:]
    held[...] = small_ref[...]
    cells = above_ref.shape[0]
    size = held.shape[0]
    held[:cells, :] = held[:cells, :] + above_ref[...]
    held[size - cells:, :] = held[size - cells:, :] + below_ref[...]
    me = me_ref[0]
    for k in range(parts):
        outs[k][...] = held[pl.ds(pl.multiple_of((me ^ k) * 2 * cells, 8), 2 * cells), :]


def probe_kernel(parts, me_ref, *refs):
    bigs, smalls, probes_ref, out_ref = refs[:parts], refs[parts:2 * parts], refs[2 * parts], refs[2 * parts + 1]
    me = me_ref[0]
    cells = smalls[0].shape[0] // 2
    inner = bigs[0].shape[0]
    piece = inner + 2 * cells
    total = None
    for k in range(parts):
        base = (me ^ k) * piece
        first = probes_ref[pl.ds(pl.multiple_of(base, 8), cells), :]
        middle = probes_ref[pl.ds(pl.multiple_of(base + cells, 8), inner), :]
        last = probes_ref[pl.ds(pl.multiple_of(base + cells + inner, 8), cells), :]
        mine = jnp.concatenate([bigs[k][...], smalls[k][...]], axis=0)
        there = jnp.concatenate([middle, first, last], axis=0)
        term = exact_dot(mine, there, ((0,), (0,)))
        total = term if total is None else total + term
    out_ref[...] = total


def block_order(parts):
    return [(a, b) for a in range(parts) for b in range(a, parts)]


def gram_kernel(parts, span, me_ref, *refs):
    bigs, smalls = refs[:parts], refs[parts:2 * parts]
    send_ref, keep_ref, wide, flat = refs[2 * parts:]
    me, owner = me_ref[0], me_ref[1]
    inner, cols = bigs[0].shape
    for k in range(parts):
        at = pl.ds(pl.multiple_of((me ^ k) * cols, cols), cols)
        wide[:inner, at] = bigs[k][...]
        wide[inner:, at] = smalls[k][...]
    where = {ab: j for j, ab in enumerate(block_order(parts))}
    for a in range(0, parts, 2):
        left = wide[:, a * cols:(a + 2) * cols]
        for b in range(a, parts, 2):
            right = wide[:, b * cols:(b + 2) * cols]
            prod = exact_dot(left, right, ((0,), (0,)))
            for i in range(2):
                for j in range(2):
                    if (a + i, b + j) in where:
                        at = where[a + i, b + j] * cols
                        flat[at:at + cols, :] = prod[i * cols:(i + 1) * cols, j * cols:(j + 1) * cols]
    size = flat.shape[0] // (parts * span)
    for k in range(parts * span):
        out = send_ref if k % 2 else keep_ref
        out[k // 2] = flat[pl.ds(pl.multiple_of((owner ^ k) * size, 8), size), :]


def split(x):
    high = x.astype(jnp.bfloat16)
    return high, (x - high.astype(F32)).astype(jnp.bfloat16)


def dot(a, b, dims):
    return lax.dot_general(a, b, (dims, ((), ())), preferred_element_type=F32)


def dot_parts(a, b, dims=((1,), (0,))):
    (ah, al), (bh, bl) = a, b
    return dot(ah, bh, dims) + (dot(ah, bl, dims) + dot(al, bh, dims))


def exact_dot(a, b, dims=((1,), (0,))):
    return lax.dot_general(a, b, (dims, ((), ())), precision=exact, preferred_element_type=F32)


def combine_of(grams):
    order = grams[0].shape[0]
    diagonal = lax.broadcasted_iota(jnp.int32, (order, order), 0) == lax.broadcasted_iota(jnp.int32, (order, order), 1)
    signs = []
    for gram in grams:
        mean = jnp.sum(jnp.where(diagonal, gram, 0.0)) / order
        shifted = jnp.where(diagonal, gram - mean, gram)
        signs.append(shifted / jnp.sqrt(jnp.sum(shifted * shifted, keepdims=True) + 1e-6))
    for _ in range(SIGN_STEPS):
        halves = [split(y) for y in signs]
        squares = [split(dot_parts(y, y)) for y in halves]
        cubes = [dot_parts(y, s) for y, s in zip(halves, squares)]
        signs = [1.5 * y - 0.5 * c for y, c in zip(signs, cubes)]
    half = order // 2
    combines = []
    for y in signs:
        projector = 0.5 * (jnp.where(diagonal, 1.0, 0.0) + y)
        combines.append(projector[:, :half] + projector[:, half:])
    return combines


def merge_kernel(parts, span, me_ref, even_ref, odd_ref, wide_ref, probe_ref, *refs):
    outs, (flat, weight, turned) = refs[:parts], refs[parts:]
    me, owner = me_ref[0], me_ref[1]
    size, cols = even_ref.shape[1:]
    for k in range(parts * span):
        source = odd_ref if k % 2 else even_ref
        flat[pl.ds(pl.multiple_of((owner ^ k) * size, 8), size), :] = source[k // 2]
    blocks = {ab: flat[j * cols:(j + 1) * cols, :] for j, ab in enumerate(block_order(parts))}
    weights, count = None, parts
    while count > 1:
        grams = []
        for p in range(0, count, 2):
            low = jnp.concatenate([blocks[p, p], blocks[p, p + 1]], axis=1)
            high = jnp.concatenate([blocks[p, p + 1].T, blocks[p + 1, p + 1]], axis=1)
            grams.append(jnp.concatenate([low, high], axis=0))
        combines = combine_of(grams)
        if weights is None:
            weights = combines
        else:
            per = len(weights) // len(combines)
            weights = [
                exact_dot(w, combines[i // per][(i % per) * cols:(i % per + 1) * cols, :])
                for i, w in enumerate(weights)
            ]
            weights = [jnp.concatenate(weights[i:i + per], axis=0) for i in range(0, len(weights), per)]
        merged = {}
        if count > 2:
            for p in range(count // 2):
                for q in range(p, count // 2):
                    if p == q:
                        cross = grams[p]
                    else:
                        cross = jnp.concatenate([
                            jnp.concatenate([blocks[2 * p + i, 2 * q], blocks[2 * p + i, 2 * q + 1]], axis=1)
                            for i in range(2)
                        ], axis=0)
                    right = exact_dot(cross, combines[q])
                    merged[p, q] = exact_dot(combines[p], right, ((0,), (0,)))
        blocks, count = merged, count // 2
    weight[...] = weights[0]
    total = dot_parts(split(wide_ref[...]), split(weight[...]))
    rows = total.shape[0]
    turned[:, :rows] = total.T
    mine = weight[pl.ds(pl.multiple_of(me * cols, cols), cols), :]
    turned[:, rows:] = exact_dot(mine, probe_ref[...], ((0,), (0,)))
    width = cols // parts
    for k in range(parts):
        outs[k][...] = turned[pl.ds(pl.multiple_of((me ^ k) * width, 8), width), :]


def final_kernel(parts, me_ref, *refs):
    pieces, (basis_ref, coef_ref) = refs[:parts], refs[parts:]
    me = me_ref[0]
    per, cells = basis_ref.shape[0] // parts, basis_ref.shape[2]
    order = list(range(1, per - 1)) + [0, per - 1]
    total = None
    for k in range(parts):
        base = (me ^ k) * per
        for at, i in enumerate(order):
            basis_ref[base + i] = pieces[k][:, at * cells:(at + 1) * cells]
        tail = pieces[k][:, per * cells:]
        total = tail if total is None else total + tail
    coef_ref[...] = total


def shape(*dims):
    return jax.ShapeDtypeStruct(dims, F32)


def local(snapshots, land_mask, taps_rows, taps_cols, probes):
    rows, grid_cols, cols = snapshots.shape
    half_rows, half_cols = rows // 2, grid_cols // 2
    parts, patches = lax.axis_size("tm"), lax.axis_size("space")
    cells = half_rows * half_cols
    piece = cells // parts
    inner = piece - 2 * half_cols
    span = 2 if patches > 1 else 1
    position, patch = lax.axis_index("tm"), lax.axis_index("space")
    me = jnp.stack([position, position + parts * (patch % span)]).astype(jnp.int32)

    outs = pl.pallas_call(
        functools.partial(filter_kernel, parts),
        out_shape=[shape(inner, cols)] * parts + [shape(2 * parts * half_cols, cols)] + [shape(half_cols, cols)] * 2,
        in_specs=[scalars(), scalars(), scalars(), pl.BlockSpec(memory_space=pltpu.HBM), whole()],
        out_specs=[whole()] * (parts + 3),
        scratch_shapes=[
            pltpu.VMEM((rows, grid_cols, cols), F32),
            pltpu.SemaphoreType.DMA((rows // CHUNK,)),
            pltpu.VMEM((grid_cols, CHUNK), F32),
            pltpu.VMEM((rows + 4, half_cols, cols), F32),
            pltpu.VMEM((cells, cols), F32),
        ],
        compiler_params=params(),
        name="filter",
    )(me, taps_rows, taps_cols, snapshots, land_mask)
    bigs, (small, to_above, to_below) = outs[:parts], outs[parts:]
    up = [(i, i + 1) for i in range(patches - 1)]
    above = lax.ppermute(to_below, "space", up)
    below = lax.ppermute(to_above, "space", [(j, i) for i, j in up])
    far_bigs = [bigs[0]] + [swap(bigs[k], "tm", k) for k in range(1, parts)]

    smalls = pl.pallas_call(
        functools.partial(edge_kernel, parts),
        out_shape=[shape(2 * half_cols, cols)] * parts,
        in_specs=[scalars()] + [whole()] * 3,
        out_specs=[whole()] * parts,
        scratch_shapes=[pltpu.VMEM((2 * parts * half_cols, cols), F32)],
        compiler_params=params(),
        name="edge",
    )(me, small, above, below)
    far_smalls = [smalls[0]] + [swap(smalls[k], "tm", k) for k in range(1, parts)]

    probe_sum = pl.pallas_call(
        functools.partial(probe_kernel, parts),
        out_shape=shape(cols, cols),
        in_specs=[scalars()] + [whole()] * (2 * parts + 1),
        out_specs=whole(),
        compiler_params=params(),
        cost_estimate=pl.CostEstimate(flops=12 * cells * cols * cols, bytes_accessed=8 * cells * cols, transcendentals=0),
        name="probe",
    )(me, *bigs, *smalls, probes.reshape(cells, cols))
    bits = [1 << b for b in range(patches.bit_length() - 1)]
    for bit in bits[:2]:
        probe_sum = probe_sum + swap(probe_sum, "space", bit)
    probe_sum, *far = lax.optimization_barrier([probe_sum] + far_bigs + far_smalls)

    blocks = parts * (parts + 1) // 2
    shares = parts * span
    size = blocks * cols // shares
    send, keep, wide = pl.pallas_call(
        functools.partial(gram_kernel, parts, span),
        out_shape=[shape(shares // 2, size, cols)] * 2 + [shape(piece, parts * cols)],
        in_specs=[scalars()] + [whole()] * (2 * parts),
        out_specs=[whole()] * 3,
        scratch_shapes=[pltpu.VMEM((blocks * cols, cols), F32)],
        compiler_params=params(),
        name="gram",
    )(me, *far)
    for bit in bits[2:]:
        probe_sum = probe_sum + swap(probe_sum, "space", bit)
    got = swap(send, "tm", 1)
    mine = keep[0] + got[0]
    for h in range(1, shares // 2):
        mine = mine + swap_both(keep[h] + got[h], 2 * h)
    mine, probe_sum = lax.optimization_barrier((mine, probe_sum))
    for bit in bits[1:]:
        mine = mine + swap(mine, "space", bit)
    even = jnp.stack([mine] + [swap_both(mine, 2 * h) for h in range(1, shares // 2)])
    odd = swap(even, "tm", 1)

    width = cols // parts
    sent = pl.pallas_call(
        functools.partial(merge_kernel, parts, span),
        out_shape=[shape(width, piece + cols)] * parts,
        in_specs=[scalars()] + [whole()] * 4,
        out_specs=[whole()] * parts,
        scratch_shapes=[
            pltpu.VMEM((blocks * cols, cols), F32),
            pltpu.VMEM((parts * cols, cols), F32),
            pltpu.VMEM((cols, piece + cols), F32),
        ],
        compiler_params=params(),
        name="merge",
    )(me, even, odd, wide, probe_sum)
    last = [sent[0]] + [swap(sent[k], "tm", k) for k in range(1, parts)]

    basis, coefficients = pl.pallas_call(
        functools.partial(final_kernel, parts),
        out_shape=(shape(half_rows, width, half_cols), shape(width, cols)),
        in_specs=[scalars()] + [whole()] * parts,
        out_specs=(whole(), whole()),
        compiler_params=params(),
        name="final",
    )(me, *last)
    return basis.transpose(0, 2, 1), coefficients


def solution(mesh):
    placed = (P("space", None, "tm"), P("space", None), P(), P(), P("space", None, None))
    return jax.shard_map(
        local,
        mesh=mesh,
        in_specs=placed,
        out_specs=(P("space", None, "tm"), P("tm", None)),
        check_vma=False,
    )
```

time: 106 us -> 93.5 us (0.88)
  waiting for transfers between devices: 52 us -> 32.3 us
  starting transfers between devices: 23.2 us -> 30.5 us
  Pallas kernels: 22.5 us -> 25.2 us
  local copies, waits for them, and re-layouts: 6.91 us -> 4.26 us
    ppermute x17 -> x16, waiting for transfers between devices: 47.2 us -> 23.9 us  [swap(): return lax.ppermute(x, axis, [(i, i ^ mask) for i in range(count)])]
    ppermute x2 -> x8, starting transfers between devices: 6.14 us -> 13.2 us  [the longest x6 7.11 us: swap_both(): return lax.ppermute(x, ('tm', 'space'), route)]
    ppermute x2 -> x8, waiting for transfers between devices: 4.85 us -> 8.45 us  [the longest x1 4.23 us: local(): below = lax.ppermute(to_above, 'space', [(j, i) for i, j in up])]
    unnamed x17 -> x10, local copies, waits for them, and re-layouts: 6.91 us -> 4.26 us
    pallas_call x1, Pallas kernels: 3.07 us -> 4.13 us  [local(): pl.pallas_call(functools.partial(filter_kernel, parts), out_shape=[shape(...]
    ppermute x17 -> x16, starting transfers between devices: 17.1 us -> 17.2 us  [swap(): return lax.ppermute(x, axis, [(i, i ^ mask) for i in range(count)])]
  transfers between devices with their start and end apart: 19 -> 24, of which waited for: 15 -> 16; matrix products, arithmetic and copies ran while one was open for 0% -> 0% of each run, Pallas kernels for 1% -> 0%
where the time goes in v2:
time: 93.5 us; the launch traced here: 93.2 us
  waiting for transfers between devices  32.3 us (35%)
  starting transfers between devices  30.5 us (33%)
  Pallas kernels  25.2 us (27%)
  local copies, waits for them, and re-layouts  4.26 us (5%)
    ppermute x16, waiting for transfers between devices, swap(): return lax.ppermute(x, axis, [(i, i ^ mask) for i in range(count)])  23.9 us
    ppermute x16, starting transfers between devices, swap(): return lax.ppermute(x, axis, [(i, i ^ mask) for i in range(count)])  17.2 us
    pallas_call x1, Pallas kernels, local(): pl.pallas_call(functools.partial(merge_kernel, parts, span), out_shape=[s...  15 us
    ppermute x6, starting transfers between devices, swap_both(): return lax.ppermute(x, ('tm', 'space'), route)  7.11 us
    ppermute x1, starting transfers between devices, local(): above = lax.ppermute(to_below, 'space', up)  4.84 us
    unnamed x10, local copies, waits for them, and re-layouts  4.26 us
    ppermute x1, waiting for transfers between devices, local(): below = lax.ppermute(to_above, 'space', [(j, i) for i, j in up])  4.23 us
    pallas_call x1, Pallas kernels, local(): pl.pallas_call(functools.partial(filter_kernel, parts), out_shape=[shape(...  4.13 us
  transfers between devices with their start and end apart: 24, of which 16 were waited for; matrix products, arithmetic and copies ran while one was open for 0% of the time, Pallas kernels for 0%

profile of v2, /device:TPU:0, one launch (start us, length us, event | category | flops | bytes accessed | tf_op | source)
XLA Modules:
  0.0 93.2 jit_solution(10382922160286115957)
XLA Ops:
  0.7 2.2 %copy-done = f32[64,128,128]{2,1,0:T(8,128)S(1)} copy-done((f32[64,128,128]{2,1,0:T(8,128)S(1)}, f32[64,128,128]{2,1,0:T(8,128)}, u32[]{:S(2)}) %copy-start) | copy-done | bytes 4194328
  5.0 4.1 %filter.1 = (f32[384,128]{1,0:T(8,128)S(1)}, f32[384,128]{1,0:T(8,128)S(1)}, f32[384,128]{1,0:T(8,128)S(1)}, f32[384,128]{1,0:T(8,128)S(1)}, f32[512,128]{1,0:T(...) custom-call(s32[2]{0:T(128)S(1)} %pad_add_fusion.me_ref, f32[6]{0:T(128)S(1)} %copy-done.3, f32[6]{0:T(128)S(1)} %copy-done.4, ...), custom_call_target="tpu_custom_call" | custom-call | tf_op jit(solution)/shard_map/filter/pallas_call | solution.py:289
  9.1 4.8 %collective-permute-start = (f32[64,128]{1,0:T(8,128)S(1)}, f32[64,128]{1,0:T(8,128)S(1)}, u32[]{:S(2)}, u32[]{:S(2)}) collective-permute-start(f32[64,128]{1,0:T(8,128)S(1)} %get-tuple-element.38), channel_id=1, source_target_pairs={{0,1},{1,2},{2,3},{3,4},{4,5},{5,6},{6,7},{8,9},{9,10},{10,11},{11... | collective-permute-start | bytes 98312 | tf_op jit(solution)/shard_map/ppermute | solution.py:306
  15.5 4.2 %collective-permute-done.1.below_ref = f32[64,128]{1,0:T(8,128)S(1)} collective-permute-done((f32[64,128]{1,0:T(8,128)S(1)}, f32[64,128]{1,0:T(8,128)S(1)}, u32[]{:S(2)}, u32[]{:S(2)}) %collective-permute-start.1) | collective-permute-done | bytes 32800 | tf_op jit(solution)/shard_map/ppermute | solution.py:307
  20.4 1.6 %probe.1 = f32[128,128]{1,0:T(8,128)S(1)} custom-call(s32[2]{0:T(128)S(1)} %pad_add_fusion.me_ref, f32[384,128]{1,0:T(8,128)S(1)} %get-tuple-element.44.refs_0_, f32[384,128]{1,0:T(8,128)S(1)} %get-tuple-element.34.refs_1_, f32[384,128]{1,0:T(8,128)S(1)} %get-tuple-element.35.refs_2_, f32[384,128]{1,0:T(8,128)S(1)} %get-tuple-element.36.refs_3_, ...), custom_call_target="tpu_custom_call" | custom-call | flops 402653184 | bytes 2097152 | tf_op jit(solution)/shard_map/probe/pallas_call | solution.py:321
  22.0 2.5 %collective-permute-start.2 = (f32[128,128]{1,0:T(8,128)S(1)}, f32[128,128]{1,0:T(8,128)S(1)}, u32[]{:S(2)}, u32[]{:S(2)}) collective-permute-start(f32[128,128]{1,0:T(8,128)S(1)} %probe.1), channel_id=1, source_target_pairs={{0,1},{1,0},{2,3},{3,2},{4,5},{5,4},{6,7},{7,6},{8,9},{9,8},{10,11... | collective-permute-start | bytes 196616 | tf_op jit(solution)/shard_map/ppermute | solution.py:32
  24.5 1.5 %collective-permute-start.5 = (f32[384,128]{1,0:T(8,128)S(1)}, f32[384,128]{1,0:T(8,128)S(1)}, u32[]{:S(2)}, u32[]{:S(2)}) collective-permute-start(f32[384,128]{1,0:T(8,128)S(1)} %get-tuple-element.35.refs_2_), channel_id=1, source_target_pairs={{0,16},{8,24},{16,0},{24,8},{1,17},{9,25},{17,1},{25,9},{2,18},{10... | collective-permute-start | bytes 589832 | tf_op jit(solution)/shard_map/ppermute | solution.py:32
  26.8 1.6 %collective-permute-start.3 = (f32[128,128]{1,0:T(8,128)S(1)}, f32[128,128]{1,0:T(8,128)S(1)}, u32[]{:S(2)}, u32[]{:S(2)}) collective-permute-start(f32[128,128]{1,0:T(8,128)S(1)} %add.57), channel_id=1, source_target_pairs={{0,2},{1,3},{2,0},{3,1},{4,6},{5,7},{6,4},{7,5},{8,10},{9,11},{10,... | collective-permute-start | bytes 196616 | tf_op jit(solution)/shard_map/ppermute | solution.py:32
  28.4 1.5 %collective-permute-start.8 = (f32[128,128]{1,0:T(8,128)S(1)}, f32[128,128]{1,0:T(8,128)S(1)}, u32[]{:S(2)}, u32[]{:S(2)}) collective-permute-start(f32[128,128]{1,0:T(8,128)S(1)} %get-tuple-element.42.refs_6_), channel_id=1, source_target_pairs={{0,16},{8,24},{16,0},{24,8},{1,17},{9,25},{17,1},{25,9},{2,18},{10... | collective-permute-start | bytes 196616 | tf_op jit(solution)/shard_map/ppermute | solution.py:32
  31.5 6.3 %collective-permute-done.8.refs_6_ = f32[128,128]{1,0:T(8,128)S(1)} collective-permute-done((f32[128,128]{1,0:T(8,128)S(1)}, f32[128,128]{1,0:T(8,128)S(1)}, u32[]{:S(2)}, u32[]{:S(2)}) %collective-permute-start.8) | collective-permute-done | bytes 65568 | tf_op jit(solution)/shard_map/ppermute | solution.py:32
  38.5 2.3 %gram.1 = (f32[4,160,128]{2,1,0:T(8,128)S(1)}, f32[4,160,128]{2,1,0:T(8,128)S(1)}, f32[512,512]{1,0:T(8,128)S(1)}) custom-call(s32[2]{0:T(128)S(1)} %pad_add_fusion.me_ref, f32[384,128]{1,0:T(8,128)S(1)} %get-tuple-element.44.refs_0_, f32[384,128]{1,0:T(8,128)S(1)} %collective-permute-done.4.refs_1_, f32[384,128]{1,0:T(8,128)S(1)} %collective-permute-done.5.refs_2_, ...), custom_call_target="tpu_custom_call" | custom-call | tf_op jit(solution)/shard_map/gram/pallas_call | solution.py:338
  42.5 1.6 %collective-permute-start.11 = (f32[160,128]{1,0:T(8,128)S(1)}, f32[160,128]{1,0:T(8,128)S(1)}, u32[]{:S(2)}, u32[]{:S(2)}) collective-permute-start(f32[160,128]{1,0:T(8,128)S(1)} %get-tuple-element.64), channel_id=1, source_target_pairs={{0,16},{1,17},{2,18},{3,19},{4,20},{5,21},{6,22},{7,23},{8,24},{9,... | collective-permute-start | bytes 245768 | tf_op jit(solution)/shard_map/ppermute | solution.py:42
  44.1 2.0 %collective-permute-start.12 = (f32[160,128]{1,0:T(8,128)S(1)}, f32[160,128]{1,0:T(8,128)S(1)}, u32[]{:S(2)}, u32[]{:S(2)}) collective-permute-start(f32[160,128]{1,0:T(8,128)S(1)} %get-tuple-element.66), channel_id=1, source_target_pairs={{0,1},{1,0},{2,3},{3,2},{4,5},{5,4},{6,7},{7,6},{8,9},{9,8},{10,11... | collective-permute-start | bytes 245768 | tf_op jit(solution)/shard_map/ppermute | solution.py:42
  46.1 2.6 %collective-permute-start.14 = (f32[128,128]{1,0:T(8,128)S(1)}, f32[128,128]{1,0:T(8,128)S(1)}, u32[]{:S(2)}, u32[]{:S(2)}) collective-permute-start(f32[128,128]{1,0:T(8,128)S(1)} %add.58), channel_id=1, source_target_pairs={{0,4},{1,5},{2,6},{3,7},{4,0},{5,1},{6,2},{7,3},{8,12},{9,13},{10,... | collective-permute-start | bytes 196616 | tf_op jit(solution)/shard_map/ppermute | solution.py:32
  48.7 2.7 %collective-permute-done.14 = f32[128,128]{1,0:T(8,128)S(1)} collective-permute-done((f32[128,128]{1,0:T(8,128)S(1)}, f32[128,128]{1,0:T(8,128)S(1)}, u32[]{:S(2)}, u32[]{:S(2)}) %collective-permute-start.14) | collective-permute-done | bytes 65568 | tf_op jit(solution)/shard_map/ppermute | solution.py:32
  51.4 1.5 %collective-permute-start.15 = (f32[160,128]{1,0:T(8,128)S(1)}, f32[160,128]{1,0:T(8,128)S(1)}, u32[]{:S(2)}, u32[]{:S(2)}) collective-permute-start(f32[160,128]{1,0:T(8,128)S(1)} %fusion.6), channel_id=1, source_target_pairs={{0,2},{1,3},{2,0},{3,1},{4,6},{5,7},{6,4},{7,5},{8,10},{9,11},{10,... | collective-permute-start | bytes 245768 | tf_op jit(solution)/shard_map/ppermute | solution.py:32
  53.0 3.0 %collective-permute-done.15 = f32[160,128]{1,0:T(8,128)S(1)} collective-permute-done((f32[160,128]{1,0:T(8,128)S(1)}, f32[160,128]{1,0:T(8,128)S(1)}, u32[]{:S(2)}, u32[]{:S(2)}) %collective-permute-start.15) | collective-permute-done | bytes 81952 | tf_op jit(solution)/shard_map/ppermute | solution.py:32
  56.0 2.6 %collective-permute-start.16 = (f32[160,128]{1,0:T(8,128)S(1)}, f32[160,128]{1,0:T(8,128)S(1)}, u32[]{:S(2)}, u32[]{:S(2)}) collective-permute-start(f32[160,128]{1,0:T(8,128)S(1)} %add.71), channel_id=1, source_target_pairs={{0,4},{1,5},{2,6},{3,7},{4,0},{5,1},{6,2},{7,3},{8,12},{9,13},{10,... | collective-permute-start | bytes 245768 | tf_op jit(solution)/shard_map/ppermute | solution.py:32
  58.6 2.8 %collective-permute-done.16 = f32[160,128]{1,0:T(8,128)S(1)} collective-permute-done((f32[160,128]{1,0:T(8,128)S(1)}, f32[160,128]{1,0:T(8,128)S(1)}, u32[]{:S(2)}, u32[]{:S(2)}) %collective-permute-start.16) | collective-permute-done | bytes 81952 | tf_op jit(solution)/shard_map/ppermute | solution.py:32
  61.4 2.2 %collective-permute-start.19 = (f32[160,128]{1,0:T(8,128)S(1)}, f32[160,128]{1,0:T(8,128)S(1)}, u32[]{:S(2)}, u32[]{:S(2)}) collective-permute-start(f32[160,128]{1,0:T(8,128)S(1)} %add.72), channel_id=1, source_target_pairs={{0,17},{1,16},{2,19},{3,18},{4,21},{5,20},{6,23},{7,22},{8,25},{9,... | collective-permute-start | bytes 245768 | tf_op jit(solution)/shard_map/ppermute | solution.py:42
  64.9 1.9 %collective-permute-done.19 = f32[160,128]{1,0:T(8,128)S(1)} collective-permute-done((f32[160,128]{1,0:T(8,128)S(1)}, f32[160,128]{1,0:T(8,128)S(1)}, u32[]{:S(2)}, u32[]{:S(2)}) %collective-permute-start.19) | collective-permute-done | bytes 81952 | tf_op jit(solution)/shard_map/ppermute | solution.py:42
  69.0 1.6 %collective-permute-done.20.odd_ref = f32[4,160,128]{2,1,0:T(8,128)S(1)} collective-permute-done((f32[4,160,128]{2,1,0:T(8,128)S(1)}, f32[4,160,128]{2,1,0:T(8,128)S(1)}, u32[]{:S(2)}, u32[]{:S(2)}) %collective-permute-start.20) | collective-permute-done | bytes 327712 | tf_op jit(solution)/shard_map/ppermute | solution.py:32
  70.6 15.0 %merge.1 = (f32[32,640]{1,0:T(8,128)S(1)}, f32[32,640]{1,0:T(8,128)S(1)}, f32[32,640]{1,0:T(8,128)S(1)}, f32[32,640]{1,0:T(8,128)S(1)}) custom-call(s32[2]{0:T(128)S(1)} %pad_add_fusion.me_ref, f32[4,160,128]{2,1,0:T(8,128)S(1)} %pad_maximum_fusion.even_ref, f32[4,160,128]{2,1,0:T(8,128)S(1)} %collective-permute-done.20.odd_ref, ...), custom_call_target="tpu_custom_call" | custom-call | tf_op jit(solution)/shard_map/merge/pallas_call | solution.py:360
  87.6 3.5 %collective-permute-done.22.refs_2_ = f32[32,640]{1,0:T(8,128)S(1)} collective-permute-done((f32[32,640]{1,0:T(8,128)S(1)}, f32[32,640]{1,0:T(8,128)S(1)}, u32[]{:S(2)}, u32[]{:S(2)}) %collective-permute-start.22) | collective-permute-done | bytes 81952 | tf_op jit(solution)/shard_map/ppermute | solution.py:32
  (49 shorter events, 16.6 us)
Async XLA Ops:
  9.1 6.4 %collective-permute-start = (f32[64,128]{1,0:T(8,128)S(1)}, f32[64,128]{1,0:T(8,128)S(1)}, u32[]{:S(2)}, u32[]{:S(2)}) collective-permute-start(f32[64,128]{1,0:T(8,128)S(1)} %get-tuple-element.38), channel_id=1, source_target_pairs={{0,1},{1,2},{2,3},{3,4},{4,5},{5,6},{6,7},{8,9},{9,10},{10,11},{11... | collective-permute-start | bytes 98312 | tf_op jit(solution)/shard_map/ppermute | solution.py:306
  14.0 5.8 %collective-permute-start.1 = (f32[64,128]{1,0:T(8,128)S(1)}, f32[64,128]{1,0:T(8,128)S(1)}, u32[]{:S(2)}, u32[]{:S(2)}) collective-permute-start(f32[64,128]{1,0:T(8,128)S(1)} %get-tuple-element.39), channel_id=1, source_target_pairs={{1,0},{2,1},{3,2},{4,3},{5,4},{6,5},{7,6},{9,8},{10,9},{11,10},{12... | collective-permute-start | bytes 98312 | tf_op jit(solution)/shard_map/ppermute | solution.py:307
  22.0 4.8 %collective-permute-start.2 = (f32[128,128]{1,0:T(8,128)S(1)}, f32[128,128]{1,0:T(8,128)S(1)}, u32[]{:S(2)}, u32[]{:S(2)}) collective-permute-start(f32[128,128]{1,0:T(8,128)S(1)} %probe.1), channel_id=1, source_target_pairs={{0,1},{1,0},{2,3},{3,2},{4,5},{5,4},{6,7},{7,6},{8,9},{9,8},{10,11... | collective-permute-start | bytes 196616 | tf_op jit(solution)/shard_map/ppermute | solution.py:32
  24.5 14.0 %collective-permute-start.4 = (f32[384,128]{1,0:T(8,128)S(1)}, f32[384,128]{1,0:T(8,128)S(1)}, u32[]{:S(2)}, u32[]{:S(2)}) collective-permute-start(f32[384,128]{1,0:T(8,128)S(1)} %get-tuple-element.34.refs_1_), channel_id=1, source_target_pairs={{0,8},{8,0},{16,24},{24,16},{1,9},{9,1},{17,25},{25,17},{2,10},{10... | collective-permute-start | bytes 589832 | tf_op jit(solution)/shard_map/ppermute | solution.py:32
  24.5 14.0 %collective-permute-start.5 = (f32[384,128]{1,0:T(8,128)S(1)}, f32[384,128]{1,0:T(8,128)S(1)}, u32[]{:S(2)}, u32[]{:S(2)}) collective-permute-start(f32[384,128]{1,0:T(8,128)S(1)} %get-tuple-element.35.refs_2_), channel_id=1, source_target_pairs={{0,16},{8,24},{16,0},{24,8},{1,17},{9,25},{17,1},{25,9},{2,18},{10... | collective-permute-start | bytes 589832 | tf_op jit(solution)/shard_map/ppermute | solution.py:32
  26.1 12.4 %collective-permute-start.6 = (f32[384,128]{1,0:T(8,128)S(1)}, f32[384,128]{1,0:T(8,128)S(1)}, u32[]{:S(2)}, u32[]{:S(2)}) collective-permute-start(f32[384,128]{1,0:T(8,128)S(1)} %get-tuple-element.36.refs_3_), channel_id=1, source_target_pairs={{0,24},{8,16},{16,8},{24,0},{1,25},{9,17},{17,9},{25,1},{2,26},{10... | collective-permute-start | bytes 589832 | tf_op jit(solution)/shard_map/ppermute | solution.py:32
  26.4 2.0 %collective-permute-start.7 = (f32[128,128]{1,0:T(8,128)S(1)}, f32[128,128]{1,0:T(8,128)S(1)}, u32[]{:S(2)}, u32[]{:S(2)}) collective-permute-start(f32[128,128]{1,0:T(8,128)S(1)} %get-tuple-element.41.refs_5_), channel_id=1, source_target_pairs={{0,8},{8,0},{16,24},{24,16},{1,9},{9,1},{17,25},{25,17},{2,10},{10... | collective-permute-start | bytes 196616 | tf_op jit(solution)/shard_map/ppermute | solution.py:32
  26.8 4.3 %collective-permute-start.3 = (f32[128,128]{1,0:T(8,128)S(1)}, f32[128,128]{1,0:T(8,128)S(1)}, u32[]{:S(2)}, u32[]{:S(2)}) collective-permute-start(f32[128,128]{1,0:T(8,128)S(1)} %add.57), channel_id=1, source_target_pairs={{0,2},{1,3},{2,0},{3,1},{4,6},{5,7},{6,4},{7,5},{8,10},{9,11},{10,... | collective-permute-start | bytes 196616 | tf_op jit(solution)/shard_map/ppermute | solution.py:32
  28.4 9.4 %collective-permute-start.8 = (f32[128,128]{1,0:T(8,128)S(1)}, f32[128,128]{1,0:T(8,128)S(1)}, u32[]{:S(2)}, u32[]{:S(2)}) collective-permute-start(f32[128,128]{1,0:T(8,128)S(1)} %get-tuple-element.42.refs_6_), channel_id=1, source_target_pairs={{0,16},{8,24},{16,0},{24,8},{1,17},{9,25},{17,1},{25,9},{2,18},{10... | collective-permute-start | bytes 196616 | tf_op jit(solution)/shard_map/ppermute | solution.py:32
  31.1 7.4 %collective-permute-start.9 = (f32[128,128]{1,0:T(8,128)S(1)}, f32[128,128]{1,0:T(8,128)S(1)}, u32[]{:S(2)}, u32[]{:S(2)}) collective-permute-start(f32[128,128]{1,0:T(8,128)S(1)} %get-tuple-element.43.refs_7_), channel_id=1, source_target_pairs={{0,24},{8,16},{16,8},{24,0},{1,25},{9,17},{17,9},{25,1},{2,26},{10... | collective-permute-start | bytes 196616 | tf_op jit(solution)/shard_map/ppermute | solution.py:32
  40.8 1.7 %collective-permute-start.10 = (f32[4,160,128]{2,1,0:T(8,128)S(1)}, f32[4,160,128]{2,1,0:T(8,128)S(1)}, u32[]{:S(2)}, u32[]{:S(2)}) collective-permute-start(f32[4,160,128]{2,1,0:T(8,128)S(1)} %get-tuple-element.53), channel_id=1, source_target_pairs={{0,8},{8,0},{16,24},{24,16},{1,9},{9,1},{17,25},{25,17},{2,10},{10... | collective-permute-start | bytes 983048 | tf_op jit(solution)/shard_map/ppermute | solution.py:32
  42.5 8.9 %collective-permute-start.11 = (f32[160,128]{1,0:T(8,128)S(1)}, f32[160,128]{1,0:T(8,128)S(1)}, u32[]{:S(2)}, u32[]{:S(2)}) collective-permute-start(f32[160,128]{1,0:T(8,128)S(1)} %get-tuple-element.64), channel_id=1, source_target_pairs={{0,16},{1,17},{2,18},{3,19},{4,20},{5,21},{6,22},{7,23},{8,24},{9,... | collective-permute-start | bytes 245768 | tf_op jit(solution)/shard_map/ppermute | solution.py:42
  44.1 7.3 %collective-permute-start.13 = (f32[160,128]{1,0:T(8,128)S(1)}, f32[160,128]{1,0:T(8,128)S(1)}, u32[]{:S(2)}, u32[]{:S(2)}) collective-permute-start(f32[160,128]{1,0:T(8,128)S(1)} %get-tuple-element.65), channel_id=1, source_target_pairs={{0,17},{1,16},{2,19},{3,18},{4,21},{5,20},{6,23},{7,22},{8,25},{9,... | collective-permute-start | bytes 245768 | tf_op jit(solution)/shard_map/ppermute | solution.py:42
  44.1 7.3 %collective-permute-start.12 = (f32[160,128]{1,0:T(8,128)S(1)}, f32[160,128]{1,0:T(8,128)S(1)}, u32[]{:S(2)}, u32[]{:S(2)}) collective-permute-start(f32[160,128]{1,0:T(8,128)S(1)} %get-tuple-element.66), channel_id=1, source_target_pairs={{0,1},{1,0},{2,3},{3,2},{4,5},{5,4},{6,7},{7,6},{8,9},{9,8},{10,11... | collective-permute-start | bytes 245768 | tf_op jit(solution)/shard_map/ppermute | solution.py:42
  46.1 5.3 %collective-permute-start.14 = (f32[128,128]{1,0:T(8,128)S(1)}, f32[128,128]{1,0:T(8,128)S(1)}, u32[]{:S(2)}, u32[]{:S(2)}) collective-permute-start(f32[128,128]{1,0:T(8,128)S(1)} %add.58), channel_id=1, source_target_pairs={{0,4},{1,5},{2,6},{3,7},{4,0},{5,1},{6,2},{7,3},{8,12},{9,13},{10,... | collective-permute-start | bytes 196616 | tf_op jit(solution)/shard_map/ppermute | solution.py:32
  51.4 4.5 %collective-permute-start.15 = (f32[160,128]{1,0:T(8,128)S(1)}, f32[160,128]{1,0:T(8,128)S(1)}, u32[]{:S(2)}, u32[]{:S(2)}) collective-permute-start(f32[160,128]{1,0:T(8,128)S(1)} %fusion.6), channel_id=1, source_target_pairs={{0,2},{1,3},{2,0},{3,1},{4,6},{5,7},{6,4},{7,5},{8,10},{9,11},{10,... | collective-permute-start | bytes 245768 | tf_op jit(solution)/shard_map/ppermute | solution.py:32
  56.0 5.4 %collective-permute-start.16 = (f32[160,128]{1,0:T(8,128)S(1)}, f32[160,128]{1,0:T(8,128)S(1)}, u32[]{:S(2)}, u32[]{:S(2)}) collective-permute-start(f32[160,128]{1,0:T(8,128)S(1)} %add.71), channel_id=1, source_target_pairs={{0,4},{1,5},{2,6},{3,7},{4,0},{5,1},{6,2},{7,3},{8,12},{9,13},{10,... | collective-permute-start | bytes 245768 | tf_op jit(solution)/shard_map/ppermute | solution.py:32
  61.4 5.4 %collective-permute-start.19 = (f32[160,128]{1,0:T(8,128)S(1)}, f32[160,128]{1,0:T(8,128)S(1)}, u32[]{:S(2)}, u32[]{:S(2)}) collective-permute-start(f32[160,128]{1,0:T(8,128)S(1)} %add.72), channel_id=1, source_target_pairs={{0,17},{1,16},{2,19},{3,18},{4,21},{5,20},{6,23},{7,22},{8,25},{9,... | collective-permute-start | bytes 245768 | tf_op jit(solution)/shard_map/ppermute | solution.py:42
  63.6 4.4 %collective-permute-start.18 = (f32[160,128]{1,0:T(8,128)S(1)}, f32[160,128]{1,0:T(8,128)S(1)}, u32[]{:S(2)}, u32[]{:S(2)}) collective-permute-start(f32[160,128]{1,0:T(8,128)S(1)} %add.72), channel_id=1, source_target_pairs={{0,1},{1,0},{2,3},{3,2},{4,5},{5,4},{6,7},{7,6},{8,9},{9,8},{10,11... | collective-permute-start | bytes 245768 | tf_op jit(solution)/shard_map/ppermute | solution.py:42
  64.4 4.4 %collective-permute-start.17 = (f32[160,128]{1,0:T(8,128)S(1)}, f32[160,128]{1,0:T(8,128)S(1)}, u32[]{:S(2)}, u32[]{:S(2)}) collective-permute-start(f32[160,128]{1,0:T(8,128)S(1)} %add.72), channel_id=1, source_target_pairs={{0,16},{1,17},{2,18},{3,19},{4,20},{5,21},{6,22},{7,23},{8,24},{9,... | collective-permute-start | bytes 245768 | tf_op jit(solution)/shard_map/ppermute | solution.py:42
  68.9 1.7 %collective-permute-start.20 = (f32[4,160,128]{2,1,0:T(8,128)S(1)}, f32[4,160,128]{2,1,0:T(8,128)S(1)}, u32[]{:S(2)}, u32[]{:S(2)}) collective-permute-start(f32[4,160,128]{2,1,0:T(8,128)S(1)} %pad_maximum_fusion.even_ref), channel_id=1, source_target_pairs={{0,8},{8,0},{16,24},{24,16},{1,9},{9,1},{17,25},{25,17},{2,10},{10... | collective-permute-start | bytes 983048 | tf_op jit(solution)/shard_map/ppermute | solution.py:32
  85.6 1.9 %collective-permute-start.21 = (f32[32,640]{1,0:T(8,128)S(1)}, f32[32,640]{1,0:T(8,128)S(1)}, u32[]{:S(2)}, u32[]{:S(2)}) collective-permute-start(f32[32,640]{1,0:T(8,128)S(1)} %get-tuple-element.59), channel_id=1, source_target_pairs={{0,8},{8,0},{16,24},{24,16},{1,9},{9,1},{17,25},{25,17},{2,10},{10... | collective-permute-start | bytes 245768 | tf_op jit(solution)/shard_map/ppermute | solution.py:32
  85.8 5.3 %collective-permute-start.22 = (f32[32,640]{1,0:T(8,128)S(1)}, f32[32,640]{1,0:T(8,128)S(1)}, u32[]{:S(2)}, u32[]{:S(2)}) collective-permute-start(f32[32,640]{1,0:T(8,128)S(1)} %get-tuple-element.60), channel_id=1, source_target_pairs={{0,16},{8,24},{16,0},{24,8},{1,17},{9,25},{17,1},{25,9},{2,18},{10... | collective-permute-start | bytes 245768 | tf_op jit(solution)/shard_map/ppermute | solution.py:32
  86.4 5.4 %collective-permute-start.23 = (f32[32,640]{1,0:T(8,128)S(1)}, f32[32,640]{1,0:T(8,128)S(1)}, u32[]{:S(2)}, u32[]{:S(2)}) collective-permute-start(f32[32,640]{1,0:T(8,128)S(1)} %get-tuple-element.61), channel_id=1, source_target_pairs={{0,24},{8,16},{16,8},{24,0},{1,25},{9,17},{17,9},{25,1},{2,26},{10... | collective-permute-start | bytes 245768 | tf_op jit(solution)/shard_map/ppermute | solution.py:32
  (5 other events, 19.6 us)

commit v3 on v2

--- a/solution.py
+++ b/solution.py
@@ -13,10 +13,11 @@
 exact = lax.Precision.HIGHEST
 F32 = jnp.float32
 VMEM_LIMIT = 48 * 1024 * 1024
-
-
-def params():
-    return pltpu.CompilerParams(vmem_limit_bytes=VMEM_LIMIT)
+FULL_VMEM = 60 * 1024 * 1024
+
+
+def params(limit=VMEM_LIMIT):
+    return pltpu.CompilerParams(vmem_limit_bytes=limit)
 
 
 def whole():
@@ -59,7 +60,7 @@
     return shift_rows(before, 1) + here + shift_rows(after, -1)
 
 
-def filter_kernel(parts, me_ref, rtaps_ref, ctaps_ref, snap_hbm, mask_ref, *rest):
+def filter_kernel(parts, me_ref, taps_ref, snap_hbm, mask_ref, *rest):
     bigs, (small_ref, up_ref, down_ref) = rest[:parts], rest[parts:parts + 3]
     snaps, sems, mask_t, narrowed, filtered = rest[parts + 3:]
     rows, cells = snaps.shape[0], narrowed.shape[1]
@@ -71,8 +72,8 @@
 
     for c in range(chunks):
         fetch(c).start()
-    ctaps = [ctaps_ref[k] for k in range(TAPS)]
-    rtaps = [rtaps_ref[k] for k in range(TAPS)]
+    rtaps = [taps_ref[k] for k in range(TAPS)]
+    ctaps = [taps_ref[TAPS + k] for k in range(TAPS)]
     edge = jnp.zeros((2,) + narrowed.shape[1:], F32)
     narrowed[0:2] = edge
     narrowed[rows + 2:rows + 4] = edge
@@ -178,7 +179,9 @@
 
 def dot_parts(a, b, dims=((1,), (0,))):
     (ah, al), (bh, bl) = a, b
-    return dot(ah, bh, dims) + (dot(ah, bl, dims) + dot(al, bh, dims))
+    rows = ah.shape[0]
+    both = dot(jnp.concatenate([ah, al], axis=0), bh, dims)
+    return both[:rows] + (dot(ah, bl, dims) + both[rows:])
 
 
 def exact_dot(a, b, dims=((1,), (0,))):
@@ -196,7 +199,7 @@
     for _ in range(SIGN_STEPS):
         halves = [split(y) for y in signs]
         squares = [split(dot_parts(y, y)) for y in halves]
-        cubes = [dot_parts(y, s) for y, s in zip(halves, squares)]
+        cubes = [dot_parts(s, y) for y, s in zip(halves, squares)]
         signs = [1.5 * y - 0.5 * c for y, c in zip(signs, cubes)]
     half = order // 2
     combines = []
@@ -289,7 +292,7 @@
     outs = pl.pallas_call(
         functools.partial(filter_kernel, parts),
         out_shape=[shape(inner, cols)] * parts + [shape(2 * parts * half_cols, cols)] + [shape(half_cols, cols)] * 2,
-        in_specs=[scalars(), scalars(), scalars(), pl.BlockSpec(memory_space=pltpu.HBM), whole()],
+        in_specs=[scalars(), scalars(), pl.BlockSpec(memory_space=pltpu.HBM), whole()],
         out_specs=[whole()] * (parts + 3),
         scratch_shapes=[
             pltpu.VMEM((rows, grid_cols, cols), F32),
@@ -298,14 +301,15 @@
             pltpu.VMEM((rows + 4, half_cols, cols), F32),
             pltpu.VMEM((cells, cols), F32),
         ],
-        compiler_params=params(),
+        compiler_params=params(FULL_VMEM),
         name="filter",
-    )(me, taps_rows, taps_cols, snapshots, land_mask)
+    )(me, jnp.concatenate([taps_rows, taps_cols]), snapshots, land_mask)
     bigs, (small, to_above, to_below) = outs[:parts], outs[parts:]
     up = [(i, i + 1) for i in range(patches - 1)]
     above = lax.ppermute(to_below, "space", up)
     below = lax.ppermute(to_above, "space", [(j, i) for i, j in up])
     far_bigs = [bigs[0]] + [swap(bigs[k], "tm", k) for k in range(1, parts)]
+    above, below, *far_bigs = lax.optimization_barrier([above, below] + far_bigs)
 
     smalls = pl.pallas_call(
         functools.partial(edge_kernel, parts),
@@ -328,7 +332,7 @@
         name="probe",
     )(me, *bigs, *smalls, probes.reshape(cells, cols))
     bits = [1 << b for b in range(patches.bit_length() - 1)]
-    for bit in bits[:2]:
+    for bit in bits[:1]:
         probe_sum = probe_sum + swap(probe_sum, "space", bit)
     probe_sum, *far = lax.optimization_barrier([probe_sum] + far_bigs + far_smalls)
 
@@ -344,7 +348,7 @@
         compiler_params=params(),
         name="gram",
     )(me, *far)
-    for bit in bits[2:]:
+    for bit in bits[1:-1]:
         probe_sum = probe_sum + swap(probe_sum, "space", bit)
     got = swap(send, "tm", 1)
     mine = keep[0] + got[0]
@@ -353,6 +357,9 @@
     mine, probe_sum = lax.optimization_barrier((mine, probe_sum))
     for bit in bits[1:]:
         mine = mine + swap(mine, "space", bit)
+    mine, probe_sum = lax.optimization_barrier((mine, probe_sum))
+    for bit in bits[1:][-1:]:
+        probe_sum = probe_sum + swap(probe_sum, "space", bit)
     even = jnp.stack([mine] + [swap_both(mine, 2 * h) for h in range(1, shares // 2)])
     odd = swap(even, "tm", 1)
 

time: 93.5 us -> 94.7 us (1.013)
  other arithmetic: 0.2 us -> 2.03 us
  waiting for transfers between devices: 32.3 us -> 30.5 us
    ppermute x16, waiting for transfers between devices: 23.9 us -> 21.9 us  [swap(): return lax.ppermute(x, axis, [(i, i ^ mask) for i in range(count)])]
    pallas_call x1, Pallas kernels: 4.13 us -> 6.04 us  [local(): pl.pallas_call(functools.partial(filter_kernel, parts), out_shape=[shape(...]
    concatenate x0 -> x1, other arithmetic: none -> 1.26 us  [local(): jnp.concatenate([taps_rows, taps_cols])]
    ppermute x1, starting transfers between devices: 4.84 us -> 3.59 us  [local(): above = lax.ppermute(to_below, 'space', up)]
    ppermute x16, starting transfers between devices: 17.2 us -> 18.3 us  [swap(): return lax.ppermute(x, axis, [(i, i ^ mask) for i in range(count)])]
    pallas_call x1, Pallas kernels: 15 us -> 14 us  [local(): pl.pallas_call(functools.partial(merge_kernel, parts, span), out_shape=[s...]
    unnamed x10 -> x14, local copies, waits for them, and re-layouts: 4.26 us -> 4.65 us
  transfers between devices with their start and end apart: 24 -> 24, of which waited for: 16 -> 15; matrix products, arithmetic and copies ran while one was open for 0% -> 0% of each run, Pallas kernels for 0% -> 0%
where the time goes in v3:
time: 94.7 us; the launch traced here: 94.4 us
  waiting for transfers between devices  30.5 us (32%)
  starting transfers between devices  30.3 us (32%)
  Pallas kernels  26 us (27%)
  local copies, waits for them, and re-layouts  4.65 us (5%)
  other arithmetic  2.03 us (2%)
    ppermute x16, waiting for transfers between devices, swap(): return lax.ppermute(x, axis, [(i, i ^ mask) for i in range(count)])  21.9 us
    ppermute x16, starting transfers between devices, swap(): return lax.ppermute(x, axis, [(i, i ^ mask) for i in range(count)])  18.3 us
    pallas_call x1, Pallas kernels, local(): pl.pallas_call(functools.partial(merge_kernel, parts, span), out_shape=[s...  14 us
    ppermute x6, starting transfers between devices, swap_both(): return lax.ppermute(x, ('tm', 'space'), route)  7.11 us
    pallas_call x1, Pallas kernels, local(): pl.pallas_call(functools.partial(filter_kernel, parts), out_shape=[shape(...  6.04 us
    unnamed x14, local copies, waits for them, and re-layouts  4.65 us
    ppermute x1, waiting for transfers between devices, local(): below = lax.ppermute(to_above, 'space', [(j, i) for i, j in up])  4.12 us
    ppermute x6, waiting for transfers between devices, swap_both(): return lax.ppermute(x, ('tm', 'space'), route)  3.87 us
  transfers between devices with their start and end apart: 24, of which 15 were waited for; matrix products, arithmetic and copies ran while one was open for 0% of the time, Pallas kernels for 0%

profile of v3, /device:TPU:0, one launch (start us, length us, event | category | flops | bytes accessed | tf_op | source)
XLA Modules:
  0.0 94.4 jit_solution(17970008752977094592)
XLA Ops:
  2.6 6.0 %filter.1 = (f32[384,128]{1,0:T(8,128)}, f32[384,128]{1,0:T(8,128)}, f32[384,128]{1,0:T(8,128)}, f32[384,128]{1,0:T(8,128)}, f32[512,128]{1,0:T(8,128)}, /*index=5*/f32[64,128]{1,0:T(8,128)}, f32[64,128]{1,0:T(8,128)}) custom-call(s32[2]{0:T(128)} %pad_add_fusion.me_ref, f32[12]{0:T(128)} %pad_maximum_fusion.1.taps_ref, f32[64,128,128]{2,1,0:T(8,128)} %snap_hbm.1, ...), custom_call_target="tpu_custom_call" | custom-call | tf_op jit(solution)/shard_map/filter/pallas_call | solution.py:292
  9.1 2.6 %collective-permute-start.3 = (f32[384,128]{1,0:T(8,128)}, f32[384,128]{1,0:T(8,128)S(1)}, u32[]{:S(2)}, u32[]{:S(2)}) collective-permute-start(f32[384,128]{1,0:T(8,128)} %get-tuple-element.43.refs_2_), channel_id=1, source_target_pairs={{0,16},{8,24},{16,0},{24,8},{1,17},{9,25},{17,1},{25,9},{2,18},{10... | collective-permute-start | bytes 589832 | tf_op jit(solution)/shard_map/ppermute | solution.py:33
  11.8 3.6 %collective-permute-start = (f32[64,128]{1,0:T(8,128)}, f32[64,128]{1,0:T(8,128)S(1)}, u32[]{:S(2)}, u32[]{:S(2)}) collective-permute-start(f32[64,128]{1,0:T(8,128)} %get-tuple-element.46), channel_id=1, source_target_pairs={{0,1},{1,2},{2,3},{3,4},{4,5},{5,6},{6,7},{8,9},{9,10},{10,11},{11... | collective-permute-start | bytes 98312 | tf_op jit(solution)/shard_map/ppermute | solution.py:309
  17.3 4.1 %collective-permute-done.1.below_ref = f32[64,128]{1,0:T(8,128)S(1)} collective-permute-done((f32[64,128]{1,0:T(8,128)}, f32[64,128]{1,0:T(8,128)S(1)}, u32[]{:S(2)}, u32[]{:S(2)}) %collective-permute-start.1) | collective-permute-done | bytes 32800 | tf_op jit(solution)/shard_map/ppermute | solution.py:310
  26.7 1.6 %probe.1 = f32[128,128]{1,0:T(8,128)S(1)} custom-call(s32[2]{0:T(128)S(1)} %copy-done.6, f32[384,128]{1,0:T(8,128)S(1)} %copy-done.1, f32[384,128]{1,0:T(8,128)S(1)} %copy-done.3, f32[384,128]{1,0:T(8,128)S(1)} %copy-done.4, f32[384,128]{1,0:T(8,128)S(1)} %copy-done.5, f32[128,128]{1,0:T(8,128)S(1)} %get-tuple-element.62.refs_4_, ...), custom_call_target="tpu_custom_call" | custom-call | flops 402653184 | bytes 2097152 | tf_op jit(solution)/shard_map/probe/pallas_call | solution.py:325
  28.3 2.5 %collective-permute-start.5 = (f32[128,128]{1,0:T(8,128)S(1)}, f32[128,128]{1,0:T(8,128)S(1)}, u32[]{:S(2)}, u32[]{:S(2)}) collective-permute-start(f32[128,128]{1,0:T(8,128)S(1)} %probe.1), channel_id=1, source_target_pairs={{0,1},{1,0},{2,3},{3,2},{4,5},{5,4},{6,7},{7,6},{8,9},{9,8},{10,11... | collective-permute-start | bytes 196616 | tf_op jit(solution)/shard_map/ppermute | solution.py:33
  30.8 1.5 %collective-permute-start.7 = (f32[128,128]{1,0:T(8,128)S(1)}, f32[128,128]{1,0:T(8,128)S(1)}, u32[]{:S(2)}, u32[]{:S(2)}) collective-permute-start(f32[128,128]{1,0:T(8,128)S(1)} %get-tuple-element.52.refs_6_), channel_id=1, source_target_pairs={{0,16},{8,24},{16,0},{24,8},{1,17},{9,25},{17,1},{25,9},{2,18},{10... | collective-permute-start | bytes 196616 | tf_op jit(solution)/shard_map/ppermute | solution.py:33
  33.1 2.2 %collective-permute-done.7.refs_6_ = f32[128,128]{1,0:T(8,128)S(1)} collective-permute-done((f32[128,128]{1,0:T(8,128)S(1)}, f32[128,128]{1,0:T(8,128)S(1)}, u32[]{:S(2)}, u32[]{:S(2)}) %collective-permute-start.7) | collective-permute-done | bytes 65568 | tf_op jit(solution)/shard_map/ppermute | solution.py:33
  36.4 2.3 %gram.1 = (f32[4,160,128]{2,1,0:T(8,128)S(1)}, f32[4,160,128]{2,1,0:T(8,128)S(1)}, f32[512,512]{1,0:T(8,128)S(1)}) custom-call(s32[2]{0:T(128)S(1)} %copy-done.6, f32[384,128]{1,0:T(8,128)S(1)} %copy-done.1, f32[384,128]{1,0:T(8,128)S(1)} %collective-permute-done.2.refs_1_, f32[384,128]{1,0:T(8,128)S(1)} %collective-permute-done.3.refs_2_, ...), custom_call_target="tpu_custom_call" | custom-call | tf_op jit(solution)/shard_map/gram/pallas_call | solution.py:342
  38.9 1.5 %collective-permute-done.9 = f32[4,160,128]{2,1,0:T(8,128)S(1)} collective-permute-done((f32[4,160,128]{2,1,0:T(8,128)S(1)}, f32[4,160,128]{2,1,0:T(8,128)S(1)}, u32[]{:S(2)}, u32[]{:S(2)}) %collective-permute-start.9) | collective-permute-done | bytes 327712 | tf_op jit(solution)/shard_map/ppermute | solution.py:33
  40.5 1.5 %collective-permute-start.10 = (f32[160,128]{1,0:T(8,128)S(1)}, f32[160,128]{1,0:T(8,128)S(1)}, u32[]{:S(2)}, u32[]{:S(2)}) collective-permute-start(f32[160,128]{1,0:T(8,128)S(1)} %get-tuple-element.80), channel_id=1, source_target_pairs={{0,16},{1,17},{2,18},{3,19},{4,20},{5,21},{6,22},{7,23},{8,24},{9,... | collective-permute-start | bytes 245768 | tf_op jit(solution)/shard_map/ppermute | solution.py:43
  42.1 1.9 %collective-permute-start.11 = (f32[160,128]{1,0:T(8,128)S(1)}, f32[160,128]{1,0:T(8,128)S(1)}, u32[]{:S(2)}, u32[]{:S(2)}) collective-permute-start(f32[160,128]{1,0:T(8,128)S(1)} %get-tuple-element.82), channel_id=1, source_target_pairs={{0,1},{1,0},{2,3},{3,2},{4,5},{5,4},{6,7},{7,6},{8,9},{9,8},{10,11... | collective-permute-start | bytes 245768 | tf_op jit(solution)/shard_map/ppermute | solution.py:43
  44.0 1.6 %collective-permute-start.13 = (f32[128,128]{1,0:T(8,128)S(1)}, f32[128,128]{1,0:T(8,128)S(1)}, u32[]{:S(2)}, u32[]{:S(2)}) collective-permute-start(f32[128,128]{1,0:T(8,128)S(1)} %add.57), channel_id=1, source_target_pairs={{0,2},{1,3},{2,0},{3,1},{4,6},{5,7},{6,4},{7,5},{8,10},{9,11},{10,... | collective-permute-start | bytes 196616 | tf_op jit(solution)/shard_map/ppermute | solution.py:33
  45.6 2.7 %collective-permute-done.13 = f32[128,128]{1,0:T(8,128)S(1)} collective-permute-done((f32[128,128]{1,0:T(8,128)S(1)}, f32[128,128]{1,0:T(8,128)S(1)}, u32[]{:S(2)}, u32[]{:S(2)}) %collective-permute-start.13) | collective-permute-done | bytes 65568 | tf_op jit(solution)/shard_map/ppermute | solution.py:33
  48.3 1.6 %collective-permute-start.14 = (f32[160,128]{1,0:T(8,128)S(1)}, f32[160,128]{1,0:T(8,128)S(1)}, u32[]{:S(2)}, u32[]{:S(2)}) collective-permute-start(f32[160,128]{1,0:T(8,128)S(1)} %fusion.6), channel_id=1, source_target_pairs={{0,2},{1,3},{2,0},{3,1},{4,6},{5,7},{6,4},{7,5},{8,10},{9,11},{10,... | collective-permute-start | bytes 245768 | tf_op jit(solution)/shard_map/ppermute | solution.py:33
  50.0 2.9 %collective-permute-done.14 = f32[160,128]{1,0:T(8,128)S(1)} collective-permute-done((f32[160,128]{1,0:T(8,128)S(1)}, f32[160,128]{1,0:T(8,128)S(1)}, u32[]{:S(2)}, u32[]{:S(2)}) %collective-permute-start.14) | collective-permute-done | bytes 81952 | tf_op jit(solution)/shard_map/ppermute | solution.py:33
  52.9 2.7 %collective-permute-start.15 = (f32[160,128]{1,0:T(8,128)S(1)}, f32[160,128]{1,0:T(8,128)S(1)}, u32[]{:S(2)}, u32[]{:S(2)}) collective-permute-start(f32[160,128]{1,0:T(8,128)S(1)} %add.70), channel_id=1, source_target_pairs={{0,4},{1,5},{2,6},{3,7},{4,0},{5,1},{6,2},{7,3},{8,12},{9,13},{10,... | collective-permute-start | bytes 245768 | tf_op jit(solution)/shard_map/ppermute | solution.py:33
  55.5 2.7 %collective-permute-done.15 = f32[160,128]{1,0:T(8,128)S(1)} collective-permute-done((f32[160,128]{1,0:T(8,128)S(1)}, f32[160,128]{1,0:T(8,128)S(1)}, u32[]{:S(2)}, u32[]{:S(2)}) %collective-permute-start.15) | collective-permute-done | bytes 81952 | tf_op jit(solution)/shard_map/ppermute | solution.py:33
  59.4 1.9 %collective-permute-start.17 = (f32[160,128]{1,0:T(8,128)S(1)}, f32[160,128]{1,0:T(8,128)S(1)}, u32[]{:S(2)}, u32[]{:S(2)}) collective-permute-start(f32[160,128]{1,0:T(8,128)S(1)} %add.71), channel_id=1, source_target_pairs={{0,1},{1,0},{2,3},{3,2},{4,5},{5,4},{6,7},{7,6},{8,9},{9,8},{10,11... | collective-permute-start | bytes 245768 | tf_op jit(solution)/shard_map/ppermute | solution.py:43
  61.8 1.9 %collective-permute-done.18 = f32[160,128]{1,0:T(8,128)S(1)} collective-permute-done((f32[160,128]{1,0:T(8,128)S(1)}, f32[160,128]{1,0:T(8,128)S(1)}, u32[]{:S(2)}, u32[]{:S(2)}) %collective-permute-start.18) | collective-permute-done | bytes 81952 | tf_op jit(solution)/shard_map/ppermute | solution.py:43
  65.8 2.7 %collective-permute-start.20 = (f32[128,128]{1,0:T(8,128)S(1)}, f32[128,128]{1,0:T(8,128)S(1)}, u32[]{:S(2)}, u32[]{:S(2)}) collective-permute-start(f32[128,128]{1,0:T(8,128)S(1)} %add.69), channel_id=1, source_target_pairs={{0,4},{1,5},{2,6},{3,7},{4,0},{5,1},{6,2},{7,3},{8,12},{9,13},{10,... | collective-permute-start | bytes 196616 | tf_op jit(solution)/shard_map/ppermute | solution.py:33
  68.5 4.1 %collective-permute-done.20 = f32[128,128]{1,0:T(8,128)S(1)} collective-permute-done((f32[128,128]{1,0:T(8,128)S(1)}, f32[128,128]{1,0:T(8,128)S(1)}, u32[]{:S(2)}, u32[]{:S(2)}) %collective-permute-start.20) | collective-permute-done | bytes 65568 | tf_op jit(solution)/shard_map/ppermute | solution.py:33
  72.7 14.0 %merge.1 = (f32[32,640]{1,0:T(8,128)S(1)}, f32[32,640]{1,0:T(8,128)S(1)}, f32[32,640]{1,0:T(8,128)S(1)}, f32[32,640]{1,0:T(8,128)S(1)}) custom-call(s32[2]{0:T(128)S(1)} %copy-done.6, f32[4,160,128]{2,1,0:T(8,128)S(1)} %pad_maximum_fusion.even_ref, f32[4,160,128]{2,1,0:T(8,128)S(1)} %collective-permute-done.19.odd_ref, ...), custom_call_target="tpu_custom_call" | custom-call | tf_op jit(solution)/shard_map/merge/pallas_call | solution.py:367
  88.6 3.4 %collective-permute-done.22.refs_2_ = f32[32,640]{1,0:T(8,128)S(1)} collective-permute-done((f32[32,640]{1,0:T(8,128)S(1)}, f32[32,640]{1,0:T(8,128)S(1)}, u32[]{:S(2)}, u32[]{:S(2)}) %collective-permute-start.22) | collective-permute-done | bytes 81952 | tf_op jit(solution)/shard_map/ppermute | solution.py:33
  (54 shorter events, 19.9 us)
Async XLA Ops:
  8.6 12.8 %collective-permute-start.2 = (f32[384,128]{1,0:T(8,128)}, f32[384,128]{1,0:T(8,128)S(1)}, u32[]{:S(2)}, u32[]{:S(2)}) collective-permute-start(f32[384,128]{1,0:T(8,128)} %get-tuple-element.42.refs_1_), channel_id=1, source_target_pairs={{0,8},{8,0},{16,24},{24,16},{1,9},{9,1},{17,25},{25,17},{2,10},{10... | collective-permute-start | bytes 589832 | tf_op jit(solution)/shard_map/ppermute | solution.py:33
  9.1 12.3 %collective-permute-start.3 = (f32[384,128]{1,0:T(8,128)}, f32[384,128]{1,0:T(8,128)S(1)}, u32[]{:S(2)}, u32[]{:S(2)}) collective-permute-start(f32[384,128]{1,0:T(8,128)} %get-tuple-element.43.refs_2_), channel_id=1, source_target_pairs={{0,16},{8,24},{16,0},{24,8},{1,17},{9,25},{17,1},{25,9},{2,18},{10... | collective-permute-start | bytes 589832 | tf_op jit(solution)/shard_map/ppermute | solution.py:33
  11.7 9.7 %collective-permute-start.4 = (f32[384,128]{1,0:T(8,128)}, f32[384,128]{1,0:T(8,128)S(1)}, u32[]{:S(2)}, u32[]{:S(2)}) collective-permute-start(f32[384,128]{1,0:T(8,128)} %get-tuple-element.44.refs_3_), channel_id=1, source_target_pairs={{0,24},{8,16},{16,8},{24,0},{1,25},{9,17},{17,9},{25,1},{2,26},{10... | collective-permute-start | bytes 589832 | tf_op jit(solution)/shard_map/ppermute | solution.py:33
  11.8 5.5 %collective-permute-start = (f32[64,128]{1,0:T(8,128)}, f32[64,128]{1,0:T(8,128)S(1)}, u32[]{:S(2)}, u32[]{:S(2)}) collective-permute-start(f32[64,128]{1,0:T(8,128)} %get-tuple-element.46), channel_id=1, source_target_pairs={{0,1},{1,2},{2,3},{3,4},{4,5},{5,6},{6,7},{8,9},{9,10},{10,11},{11... | collective-permute-start | bytes 98312 | tf_op jit(solution)/shard_map/ppermute | solution.py:309
  15.4 6.0 %collective-permute-start.1 = (f32[64,128]{1,0:T(8,128)}, f32[64,128]{1,0:T(8,128)S(1)}, u32[]{:S(2)}, u32[]{:S(2)}) collective-permute-start(f32[64,128]{1,0:T(8,128)} %get-tuple-element.47), channel_id=1, source_target_pairs={{1,0},{2,1},{3,2},{4,3},{5,4},{6,5},{7,6},{9,8},{10,9},{11,10},{12... | collective-permute-start | bytes 98312 | tf_op jit(solution)/shard_map/ppermute | solution.py:310
  28.3 4.8 %collective-permute-start.5 = (f32[128,128]{1,0:T(8,128)S(1)}, f32[128,128]{1,0:T(8,128)S(1)}, u32[]{:S(2)}, u32[]{:S(2)}) collective-permute-start(f32[128,128]{1,0:T(8,128)S(1)} %probe.1), channel_id=1, source_target_pairs={{0,1},{1,0},{2,3},{3,2},{4,5},{5,4},{6,7},{7,6},{8,9},{9,8},{10,11... | collective-permute-start | bytes 196616 | tf_op jit(solution)/shard_map/ppermute | solution.py:33
  30.8 2.3 %collective-permute-start.6 = (f32[128,128]{1,0:T(8,128)S(1)}, f32[128,128]{1,0:T(8,128)S(1)}, u32[]{:S(2)}, u32[]{:S(2)}) collective-permute-start(f32[128,128]{1,0:T(8,128)S(1)} %get-tuple-element.51.refs_5_), channel_id=1, source_target_pairs={{0,8},{8,0},{16,24},{24,16},{1,9},{9,1},{17,25},{25,17},{2,10},{10... | collective-permute-start | bytes 196616 | tf_op jit(solution)/shard_map/ppermute | solution.py:33
  30.8 4.5 %collective-permute-start.7 = (f32[128,128]{1,0:T(8,128)S(1)}, f32[128,128]{1,0:T(8,128)S(1)}, u32[]{:S(2)}, u32[]{:S(2)}) collective-permute-start(f32[128,128]{1,0:T(8,128)S(1)} %get-tuple-element.52.refs_6_), channel_id=1, source_target_pairs={{0,16},{8,24},{16,0},{24,8},{1,17},{9,25},{17,1},{25,9},{2,18},{10... | collective-permute-start | bytes 196616 | tf_op jit(solution)/shard_map/ppermute | solution.py:33
  32.4 4.1 %collective-permute-start.8 = (f32[128,128]{1,0:T(8,128)S(1)}, f32[128,128]{1,0:T(8,128)S(1)}, u32[]{:S(2)}, u32[]{:S(2)}) collective-permute-start(f32[128,128]{1,0:T(8,128)S(1)} %get-tuple-element.53.refs_7_), channel_id=1, source_target_pairs={{0,24},{8,16},{16,8},{24,0},{1,25},{9,17},{17,9},{25,1},{2,26},{10... | collective-permute-start | bytes 196616 | tf_op jit(solution)/shard_map/ppermute | solution.py:33
  38.7 1.7 %collective-permute-start.9 = (f32[4,160,128]{2,1,0:T(8,128)S(1)}, f32[4,160,128]{2,1,0:T(8,128)S(1)}, u32[]{:S(2)}, u32[]{:S(2)}) collective-permute-start(f32[4,160,128]{2,1,0:T(8,128)S(1)} %get-tuple-element.67), channel_id=1, source_target_pairs={{0,8},{8,0},{16,24},{24,16},{1,9},{9,1},{17,25},{25,17},{2,10},{10... | collective-permute-start | bytes 983048 | tf_op jit(solution)/shard_map/ppermute | solution.py:33
  40.5 7.8 %collective-permute-start.10 = (f32[160,128]{1,0:T(8,128)S(1)}, f32[160,128]{1,0:T(8,128)S(1)}, u32[]{:S(2)}, u32[]{:S(2)}) collective-permute-start(f32[160,128]{1,0:T(8,128)S(1)} %get-tuple-element.80), channel_id=1, source_target_pairs={{0,16},{1,17},{2,18},{3,19},{4,20},{5,21},{6,22},{7,23},{8,24},{9,... | collective-permute-start | bytes 245768 | tf_op jit(solution)/shard_map/ppermute | solution.py:43
  42.0 6.3 %collective-permute-start.12 = (f32[160,128]{1,0:T(8,128)S(1)}, f32[160,128]{1,0:T(8,128)S(1)}, u32[]{:S(2)}, u32[]{:S(2)}) collective-permute-start(f32[160,128]{1,0:T(8,128)S(1)} %get-tuple-element.81), channel_id=1, source_target_pairs={{0,17},{1,16},{2,19},{3,18},{4,21},{5,20},{6,23},{7,22},{8,25},{9,... | collective-permute-start | bytes 245768 | tf_op jit(solution)/shard_map/ppermute | solution.py:43
  42.1 6.2 %collective-permute-start.11 = (f32[160,128]{1,0:T(8,128)S(1)}, f32[160,128]{1,0:T(8,128)S(1)}, u32[]{:S(2)}, u32[]{:S(2)}) collective-permute-start(f32[160,128]{1,0:T(8,128)S(1)} %get-tuple-element.82), channel_id=1, source_target_pairs={{0,1},{1,0},{2,3},{3,2},{4,5},{5,4},{6,7},{7,6},{8,9},{9,8},{10,11... | collective-permute-start | bytes 245768 | tf_op jit(solution)/shard_map/ppermute | solution.py:43
  44.0 4.3 %collective-permute-start.13 = (f32[128,128]{1,0:T(8,128)S(1)}, f32[128,128]{1,0:T(8,128)S(1)}, u32[]{:S(2)}, u32[]{:S(2)}) collective-permute-start(f32[128,128]{1,0:T(8,128)S(1)} %add.57), channel_id=1, source_target_pairs={{0,2},{1,3},{2,0},{3,1},{4,6},{5,7},{6,4},{7,5},{8,10},{9,11},{10,... | collective-permute-start | bytes 196616 | tf_op jit(solution)/shard_map/ppermute | solution.py:33
  48.3 4.5 %collective-permute-start.14 = (f32[160,128]{1,0:T(8,128)S(1)}, f32[160,128]{1,0:T(8,128)S(1)}, u32[]{:S(2)}, u32[]{:S(2)}) collective-permute-start(f32[160,128]{1,0:T(8,128)S(1)} %fusion.6), channel_id=1, source_target_pairs={{0,2},{1,3},{2,0},{3,1},{4,6},{5,7},{6,4},{7,5},{8,10},{9,11},{10,... | collective-permute-start | bytes 245768 | tf_op jit(solution)/shard_map/ppermute | solution.py:33
  52.9 5.4 %collective-permute-start.15 = (f32[160,128]{1,0:T(8,128)S(1)}, f32[160,128]{1,0:T(8,128)S(1)}, u32[]{:S(2)}, u32[]{:S(2)}) collective-permute-start(f32[160,128]{1,0:T(8,128)S(1)} %add.70), channel_id=1, source_target_pairs={{0,4},{1,5},{2,6},{3,7},{4,0},{5,1},{6,2},{7,3},{8,12},{9,13},{10,... | collective-permute-start | bytes 245768 | tf_op jit(solution)/shard_map/ppermute | solution.py:33
  58.3 5.4 %collective-permute-start.18 = (f32[160,128]{1,0:T(8,128)S(1)}, f32[160,128]{1,0:T(8,128)S(1)}, u32[]{:S(2)}, u32[]{:S(2)}) collective-permute-start(f32[160,128]{1,0:T(8,128)S(1)} %add.71), channel_id=1, source_target_pairs={{0,17},{1,16},{2,19},{3,18},{4,21},{5,20},{6,23},{7,22},{8,25},{9,... | collective-permute-start | bytes 245768 | tf_op jit(solution)/shard_map/ppermute | solution.py:43
  59.4 5.2 %collective-permute-start.17 = (f32[160,128]{1,0:T(8,128)S(1)}, f32[160,128]{1,0:T(8,128)S(1)}, u32[]{:S(2)}, u32[]{:S(2)}) collective-permute-start(f32[160,128]{1,0:T(8,128)S(1)} %add.71), channel_id=1, source_target_pairs={{0,1},{1,0},{2,3},{3,2},{4,5},{5,4},{6,7},{7,6},{8,9},{9,8},{10,11... | collective-permute-start | bytes 245768 | tf_op jit(solution)/shard_map/ppermute | solution.py:43
  61.3 4.4 %collective-permute-start.16 = (f32[160,128]{1,0:T(8,128)S(1)}, f32[160,128]{1,0:T(8,128)S(1)}, u32[]{:S(2)}, u32[]{:S(2)}) collective-permute-start(f32[160,128]{1,0:T(8,128)S(1)} %add.71), channel_id=1, source_target_pairs={{0,16},{1,17},{2,18},{3,19},{4,20},{5,21},{6,22},{7,23},{8,24},{9,... | collective-permute-start | bytes 245768 | tf_op jit(solution)/shard_map/ppermute | solution.py:43
  65.7 6.9 %collective-permute-start.19 = (f32[4,160,128]{2,1,0:T(8,128)S(1)}, f32[4,160,128]{2,1,0:T(8,128)S(1)}, u32[]{:S(2)}, u32[]{:S(2)}) collective-permute-start(f32[4,160,128]{2,1,0:T(8,128)S(1)} %pad_maximum_fusion.even_ref), channel_id=1, source_target_pairs={{0,8},{8,0},{16,24},{24,16},{1,9},{9,1},{17,25},{25,17},{2,10},{10... | collective-permute-start | bytes 983048 | tf_op jit(solution)/shard_map/ppermute | solution.py:33
  65.8 6.8 %collective-permute-start.20 = (f32[128,128]{1,0:T(8,128)S(1)}, f32[128,128]{1,0:T(8,128)S(1)}, u32[]{:S(2)}, u32[]{:S(2)}) collective-permute-start(f32[128,128]{1,0:T(8,128)S(1)} %add.69), channel_id=1, source_target_pairs={{0,4},{1,5},{2,6},{3,7},{4,0},{5,1},{6,2},{7,3},{8,12},{9,13},{10,... | collective-permute-start | bytes 196616 | tf_op jit(solution)/shard_map/ppermute | solution.py:33
  86.7 1.9 %collective-permute-start.21 = (f32[32,640]{1,0:T(8,128)S(1)}, f32[32,640]{1,0:T(8,128)S(1)}, u32[]{:S(2)}, u32[]{:S(2)}) collective-permute-start(f32[32,640]{1,0:T(8,128)S(1)} %get-tuple-element.75), channel_id=1, source_target_pairs={{0,8},{8,0},{16,24},{24,16},{1,9},{9,1},{17,25},{25,17},{2,10},{10... | collective-permute-start | bytes 245768 | tf_op jit(solution)/shard_map/ppermute | solution.py:33
  86.7 5.3 %collective-permute-start.22 = (f32[32,640]{1,0:T(8,128)S(1)}, f32[32,640]{1,0:T(8,128)S(1)}, u32[]{:S(2)}, u32[]{:S(2)}) collective-permute-start(f32[32,640]{1,0:T(8,128)S(1)} %get-tuple-element.76), channel_id=1, source_target_pairs={{0,16},{8,24},{16,0},{24,8},{1,17},{9,25},{17,1},{25,9},{2,18},{10... | collective-permute-start | bytes 245768 | tf_op jit(solution)/shard_map/ppermute | solution.py:33
  87.4 5.5 %collective-permute-start.23 = (f32[32,640]{1,0:T(8,128)S(1)}, f32[32,640]{1,0:T(8,128)S(1)}, u32[]{:S(2)}, u32[]{:S(2)}) collective-permute-start(f32[32,640]{1,0:T(8,128)S(1)} %get-tuple-element.77), channel_id=1, source_target_pairs={{0,24},{8,16},{16,8},{24,0},{1,25},{9,17},{17,9},{25,1},{2,26},{10... | collective-permute-start | bytes 245768 | tf_op jit(solution)/shard_map/ppermute | solution.py:33
  (7 other events, 47.1 us)

commit v4 on v3

--- a/solution.py
+++ b/solution.py
@@ -13,11 +13,10 @@
 exact = lax.Precision.HIGHEST
 F32 = jnp.float32
 VMEM_LIMIT = 48 * 1024 * 1024
-FULL_VMEM = 60 * 1024 * 1024
-
-
-def params(limit=VMEM_LIMIT):
-    return pltpu.CompilerParams(vmem_limit_bytes=limit)
+
+
+def params():
+    return pltpu.CompilerParams(vmem_limit_bytes=VMEM_LIMIT)
 
 
 def whole():
@@ -43,6 +42,15 @@
     return lax.ppermute(x, ("tm", "space"), route)
 
 
+def to_edge_owner(x, k):
+    parts, patches = lax.axis_size("tm"), lax.axis_size("space")
+    route = []
+    for s in range(patches - 1):
+        route.append((k * patches + s, s + 1))
+        route.append(((k ^ (parts - 1)) * patches + s + 1, (parts - 1) * patches + s))
+    return lax.ppermute(x, ("tm", "space"), route)
+
+
 def shift_rows(x, by):
     edge = jnp.zeros((1, x.shape[1]), x.dtype)
     if by > 0:
@@ -61,8 +69,8 @@
 
 
 def filter_kernel(parts, me_ref, taps_ref, snap_hbm, mask_ref, *rest):
-    bigs, (small_ref, up_ref, down_ref) = rest[:parts], rest[parts:parts + 3]
-    snaps, sems, mask_t, narrowed, filtered = rest[parts + 3:]
+    pieces, shares, edges_ref = rest[:parts], rest[parts:2 * parts], rest[2 * parts]
+    snaps, sems, mask_t, narrowed, filtered = rest[2 * parts + 1:]
     rows, cells = snaps.shape[0], narrowed.shape[1]
     chunks = rows // CHUNK
 
@@ -95,46 +103,24 @@
         for k in range(1, TAPS):
             total = total + rtaps[k] * narrowed[2 * i + k]
         filtered[i * cells:(i + 1) * cells, :] = total
-    up_ref[...] = rtaps[4] * narrowed[2] + rtaps[5] * narrowed[3]
-    down_ref[...] = rtaps[0] * narrowed[rows] + rtaps[1] * narrowed[rows + 1]
+    edges_ref[:cells, :] = rtaps[0] * narrowed[rows] + rtaps[1] * narrowed[rows + 1]
+    edges_ref[cells:, :] = rtaps[4] * narrowed[2] + rtaps[5] * narrowed[3]
     me = me_ref[0]
-    piece = filtered.shape[0] // parts
-    for k in range(parts):
-        inner = pl.multiple_of((me ^ k) * piece + cells, 8)
-        bigs[k][...] = filtered[pl.ds(inner, piece - 2 * cells), :]
-    for d in range(parts):
-        small_ref[2 * d * cells:(2 * d + 1) * cells, :] = filtered[d * piece:d * piece + cells, :]
-        small_ref[(2 * d + 1) * cells:(2 * d + 2) * cells, :] = filtered[(d + 1) * piece - cells:(d + 1) * piece, :]
-
-
-def edge_kernel(parts, me_ref, small_ref, above_ref, below_ref, *rest):
-    outs, (held,) = rest[:parts], rest[parts:]
-    held[...] = small_ref[...]
-    cells = above_ref.shape[0]
-    size = held.shape[0]
-    held[:cells, :] = held[:cells, :] + above_ref[...]
-    held[size - cells:, :] = held[size - cells:, :] + below_ref[...]
+    size = filtered.shape[0] // parts
+    for k in range(parts):
+        pieces[k][...] = filtered[pl.ds(pl.multiple_of((me ^ k) * size, 8), size), :]
+        which = jnp.where((me ^ k) == 0, 0, 1)
+        shares[k][...] = edges_ref[pl.ds(pl.multiple_of(which * cells, 8), cells), :]
+
+
+def probe_kernel(parts, me_ref, *refs):
+    pieces, (edges_ref, probes_ref, below_ref, above_ref, out_ref) = refs[:parts], refs[parts:]
     me = me_ref[0]
-    for k in range(parts):
-        outs[k][...] = held[pl.ds(pl.multiple_of((me ^ k) * 2 * cells, 8), 2 * cells), :]
-
-
-def probe_kernel(parts, me_ref, *refs):
-    bigs, smalls, probes_ref, out_ref = refs[:parts], refs[parts:2 * parts], refs[2 * parts], refs[2 * parts + 1]
-    me = me_ref[0]
-    cells = smalls[0].shape[0] // 2
-    inner = bigs[0].shape[0]
-    piece = inner + 2 * cells
-    total = None
-    for k in range(parts):
-        base = (me ^ k) * piece
-        first = probes_ref[pl.ds(pl.multiple_of(base, 8), cells), :]
-        middle = probes_ref[pl.ds(pl.multiple_of(base + cells, 8), inner), :]
-        last = probes_ref[pl.ds(pl.multiple_of(base + cells + inner, 8), cells), :]
-        mine = jnp.concatenate([bigs[k][...], smalls[k][...]], axis=0)
-        there = jnp.concatenate([middle, first, last], axis=0)
-        term = exact_dot(mine, there, ((0,), (0,)))
-        total = term if total is None else total + term
+    size = pieces[0].shape[0]
+    total = exact_dot(edges_ref[...], jnp.concatenate([below_ref[...], above_ref[...]], axis=0), ((0,), (0,)))
+    for k in range(parts):
+        there = probes_ref[pl.ds(pl.multiple_of((me ^ k) * size, 8), size), :]
+        total = total + exact_dot(pieces[k][...], there, ((0,), (0,)))
     out_ref[...] = total
 
 
@@ -143,14 +129,16 @@
 
 
 def gram_kernel(parts, span, me_ref, *refs):
-    bigs, smalls = refs[:parts], refs[parts:2 * parts]
+    pieces, shares = refs[:parts], refs[parts:2 * parts]
     send_ref, keep_ref, wide, flat = refs[2 * parts:]
     me, owner = me_ref[0], me_ref[1]
-    inner, cols = bigs[0].shape
+    size, cols = pieces[0].shape
+    cells = shares[0].shape[0]
+    edge = pl.ds(pl.multiple_of(jnp.where(me == parts - 1, size - cells, 0), 8), cells)
     for k in range(parts):
         at = pl.ds(pl.multiple_of((me ^ k) * cols, cols), cols)
-        wide[:inner, at] = bigs[k][...]
-        wide[inner:, at] = smalls[k][...]
+        wide[:, at] = pieces[k][...]
+        wide[edge, at] = wide[edge, at] + shares[k][...]
     where = {ab: j for j, ab in enumerate(block_order(parts))}
     for a in range(0, parts, 2):
         left = wide[:, a * cols:(a + 2) * cols]
@@ -263,12 +251,11 @@
     pieces, (basis_ref, coef_ref) = refs[:parts], refs[parts:]
     me = me_ref[0]
     per, cells = basis_ref.shape[0] // parts, basis_ref.shape[2]
-    order = list(range(1, per - 1)) + [0, per - 1]
     total = None
     for k in range(parts):
         base = (me ^ k) * per
-        for at, i in enumerate(order):
-            basis_ref[base + i] = pieces[k][:, at * cells:(at + 1) * cells]
+        for i in range(per):
+            basis_ref[base + i] = pieces[k][:, i * cells:(i + 1) * cells]
         tail = pieces[k][:, per * cells:]
         total = tail if total is None else total + tail
     coef_ref[...] = total
@@ -284,16 +271,15 @@
     parts, patches = lax.axis_size("tm"), lax.axis_size("space")
     cells = half_rows * half_cols
     piece = cells // parts
-    inner = piece - 2 * half_cols
     span = 2 if patches > 1 else 1
     position, patch = lax.axis_index("tm"), lax.axis_index("space")
     me = jnp.stack([position, position + parts * (patch % span)]).astype(jnp.int32)
 
     outs = pl.pallas_call(
         functools.partial(filter_kernel, parts),
-        out_shape=[shape(inner, cols)] * parts + [shape(2 * parts * half_cols, cols)] + [shape(half_cols, cols)] * 2,
+        out_shape=[shape(piece, cols)] * parts + [shape(half_cols, cols)] * parts + [shape(2 * half_cols, cols)],
         in_specs=[scalars(), scalars(), pl.BlockSpec(memory_space=pltpu.HBM), whole()],
-        out_specs=[whole()] * (parts + 3),
+        out_specs=[whole()] * (2 * parts + 1),
         scratch_shapes=[
             pltpu.VMEM((rows, grid_cols, cols), F32),
             pltpu.SemaphoreType.DMA((rows // CHUNK,)),
@@ -301,47 +287,35 @@
             pltpu.VMEM((rows + 4, half_cols, cols), F32),
             pltpu.VMEM((cells, cols), F32),
         ],
-        compiler_params=params(FULL_VMEM),
+        compiler_params=params(),
         name="filter",
-    )(me, jnp.concatenate([taps_rows, taps_cols]), snapshots, land_mask)
-    bigs, (small, to_above, to_below) = outs[:parts], outs[parts:]
+    )(me, jnp.concatenate([taps_rows, taps_cols]), pltpu.with_memory_space_constraint(snapshots, pltpu.HBM), land_mask)
+    pieces, shares, edges = outs[:parts], outs[parts:2 * parts], outs[2 * parts]
+    far = [pieces[0]] + [swap(pieces[k], "tm", k) for k in range(1, parts)]
+    far += [to_edge_owner(shares[k], k) for k in range(parts)]
+
     up = [(i, i + 1) for i in range(patches - 1)]
-    above = lax.ppermute(to_below, "space", up)
-    below = lax.ppermute(to_above, "space", [(j, i) for i, j in up])
-    far_bigs = [bigs[0]] + [swap(bigs[k], "tm", k) for k in range(1, parts)]
-    above, below, *far_bigs = lax.optimization_barrier([above, below] + far_bigs)
-
-    smalls = pl.pallas_call(
-        functools.partial(edge_kernel, parts),
-        out_shape=[shape(2 * half_cols, cols)] * parts,
-        in_specs=[scalars()] + [whole()] * 3,
-        out_specs=[whole()] * parts,
-        scratch_shapes=[pltpu.VMEM((2 * parts * half_cols, cols), F32)],
-        compiler_params=params(),
-        name="edge",
-    )(me, small, above, below)
-    far_smalls = [smalls[0]] + [swap(smalls[k], "tm", k) for k in range(1, parts)]
-
+    probes_below = lax.ppermute(probes[0], "space", [(j, i) for i, j in up])
+    probes_above = lax.ppermute(probes[-1], "space", up)
     probe_sum = pl.pallas_call(
         functools.partial(probe_kernel, parts),
         out_shape=shape(cols, cols),
-        in_specs=[scalars()] + [whole()] * (2 * parts + 1),
+        in_specs=[scalars()] + [whole()] * (parts + 4),
         out_specs=whole(),
         compiler_params=params(),
-        cost_estimate=pl.CostEstimate(flops=12 * cells * cols * cols, bytes_accessed=8 * cells * cols, transcendentals=0),
         name="probe",
-    )(me, *bigs, *smalls, probes.reshape(cells, cols))
+    )(me, *pieces, edges, probes.reshape(cells, cols), probes_below, probes_above)
     bits = [1 << b for b in range(patches.bit_length() - 1)]
     for bit in bits[:1]:
         probe_sum = probe_sum + swap(probe_sum, "space", bit)
-    probe_sum, *far = lax.optimization_barrier([probe_sum] + far_bigs + far_smalls)
+    probe_sum, *far = lax.optimization_barrier([probe_sum] + far)
 
     blocks = parts * (parts + 1) // 2
-    shares = parts * span
-    size = blocks * cols // shares
+    owners = parts * span
+    size = blocks * cols // owners
     send, keep, wide = pl.pallas_call(
         functools.partial(gram_kernel, parts, span),
-        out_shape=[shape(shares // 2, size, cols)] * 2 + [shape(piece, parts * cols)],
+        out_shape=[shape(owners // 2, size, cols)] * 2 + [shape(piece, parts * cols)],
         in_specs=[scalars()] + [whole()] * (2 * parts),
         out_specs=[whole()] * 3,
         scratch_shapes=[pltpu.VMEM((blocks * cols, cols), F32)],
@@ -352,7 +326,7 @@
         probe_sum = probe_sum + swap(probe_sum, "space", bit)
     got = swap(send, "tm", 1)
     mine = keep[0] + got[0]
-    for h in range(1, shares // 2):
+    for h in range(1, owners // 2):
         mine = mine + swap_both(keep[h] + got[h], 2 * h)
     mine, probe_sum = lax.optimization_barrier((mine, probe_sum))
     for bit in bits[1:]:
@@ -360,7 +334,9 @@
     mine, probe_sum = lax.optimization_barrier((mine, probe_sum))
     for bit in bits[1:][-1:]:
         probe_sum = probe_sum + swap(probe_sum, "space", bit)
-    even = jnp.stack([mine] + [swap_both(mine, 2 * h) for h in range(1, shares // 2)])
+    even = [mine] + [swap_both(mine, 2 * h) for h in range(1, owners // 2)]
+    probe_sum, *even = lax.optimization_barrier([probe_sum] + even)
+    even = jnp.stack(even)
     odd = swap(even, "tm", 1)
 
     width = cols // parts

time: 94.7 us -> 92.7 us (0.979)
  starting transfers between devices: 30.3 us -> 47.6 us
  waiting for transfers between devices: 30.5 us -> 17.6 us
  local copies, waits for them, and re-layouts: 4.65 us -> 0.77 us
  Pallas kernels: 26 us -> 24.4 us
  other arithmetic: 2.03 us -> 1.02 us
    ppermute x6, starting transfers between devices: 7.11 us -> 14.8 us  [swap_both(): return lax.ppermute(x, ('tm', 'space'), route)]
    ppermute x2 -> x6, starting transfers between devices: 4.88 us -> 11.3 us  [the longest x4 6.43 us: to_edge_owner(): return lax.ppermute(x, ('tm', 'space'), route)]
    ppermute x16 -> x13, waiting for transfers between devices: 21.9 us -> 17.3 us  [swap(): return lax.ppermute(x, axis, [(i, i ^ mask) for i in range(count)])]
    ppermute x2 -> x6, waiting for transfers between devices: 4.72 us -> 0.29 us  [the longest x1 0.28 us: local(): probes_above = lax.ppermute(probes[-1], 'space', up)]
    unnamed x14 -> x4, local copies, waits for them, and re-layouts: 4.65 us -> 0.76 us
    ppermute x6, waiting for transfers between devices: 3.87 us -> 0.02 us  [swap_both(): return lax.ppermute(x, ('tm', 'space'), route)]
    ppermute x16 -> x13, starting transfers between devices: 18.3 us -> 21.5 us  [swap(): return lax.ppermute(x, axis, [(i, i ^ mask) for i in range(count)])]
    pallas_call x1, Pallas kernels: 6.04 us -> 4.89 us  [local(): pl.pallas_call(functools.partial(filter_kernel, parts), out_shape=[shape(...]
  transfers between devices with their start and end apart: 24 -> 25, of which waited for: 15 -> 10; matrix products, arithmetic and copies ran while one was open for 0% -> 0% of each run, Pallas kernels for 0% -> 2%
where the time goes in v4:
time: 92.7 us; the launch traced here: 92.3 us
  starting transfers between devices  47.6 us (51%)
  Pallas kernels  24.4 us (26%)
  waiting for transfers between devices  17.6 us (19%)
  other arithmetic  1.02 us (1%)
    ppermute x13, starting transfers between devices, swap(): return lax.ppermute(x, axis, [(i, i ^ mask) for i in range(count)])  21.5 us
    ppermute x13, waiting for transfers between devices, swap(): return lax.ppermute(x, axis, [(i, i ^ mask) for i in range(count)])  17.3 us
    ppermute x6, starting transfers between devices, swap_both(): return lax.ppermute(x, ('tm', 'space'), route)  14.8 us
    pallas_call x1, Pallas kernels, local(): pl.pallas_call(functools.partial(merge_kernel, parts, span), out_shape=[s...  14 us
    ppermute x4, starting transfers between devices, to_edge_owner(): return lax.ppermute(x, ('tm', 'space'), route)  6.43 us
    pallas_call x1, Pallas kernels, local(): pl.pallas_call(functools.partial(filter_kernel, parts), out_shape=[shape(...  4.89 us
    ppermute x1, starting transfers between devices, local(): probes_above = lax.ppermute(probes[-1], 'space', up)  3.6 us
    pallas_call x1, Pallas kernels, local(): pl.pallas_call(functools.partial(gram_kernel, parts, span), out_shape=[sh...  2.32 us
  transfers between devices with their start and end apart: 25, of which 10 were waited for; matrix products, arithmetic and copies ran while one was open for 0% of the time, Pallas kernels for 2%

profile of v4, /device:TPU:0, one launch (start us, length us, event | category | flops | bytes accessed | tf_op | source)
XLA Modules:
  0.0 92.3 jit_solution(17103761090768477042)
XLA Ops:
  2.3 4.9 %filter.1 = (f32[512,128]{1,0:T(8,128)S(1)}, f32[512,128]{1,0:T(8,128)S(1)}, f32[512,128]{1,0:T(8,128)S(1)}, f32[512,128]{1,0:T(8,128)S(1)}, f32[64,128]{1,0:T(8...) custom-call(s32[2]{0:T(128)S(1)} %pad_add_fusion.me_ref, ...), custom_call_target="tpu_custom_call" | custom-call | tf_op jit(solution)/shard_map/filter/pallas_call | solution.py:278
  7.7 2.6 %collective-permute-start.4 = (f32[512,128]{1,0:T(8,128)S(1)}, f32[512,128]{1,0:T(8,128)S(1)}, u32[]{:S(2)}, u32[]{:S(2)}) collective-permute-start(f32[512,128]{1,0:T(8,128)S(1)} %get-tuple-element.40.refs_2_), channel_id=1, source_target_pairs={{0,16},{8,24},{16,0},{24,8},{1,17},{9,25},{17,1},{25,9},{2,18},{10... | collective-permute-start | bytes 786440 | tf_op jit(solution)/shard_map/ppermute | solution.py:32
  10.4 3.6 %collective-permute-start.1 = (f32[64,128]{1,0:T(8,128)S(1)}, f32[64,128]{1,0:T(8,128)S(1)}, u32[]{:S(2)}, u32[]{:S(2)}) collective-permute-start(f32[64,128]{1,0:T(8,128)S(1)} %get-tuple-element.74), channel_id=1, source_target_pairs={{0,1},{1,2},{2,3},{3,4},{4,5},{5,6},{6,7},{8,9},{9,10},{10,11},{11... | collective-permute-start | bytes 98312 | tf_op jit(solution)/shard_map/ppermute | solution.py:299
  15.6 4.3 %collective-permute-start.6 = (f32[64,128]{1,0:T(8,128)S(1)}, f32[64,128]{1,0:T(8,128)S(1)}, u32[]{:S(2)}, u32[]{:S(2)}) collective-permute-start(f32[64,128]{1,0:T(8,128)S(1)} %get-tuple-element.43), channel_id=1, source_target_pairs={{0,1},{25,24},{1,2},{26,25},{2,3},{27,26},{3,4},{28,27},{4,5},{29,... | collective-permute-start | bytes 98312 | tf_op jit(solution)/shard_map/ppermute | solution.py:51
  19.9 1.7 %probe.1 = f32[128,128]{1,0:T(8,128)S(1)} custom-call(s32[2]{0:T(128)S(1)} %pad_add_fusion.me_ref, f32[512,128]{1,0:T(8,128)S(1)} %get-tuple-element.47.refs_0_, f32[512,128]{1,0:T(8,128)S(1)} %get-tuple-element.39.refs_1_, f32[512,128]{1,0:T(8,128)S(1)} %get-tuple-element.40.refs_2_, f32[512,128]{1,0:T(8,128)S(1)} %get-tuple-element.41.refs_3_, ...), custom_call_target="tpu_custom_call" | custom-call | tf_op jit(solution)/shard_map/probe/pallas_call | solution.py:300
  21.6 2.5 %collective-permute-start.2 = (f32[128,128]{1,0:T(8,128)S(1)}, f32[128,128]{1,0:T(8,128)S(1)}, u32[]{:S(2)}, u32[]{:S(2)}) collective-permute-start(f32[128,128]{1,0:T(8,128)S(1)} %probe.1), channel_id=1, source_target_pairs={{0,1},{1,0},{2,3},{3,2},{4,5},{5,4},{6,7},{7,6},{8,9},{9,8},{10,11... | collective-permute-start | bytes 196616 | tf_op jit(solution)/shard_map/ppermute | solution.py:32
  27.3 2.3 %gram.1 = (f32[4,160,128]{2,1,0:T(8,128)S(1)}, f32[4,160,128]{2,1,0:T(8,128)S(1)}, f32[512,512]{1,0:T(8,128)S(1)}) custom-call(s32[2]{0:T(128)S(1)} %pad_add_fusion.me_ref, f32[512,128]{1,0:T(8,128)S(1)} %get-tuple-element.47.refs_0_, f32[512,128]{1,0:T(8,128)S(1)} %collective-permute-done.3.refs_1_, f32[512,128]{1,0:T(8,128)S(1)} %collective-permute-done.4.refs_2_, ...), custom_call_target="tpu_custom_call" | custom-call | tf_op jit(solution)/shard_map/gram/pallas_call | solution.py:316
  29.6 1.6 %collective-permute-start.10 = (f32[4,160,128]{2,1,0:T(8,128)S(1)}, f32[4,160,128]{2,1,0:T(8,128)S(1)}, u32[]{:S(2)}, u32[]{:S(2)}) collective-permute-start(f32[4,160,128]{2,1,0:T(8,128)S(1)} %get-tuple-element.56), channel_id=1, source_target_pairs={{0,8},{8,0},{16,24},{24,16},{1,9},{9,1},{17,25},{25,17},{2,10},{10... | collective-permute-start | bytes 983048 | tf_op jit(solution)/shard_map/ppermute | solution.py:32
  32.4 8.2 %collective-permute-start.11 = (f32[160,128]{1,0:T(8,128)S(1)}, f32[160,128]{1,0:T(8,128)S(1)}, u32[]{:S(2)}, u32[]{:S(2)}) collective-permute-start(f32[160,128]{1,0:T(8,128)S(1)} %get-tuple-element.76), channel_id=1, source_target_pairs={{0,16},{1,17},{2,18},{3,19},{4,20},{5,21},{6,22},{7,23},{8,24},{9,... | collective-permute-start | bytes 245768 | tf_op jit(solution)/shard_map/ppermute | solution.py:42
  40.6 2.6 %collective-permute-start.13 = (f32[160,128]{1,0:T(8,128)S(1)}, f32[160,128]{1,0:T(8,128)S(1)}, u32[]{:S(2)}, u32[]{:S(2)}) collective-permute-start(f32[160,128]{1,0:T(8,128)S(1)} %get-tuple-element.77), channel_id=1, source_target_pairs={{0,17},{1,16},{2,19},{3,18},{4,21},{5,20},{6,23},{7,22},{8,25},{9,... | collective-permute-start | bytes 245768 | tf_op jit(solution)/shard_map/ppermute | solution.py:42
  43.7 4.1 %collective-permute-start.14 = (f32[128,128]{1,0:T(8,128)S(1)}, f32[128,128]{1,0:T(8,128)S(1)}, u32[]{:S(2)}, u32[]{:S(2)}) collective-permute-start(f32[128,128]{1,0:T(8,128)S(1)} %add.57), channel_id=1, source_target_pairs={{0,2},{1,3},{2,0},{3,1},{4,6},{5,7},{6,4},{7,5},{8,10},{9,11},{10,... | collective-permute-start | bytes 196616 | tf_op jit(solution)/shard_map/ppermute | solution.py:32
  47.8 2.2 %collective-permute-done.14 = f32[128,128]{1,0:T(8,128)S(1)} collective-permute-done((f32[128,128]{1,0:T(8,128)S(1)}, f32[128,128]{1,0:T(8,128)S(1)}, u32[]{:S(2)}, u32[]{:S(2)}) %collective-permute-start.14) | collective-permute-done | bytes 65568 | tf_op jit(solution)/shard_map/ppermute | solution.py:32
  50.1 2.1 %collective-permute-start.15 = (f32[160,128]{1,0:T(8,128)S(1)}, f32[160,128]{1,0:T(8,128)S(1)}, u32[]{:S(2)}, u32[]{:S(2)}) collective-permute-start(f32[160,128]{1,0:T(8,128)S(1)} %fusion.6), channel_id=1, source_target_pairs={{0,2},{1,3},{2,0},{3,1},{4,6},{5,7},{6,4},{7,5},{8,10},{9,11},{10,... | collective-permute-start | bytes 245768 | tf_op jit(solution)/shard_map/ppermute | solution.py:32
  52.2 2.4 %collective-permute-done.15 = f32[160,128]{1,0:T(8,128)S(1)} collective-permute-done((f32[160,128]{1,0:T(8,128)S(1)}, f32[160,128]{1,0:T(8,128)S(1)}, u32[]{:S(2)}, u32[]{:S(2)}) %collective-permute-start.15) | collective-permute-done | bytes 81952 | tf_op jit(solution)/shard_map/ppermute | solution.py:32
  54.6 3.1 %collective-permute-start.16 = (f32[160,128]{1,0:T(8,128)S(1)}, f32[160,128]{1,0:T(8,128)S(1)}, u32[]{:S(2)}, u32[]{:S(2)}) collective-permute-start(f32[160,128]{1,0:T(8,128)S(1)} %add.70), channel_id=1, source_target_pairs={{0,4},{1,5},{2,6},{3,7},{4,0},{5,1},{6,2},{7,3},{8,12},{9,13},{10,... | collective-permute-start | bytes 245768 | tf_op jit(solution)/shard_map/ppermute | solution.py:32
  57.7 2.4 %collective-permute-done.16 = f32[160,128]{1,0:T(8,128)S(1)} collective-permute-done((f32[160,128]{1,0:T(8,128)S(1)}, f32[160,128]{1,0:T(8,128)S(1)}, u32[]{:S(2)}, u32[]{:S(2)}) %collective-permute-start.16) | collective-permute-done | bytes 81952 | tf_op jit(solution)/shard_map/ppermute | solution.py:32
  61.9 1.8 %collective-permute-start.18 = (f32[160,128]{1,0:T(8,128)S(1)}, f32[160,128]{1,0:T(8,128)S(1)}, u32[]{:S(2)}, u32[]{:S(2)}) collective-permute-start(f32[160,128]{1,0:T(8,128)S(1)} %add.71), channel_id=1, source_target_pairs={{0,16},{1,17},{2,18},{3,19},{4,20},{5,21},{6,22},{7,23},{8,24},{9,... | collective-permute-start | bytes 245768 | tf_op jit(solution)/shard_map/ppermute | solution.py:42
  63.7 3.0 %collective-permute-start.17 = (f32[128,128]{1,0:T(8,128)S(1)}, f32[128,128]{1,0:T(8,128)S(1)}, u32[]{:S(2)}, u32[]{:S(2)}) collective-permute-start(f32[128,128]{1,0:T(8,128)S(1)} %add.69), channel_id=1, source_target_pairs={{0,4},{1,5},{2,6},{3,7},{4,0},{5,1},{6,2},{7,3},{8,12},{9,13},{10,... | collective-permute-start | bytes 196616 | tf_op jit(solution)/shard_map/ppermute | solution.py:32
  66.7 2.2 %collective-permute-done.17 = f32[128,128]{1,0:T(8,128)S(1)} collective-permute-done((f32[128,128]{1,0:T(8,128)S(1)}, f32[128,128]{1,0:T(8,128)S(1)}, u32[]{:S(2)}, u32[]{:S(2)}) %collective-permute-start.17) | collective-permute-done | bytes 65568 | tf_op jit(solution)/shard_map/ppermute | solution.py:32
  69.1 1.6 %collective-permute-done.21.odd_ref = f32[4,160,128]{2,1,0:T(8,128)S(1)} collective-permute-done((f32[4,160,128]{2,1,0:T(8,128)S(1)}, f32[4,160,128]{2,1,0:T(8,128)S(1)}, u32[]{:S(2)}, u32[]{:S(2)}) %collective-permute-start.21) | collective-permute-done | bytes 327712 | tf_op jit(solution)/shard_map/ppermute | solution.py:32
  70.7 14.0 %merge.1 = (f32[32,640]{1,0:T(8,128)S(1)}, f32[32,640]{1,0:T(8,128)S(1)}, f32[32,640]{1,0:T(8,128)S(1)}, f32[32,640]{1,0:T(8,128)S(1)}) custom-call(s32[2]{0:T(128)S(1)} %pad_add_fusion.me_ref, f32[4,160,128]{2,1,0:T(8,128)S(1)} %pad_maximum_fusion.even_ref, f32[4,160,128]{2,1,0:T(8,128)S(1)} %collective-permute-done.21.odd_ref, ...), custom_call_target="tpu_custom_call" | custom-call | tf_op jit(solution)/shard_map/merge/pallas_call | solution.py:343
  85.1 1.5 %collective-permute-start.24 = (f32[32,640]{1,0:T(8,128)S(1)}, f32[32,640]{1,0:T(8,128)S(1)}, u32[]{:S(2)}, u32[]{:S(2)}) collective-permute-start(f32[32,640]{1,0:T(8,128)S(1)} %get-tuple-element.71), channel_id=1, source_target_pairs={{0,24},{8,16},{16,8},{24,0},{1,25},{9,17},{17,9},{25,1},{2,26},{10... | collective-permute-start | bytes 245768 | tf_op jit(solution)/shard_map/ppermute | solution.py:32
  86.6 3.6 %collective-permute-done.23.refs_2_ = f32[32,640]{1,0:T(8,128)S(1)} collective-permute-done((f32[32,640]{1,0:T(8,128)S(1)}, f32[32,640]{1,0:T(8,128)S(1)}, u32[]{:S(2)}, u32[]{:S(2)}) %collective-permute-start.23) | collective-permute-done | bytes 81952 | tf_op jit(solution)/shard_map/ppermute | solution.py:32
  90.8 1.5 %final.1 = (f32[32,32,64]{2,1,0:T(8,128)}, f32[32,128]{1,0:T(8,128)}) custom-call(s32[2]{0:T(128)S(1)} %pad_add_fusion.me_ref, f32[32,640]{1,0:T(8,128)S(1)} %get-tuple-element.68.refs_0_, f32[32,640]{1,0:T(8,128)S(1)} %collective-permute-done.22.refs_1_, f32[32,640]{1,0:T(8,128)S(1)} %collective-permute-done.23.refs_2_, ...), custom_call_target="tpu_custom_call" | custom-call | tf_op jit(solution)/shard_map/final/pallas_call | solution.py:358
  (46 shorter events, 11.6 us)
Async XLA Ops:
  7.2 20.0 %collective-permute-start.3 = (f32[512,128]{1,0:T(8,128)S(1)}, f32[512,128]{1,0:T(8,128)S(1)}, u32[]{:S(2)}, u32[]{:S(2)}) collective-permute-start(f32[512,128]{1,0:T(8,128)S(1)} %get-tuple-element.39.refs_1_), channel_id=1, source_target_pairs={{0,8},{8,0},{16,24},{24,16},{1,9},{9,1},{17,25},{25,17},{2,10},{10... | collective-permute-start | bytes 786440 | tf_op jit(solution)/shard_map/ppermute | solution.py:32
  7.7 19.5 %collective-permute-start.4 = (f32[512,128]{1,0:T(8,128)S(1)}, f32[512,128]{1,0:T(8,128)S(1)}, u32[]{:S(2)}, u32[]{:S(2)}) collective-permute-start(f32[512,128]{1,0:T(8,128)S(1)} %get-tuple-element.40.refs_2_), channel_id=1, source_target_pairs={{0,16},{8,24},{16,0},{24,8},{1,17},{9,25},{17,1},{25,9},{2,18},{10... | collective-permute-start | bytes 786440 | tf_op jit(solution)/shard_map/ppermute | solution.py:32
  10.3 16.9 %collective-permute-start.5 = (f32[512,128]{1,0:T(8,128)S(1)}, f32[512,128]{1,0:T(8,128)S(1)}, u32[]{:S(2)}, u32[]{:S(2)}) collective-permute-start(f32[512,128]{1,0:T(8,128)S(1)} %get-tuple-element.41.refs_3_), channel_id=1, source_target_pairs={{0,24},{8,16},{16,8},{24,0},{1,25},{9,17},{17,9},{25,1},{2,26},{10... | collective-permute-start | bytes 786440 | tf_op jit(solution)/shard_map/ppermute | solution.py:32
  10.4 5.2 %collective-permute-start.1 = (f32[64,128]{1,0:T(8,128)S(1)}, f32[64,128]{1,0:T(8,128)S(1)}, u32[]{:S(2)}, u32[]{:S(2)}) collective-permute-start(f32[64,128]{1,0:T(8,128)S(1)} %get-tuple-element.74), channel_id=1, source_target_pairs={{0,1},{1,2},{2,3},{3,4},{4,5},{5,6},{6,7},{8,9},{9,10},{10,11},{11... | collective-permute-start | bytes 98312 | tf_op jit(solution)/shard_map/ppermute | solution.py:299
  14.0 5.9 %collective-permute-start = (f32[64,128]{1,0:T(8,128)S(1)}, f32[64,128]{1,0:T(8,128)S(1)}, u32[]{:S(2)}, u32[]{:S(2)}) collective-permute-start(f32[64,128]{1,0:T(8,128)S(1)} %get-tuple-element.75), channel_id=1, source_target_pairs={{1,0},{2,1},{3,2},{4,3},{5,4},{6,5},{7,6},{9,8},{10,9},{11,10},{12... | collective-permute-start | bytes 98312 | tf_op jit(solution)/shard_map/ppermute | solution.py:298
  15.6 8.5 %collective-permute-start.6 = (f32[64,128]{1,0:T(8,128)S(1)}, f32[64,128]{1,0:T(8,128)S(1)}, u32[]{:S(2)}, u32[]{:S(2)}) collective-permute-start(f32[64,128]{1,0:T(8,128)S(1)} %get-tuple-element.43), channel_id=1, source_target_pairs={{0,1},{25,24},{1,2},{26,25},{2,3},{27,26},{3,4},{28,27},{4,5},{29,... | collective-permute-start | bytes 98312 | tf_op jit(solution)/shard_map/ppermute | solution.py:51
  21.6 4.8 %collective-permute-start.2 = (f32[128,128]{1,0:T(8,128)S(1)}, f32[128,128]{1,0:T(8,128)S(1)}, u32[]{:S(2)}, u32[]{:S(2)}) collective-permute-start(f32[128,128]{1,0:T(8,128)S(1)} %probe.1), channel_id=1, source_target_pairs={{0,1},{1,0},{2,3},{3,2},{4,5},{5,4},{6,7},{7,6},{8,9},{9,8},{10,11... | collective-permute-start | bytes 196616 | tf_op jit(solution)/shard_map/ppermute | solution.py:32
  24.8 2.4 %collective-permute-start.8 = (f32[64,128]{1,0:T(8,128)S(1)}, f32[64,128]{1,0:T(8,128)S(1)}, u32[]{:S(2)}, u32[]{:S(2)}) collective-permute-start(f32[64,128]{1,0:T(8,128)S(1)} %get-tuple-element.45), channel_id=1, source_target_pairs={{16,1},{9,24},{17,2},{10,25},{18,3},{11,26},{19,4},{12,27},{20,5},... | collective-permute-start | bytes 98312 | tf_op jit(solution)/shard_map/ppermute | solution.py:51
  26.4 0.9 collective-permute-start.9
  29.6 2.8 %collective-permute-start.10 = (f32[4,160,128]{2,1,0:T(8,128)S(1)}, f32[4,160,128]{2,1,0:T(8,128)S(1)}, u32[]{:S(2)}, u32[]{:S(2)}) collective-permute-start(f32[4,160,128]{2,1,0:T(8,128)S(1)} %get-tuple-element.56), channel_id=1, source_target_pairs={{0,8},{8,0},{16,24},{24,16},{1,9},{9,1},{17,25},{25,17},{2,10},{10... | collective-permute-start | bytes 983048 | tf_op jit(solution)/shard_map/ppermute | solution.py:32
  32.4 17.6 %collective-permute-start.11 = (f32[160,128]{1,0:T(8,128)S(1)}, f32[160,128]{1,0:T(8,128)S(1)}, u32[]{:S(2)}, u32[]{:S(2)}) collective-permute-start(f32[160,128]{1,0:T(8,128)S(1)} %get-tuple-element.76), channel_id=1, source_target_pairs={{0,16},{1,17},{2,18},{3,19},{4,20},{5,21},{6,22},{7,23},{8,24},{9,... | collective-permute-start | bytes 245768 | tf_op jit(solution)/shard_map/ppermute | solution.py:42
  40.6 9.4 %collective-permute-start.13 = (f32[160,128]{1,0:T(8,128)S(1)}, f32[160,128]{1,0:T(8,128)S(1)}, u32[]{:S(2)}, u32[]{:S(2)}) collective-permute-start(f32[160,128]{1,0:T(8,128)S(1)} %get-tuple-element.77), channel_id=1, source_target_pairs={{0,17},{1,16},{2,19},{3,18},{4,21},{5,20},{6,23},{7,22},{8,25},{9,... | collective-permute-start | bytes 245768 | tf_op jit(solution)/shard_map/ppermute | solution.py:42
  43.2 6.8 %collective-permute-start.12 = (f32[160,128]{1,0:T(8,128)S(1)}, f32[160,128]{1,0:T(8,128)S(1)}, u32[]{:S(2)}, u32[]{:S(2)}) collective-permute-start(f32[160,128]{1,0:T(8,128)S(1)} %get-tuple-element.78), channel_id=1, source_target_pairs={{0,1},{1,0},{2,3},{3,2},{4,5},{5,4},{6,7},{7,6},{8,9},{9,8},{10,11... | collective-permute-start | bytes 245768 | tf_op jit(solution)/shard_map/ppermute | solution.py:42
  43.7 6.3 %collective-permute-start.14 = (f32[128,128]{1,0:T(8,128)S(1)}, f32[128,128]{1,0:T(8,128)S(1)}, u32[]{:S(2)}, u32[]{:S(2)}) collective-permute-start(f32[128,128]{1,0:T(8,128)S(1)} %add.57), channel_id=1, source_target_pairs={{0,2},{1,3},{2,0},{3,1},{4,6},{5,7},{6,4},{7,5},{8,10},{9,11},{10,... | collective-permute-start | bytes 196616 | tf_op jit(solution)/shard_map/ppermute | solution.py:32
  50.1 4.5 %collective-permute-start.15 = (f32[160,128]{1,0:T(8,128)S(1)}, f32[160,128]{1,0:T(8,128)S(1)}, u32[]{:S(2)}, u32[]{:S(2)}) collective-permute-start(f32[160,128]{1,0:T(8,128)S(1)} %fusion.6), channel_id=1, source_target_pairs={{0,2},{1,3},{2,0},{3,1},{4,6},{5,7},{6,4},{7,5},{8,10},{9,11},{10,... | collective-permute-start | bytes 245768 | tf_op jit(solution)/shard_map/ppermute | solution.py:32
  54.6 5.5 %collective-permute-start.16 = (f32[160,128]{1,0:T(8,128)S(1)}, f32[160,128]{1,0:T(8,128)S(1)}, u32[]{:S(2)}, u32[]{:S(2)}) collective-permute-start(f32[160,128]{1,0:T(8,128)S(1)} %add.70), channel_id=1, source_target_pairs={{0,4},{1,5},{2,6},{3,7},{4,0},{5,1},{6,2},{7,3},{8,12},{9,13},{10,... | collective-permute-start | bytes 245768 | tf_op jit(solution)/shard_map/ppermute | solution.py:32
  60.1 8.8 %collective-permute-start.20 = (f32[160,128]{1,0:T(8,128)S(1)}, f32[160,128]{1,0:T(8,128)S(1)}, u32[]{:S(2)}, u32[]{:S(2)}) collective-permute-start(f32[160,128]{1,0:T(8,128)S(1)} %add.71), channel_id=1, source_target_pairs={{0,17},{1,16},{2,19},{3,18},{4,21},{5,20},{6,23},{7,22},{8,25},{9,... | collective-permute-start | bytes 245768 | tf_op jit(solution)/shard_map/ppermute | solution.py:42
  61.0 8.0 %collective-permute-start.19 = (f32[160,128]{1,0:T(8,128)S(1)}, f32[160,128]{1,0:T(8,128)S(1)}, u32[]{:S(2)}, u32[]{:S(2)}) collective-permute-start(f32[160,128]{1,0:T(8,128)S(1)} %add.71), channel_id=1, source_target_pairs={{0,1},{1,0},{2,3},{3,2},{4,5},{5,4},{6,7},{7,6},{8,9},{9,8},{10,11... | collective-permute-start | bytes 245768 | tf_op jit(solution)/shard_map/ppermute | solution.py:42
  61.9 7.1 %collective-permute-start.18 = (f32[160,128]{1,0:T(8,128)S(1)}, f32[160,128]{1,0:T(8,128)S(1)}, u32[]{:S(2)}, u32[]{:S(2)}) collective-permute-start(f32[160,128]{1,0:T(8,128)S(1)} %add.71), channel_id=1, source_target_pairs={{0,16},{1,17},{2,18},{3,19},{4,20},{5,21},{6,22},{7,23},{8,24},{9,... | collective-permute-start | bytes 245768 | tf_op jit(solution)/shard_map/ppermute | solution.py:42
  63.7 5.2 %collective-permute-start.17 = (f32[128,128]{1,0:T(8,128)S(1)}, f32[128,128]{1,0:T(8,128)S(1)}, u32[]{:S(2)}, u32[]{:S(2)}) collective-permute-start(f32[128,128]{1,0:T(8,128)S(1)} %add.69), channel_id=1, source_target_pairs={{0,4},{1,5},{2,6},{3,7},{4,0},{5,1},{6,2},{7,3},{8,12},{9,13},{10,... | collective-permute-start | bytes 196616 | tf_op jit(solution)/shard_map/ppermute | solution.py:32
  69.0 1.7 %collective-permute-start.21 = (f32[4,160,128]{2,1,0:T(8,128)S(1)}, f32[4,160,128]{2,1,0:T(8,128)S(1)}, u32[]{:S(2)}, u32[]{:S(2)}) collective-permute-start(f32[4,160,128]{2,1,0:T(8,128)S(1)} %pad_maximum_fusion.even_ref), channel_id=1, source_target_pairs={{0,8},{8,0},{16,24},{24,16},{1,9},{9,1},{17,25},{25,17},{2,10},{10... | collective-permute-start | bytes 983048 | tf_op jit(solution)/shard_map/ppermute | solution.py:32
  84.7 1.9 %collective-permute-start.22 = (f32[32,640]{1,0:T(8,128)S(1)}, f32[32,640]{1,0:T(8,128)S(1)}, u32[]{:S(2)}, u32[]{:S(2)}) collective-permute-start(f32[32,640]{1,0:T(8,128)S(1)} %get-tuple-element.69), channel_id=1, source_target_pairs={{0,8},{8,0},{16,24},{24,16},{1,9},{9,1},{17,25},{25,17},{2,10},{10... | collective-permute-start | bytes 245768 | tf_op jit(solution)/shard_map/ppermute | solution.py:32
  84.9 5.3 %collective-permute-start.23 = (f32[32,640]{1,0:T(8,128)S(1)}, f32[32,640]{1,0:T(8,128)S(1)}, u32[]{:S(2)}, u32[]{:S(2)}) collective-permute-start(f32[32,640]{1,0:T(8,128)S(1)} %get-tuple-element.70), channel_id=1, source_target_pairs={{0,16},{8,24},{16,0},{24,8},{1,17},{9,25},{17,1},{25,9},{2,18},{10... | collective-permute-start | bytes 245768 | tf_op jit(solution)/shard_map/ppermute | solution.py:32
  85.1 5.7 %collective-permute-start.24 = (f32[32,640]{1,0:T(8,128)S(1)}, f32[32,640]{1,0:T(8,128)S(1)}, u32[]{:S(2)}, u32[]{:S(2)}) collective-permute-start(f32[32,640]{1,0:T(8,128)S(1)} %get-tuple-element.71), channel_id=1, source_target_pairs={{0,24},{8,16},{16,8},{24,0},{1,25},{9,17},{17,9},{25,1},{2,26},{10... | collective-permute-start | bytes 245768 | tf_op jit(solution)/shard_map/ppermute | solution.py:32
  (3 other events, 11.2 us)

commit v5 on v4

v5 whole, which is shorter than its diff:
```python
import functools

import jax
import jax.numpy as jnp
from jax import lax
from jax.experimental import pallas as pl
from jax.experimental.pallas import tpu as pltpu
from jax.sharding import PartitionSpec as P

SIGN_STEPS = 8
TAPS = 6
CHUNK = 8
exact = lax.Precision.HIGHEST
F32 = jnp.float32
VMEM_LIMIT = 48 * 1024 * 1024


def params():
    return pltpu.CompilerParams(vmem_limit_bytes=VMEM_LIMIT)


def whole():
    return pl.BlockSpec(memory_space=pltpu.VMEM)


def scalars():
    return pl.BlockSpec(memory_space=pltpu.SMEM)


def swap(x, axis, mask):
    count = lax.axis_size(axis)
    return lax.ppermute(x, axis, [(i, i ^ mask) for i in range(count)])


def swap_both(x, mask):
    parts, patches = lax.axis_size("tm"), lax.axis_size("space")
    route = []
    for t in range(parts):
        for s in range(patches):
            there = (t ^ (mask % parts)) * patches + (s ^ (mask // parts))
            route.append((t * patches + s, there))
    return lax.ppermute(x, ("tm", "space"), route)


def shift_rows(x, by):
    edge = jnp.zeros((1, x.shape[1]), x.dtype)
    if by > 0:
        return jnp.concatenate([edge, x[:-1]], axis=0)
    return jnp.concatenate([x[1:], edge], axis=0)


def narrow_row(snap_ref, x, mask_even, mask_odd, taps):
    half = snap_ref.shape[1] // 2
    even = snap_ref[x, pl.ds(0, half, stride=2), :] * mask_even
    odd = snap_ref[x, pl.ds(1, half, stride=2), :] * mask_odd
    before = taps[0] * even + taps[1] * odd
    here = taps[2] * even + taps[3] * odd
    after = taps[4] * even + taps[5] * odd
    return shift_rows(before, 1) + here + shift_rows(after, -1)


def mask_columns(mask, mask_t, cells):
    mask_t[...] = mask.astype(F32).T
    return mask_t[pl.ds(0, cells, stride=2), :], mask_t[pl.ds(1, cells, stride=2), :]


def edge_kernel(rtaps_ref, ctaps_ref, first_ref, last_ref, mask_first_ref, mask_last_ref, up_ref, down_ref, mask_t):
    ctaps = [ctaps_ref[k] for k in range(TAPS)]
    cells = up_ref.shape[0]
    for out, snaps, mask_ref, taps, at in (
        (up_ref, first_ref, mask_first_ref, (rtaps_ref[4], rtaps_ref[5]), 0),
        (down_ref, last_ref, mask_last_ref, (rtaps_ref[0], rtaps_ref[1]), CHUNK - 2),
    ):
        even, odd = mask_columns(mask_ref[...], mask_t, cells)
        total = taps[0] * narrow_row(snaps, 0, even[:, at:at + 1], odd[:, at:at + 1], ctaps)
        out[...] = total + taps[1] * narrow_row(snaps, 1, even[:, at + 1:at + 2], odd[:, at + 1:at + 2], ctaps)


def filter_kernel(parts, me_ref, rtaps_ref, ctaps_ref, snap_hbm, mask_ref, *rest):
    pieces, (snaps, sems, mask_t, narrowed, filtered) = rest[:parts], rest[parts:]
    rows, cells = snaps.shape[0], narrowed.shape[1]
    chunks = rows // CHUNK

    def fetch(c):
        at = pl.ds(c * CHUNK, CHUNK)
        return pltpu.make_async_copy(snap_hbm.at[at], snaps.at[at], sems.at[c])

    for c in range(chunks):
        fetch(c).start()
    rtaps = [rtaps_ref[k] for k in range(TAPS)]
    ctaps = [ctaps_ref[k] for k in range(TAPS)]
    edge = jnp.zeros((2,) + narrowed.shape[1:], F32)
    narrowed[0:2] = edge
    narrowed[rows + 2:rows + 4] = edge

    def narrow(c, carry):
        fetch(c).wait()
        base = pl.multiple_of(c * CHUNK, CHUNK)
        even, odd = mask_columns(mask_ref[pl.ds(base, CHUNK), :], mask_t, cells)
        for x in range(CHUNK):
            row = narrow_row(snaps, base + x, even[:, x:x + 1], odd[:, x:x + 1], ctaps)
            narrowed[2 + base + x] = row
        return carry

    lax.fori_loop(0, chunks, narrow, 0)
    for i in range(rows // 2):
        total = rtaps[0] * narrowed[2 * i]
        for k in range(1, TAPS):
            total = total + rtaps[k] * narrowed[2 * i + k]
        filtered[i * cells:(i + 1) * cells, :] = total
    me = me_ref[0]
    size = filtered.shape[0] // parts
    for k in range(parts):
        pieces[k][...] = filtered[pl.ds(pl.multiple_of((me ^ k) * size, 8), size), :]


def halo_kernel(parts, me_ref, above_ref, below_ref, *refs):
    outs = refs[parts:]
    me = me_ref[0]
    cells = above_ref.shape[0]
    for k in range(parts):
        outs[k][...] = refs[k][...]

        @pl.when((me ^ k) == 0)
        def _():
            outs[k][:cells, :] = outs[k][:cells, :] + above_ref[...]

        @pl.when((me ^ k) == parts - 1)
        def _():
            outs[k][-cells:, :] = outs[k][-cells:, :] + below_ref[...]


def block_order(parts):
    return [(a, b) for a in range(parts) for b in range(a, parts)] + [(a, parts) for a in range(parts)]


def gram_kernel(parts, span, me_ref, probes_ref, *refs):
    pieces, (send_ref, keep_ref, wide, flat) = refs[:parts], refs[parts:]
    me, owner = me_ref[0], me_ref[1]
    size, cols = pieces[0].shape
    for k in range(parts):
        wide[:, pl.ds(pl.multiple_of((me ^ k) * cols, cols), cols)] = pieces[k][...]
    where = {ab: j for j, ab in enumerate(block_order(parts))}
    for a in range(0, parts, 2):
        left = wide[:, a * cols:(a + 2) * cols]
        for b in range(a, parts + 2, 2):
            if b < parts:
                right = wide[:, b * cols:(b + 2) * cols]
            else:
                right = probes_ref[pl.ds(pl.multiple_of(me * size, 8), size), :]
            prod = exact_dot(left, right, ((0,), (0,)))
            for i in range(2):
                for j in range(right.shape[1] // cols):
                    if (a + i, b + j) in where:
                        at = where[a + i, b + j] * cols
                        flat[at:at + cols, :] = prod[i * cols:(i + 1) * cols, j * cols:(j + 1) * cols]
    share = flat.shape[0] // (parts * span)
    for k in range(parts * span):
        out = send_ref if k % 2 else keep_ref
        out[k // 2] = flat[pl.ds(pl.multiple_of((owner ^ k) * share, 8), share), :]


def split(x):
    high = x.astype(jnp.bfloat16)
    return high, (x - high.astype(F32)).astype(jnp.bfloat16)


def dot(a, b, dims):
    return lax.dot_general(a, b, (dims, ((), ())), preferred_element_type=F32)


def dot_parts(a, b, dims=((1,), (0,))):
    (ah, al), (bh, bl) = a, b
    rows = ah.shape[0]
    both = dot(jnp.concatenate([ah, al], axis=0), bh, dims)
    return both[:rows] + (dot(ah, bl, dims) + both[rows:])


def exact_dot(a, b, dims=((1,), (0,))):
    return lax.dot_general(a, b, (dims, ((), ())), precision=exact, preferred_element_type=F32)


def combine_of(grams):
    order = grams[0].shape[0]
    diagonal = lax.broadcasted_iota(jnp.int32, (order, order), 0) == lax.broadcasted_iota(jnp.int32, (order, order), 1)
    signs = []
    for gram in grams:
        mean = jnp.sum(jnp.where(diagonal, gram, 0.0)) / order
        shifted = jnp.where(diagonal, gram - mean, gram)
        signs.append(shifted / jnp.sqrt(jnp.sum(shifted * shifted, keepdims=True) + 1e-6))
    for _ in range(SIGN_STEPS):
        halves = [split(y) for y in signs]
        squares = [split(dot_parts(y, y)) for y in halves]
        cubes = [dot_parts(s, y) for y, s in zip(halves, squares)]
        signs = [1.5 * y - 0.5 * c for y, c in zip(signs, cubes)]
    half = order // 2
    combines = []
    for y in signs:
        projector = 0.5 * (jnp.where(diagonal, 1.0, 0.0) + y)
        combines.append(projector[:, :half] + projector[:, half:])
    return combines


def merge_kernel(parts, span, me_ref, even_ref, odd_ref, wide_ref, out_ref, coef_ref, flat, weight, turned):
    me, owner = me_ref[0], me_ref[1]
    size, cols = even_ref.shape[1:]
    for k in range(parts * span):
        source = odd_ref if k % 2 else even_ref
        flat[pl.ds(pl.multiple_of((owner ^ k) * size, 8), size), :] = source[k // 2]
    blocks = {ab: flat[j * cols:(j + 1) * cols, :] for j, ab in enumerate(block_order(parts))}
    weights, count = None, parts
    while count > 1:
        grams = []
        for p in range(0, count, 2):
            low = jnp.concatenate([blocks[p, p], blocks[p, p + 1]], axis=1)
            high = jnp.concatenate([blocks[p, p + 1].T, blocks[p + 1, p + 1]], axis=1)
            grams.append(jnp.concatenate([low, high], axis=0))
        combines = combine_of(grams)
        if weights is None:
            weights = combines
        else:
            per = len(weights) // len(combines)
            weights = [
                exact_dot(w, combines[i // per][(i % per) * cols:(i % per + 1) * cols, :])
                for i, w in enumerate(weights)
            ]
            weights = [jnp.concatenate(weights[i:i + per], axis=0) for i in range(0, len(weights), per)]
        merged = {}
        if count > 2:
            for p in range(count // 2):
                for q in range(p, count // 2):
                    if p == q:
                        cross = grams[p]
                    else:
                        cross = jnp.concatenate([
                            jnp.concatenate([blocks[2 * p + i, 2 * q], blocks[2 * p + i, 2 * q + 1]], axis=1)
                            for i in range(2)
                        ], axis=0)
                    right = exact_dot(cross, combines[q])
                    merged[p, q] = exact_dot(combines[p], right, ((0,), (0,)))
        blocks, count = merged, count // 2
    weight[...] = weights[0]
    total = dot_parts(split(wide_ref[...]), split(weight[...]))
    width = cols // parts
    turned_basis = total.T
    for d in range(parts):
        out_ref[d] = turned_basis[d * width:(d + 1) * width, :]
    turned[...] = exact_dot(weight[...], flat[-parts * cols:, :], ((0,), (0,)))
    coef_ref[...] = turned[pl.ds(pl.multiple_of(me * width, 8), width), :]


def final_kernel(pieces_ref, basis_ref):
    parts = pieces_ref.shape[0]
    per, cells = basis_ref.shape[0] // parts, basis_ref.shape[2]
    for t in range(parts):
        for i in range(per):
            basis_ref[t * per + i] = pieces_ref[t, :, i * cells:(i + 1) * cells]


def shape(*dims):
    return jax.ShapeDtypeStruct(dims, F32)


def local(snapshots, land_mask, taps_rows, taps_cols, probes):
    rows, grid_cols, cols = snapshots.shape
    half_rows, half_cols = rows // 2, grid_cols // 2
    parts, patches = lax.axis_size("tm"), lax.axis_size("space")
    cells = half_rows * half_cols
    piece = cells // parts
    span = 2 if patches > 1 else 1
    position, patch = lax.axis_index("tm"), lax.axis_index("space")
    me = jnp.stack([position, position + parts * (patch % span)]).astype(jnp.int32)

    snapshots, land_mask, taps_rows, taps_cols = (
        pltpu.with_memory_space_constraint(x, pltpu.HBM) for x in (snapshots, land_mask, taps_rows, taps_cols)
    )

    row_block, mask_block = (2, grid_cols, cols), (CHUNK, grid_cols)
    to_above, to_below = pl.pallas_call(
        edge_kernel,
        out_shape=[shape(half_cols, cols)] * 2,
        grid=(1,),
        in_specs=[
            scalars(), scalars(),
            pl.BlockSpec(row_block, lambda i: (0, 0, 0)),
            pl.BlockSpec(row_block, lambda i: (rows // 2 - 1, 0, 0)),
            pl.BlockSpec(mask_block, lambda i: (0, 0)),
            pl.BlockSpec(mask_block, lambda i: (rows // CHUNK - 1, 0)),
        ],
        out_specs=[pl.BlockSpec((half_cols, cols), lambda i: (0, 0))] * 2,
        scratch_shapes=[pltpu.VMEM((grid_cols, CHUNK), F32)],
        compiler_params=params(),
        name="edge",
    )(taps_rows, taps_cols, snapshots, snapshots, land_mask, land_mask)
    up = [(i, i + 1) for i in range(patches - 1)]
    above = lax.ppermute(to_below, "space", up)
    below = lax.ppermute(to_above, "space", [(j, i) for i, j in up])

    pieces = pl.pallas_call(
        functools.partial(filter_kernel, parts),
        out_shape=[shape(piece, cols)] * parts,
        in_specs=[scalars(), scalars(), scalars(), pl.BlockSpec(memory_space=pltpu.HBM), whole()],
        out_specs=[whole()] * parts,
        scratch_shapes=[
            pltpu.VMEM((rows, grid_cols, cols), F32),
            pltpu.SemaphoreType.DMA((rows // CHUNK,)),
            pltpu.VMEM((grid_cols, CHUNK), F32),
            pltpu.VMEM((rows + 4, half_cols, cols), F32),
            pltpu.VMEM((cells, cols), F32),
        ],
        compiler_params=params(),
        cost_estimate=pl.CostEstimate(flops=0, bytes_accessed=4 * snapshots.size, transcendentals=0),
        name="filter",
    )(me, taps_rows, taps_cols, snapshots, land_mask)
    pieces = pl.pallas_call(
        functools.partial(halo_kernel, parts),
        out_shape=[shape(piece, cols)] * parts,
        in_specs=[scalars()] + [whole()] * (parts + 2),
        out_specs=[whole()] * parts,
        input_output_aliases={3 + k: k for k in range(parts)},
        compiler_params=params(),
        name="halo",
    )(me, above, below, *pieces)
    far = [pieces[0]] + [swap(pieces[k], "tm", k) for k in range(1, parts)]

    blocks = len(block_order(parts))
    owners = parts * span
    size = blocks * cols // owners
    send, keep, wide = pl.pallas_call(
        functools.partial(gram_kernel, parts, span),
        out_shape=[shape(owners // 2, size, cols)] * 2 + [shape(piece, parts * cols)],
        in_specs=[scalars()] + [whole()] * (parts + 1),
        out_specs=[whole()] * 3,
        scratch_shapes=[pltpu.VMEM((blocks * cols, cols), F32)],
        compiler_params=params(),
        name="gram",
    )(me, probes.reshape(cells, cols), *far)
    got = swap(send, "tm", 1)
    mine = keep[0] + got[0]
    for h in range(1, owners // 2):
        mine = mine + swap_both(keep[h] + got[h], 2 * h)
    bits = [1 << b for b in range(1, patches.bit_length() - 1)]
    for bit in bits:
        mine = mine + swap(mine, "space", bit)
    even = jnp.stack([mine] + [swap_both(mine, 2 * h) for h in range(1, owners // 2)])
    odd = swap(even, "tm", 1)

    width = cols // parts
    sent, coefficients = pl.pallas_call(
        functools.partial(merge_kernel, parts, span),
        out_shape=[shape(parts, width, piece), shape(width, cols)],
        in_specs=[scalars()] + [whole()] * 3,
        out_specs=[whole()] * 2,
        scratch_shapes=[
            pltpu.VMEM((blocks * cols, cols), F32),
            pltpu.VMEM((parts * cols, cols), F32),
            pltpu.VMEM((cols, cols), F32),
        ],
        compiler_params=params(),
        name="merge",
    )(me, even, odd, wide)
    last = lax.all_to_all(sent, "tm", 0, 0)

    basis = pl.pallas_call(
        final_kernel,
        out_shape=shape(half_rows, width, half_cols),
        in_specs=[whole()],
        out_specs=whole(),
        compiler_params=params(),
        name="final",
    )(last)
    return basis.transpose(0, 2, 1), coefficients


def solution(mesh):
    placed = (P("space", None, "tm"), P("space", None), P(), P(), P("space", None, None))
    return jax.shard_map(
        local,
        mesh=mesh,
        in_specs=placed,
        out_specs=(P("space", None, "tm"), P("tm", None)),
        check_vma=False,
    )
```

time: 92.7 us -> 88.7 us (0.957)
  starting transfers between devices: 47.6 us -> 22.5 us
  waiting for transfers between devices: 17.6 us -> 30.9 us
  blocking collectives: 0 us -> 8.41 us
  Pallas kernels: 24.4 us -> 25.6 us
    ppermute x13 -> x7, starting transfers between devices: 21.5 us -> 8.17 us  [swap(): return lax.ppermute(x, axis, [(i, i ^ mask) for i in range(count)])]
    ppermute x6, waiting for transfers between devices: 0.02 us -> 9.95 us  [swap_both(): return lax.ppermute(x, ('tm', 'space'), route)]
    all_to_all x0 -> x1, blocking collectives: none -> 8.41 us  [local(): last = lax.all_to_all(sent, 'tm', 0, 0)]
    ppermute x6, starting transfers between devices: 14.8 us -> 8.05 us  [swap_both(): return lax.ppermute(x, ('tm', 'space'), route)]
    ppermute x6 -> x2, starting transfers between devices: 11.3 us -> 6.27 us  [the longest x1 4.98 us: local(): above = lax.ppermute(to_below, 'space', up)]
    ppermute x13 -> x7, waiting for transfers between devices: 17.3 us -> 20.9 us  [swap(): return lax.ppermute(x, axis, [(i, i ^ mask) for i in range(count)])]
    pallas_call x2 -> x3, Pallas kernels: 3.18 us -> 2.89 us  [the longest x1 1.24 us: local(): pl.pallas_call(edge_kernel, out_shape=[shape(half_cols, cols)] * 2, grid=...]
  transfers between devices with their start and end apart: 25 -> 15, of which waited for: 10 -> 10; matrix products, arithmetic and copies ran while one was open for 0% -> 0% of each run, Pallas kernels for 2% -> 6%
where the time goes in v5:
time: 88.7 us; the launch traced here: 88.4 us
  waiting for transfers between devices  30.9 us (35%)
  Pallas kernels  25.6 us (29%)
  starting transfers between devices  22.5 us (25%)
  blocking collectives  8.41 us (9%)
    ppermute x7, waiting for transfers between devices, swap(): return lax.ppermute(x, axis, [(i, i ^ mask) for i in range(count)])  20.9 us
    pallas_call x1, Pallas kernels, local(): pl.pallas_call(functools.partial(merge_kernel, parts, span), out_shape=[s...  14.5 us
    ppermute x6, waiting for transfers between devices, swap_both(): return lax.ppermute(x, ('tm', 'space'), route)  9.95 us
    all_to_all x1, blocking collectives, local(): last = lax.all_to_all(sent, 'tm', 0, 0)  8.41 us
    ppermute x7, starting transfers between devices, swap(): return lax.ppermute(x, axis, [(i, i ^ mask) for i in range(count)])  8.17 us
    ppermute x6, starting transfers between devices, swap_both(): return lax.ppermute(x, ('tm', 'space'), route)  8.05 us
    pallas_call x1, Pallas kernels, local(): pl.pallas_call(functools.partial(filter_kernel, parts), out_shape=[shape(...  5.1 us
    ppermute x1, starting transfers between devices, local(): above = lax.ppermute(to_below, 'space', up)  4.98 us
  transfers between devices with their start and end apart: 15, of which 10 were waited for; matrix products, arithmetic and copies ran while one was open for 0% of the time, Pallas kernels for 6%

profile of v5, /device:TPU:0, one launch (start us, length us, event | category | flops | bytes accessed | tf_op | source)
XLA Modules:
  0.0 88.4 jit_solution(18091370770191012383)
XLA Ops:
  0.6 1.2 %edge.1 = (f32[64,128]{1,0:T(8,128)S(1)}, f32[64,128]{1,0:T(8,128)S(1)}) custom-call(f32[6]{0:T(128)} %rtaps_ref.3, f32[6]{0:T(128)} %ctaps_ref.3, f32[64,128,128]{2,1,0:T(8,128)} %snap_hbm.1, f32[64,128,128]{2,1,0:T(8,128)} %snap_hbm.1, s32[64,128]{1,0:T(8,128)} %mask_ref.1, s32[64,128]{1,0:T(8,128)} %mask_ref.1), custom_call_target="tpu_custom_call" | custom-call | tf_op jit(solution)/shard_map/edge/pallas_call | solution.py:279
  1.9 5.0 %collective-permute-start = (f32[64,128]{1,0:T(8,128)S(1)}, f32[64,128]{1,0:T(8,128)S(1)}, u32[]{:S(2)}, u32[]{:S(2)}) collective-permute-start(f32[64,128]{1,0:T(8,128)S(1)} %get-tuple-element.17), channel_id=1, source_target_pairs={{0,1},{1,2},{2,3},{3,4},{4,5},{5,6},{6,7},{8,9},{9,10},{10,11},{11... | collective-permute-start | bytes 98312 | tf_op jit(solution)/shard_map/ppermute | solution.py:296
  6.9 1.3 %collective-permute-start.1 = (f32[64,128]{1,0:T(8,128)S(1)}, f32[64,128]{1,0:T(8,128)S(1)}, u32[]{:S(2)}, u32[]{:S(2)}) collective-permute-start(f32[64,128]{1,0:T(8,128)S(1)} %get-tuple-element.18), channel_id=1, source_target_pairs={{1,0},{2,1},{3,2},{4,3},{5,4},{6,5},{7,6},{9,8},{10,9},{11,10},{12... | collective-permute-start | bytes 98312 | tf_op jit(solution)/shard_map/ppermute | solution.py:297
  8.3 5.1 %filter.1 = (f32[512,128]{1,0:T(8,128)S(1)}, f32[512,128]{1,0:T(8,128)S(1)}, f32[512,128]{1,0:T(8,128)S(1)}, f32[512,128]{1,0:T(8,128)S(1)}) custom-call(s32[2]{0:T(128)S(1)} %pad_add_fusion.me_ref, f32[6]{0:T(128)} %rtaps_ref.3, f32[6]{0:T(128)} %ctaps_ref.3, f32[64,128,128]{2,1,0:T(8,128)} %snap_hbm.1, s32[64,128]{1,0:T(8,128)} %mask_ref.1), custom_call_target="tpu_custom_call" | custom-call | bytes 4194304 | tf_op jit(solution)/shard_map/filter/pallas_call | solution.py:299
  14.2 1.6 %collective-permute-start.3 = (f32[512,128]{1,0:T(8,128)S(1)}, f32[512,128]{1,0:T(8,128)S(1)}, u32[]{:S(2)}, u32[]{:S(2)}) collective-permute-start(f32[512,128]{1,0:T(8,128)S(1)} %get-tuple-element.25), channel_id=1, source_target_pairs={{0,16},{8,24},{16,0},{24,8},{1,17},{9,25},{17,1},{25,9},{2,18},{10... | collective-permute-start | bytes 786440 | tf_op jit(solution)/shard_map/ppermute | solution.py:32
  16.1 7.3 %collective-permute-done.3.refs_2_ = f32[512,128]{1,0:T(8,128)S(1)} collective-permute-done((f32[512,128]{1,0:T(8,128)S(1)}, f32[512,128]{1,0:T(8,128)S(1)}, u32[]{:S(2)}, u32[]{:S(2)}) %collective-permute-start.3) | collective-permute-done | bytes 262176 | tf_op jit(solution)/shard_map/ppermute | solution.py:32
  23.4 4.7 %collective-permute-done.4.refs_3_ = f32[512,128]{1,0:T(8,128)S(1)} collective-permute-done((f32[512,128]{1,0:T(8,128)S(1)}, f32[512,128]{1,0:T(8,128)S(1)}, u32[]{:S(2)}, u32[]{:S(2)}) %collective-permute-start.4) | collective-permute-done | bytes 262176 | tf_op jit(solution)/shard_map/ppermute | solution.py:32
  28.1 3.1 %gram.1 = (f32[4,224,128]{2,1,0:T(8,128)S(1)}, f32[4,224,128]{2,1,0:T(8,128)S(1)}, f32[512,512]{1,0:T(8,128)S(1)}) custom-call(s32[2]{0:T(128)S(1)} %pad_add_fusion.me_ref, f32[2048,128]{1,0:T(8,128)S(1)} %bitcast.22, f32[512,128]{1,0:T(8,128)S(1)} %get-tuple-element.23.refs_0_, f32[512,128]{1,0:T(8,128)S(1)} %collective-permute-done.2.refs_1_, ...), custom_call_target="tpu_custom_call" | custom-call | tf_op jit(solution)/shard_map/gram/pallas_call | solution.py:329
  31.6 1.5 %collective-permute-done.5 = f32[4,224,128]{2,1,0:T(8,128)S(1)} collective-permute-done((f32[4,224,128]{2,1,0:T(8,128)S(1)}, f32[4,224,128]{2,1,0:T(8,128)S(1)}, u32[]{:S(2)}, u32[]{:S(2)}) %collective-permute-start.5) | collective-permute-done | bytes 458784 | tf_op jit(solution)/shard_map/ppermute | solution.py:32
  33.1 1.6 %collective-permute-start.6 = (f32[224,128]{1,0:T(8,128)S(1)}, f32[224,128]{1,0:T(8,128)S(1)}, u32[]{:S(2)}, u32[]{:S(2)}) collective-permute-start(f32[224,128]{1,0:T(8,128)S(1)} %get-tuple-element.32), channel_id=1, source_target_pairs={{0,16},{1,17},{2,18},{3,19},{4,20},{5,21},{6,22},{7,23},{8,24},{9,... | collective-permute-start | bytes 344072 | tf_op jit(solution)/shard_map/ppermute | solution.py:42
  34.7 2.6 %collective-permute-start.8 = (f32[224,128]{1,0:T(8,128)S(1)}, f32[224,128]{1,0:T(8,128)S(1)}, u32[]{:S(2)}, u32[]{:S(2)}) collective-permute-start(f32[224,128]{1,0:T(8,128)S(1)} %get-tuple-element.33), channel_id=1, source_target_pairs={{0,17},{1,16},{2,19},{3,18},{4,21},{5,20},{6,23},{7,22},{8,25},{9,... | collective-permute-start | bytes 344072 | tf_op jit(solution)/shard_map/ppermute | solution.py:42
  37.4 3.6 %collective-permute-done.6 = f32[224,128]{1,0:T(8,128)S(1)} collective-permute-done((f32[224,128]{1,0:T(8,128)S(1)}, f32[224,128]{1,0:T(8,128)S(1)}, u32[]{:S(2)}, u32[]{:S(2)}) %collective-permute-start.6) | collective-permute-done | bytes 114720 | tf_op jit(solution)/shard_map/ppermute | solution.py:42
  41.0 2.2 %collective-permute-done.7 = f32[224,128]{1,0:T(8,128)S(1)} collective-permute-done((f32[224,128]{1,0:T(8,128)S(1)}, f32[224,128]{1,0:T(8,128)S(1)}, u32[]{:S(2)}, u32[]{:S(2)}) %collective-permute-start.7) | collective-permute-done | bytes 114720 | tf_op jit(solution)/shard_map/ppermute | solution.py:42
  43.2 2.7 %collective-permute-start.9 = (f32[224,128]{1,0:T(8,128)S(1)}, f32[224,128]{1,0:T(8,128)S(1)}, u32[]{:S(2)}, u32[]{:S(2)}) collective-permute-start(f32[224,128]{1,0:T(8,128)S(1)} %fusion.6), channel_id=1, source_target_pairs={{0,2},{1,3},{2,0},{3,1},{4,6},{5,7},{6,4},{7,5},{8,10},{9,11},{10,... | collective-permute-start | bytes 344072 | tf_op jit(solution)/shard_map/ppermute | solution.py:32
  46.0 2.8 %collective-permute-done.9 = f32[224,128]{1,0:T(8,128)S(1)} collective-permute-done((f32[224,128]{1,0:T(8,128)S(1)}, f32[224,128]{1,0:T(8,128)S(1)}, u32[]{:S(2)}, u32[]{:S(2)}) %collective-permute-start.9) | collective-permute-done | bytes 114720 | tf_op jit(solution)/shard_map/ppermute | solution.py:32
  48.7 3.1 %collective-permute-start.10 = (f32[224,128]{1,0:T(8,128)S(1)}, f32[224,128]{1,0:T(8,128)S(1)}, u32[]{:S(2)}, u32[]{:S(2)}) collective-permute-start(f32[224,128]{1,0:T(8,128)S(1)} %add.59), channel_id=1, source_target_pairs={{0,4},{1,5},{2,6},{3,7},{4,0},{5,1},{6,2},{7,3},{8,12},{9,13},{10,... | collective-permute-start | bytes 344072 | tf_op jit(solution)/shard_map/ppermute | solution.py:32
  51.8 2.8 %collective-permute-done.10 = f32[224,128]{1,0:T(8,128)S(1)} collective-permute-done((f32[224,128]{1,0:T(8,128)S(1)}, f32[224,128]{1,0:T(8,128)S(1)}, u32[]{:S(2)}, u32[]{:S(2)}) %collective-permute-start.10) | collective-permute-done | bytes 114720 | tf_op jit(solution)/shard_map/ppermute | solution.py:32
  54.6 3.2 %collective-permute-start.13 = (f32[224,128]{1,0:T(8,128)S(1)}, f32[224,128]{1,0:T(8,128)S(1)}, u32[]{:S(2)}, u32[]{:S(2)}) collective-permute-start(f32[224,128]{1,0:T(8,128)S(1)} %add.60), channel_id=1, source_target_pairs={{0,17},{1,16},{2,19},{3,18},{4,21},{5,20},{6,23},{7,22},{8,25},{9,... | collective-permute-start | bytes 344072 | tf_op jit(solution)/shard_map/ppermute | solution.py:42
  58.4 2.1 %collective-permute-done.13 = f32[224,128]{1,0:T(8,128)S(1)} collective-permute-done((f32[224,128]{1,0:T(8,128)S(1)}, f32[224,128]{1,0:T(8,128)S(1)}, u32[]{:S(2)}, u32[]{:S(2)}) %collective-permute-start.13) | collective-permute-done | bytes 114720 | tf_op jit(solution)/shard_map/ppermute | solution.py:42
  60.6 2.0 %collective-permute-done.12 = f32[224,128]{1,0:T(8,128)S(1)} collective-permute-done((f32[224,128]{1,0:T(8,128)S(1)}, f32[224,128]{1,0:T(8,128)S(1)}, u32[]{:S(2)}, u32[]{:S(2)}) %collective-permute-start.12) | collective-permute-done | bytes 114720 | tf_op jit(solution)/shard_map/ppermute | solution.py:42
  62.7 1.8 %collective-permute-done.14.odd_ref = f32[4,224,128]{2,1,0:T(8,128)S(1)} collective-permute-done((f32[4,224,128]{2,1,0:T(8,128)S(1)}, f32[4,224,128]{2,1,0:T(8,128)S(1)}, u32[]{:S(2)}, u32[]{:S(2)}) %collective-permute-start.14) | collective-permute-done | bytes 458784 | tf_op jit(solution)/shard_map/ppermute | solution.py:32
  64.5 14.5 %merge.1 = (f32[4,32,512]{2,1,0:T(8,128)S(1)}, f32[32,128]{1,0:T(8,128)}) custom-call(s32[2]{0:T(128)S(1)} %pad_add_fusion.me_ref, f32[4,224,128]{2,1,0:T(8,128)S(1)} %pad_maximum_fusion.even_ref, f32[4,224,128]{2,1,0:T(8,128)S(1)} %collective-permute-done.14.odd_ref, f32[512,512]{1,0:T(8,128)S(1)} %get-tuple-element.29.wide_ref), custom_call_target="tpu_custom_call" | custom-call | tf_op jit(solution)/shard_map/merge/pallas_call | solution.py:349
  79.1 8.4 %all_to_all.5.pieces_ref = f32[4,32,512]{2,1,0:T(8,128)S(1)} all-to-all(f32[4,32,512]{2,1,0:T(8,128)S(1)} %get-tuple-element.30), channel_id=1, replica_groups=mesh['tm'=4,'space'=8] {'tm'}, dimensions={0} | all-to-all | bytes 524288 | tf_op jit(solution)/shard_map/all_to_all | solution.py:362
  87.5 0.9 %final.1 = f32[32,32,64]{2,1,0:T(8,128)} custom-call(f32[4,32,512]{2,1,0:T(8,128)S(1)} %all_to_all.5.pieces_ref), custom_call_target="tpu_custom_call" | custom-call | tf_op jit(solution)/shard_map/final/pallas_call | solution.py:364
  (21 shorter events, 2.4 us)
Async XLA Ops:
  1.9 26.2 %copy-start = (f32[32,64,128]{2,1,0:T(8,128)S(1)}, f32[32,64,128]{2,1,0:T(8,128)}, u32[]{:S(2)}) copy-start(f32[32,64,128]{2,1,0:T(8,128)} %param.9) | copy-start | bytes 3145732
  1.9 11.5 %collective-permute-start = (f32[64,128]{1,0:T(8,128)S(1)}, f32[64,128]{1,0:T(8,128)S(1)}, u32[]{:S(2)}, u32[]{:S(2)}) collective-permute-start(f32[64,128]{1,0:T(8,128)S(1)} %get-tuple-element.17), channel_id=1, source_target_pairs={{0,1},{1,2},{2,3},{3,4},{4,5},{5,6},{6,7},{8,9},{9,10},{10,11},{11... | collective-permute-start | bytes 98312 | tf_op jit(solution)/shard_map/ppermute | solution.py:296
  6.9 6.5 %collective-permute-start.1 = (f32[64,128]{1,0:T(8,128)S(1)}, f32[64,128]{1,0:T(8,128)S(1)}, u32[]{:S(2)}, u32[]{:S(2)}) collective-permute-start(f32[64,128]{1,0:T(8,128)S(1)} %get-tuple-element.18), channel_id=1, source_target_pairs={{1,0},{2,1},{3,2},{4,3},{5,4},{6,5},{7,6},{9,8},{10,9},{11,10},{12... | collective-permute-start | bytes 98312 | tf_op jit(solution)/shard_map/ppermute | solution.py:297
  14.1 1.9 %collective-permute-start.2 = (f32[512,128]{1,0:T(8,128)S(1)}, f32[512,128]{1,0:T(8,128)S(1)}, u32[]{:S(2)}, u32[]{:S(2)}) collective-permute-start(f32[512,128]{1,0:T(8,128)S(1)} %get-tuple-element.24), channel_id=1, source_target_pairs={{0,8},{8,0},{16,24},{24,16},{1,9},{9,1},{17,25},{25,17},{2,10},{10... | collective-permute-start | bytes 786440 | tf_op jit(solution)/shard_map/ppermute | solution.py:32
  14.2 9.2 %collective-permute-start.3 = (f32[512,128]{1,0:T(8,128)S(1)}, f32[512,128]{1,0:T(8,128)S(1)}, u32[]{:S(2)}, u32[]{:S(2)}) collective-permute-start(f32[512,128]{1,0:T(8,128)S(1)} %get-tuple-element.25), channel_id=1, source_target_pairs={{0,16},{8,24},{16,0},{24,8},{1,17},{9,25},{17,1},{25,9},{2,18},{10... | collective-permute-start | bytes 786440 | tf_op jit(solution)/shard_map/ppermute | solution.py:32
  15.8 12.3 %collective-permute-start.4 = (f32[512,128]{1,0:T(8,128)S(1)}, f32[512,128]{1,0:T(8,128)S(1)}, u32[]{:S(2)}, u32[]{:S(2)}) collective-permute-start(f32[512,128]{1,0:T(8,128)S(1)} %get-tuple-element.26), channel_id=1, source_target_pairs={{0,24},{8,16},{16,8},{24,0},{1,25},{9,17},{17,9},{25,1},{2,26},{10... | collective-permute-start | bytes 786440 | tf_op jit(solution)/shard_map/ppermute | solution.py:32
  31.2 1.9 %collective-permute-start.5 = (f32[4,224,128]{2,1,0:T(8,128)S(1)}, f32[4,224,128]{2,1,0:T(8,128)S(1)}, u32[]{:S(2)}, u32[]{:S(2)}) collective-permute-start(f32[4,224,128]{2,1,0:T(8,128)S(1)} %get-tuple-element.28), channel_id=1, source_target_pairs={{0,8},{8,0},{16,24},{24,16},{1,9},{9,1},{17,25},{25,17},{2,10},{10... | collective-permute-start | bytes 1376264 | tf_op jit(solution)/shard_map/ppermute | solution.py:32
  33.1 7.9 %collective-permute-start.6 = (f32[224,128]{1,0:T(8,128)S(1)}, f32[224,128]{1,0:T(8,128)S(1)}, u32[]{:S(2)}, u32[]{:S(2)}) collective-permute-start(f32[224,128]{1,0:T(8,128)S(1)} %get-tuple-element.32), channel_id=1, source_target_pairs={{0,16},{1,17},{2,18},{3,19},{4,20},{5,21},{6,22},{7,23},{8,24},{9,... | collective-permute-start | bytes 344072 | tf_op jit(solution)/shard_map/ppermute | solution.py:42
  34.7 6.3 %collective-permute-start.8 = (f32[224,128]{1,0:T(8,128)S(1)}, f32[224,128]{1,0:T(8,128)S(1)}, u32[]{:S(2)}, u32[]{:S(2)}) collective-permute-start(f32[224,128]{1,0:T(8,128)S(1)} %get-tuple-element.33), channel_id=1, source_target_pairs={{0,17},{1,16},{2,19},{3,18},{4,21},{5,20},{6,23},{7,22},{8,25},{9,... | collective-permute-start | bytes 344072 | tf_op jit(solution)/shard_map/ppermute | solution.py:42
  37.3 5.9 %collective-permute-start.7 = (f32[224,128]{1,0:T(8,128)S(1)}, f32[224,128]{1,0:T(8,128)S(1)}, u32[]{:S(2)}, u32[]{:S(2)}) collective-permute-start(f32[224,128]{1,0:T(8,128)S(1)} %get-tuple-element.34), channel_id=1, source_target_pairs={{0,1},{1,0},{2,3},{3,2},{4,5},{5,4},{6,7},{7,6},{8,9},{9,8},{10,11... | collective-permute-start | bytes 344072 | tf_op jit(solution)/shard_map/ppermute | solution.py:42
  43.2 5.5 %collective-permute-start.9 = (f32[224,128]{1,0:T(8,128)S(1)}, f32[224,128]{1,0:T(8,128)S(1)}, u32[]{:S(2)}, u32[]{:S(2)}) collective-permute-start(f32[224,128]{1,0:T(8,128)S(1)} %fusion.6), channel_id=1, source_target_pairs={{0,2},{1,3},{2,0},{3,1},{4,6},{5,7},{6,4},{7,5},{8,10},{9,11},{10,... | collective-permute-start | bytes 344072 | tf_op jit(solution)/shard_map/ppermute | solution.py:32
  48.7 5.9 %collective-permute-start.10 = (f32[224,128]{1,0:T(8,128)S(1)}, f32[224,128]{1,0:T(8,128)S(1)}, u32[]{:S(2)}, u32[]{:S(2)}) collective-permute-start(f32[224,128]{1,0:T(8,128)S(1)} %add.59), channel_id=1, source_target_pairs={{0,4},{1,5},{2,6},{3,7},{4,0},{5,1},{6,2},{7,3},{8,12},{9,13},{10,... | collective-permute-start | bytes 344072 | tf_op jit(solution)/shard_map/ppermute | solution.py:32
  54.6 5.9 %collective-permute-start.13 = (f32[224,128]{1,0:T(8,128)S(1)}, f32[224,128]{1,0:T(8,128)S(1)}, u32[]{:S(2)}, u32[]{:S(2)}) collective-permute-start(f32[224,128]{1,0:T(8,128)S(1)} %add.60), channel_id=1, source_target_pairs={{0,17},{1,16},{2,19},{3,18},{4,21},{5,20},{6,23},{7,22},{8,25},{9,... | collective-permute-start | bytes 344072 | tf_op jit(solution)/shard_map/ppermute | solution.py:42
  57.8 4.8 %collective-permute-start.12 = (f32[224,128]{1,0:T(8,128)S(1)}, f32[224,128]{1,0:T(8,128)S(1)}, u32[]{:S(2)}, u32[]{:S(2)}) collective-permute-start(f32[224,128]{1,0:T(8,128)S(1)} %add.60), channel_id=1, source_target_pairs={{0,1},{1,0},{2,3},{3,2},{4,5},{5,4},{6,7},{7,6},{8,9},{9,8},{10,11... | collective-permute-start | bytes 344072 | tf_op jit(solution)/shard_map/ppermute | solution.py:42
  57.8 4.8 %collective-permute-start.11 = (f32[224,128]{1,0:T(8,128)S(1)}, f32[224,128]{1,0:T(8,128)S(1)}, u32[]{:S(2)}, u32[]{:S(2)}) collective-permute-start(f32[224,128]{1,0:T(8,128)S(1)} %add.60), channel_id=1, source_target_pairs={{0,16},{1,17},{2,18},{3,19},{4,20},{5,21},{6,22},{7,23},{8,24},{9,... | collective-permute-start | bytes 344072 | tf_op jit(solution)/shard_map/ppermute | solution.py:42
  62.6 1.9 %collective-permute-start.14 = (f32[4,224,128]{2,1,0:T(8,128)S(1)}, f32[4,224,128]{2,1,0:T(8,128)S(1)}, u32[]{:S(2)}, u32[]{:S(2)}) collective-permute-start(f32[4,224,128]{2,1,0:T(8,128)S(1)} %pad_maximum_fusion.even_ref), channel_id=1, source_target_pairs={{0,8},{8,0},{16,24},{24,16},{1,9},{9,1},{17,25},{25,17},{2,10},{10... | collective-permute-start | bytes 1376264 | tf_op jit(solution)/shard_map/ppermute | solution.py:32

commit v6 on v5

--- a/solution.py
+++ b/solution.py
@@ -49,85 +49,92 @@
     return jnp.concatenate([x[1:], edge], axis=0)
 
 
-def narrow_row(snap_ref, x, mask_even, mask_odd, taps):
-    half = snap_ref.shape[1] // 2
-    even = snap_ref[x, pl.ds(0, half, stride=2), :] * mask_even
-    odd = snap_ref[x, pl.ds(1, half, stride=2), :] * mask_odd
+def mask_columns(mask, mask_t):
+    mask_t[...] = mask.astype(F32).T
+    return mask_t[...]
+
+
+def narrowed_row(held, taps):
+    half = held.shape[0] // 2
+    even = held[pl.ds(0, half, stride=2), :]
+    odd = held[pl.ds(1, half, stride=2), :]
     before = taps[0] * even + taps[1] * odd
     here = taps[2] * even + taps[3] * odd
     after = taps[4] * even + taps[5] * odd
     return shift_rows(before, 1) + here + shift_rows(after, -1)
 
 
-def mask_columns(mask, mask_t, cells):
-    mask_t[...] = mask.astype(F32).T
-    return mask_t[pl.ds(0, cells, stride=2), :], mask_t[pl.ds(1, cells, stride=2), :]
-
-
-def edge_kernel(rtaps_ref, ctaps_ref, first_ref, last_ref, mask_first_ref, mask_last_ref, up_ref, down_ref, mask_t):
+def edge_kernel(rtaps_ref, ctaps_ref, first_ref, last_ref, mask_first_ref, mask_last_ref, up_ref, down_ref, mask_t, held):
     ctaps = [ctaps_ref[k] for k in range(TAPS)]
-    cells = up_ref.shape[0]
     for out, snaps, mask_ref, taps, at in (
         (up_ref, first_ref, mask_first_ref, (rtaps_ref[4], rtaps_ref[5]), 0),
         (down_ref, last_ref, mask_last_ref, (rtaps_ref[0], rtaps_ref[1]), CHUNK - 2),
     ):
-        even, odd = mask_columns(mask_ref[...], mask_t, cells)
-        total = taps[0] * narrow_row(snaps, 0, even[:, at:at + 1], odd[:, at:at + 1], ctaps)
-        out[...] = total + taps[1] * narrow_row(snaps, 1, even[:, at + 1:at + 2], odd[:, at + 1:at + 2], ctaps)
-
-
-def filter_kernel(parts, me_ref, rtaps_ref, ctaps_ref, snap_hbm, mask_ref, *rest):
-    pieces, (snaps, sems, mask_t, narrowed, filtered) = rest[:parts], rest[parts:]
-    rows, cells = snaps.shape[0], narrowed.shape[1]
-    chunks = rows // CHUNK
+        mask = mask_columns(mask_ref[...], mask_t)
+        held[...] = taps[0] * (snaps[0] * mask[:, at:at + 1]) + taps[1] * (snaps[1] * mask[:, at + 1:at + 2])
+        out[...] = narrowed_row(held, ctaps)
+
+
+def filter_kernel(parts, other, me_ref, rtaps_ref, ctaps_ref, snap_hbm, mask_ref, *rest):
+    count = parts // 2
+    pieces, (ocean, sems, mask_t, held, filtered) = rest[:count], rest[count:]
+    rows, grid_cols = ocean.shape[0] - 4, ocean.shape[1]
+    cells = grid_cols // 2
+    me = me_ref[0]
+    side = me // count
+    if other:
+        side = 1 - side
+    chunks = (rows // 2 + 2 + CHUNK - 1) // CHUNK
+    start = side * (rows - chunks * CHUNK)
 
     def fetch(c):
-        at = pl.ds(c * CHUNK, CHUNK)
-        return pltpu.make_async_copy(snap_hbm.at[at], snaps.at[at], sems.at[c])
+        at = pl.multiple_of(start + c * CHUNK, CHUNK)
+        return pltpu.make_async_copy(snap_hbm.at[pl.ds(at, CHUNK)], ocean.at[pl.ds(at + 2, CHUNK)], sems.at[c])
 
     for c in range(chunks):
         fetch(c).start()
     rtaps = [rtaps_ref[k] for k in range(TAPS)]
     ctaps = [ctaps_ref[k] for k in range(TAPS)]
-    edge = jnp.zeros((2,) + narrowed.shape[1:], F32)
-    narrowed[0:2] = edge
-    narrowed[rows + 2:rows + 4] = edge
-
-    def narrow(c, carry):
+    edge = jnp.zeros((2,) + ocean.shape[1:], F32)
+    ocean[0:2] = edge
+    ocean[rows + 2:rows + 4] = edge
+
+    def mask_chunk(c, carry):
         fetch(c).wait()
-        base = pl.multiple_of(c * CHUNK, CHUNK)
-        even, odd = mask_columns(mask_ref[pl.ds(base, CHUNK), :], mask_t, cells)
+        base = pl.multiple_of(start + c * CHUNK, CHUNK)
+        mask = mask_columns(mask_ref[pl.ds(base, CHUNK), :], mask_t)
         for x in range(CHUNK):
-            row = narrow_row(snaps, base + x, even[:, x:x + 1], odd[:, x:x + 1], ctaps)
-            narrowed[2 + base + x] = row
+            ocean[base + 2 + x] = ocean[base + 2 + x] * mask[:, x:x + 1]
         return carry
 
-    lax.fori_loop(0, chunks, narrow, 0)
-    for i in range(rows // 2):
-        total = rtaps[0] * narrowed[2 * i]
+    lax.fori_loop(0, chunks, mask_chunk, 0)
+    first = side * (rows // 2)
+    for i in range(rows // 4):
+        total = rtaps[0] * ocean[first + 2 * i]
         for k in range(1, TAPS):
-            total = total + rtaps[k] * narrowed[2 * i + k]
-        filtered[i * cells:(i + 1) * cells, :] = total
-    me = me_ref[0]
-    size = filtered.shape[0] // parts
-    for k in range(parts):
-        pieces[k][...] = filtered[pl.ds(pl.multiple_of((me ^ k) * size, 8), size), :]
-
-
-def halo_kernel(parts, me_ref, above_ref, below_ref, *refs):
-    outs = refs[parts:]
+            total = total + rtaps[k] * ocean[first + 2 * i + k]
+        held[i % 2] = total
+        filtered[i * cells:(i + 1) * cells, :] = narrowed_row(held.at[i % 2], ctaps)
+    size = filtered.shape[0] // count
+    for k in range(count):
+        at = ((me ^ k) % count) * size
+        pieces[k][...] = filtered[pl.ds(pl.multiple_of(at, 8), size), :]
+
+
+def halo_kernel(parts, offset, me_ref, above_ref, below_ref, *refs):
+    outs = refs[len(refs) // 2:]
     me = me_ref[0]
     cells = above_ref.shape[0]
-    for k in range(parts):
-        outs[k][...] = refs[k][...]
-
-        @pl.when((me ^ k) == 0)
+    for k, out in enumerate(outs):
+        out[...] = refs[k][...]
+
+        @pl.when((me ^ (k + offset)) == 0)
         def _():
-            outs[k][:cells, :] = outs[k][:cells, :] + above_ref[...]
-
-        @pl.when((me ^ k) == parts - 1)
+            out[:cells, :] = out[:cells, :] + above_ref[...]
+
+        @pl.when((me ^ (k + offset)) == parts - 1)
         def _():
-            outs[k][-cells:, :] = outs[k][-cells:, :] + below_ref[...]
+            out[-cells:, :] = out[-cells:, :] + below_ref[...]
 
 
 def block_order(parts):
@@ -141,16 +148,14 @@
     for k in range(parts):
         wide[:, pl.ds(pl.multiple_of((me ^ k) * cols, cols), cols)] = pieces[k][...]
     where = {ab: j for j, ab in enumerate(block_order(parts))}
+    sides = [split(wide[:, a * cols:(a + 2) * cols]) for a in range(0, parts, 2)]
+    sides.append(split(probes_ref[pl.ds(pl.multiple_of(me * size, 8), size), :]))
     for a in range(0, parts, 2):
-        left = wide[:, a * cols:(a + 2) * cols]
         for b in range(a, parts + 2, 2):
-            if b < parts:
-                right = wide[:, b * cols:(b + 2) * cols]
-            else:
-                right = probes_ref[pl.ds(pl.multiple_of(me * size, 8), size), :]
-            prod = exact_dot(left, right, ((0,), (0,)))
+            right = sides[b // 2]
+            prod = dot_parts(sides[a // 2], right, ((0,), (0,)))
             for i in range(2):
-                for j in range(right.shape[1] // cols):
+                for j in range(right[0].shape[1] // cols):
                     if (a + i, b + j) in where:
                         at = where[a + i, b + j] * cols
                         flat[at:at + cols, :] = prod[i * cols:(i + 1) * cols, j * cols:(j + 1) * cols]
@@ -171,8 +176,9 @@
 
 def dot_parts(a, b, dims=((1,), (0,))):
     (ah, al), (bh, bl) = a, b
-    rows = ah.shape[0]
-    both = dot(jnp.concatenate([ah, al], axis=0), bh, dims)
+    free = 1 - dims[0][0]
+    rows = ah.shape[free]
+    both = dot(jnp.concatenate([ah, al], axis=free), bh, dims)
     return both[:rows] + (dot(ah, bl, dims) + both[rows:])
 
 
@@ -201,7 +207,8 @@
     return combines
 
 
-def merge_kernel(parts, span, me_ref, even_ref, odd_ref, wide_ref, out_ref, coef_ref, flat, weight, turned):
+def merge_kernel(parts, span, me_ref, even_ref, odd_ref, wide_ref, *refs):
+    outs, (coef_ref, flat, weight, turned) = refs[:parts], refs[parts:]
     me, owner = me_ref[0], me_ref[1]
     size, cols = even_ref.shape[1:]
     for k in range(parts * span):
@@ -242,19 +249,22 @@
     weight[...] = weights[0]
     total = dot_parts(split(wide_ref[...]), split(weight[...]))
     width = cols // parts
-    turned_basis = total.T
-    for d in range(parts):
-        out_ref[d] = turned_basis[d * width:(d + 1) * width, :]
-    turned[...] = exact_dot(weight[...], flat[-parts * cols:, :], ((0,), (0,)))
-    coef_ref[...] = turned[pl.ds(pl.multiple_of(me * width, 8), width), :]
-
-
-def final_kernel(pieces_ref, basis_ref):
-    parts = pieces_ref.shape[0]
+    rows = total.shape[0]
+    turned[:, :rows] = total.T
+    turned[:, rows:] = exact_dot(weight[...], flat[-parts * cols:, :], ((0,), (0,)))
+    for k in range(parts):
+        outs[k][...] = turned[pl.ds(pl.multiple_of((me ^ k) * width, 8), width), :rows]
+    coef_ref[...] = turned[pl.ds(pl.multiple_of(me * width, 8), width), rows:]
+
+
+def final_kernel(parts, me_ref, *refs):
+    pieces, basis_ref = refs[:parts], refs[parts]
+    me = me_ref[0]
     per, cells = basis_ref.shape[0] // parts, basis_ref.shape[2]
-    for t in range(parts):
+    for k in range(parts):
+        base = (me ^ k) * per
         for i in range(per):
-            basis_ref[t * per + i] = pieces_ref[t, :, i * cells:(i + 1) * cells]
+            basis_ref[base + i] = pieces[k][:, i * cells:(i + 1) * cells]
 
 
 def shape(*dims):
@@ -288,7 +298,7 @@
             pl.BlockSpec(mask_block, lambda i: (rows // CHUNK - 1, 0)),
         ],
         out_specs=[pl.BlockSpec((half_cols, cols), lambda i: (0, 0))] * 2,
-        scratch_shapes=[pltpu.VMEM((grid_cols, CHUNK), F32)],
+        scratch_shapes=[pltpu.VMEM((grid_cols, CHUNK), F32), pltpu.VMEM((grid_cols, cols), F32)],
         compiler_params=params(),
         name="edge",
     )(taps_rows, taps_cols, snapshots, snapshots, land_mask, land_mask)
@@ -296,32 +306,41 @@
     above = lax.ppermute(to_below, "space", up)
     below = lax.ppermute(to_above, "space", [(j, i) for i, j in up])
 
-    pieces = pl.pallas_call(
-        functools.partial(filter_kernel, parts),
-        out_shape=[shape(piece, cols)] * parts,
-        in_specs=[scalars(), scalars(), scalars(), pl.BlockSpec(memory_space=pltpu.HBM), whole()],
-        out_specs=[whole()] * parts,
-        scratch_shapes=[
-            pltpu.VMEM((rows, grid_cols, cols), F32),
-            pltpu.SemaphoreType.DMA((rows // CHUNK,)),
-            pltpu.VMEM((grid_cols, CHUNK), F32),
-            pltpu.VMEM((rows + 4, half_cols, cols), F32),
-            pltpu.VMEM((cells, cols), F32),
-        ],
-        compiler_params=params(),
-        cost_estimate=pl.CostEstimate(flops=0, bytes_accessed=4 * snapshots.size, transcendentals=0),
-        name="filter",
-    )(me, taps_rows, taps_cols, snapshots, land_mask)
-    pieces = pl.pallas_call(
-        functools.partial(halo_kernel, parts),
-        out_shape=[shape(piece, cols)] * parts,
-        in_specs=[scalars()] + [whole()] * (parts + 2),
-        out_specs=[whole()] * parts,
-        input_output_aliases={3 + k: k for k in range(parts)},
-        compiler_params=params(),
-        name="halo",
-    )(me, above, below, *pieces)
-    far = [pieces[0]] + [swap(pieces[k], "tm", k) for k in range(1, parts)]
+    count = parts // 2
+    chunks = (rows // 2 + 2 + CHUNK - 1) // CHUNK
+
+    def half_of_rows(other, after):
+        halves = pl.pallas_call(
+            functools.partial(filter_kernel, parts, other),
+            out_shape=[shape(piece, cols)] * count,
+            in_specs=[scalars(), scalars(), scalars(), pl.BlockSpec(memory_space=pltpu.HBM), whole()],
+            out_specs=[whole()] * count,
+            scratch_shapes=[
+                pltpu.VMEM((rows + 4, grid_cols, cols), F32),
+                pltpu.SemaphoreType.DMA((chunks,)),
+                pltpu.VMEM((grid_cols, CHUNK), F32),
+                pltpu.VMEM((2, grid_cols, cols), F32),
+                pltpu.VMEM((cells // 2, cols), F32),
+            ],
+            compiler_params=params(),
+            cost_estimate=pl.CostEstimate(flops=0, bytes_accessed=4 * snapshots.size, transcendentals=0),
+            name="filter",
+        )(after, taps_rows, taps_cols, snapshots, land_mask)
+        return pl.pallas_call(
+            functools.partial(halo_kernel, parts, count if other else 0),
+            out_shape=[shape(piece, cols)] * count,
+            in_specs=[scalars()] + [whole()] * (count + 2),
+            out_specs=[whole()] * count,
+            input_output_aliases={3 + k: k for k in range(count)},
+            compiler_params=params(),
+            name="halo",
+        )(me, above, below, *halves)
+
+    leaving = half_of_rows(True, me)
+    far = [swap(leaving[k], "tm", k + count) for k in range(count)]
+    after, *leaving = lax.optimization_barrier([me] + list(leaving))
+    staying = half_of_rows(False, after)
+    far = [staying[0]] + [swap(staying[k], "tm", k) for k in range(1, count)] + far
 
     blocks = len(block_order(parts))
     owners = parts * span
@@ -346,29 +365,29 @@
     odd = swap(even, "tm", 1)
 
     width = cols // parts
-    sent, coefficients = pl.pallas_call(
+    *sent, coefficients = pl.pallas_call(
         functools.partial(merge_kernel, parts, span),
-        out_shape=[shape(parts, width, piece), shape(width, cols)],
+        out_shape=[shape(width, piece)] * parts + [shape(width, cols)],
         in_specs=[scalars()] + [whole()] * 3,
-        out_specs=[whole()] * 2,
+        out_specs=[whole()] * (parts + 1),
         scratch_shapes=[
             pltpu.VMEM((blocks * cols, cols), F32),
             pltpu.VMEM((parts * cols, cols), F32),
-            pltpu.VMEM((cols, cols), F32),
+            pltpu.VMEM((cols, piece + cols), F32),
         ],
         compiler_params=params(),
         name="merge",
     )(me, even, odd, wide)
-    last = lax.all_to_all(sent, "tm", 0, 0)
+    last = [sent[0]] + [swap(sent[k], "tm", k) for k in range(1, parts)]
 
     basis = pl.pallas_call(
-        final_kernel,
+        functools.partial(final_kernel, parts),
         out_shape=shape(half_rows, width, half_cols),
-        in_specs=[whole()],
+        in_specs=[scalars()] + [whole()] * parts,
         out_specs=whole(),
         compiler_params=params(),
         name="final",
-    )(last)
+    )(me, *last)
     return basis.transpose(0, 2, 1), coefficients
 
 

time: 88.7 us -> 83.9 us (0.946)
  blocking collectives: 8.41 us -> 0 us
  Pallas kernels: 25.6 us -> 30 us
  waiting for transfers between devices: 30.9 us -> 27.4 us
  starting transfers between devices: 22.5 us -> 24.8 us
    all_to_all x1 -> x0, blocking collectives: 8.41 us -> none  [local(): last = lax.all_to_all(sent, 'tm', 0, 0)]
    pallas_call x3 -> x5, Pallas kernels: 6.75 us -> 11.6 us  [the longest x2 8.73 us: half_of_rows(): pl.pallas_call(functools.partial(filter_kernel, parts, other), out_shape=...]
    ppermute x7 -> x10, waiting for transfers between devices: 20.9 us -> 17.3 us  [swap(): return lax.ppermute(x, axis, [(i, i ^ mask) for i in range(count)])]
    ppermute x7 -> x10, starting transfers between devices: 8.17 us -> 10.9 us  [swap(): return lax.ppermute(x, axis, [(i, i ^ mask) for i in range(count)])]
    pallas_call x1, Pallas kernels: 3.12 us -> 1.97 us  [local(): pl.pallas_call(functools.partial(gram_kernel, parts, span), out_shape=[sh...]
  transfers between devices with their start and end apart: 15 -> 18, of which waited for: 10 -> 13; matrix products, arithmetic and copies ran while one was open for 0% -> 0% of each run, Pallas kernels for 6% -> 11%
where the time goes in v6:
time: 83.9 us; the launch traced here: 83.2 us
  Pallas kernels  30 us (36%)
  waiting for transfers between devices  27.4 us (33%)
  starting transfers between devices  24.8 us (30%)
    ppermute x10, waiting for transfers between devices, swap(): return lax.ppermute(x, axis, [(i, i ^ mask) for i in range(count)])  17.3 us
    pallas_call x1, Pallas kernels, local(): pl.pallas_call(functools.partial(merge_kernel, parts, span), out_shape=[s...  15 us
    ppermute x10, starting transfers between devices, swap(): return lax.ppermute(x, axis, [(i, i ^ mask) for i in range(count)])  10.9 us
    ppermute x6, waiting for transfers between devices, swap_both(): return lax.ppermute(x, ('tm', 'space'), route)  10 us
    pallas_call x2, Pallas kernels, half_of_rows(): pl.pallas_call(functools.partial(filter_kernel, parts, other), out_shape=...  8.73 us
    ppermute x6, starting transfers between devices, swap_both(): return lax.ppermute(x, ('tm', 'space'), route)  7.77 us
    ppermute x1, starting transfers between devices, local(): above = lax.ppermute(to_below, 'space', up)  4.84 us
    pallas_call x1, Pallas kernels, local(): pl.pallas_call(functools.partial(gram_kernel, parts, span), out_shape=[sh...  1.97 us
  transfers between devices with their start and end apart: 18, of which 13 were waited for; matrix products, arithmetic and copies ran while one was open for 0% of the time, Pallas kernels for 11%

profile of v6, /device:TPU:0, one launch (start us, length us, event | category | flops | bytes accessed | tf_op | source)
XLA Modules:
  0.0 83.2 jit_solution(332626207403389533)
XLA Ops:
  0.6 1.4 %edge.1 = (f32[64,128]{1,0:T(8,128)S(1)}, f32[64,128]{1,0:T(8,128)S(1)}) custom-call(f32[6]{0:T(128)} %rtaps_ref.5, f32[6]{0:T(128)} %ctaps_ref.5, f32[64,128,128]{2,1,0:T(8,128)} %snap_hbm.3, f32[64,128,128]{2,1,0:T(8,128)} %snap_hbm.3, s32[64,128]{1,0:T(8,128)} %mask_ref.3, s32[64,128]{1,0:T(8,128)} %mask_ref.3), custom_call_target="tpu_custom_call" | custom-call | tf_op jit(solution)/shard_map/edge/pallas_call | solution.py:289
  2.1 4.8 %collective-permute-start = (f32[64,128]{1,0:T(8,128)S(1)}, f32[64,128]{1,0:T(8,128)S(1)}, u32[]{:S(2)}, u32[]{:S(2)}) collective-permute-start(f32[64,128]{1,0:T(8,128)S(1)} %get-tuple-element.21), channel_id=1, source_target_pairs={{0,1},{1,2},{2,3},{3,4},{4,5},{5,6},{6,7},{8,9},{9,10},{10,11},{11... | collective-permute-start | bytes 98312 | tf_op jit(solution)/shard_map/ppermute | solution.py:306
  8.3 4.4 %filter.2 = (f32[512,128]{1,0:T(8,128)S(1)}, f32[512,128]{1,0:T(8,128)S(1)}) custom-call(s32[2]{0:T(128)S(1)} %pad_add_fusion.me_ref, f32[6]{0:T(128)} %rtaps_ref.5, f32[6]{0:T(128)} %ctaps_ref.5, f32[64,128,128]{2,1,0:T(8,128)} %snap_hbm.3, s32[64,128]{1,0:T(8,128)} %mask_ref.3), custom_call_target="tpu_custom_call" | custom-call | bytes 4194304 | tf_op jit(solution)/shard_map/filter/pallas_call | solution.py:313
  13.4 1.6 %collective-permute-start.3 = (f32[512,128]{1,0:T(8,128)S(1)}, f32[512,128]{1,0:T(8,128)S(1)}, u32[]{:S(2)}, u32[]{:S(2)}) collective-permute-start(f32[512,128]{1,0:T(8,128)S(1)} %get-tuple-element.25), channel_id=1, source_target_pairs={{0,16},{8,24},{16,0},{24,8},{1,17},{9,25},{17,1},{25,9},{2,18},{10... | collective-permute-start | bytes 786440 | tf_op jit(solution)/shard_map/ppermute | solution.py:32
  15.0 4.3 %filter.3 = (f32[512,128]{1,0:T(8,128)S(1)}, f32[512,128]{1,0:T(8,128)S(1)}) custom-call(s32[2]{0:T(128)S(1)} %pad_add_fusion.me_ref, f32[6]{0:T(128)} %rtaps_ref.5, f32[6]{0:T(128)} %ctaps_ref.5, f32[64,128,128]{2,1,0:T(8,128)} %snap_hbm.3, s32[64,128]{1,0:T(8,128)} %mask_ref.3), custom_call_target="tpu_custom_call" | custom-call | bytes 4194304 | tf_op jit(solution)/shard_map/filter/pallas_call | solution.py:313
  20.8 1.9 %collective-permute-done.3.refs_2_ = f32[512,128]{1,0:T(8,128)S(1)} collective-permute-done((f32[512,128]{1,0:T(8,128)S(1)}, f32[512,128]{1,0:T(8,128)S(1)}, u32[]{:S(2)}, u32[]{:S(2)}) %collective-permute-start.3) | collective-permute-done | bytes 262176 | tf_op jit(solution)/shard_map/ppermute | solution.py:32
  22.7 3.2 %collective-permute-done.4.refs_3_ = f32[512,128]{1,0:T(8,128)S(1)} collective-permute-done((f32[512,128]{1,0:T(8,128)S(1)}, f32[512,128]{1,0:T(8,128)S(1)}, u32[]{:S(2)}, u32[]{:S(2)}) %collective-permute-start.4) | collective-permute-done | bytes 262176 | tf_op jit(solution)/shard_map/ppermute | solution.py:32
  25.9 2.0 %gram.1 = (f32[4,224,128]{2,1,0:T(8,128)S(1)}, f32[4,224,128]{2,1,0:T(8,128)S(1)}, f32[512,512]{1,0:T(8,128)S(1)}) custom-call(s32[2]{0:T(128)S(1)} %pad_add_fusion.me_ref, f32[2048,128]{1,0:T(8,128)S(1)} %bitcast.22, f32[512,128]{1,0:T(8,128)S(1)} %get-tuple-element.30.refs_0_, f32[512,128]{1,0:T(8,128)S(1)} %collective-permute-done.2.refs_1_, ...), custom_call_target="tpu_custom_call" | custom-call | tf_op jit(solution)/shard_map/gram/pallas_call | solution.py:348
  28.7 1.4 %collective-permute-done.5 = f32[4,224,128]{2,1,0:T(8,128)S(1)} collective-permute-done((f32[4,224,128]{2,1,0:T(8,128)S(1)}, f32[4,224,128]{2,1,0:T(8,128)S(1)}, u32[]{:S(2)}, u32[]{:S(2)}) %collective-permute-start.5) | collective-permute-done | bytes 458784 | tf_op jit(solution)/shard_map/ppermute | solution.py:32
  30.2 1.6 %collective-permute-start.6 = (f32[224,128]{1,0:T(8,128)S(1)}, f32[224,128]{1,0:T(8,128)S(1)}, u32[]{:S(2)}, u32[]{:S(2)}) collective-permute-start(f32[224,128]{1,0:T(8,128)S(1)} %get-tuple-element.40), channel_id=1, source_target_pairs={{0,16},{1,17},{2,18},{3,19},{4,20},{5,21},{6,22},{7,23},{8,24},{9,... | collective-permute-start | bytes 344072 | tf_op jit(solution)/shard_map/ppermute | solution.py:42
  31.8 2.3 %collective-permute-start.8 = (f32[224,128]{1,0:T(8,128)S(1)}, f32[224,128]{1,0:T(8,128)S(1)}, u32[]{:S(2)}, u32[]{:S(2)}) collective-permute-start(f32[224,128]{1,0:T(8,128)S(1)} %get-tuple-element.41), channel_id=1, source_target_pairs={{0,17},{1,16},{2,19},{3,18},{4,21},{5,20},{6,23},{7,22},{8,25},{9,... | collective-permute-start | bytes 344072 | tf_op jit(solution)/shard_map/ppermute | solution.py:42
  34.2 3.8 %collective-permute-done.6 = f32[224,128]{1,0:T(8,128)S(1)} collective-permute-done((f32[224,128]{1,0:T(8,128)S(1)}, f32[224,128]{1,0:T(8,128)S(1)}, u32[]{:S(2)}, u32[]{:S(2)}) %collective-permute-start.6) | collective-permute-done | bytes 114720 | tf_op jit(solution)/shard_map/ppermute | solution.py:42
  38.3 1.8 %collective-permute-done.7 = f32[224,128]{1,0:T(8,128)S(1)} collective-permute-done((f32[224,128]{1,0:T(8,128)S(1)}, f32[224,128]{1,0:T(8,128)S(1)}, u32[]{:S(2)}, u32[]{:S(2)}) %collective-permute-start.7) | collective-permute-done | bytes 114720 | tf_op jit(solution)/shard_map/ppermute | solution.py:42
  40.1 2.7 %collective-permute-start.9 = (f32[224,128]{1,0:T(8,128)S(1)}, f32[224,128]{1,0:T(8,128)S(1)}, u32[]{:S(2)}, u32[]{:S(2)}) collective-permute-start(f32[224,128]{1,0:T(8,128)S(1)} %fusion.6), channel_id=1, source_target_pairs={{0,2},{1,3},{2,0},{3,1},{4,6},{5,7},{6,4},{7,5},{8,10},{9,11},{10,... | collective-permute-start | bytes 344072 | tf_op jit(solution)/shard_map/ppermute | solution.py:32
  42.8 2.8 %collective-permute-done.9 = f32[224,128]{1,0:T(8,128)S(1)} collective-permute-done((f32[224,128]{1,0:T(8,128)S(1)}, f32[224,128]{1,0:T(8,128)S(1)}, u32[]{:S(2)}, u32[]{:S(2)}) %collective-permute-start.9) | collective-permute-done | bytes 114720 | tf_op jit(solution)/shard_map/ppermute | solution.py:32
  45.6 3.1 %collective-permute-start.10 = (f32[224,128]{1,0:T(8,128)S(1)}, f32[224,128]{1,0:T(8,128)S(1)}, u32[]{:S(2)}, u32[]{:S(2)}) collective-permute-start(f32[224,128]{1,0:T(8,128)S(1)} %add.59), channel_id=1, source_target_pairs={{0,4},{1,5},{2,6},{3,7},{4,0},{5,1},{6,2},{7,3},{8,12},{9,13},{10,... | collective-permute-start | bytes 344072 | tf_op jit(solution)/shard_map/ppermute | solution.py:32
  48.7 2.8 %collective-permute-done.10 = f32[224,128]{1,0:T(8,128)S(1)} collective-permute-done((f32[224,128]{1,0:T(8,128)S(1)}, f32[224,128]{1,0:T(8,128)S(1)}, u32[]{:S(2)}, u32[]{:S(2)}) %collective-permute-start.10) | collective-permute-done | bytes 114720 | tf_op jit(solution)/shard_map/ppermute | solution.py:32
  51.5 3.2 %collective-permute-start.13 = (f32[224,128]{1,0:T(8,128)S(1)}, f32[224,128]{1,0:T(8,128)S(1)}, u32[]{:S(2)}, u32[]{:S(2)}) collective-permute-start(f32[224,128]{1,0:T(8,128)S(1)} %add.60), channel_id=1, source_target_pairs={{0,17},{1,16},{2,19},{3,18},{4,21},{5,20},{6,23},{7,22},{8,25},{9,... | collective-permute-start | bytes 344072 | tf_op jit(solution)/shard_map/ppermute | solution.py:42
  55.3 2.2 %collective-permute-done.13 = f32[224,128]{1,0:T(8,128)S(1)} collective-permute-done((f32[224,128]{1,0:T(8,128)S(1)}, f32[224,128]{1,0:T(8,128)S(1)}, u32[]{:S(2)}, u32[]{:S(2)}) %collective-permute-start.13) | collective-permute-done | bytes 114720 | tf_op jit(solution)/shard_map/ppermute | solution.py:42
  57.5 2.0 %collective-permute-done.12 = f32[224,128]{1,0:T(8,128)S(1)} collective-permute-done((f32[224,128]{1,0:T(8,128)S(1)}, f32[224,128]{1,0:T(8,128)S(1)}, u32[]{:S(2)}, u32[]{:S(2)}) %collective-permute-start.12) | collective-permute-done | bytes 114720 | tf_op jit(solution)/shard_map/ppermute | solution.py:42
  59.6 1.8 %collective-permute-done.14.odd_ref = f32[4,224,128]{2,1,0:T(8,128)S(1)} collective-permute-done((f32[4,224,128]{2,1,0:T(8,128)S(1)}, f32[4,224,128]{2,1,0:T(8,128)S(1)}, u32[]{:S(2)}, u32[]{:S(2)}) %collective-permute-start.14) | collective-permute-done | bytes 458784 | tf_op jit(solution)/shard_map/ppermute | solution.py:32
  61.4 15.0 %merge.1 = (f32[32,512]{1,0:T(8,128)S(1)}, f32[32,512]{1,0:T(8,128)S(1)}, f32[32,512]{1,0:T(8,128)S(1)}, f32[32,512]{1,0:T(8,128)S(1)}, f32[32,128]{1,0:T(8,128)}) custom-call(s32[2]{0:T(128)S(1)} %pad_add_fusion.me_ref, f32[4,224,128]{2,1,0:T(8,128)S(1)} %pad_maximum_fusion.even_ref, f32[4,224,128]{2,1,0:T(8,128)S(1)} %collective-permute-done.14.odd_ref, ...), custom_call_target="tpu_custom_call" | custom-call | tf_op jit(solution)/shard_map/merge/pallas_call | solution.py:368
  78.2 3.2 %collective-permute-done.16.refs_2_ = f32[32,512]{1,0:T(8,128)S(1)} collective-permute-done((f32[32,512]{1,0:T(8,128)S(1)}, f32[32,512]{1,0:T(8,128)S(1)}, u32[]{:S(2)}, u32[]{:S(2)}) %collective-permute-start.16) | collective-permute-done | bytes 65568 | tf_op jit(solution)/shard_map/ppermute | solution.py:32
  81.7 1.5 %final.1 = f32[32,32,64]{2,1,0:T(8,128)} custom-call(s32[2]{0:T(128)S(1)} %pad_add_fusion.me_ref, f32[32,512]{1,0:T(8,128)S(1)} %get-tuple-element.35.refs_0_, f32[32,512]{1,0:T(8,128)S(1)} %collective-permute-done.15.refs_1_, f32[32,512]{1,0:T(8,128)S(1)} %collective-permute-done.16.refs_2_, f32[32,512]{1,0:T(8,128)S(1)} %collective-permute-done.17.refs_3_), custom_call_target="tpu_custom_call" | custom-call | tf_op jit(solution)/shard_map/final/pallas_call | solution.py:383
  (28 shorter events, 7.7 us)
Async XLA Ops:
  2.1 10.7 %collective-permute-start = (f32[64,128]{1,0:T(8,128)S(1)}, f32[64,128]{1,0:T(8,128)S(1)}, u32[]{:S(2)}, u32[]{:S(2)}) collective-permute-start(f32[64,128]{1,0:T(8,128)S(1)} %get-tuple-element.21), channel_id=1, source_target_pairs={{0,1},{1,2},{2,3},{3,4},{4,5},{5,6},{6,7},{8,9},{9,10},{10,11},{11... | collective-permute-start | bytes 98312 | tf_op jit(solution)/shard_map/ppermute | solution.py:306
  6.9 5.8 %collective-permute-start.1 = (f32[64,128]{1,0:T(8,128)S(1)}, f32[64,128]{1,0:T(8,128)S(1)}, u32[]{:S(2)}, u32[]{:S(2)}) collective-permute-start(f32[64,128]{1,0:T(8,128)S(1)} %get-tuple-element.22), channel_id=1, source_target_pairs={{1,0},{2,1},{3,2},{4,3},{5,4},{6,5},{7,6},{9,8},{10,9},{11,10},{12... | collective-permute-start | bytes 98312 | tf_op jit(solution)/shard_map/ppermute | solution.py:307
  8.3 17.6 %copy-start = (f32[32,64,128]{2,1,0:T(8,128)S(1)}, f32[32,64,128]{2,1,0:T(8,128)}, u32[]{:S(2)}) copy-start(f32[32,64,128]{2,1,0:T(8,128)} %param.9) | copy-start | bytes 3145732
  13.4 9.3 %collective-permute-start.3 = (f32[512,128]{1,0:T(8,128)S(1)}, f32[512,128]{1,0:T(8,128)S(1)}, u32[]{:S(2)}, u32[]{:S(2)}) collective-permute-start(f32[512,128]{1,0:T(8,128)S(1)} %get-tuple-element.25), channel_id=1, source_target_pairs={{0,16},{8,24},{16,0},{24,8},{1,17},{9,25},{17,1},{25,9},{2,18},{10... | collective-permute-start | bytes 786440 | tf_op jit(solution)/shard_map/ppermute | solution.py:32
  15.0 10.9 %collective-permute-start.4 = (f32[512,128]{1,0:T(8,128)S(1)}, f32[512,128]{1,0:T(8,128)S(1)}, u32[]{:S(2)}, u32[]{:S(2)}) collective-permute-start(f32[512,128]{1,0:T(8,128)S(1)} %get-tuple-element.26), channel_id=1, source_target_pairs={{0,24},{8,16},{16,8},{24,0},{1,25},{9,17},{17,9},{25,1},{2,26},{10... | collective-permute-start | bytes 786440 | tf_op jit(solution)/shard_map/ppermute | solution.py:32
  20.1 5.8 %collective-permute-start.2 = (f32[512,128]{1,0:T(8,128)S(1)}, f32[512,128]{1,0:T(8,128)S(1)}, u32[]{:S(2)}, u32[]{:S(2)}) collective-permute-start(f32[512,128]{1,0:T(8,128)S(1)} %get-tuple-element.31), channel_id=1, source_target_pairs={{0,8},{8,0},{16,24},{24,16},{1,9},{9,1},{17,25},{25,17},{2,10},{10... | collective-permute-start | bytes 786440 | tf_op jit(solution)/shard_map/ppermute | solution.py:32
  27.9 2.3 %collective-permute-start.5 = (f32[4,224,128]{2,1,0:T(8,128)S(1)}, f32[4,224,128]{2,1,0:T(8,128)S(1)}, u32[]{:S(2)}, u32[]{:S(2)}) collective-permute-start(f32[4,224,128]{2,1,0:T(8,128)S(1)} %get-tuple-element.33), channel_id=1, source_target_pairs={{0,8},{8,0},{16,24},{24,16},{1,9},{9,1},{17,25},{25,17},{2,10},{10... | collective-permute-start | bytes 1376264 | tf_op jit(solution)/shard_map/ppermute | solution.py:32
  30.2 7.8 %collective-permute-start.6 = (f32[224,128]{1,0:T(8,128)S(1)}, f32[224,128]{1,0:T(8,128)S(1)}, u32[]{:S(2)}, u32[]{:S(2)}) collective-permute-start(f32[224,128]{1,0:T(8,128)S(1)} %get-tuple-element.40), channel_id=1, source_target_pairs={{0,16},{1,17},{2,18},{3,19},{4,20},{5,21},{6,22},{7,23},{8,24},{9,... | collective-permute-start | bytes 344072 | tf_op jit(solution)/shard_map/ppermute | solution.py:42
  31.8 6.5 %collective-permute-start.8 = (f32[224,128]{1,0:T(8,128)S(1)}, f32[224,128]{1,0:T(8,128)S(1)}, u32[]{:S(2)}, u32[]{:S(2)}) collective-permute-start(f32[224,128]{1,0:T(8,128)S(1)} %get-tuple-element.41), channel_id=1, source_target_pairs={{0,17},{1,16},{2,19},{3,18},{4,21},{5,20},{6,23},{7,22},{8,25},{9,... | collective-permute-start | bytes 344072 | tf_op jit(solution)/shard_map/ppermute | solution.py:42
  34.1 5.9 %collective-permute-start.7 = (f32[224,128]{1,0:T(8,128)S(1)}, f32[224,128]{1,0:T(8,128)S(1)}, u32[]{:S(2)}, u32[]{:S(2)}) collective-permute-start(f32[224,128]{1,0:T(8,128)S(1)} %get-tuple-element.42), channel_id=1, source_target_pairs={{0,1},{1,0},{2,3},{3,2},{4,5},{5,4},{6,7},{7,6},{8,9},{9,8},{10,11... | collective-permute-start | bytes 344072 | tf_op jit(solution)/shard_map/ppermute | solution.py:42
  40.1 5.5 %collective-permute-start.9 = (f32[224,128]{1,0:T(8,128)S(1)}, f32[224,128]{1,0:T(8,128)S(1)}, u32[]{:S(2)}, u32[]{:S(2)}) collective-permute-start(f32[224,128]{1,0:T(8,128)S(1)} %fusion.6), channel_id=1, source_target_pairs={{0,2},{1,3},{2,0},{3,1},{4,6},{5,7},{6,4},{7,5},{8,10},{9,11},{10,... | collective-permute-start | bytes 344072 | tf_op jit(solution)/shard_map/ppermute | solution.py:32
  45.6 5.9 %collective-permute-start.10 = (f32[224,128]{1,0:T(8,128)S(1)}, f32[224,128]{1,0:T(8,128)S(1)}, u32[]{:S(2)}, u32[]{:S(2)}) collective-permute-start(f32[224,128]{1,0:T(8,128)S(1)} %add.59), channel_id=1, source_target_pairs={{0,4},{1,5},{2,6},{3,7},{4,0},{5,1},{6,2},{7,3},{8,12},{9,13},{10,... | collective-permute-start | bytes 344072 | tf_op jit(solution)/shard_map/ppermute | solution.py:32
  51.5 6.0 %collective-permute-start.13 = (f32[224,128]{1,0:T(8,128)S(1)}, f32[224,128]{1,0:T(8,128)S(1)}, u32[]{:S(2)}, u32[]{:S(2)}) collective-permute-start(f32[224,128]{1,0:T(8,128)S(1)} %add.60), channel_id=1, source_target_pairs={{0,17},{1,16},{2,19},{3,18},{4,21},{5,20},{6,23},{7,22},{8,25},{9,... | collective-permute-start | bytes 344072 | tf_op jit(solution)/shard_map/ppermute | solution.py:42
  54.7 4.8 %collective-permute-start.12 = (f32[224,128]{1,0:T(8,128)S(1)}, f32[224,128]{1,0:T(8,128)S(1)}, u32[]{:S(2)}, u32[]{:S(2)}) collective-permute-start(f32[224,128]{1,0:T(8,128)S(1)} %add.60), channel_id=1, source_target_pairs={{0,1},{1,0},{2,3},{3,2},{4,5},{5,4},{6,7},{7,6},{8,9},{9,8},{10,11... | collective-permute-start | bytes 344072 | tf_op jit(solution)/shard_map/ppermute | solution.py:42
  54.7 4.8 %collective-permute-start.11 = (f32[224,128]{1,0:T(8,128)S(1)}, f32[224,128]{1,0:T(8,128)S(1)}, u32[]{:S(2)}, u32[]{:S(2)}) collective-permute-start(f32[224,128]{1,0:T(8,128)S(1)} %add.60), channel_id=1, source_target_pairs={{0,16},{1,17},{2,18},{3,19},{4,20},{5,21},{6,22},{7,23},{8,24},{9,... | collective-permute-start | bytes 344072 | tf_op jit(solution)/shard_map/ppermute | solution.py:42
  59.5 1.9 %collective-permute-start.14 = (f32[4,224,128]{2,1,0:T(8,128)S(1)}, f32[4,224,128]{2,1,0:T(8,128)S(1)}, u32[]{:S(2)}, u32[]{:S(2)}) collective-permute-start(f32[4,224,128]{2,1,0:T(8,128)S(1)} %pad_maximum_fusion.even_ref), channel_id=1, source_target_pairs={{0,8},{8,0},{16,24},{24,16},{1,9},{9,1},{17,25},{25,17},{2,10},{10... | collective-permute-start | bytes 1376264 | tf_op jit(solution)/shard_map/ppermute | solution.py:32
  76.3 1.9 %collective-permute-start.15 = (f32[32,512]{1,0:T(8,128)S(1)}, f32[32,512]{1,0:T(8,128)S(1)}, u32[]{:S(2)}, u32[]{:S(2)}) collective-permute-start(f32[32,512]{1,0:T(8,128)S(1)} %get-tuple-element.36), channel_id=1, source_target_pairs={{0,8},{8,0},{16,24},{24,16},{1,9},{9,1},{17,25},{25,17},{2,10},{10... | collective-permute-start | bytes 196616 | tf_op jit(solution)/shard_map/ppermute | solution.py:32
  76.5 4.9 %collective-permute-start.16 = (f32[32,512]{1,0:T(8,128)S(1)}, f32[32,512]{1,0:T(8,128)S(1)}, u32[]{:S(2)}, u32[]{:S(2)}) collective-permute-start(f32[32,512]{1,0:T(8,128)S(1)} %get-tuple-element.37), channel_id=1, source_target_pairs={{0,16},{8,24},{16,0},{24,8},{1,17},{9,25},{17,1},{25,9},{2,18},{10... | collective-permute-start | bytes 196616 | tf_op jit(solution)/shard_map/ppermute | solution.py:32
  77.1 4.6 %collective-permute-start.17 = (f32[32,512]{1,0:T(8,128)S(1)}, f32[32,512]{1,0:T(8,128)S(1)}, u32[]{:S(2)}, u32[]{:S(2)}) collective-permute-start(f32[32,512]{1,0:T(8,128)S(1)} %get-tuple-element.38), channel_id=1, source_target_pairs={{0,24},{8,16},{16,8},{24,0},{1,25},{9,17},{17,9},{25,1},{2,26},{10... | collective-permute-start | bytes 196616 | tf_op jit(solution)/shard_map/ppermute | solution.py:32

commit v7 on v6

--- a/solution.py
+++ b/solution.py
@@ -10,7 +10,7 @@
 SIGN_STEPS = 8
 TAPS = 6
 CHUNK = 8
-exact = lax.Precision.HIGHEST
+ROW_BLOCKS = 2
 F32 = jnp.float32
 VMEM_LIMIT = 48 * 1024 * 1024
 
@@ -51,35 +51,35 @@
 
 def mask_columns(mask, mask_t):
     mask_t[...] = mask.astype(F32).T
-    return mask_t[...]
-
-
-def narrowed_row(held, taps):
-    half = held.shape[0] // 2
-    even = held[pl.ds(0, half, stride=2), :]
-    odd = held[pl.ds(1, half, stride=2), :]
+    half = mask.shape[1] // 2
+    return mask_t[pl.ds(0, half, stride=2), :], mask_t[pl.ds(1, half, stride=2), :]
+
+
+def narrowed_row(snaps, x, mask, taps):
+    half = snaps.shape[1] // 2
+    even = snaps[x, pl.ds(0, half, stride=2), :] * mask[0]
+    odd = snaps[x, pl.ds(1, half, stride=2), :] * mask[1]
     before = taps[0] * even + taps[1] * odd
     here = taps[2] * even + taps[3] * odd
     after = taps[4] * even + taps[5] * odd
     return shift_rows(before, 1) + here + shift_rows(after, -1)
 
 
-def edge_kernel(rtaps_ref, ctaps_ref, first_ref, last_ref, mask_first_ref, mask_last_ref, up_ref, down_ref, mask_t, held):
+def edge_kernel(rtaps_ref, ctaps_ref, first_ref, last_ref, mask_first_ref, mask_last_ref, up_ref, down_ref, mask_t):
     ctaps = [ctaps_ref[k] for k in range(TAPS)]
     for out, snaps, mask_ref, taps, at in (
         (up_ref, first_ref, mask_first_ref, (rtaps_ref[4], rtaps_ref[5]), 0),
         (down_ref, last_ref, mask_last_ref, (rtaps_ref[0], rtaps_ref[1]), CHUNK - 2),
     ):
-        mask = mask_columns(mask_ref[...], mask_t)
-        held[...] = taps[0] * (snaps[0] * mask[:, at:at + 1]) + taps[1] * (snaps[1] * mask[:, at + 1:at + 2])
-        out[...] = narrowed_row(held, ctaps)
-
-
-def filter_kernel(parts, other, me_ref, rtaps_ref, ctaps_ref, snap_hbm, mask_ref, *rest):
+        masks = mask_columns(mask_ref[...], mask_t)
+        rows = [narrowed_row(snaps, x, [m[:, at + x:at + x + 1] for m in masks], ctaps) for x in range(2)]
+        out[...] = taps[0] * rows[0] + taps[1] * rows[1]
+
+
+def filter_kernel(parts, other, me_ref, rtaps_ref, ctaps_ref, snaps, mask_ref, *rest):
     count = parts // 2
-    pieces, (ocean, sems, mask_t, held, filtered) = rest[:count], rest[count:]
-    rows, grid_cols = ocean.shape[0] - 4, ocean.shape[1]
-    cells = grid_cols // 2
+    pieces, (mask_t, narrowed, filtered) = rest[:count], rest[count:]
+    rows, cells = narrowed.shape[0] - 4, narrowed.shape[1]
     me = me_ref[0]
     side = me // count
     if other:
@@ -87,34 +87,27 @@
     chunks = (rows // 2 + 2 + CHUNK - 1) // CHUNK
     start = side * (rows - chunks * CHUNK)
 
-    def fetch(c):
-        at = pl.multiple_of(start + c * CHUNK, CHUNK)
-        return pltpu.make_async_copy(snap_hbm.at[pl.ds(at, CHUNK)], ocean.at[pl.ds(at + 2, CHUNK)], sems.at[c])
-
-    for c in range(chunks):
-        fetch(c).start()
     rtaps = [rtaps_ref[k] for k in range(TAPS)]
     ctaps = [ctaps_ref[k] for k in range(TAPS)]
-    edge = jnp.zeros((2,) + ocean.shape[1:], F32)
-    ocean[0:2] = edge
-    ocean[rows + 2:rows + 4] = edge
-
-    def mask_chunk(c, carry):
-        fetch(c).wait()
+    edge = jnp.zeros((2,) + narrowed.shape[1:], F32)
+    narrowed[0:2] = edge
+    narrowed[rows + 2:rows + 4] = edge
+
+    def narrow(c, carry):
         base = pl.multiple_of(start + c * CHUNK, CHUNK)
-        mask = mask_columns(mask_ref[pl.ds(base, CHUNK), :], mask_t)
+        masks = mask_columns(mask_ref[pl.ds(base, CHUNK), :], mask_t)
         for x in range(CHUNK):
-            ocean[base + 2 + x] = ocean[base + 2 + x] * mask[:, x:x + 1]
+            row = narrowed_row(snaps, base + x, [m[:, x:x + 1] for m in masks], ctaps)
+            narrowed[base + 2 + x] = row
         return carry
 
-    lax.fori_loop(0, chunks, mask_chunk, 0)
+    lax.fori_loop(0, chunks, narrow, 0)
     first = side * (rows // 2)
     for i in range(rows // 4):
-        total = rtaps[0] * ocean[first + 2 * i]
+        total = rtaps[0] * narrowed[first + 2 * i]
         for k in range(1, TAPS):
-            total = total + rtaps[k] * ocean[first + 2 * i + k]
-        held[i % 2] = total
-        filtered[i * cells:(i + 1) * cells, :] = narrowed_row(held.at[i % 2], ctaps)
+            total = total + rtaps[k] * narrowed[first + 2 * i + k]
+        filtered[i * cells:(i + 1) * cells, :] = total
     size = filtered.shape[0] // count
     for k in range(count):
         at = ((me ^ k) % count) * size
@@ -182,8 +175,18 @@
     return both[:rows] + (dot(ah, bl, dims) + both[rows:])
 
 
-def exact_dot(a, b, dims=((1,), (0,))):
-    return lax.dot_general(a, b, (dims, ((), ())), precision=exact, preferred_element_type=F32)
+def split_dot(a, b, dims=((1,), (0,))):
+    return dot_parts(split(a), split(b), dims)
+
+
+def next_sign(y):
+    whole_y = split(y)
+    size = y.shape[0] // ROW_BLOCKS
+    blocks = []
+    for at in range(0, y.shape[0], size):
+        square = dot_parts([part[at:at + size] for part in whole_y], whole_y)
+        blocks.append(1.5 * y[at:at + size] - 0.5 * dot_parts(split(square), whole_y))
+    return jnp.concatenate(blocks, axis=0)
 
 
 def combine_of(grams):
@@ -195,10 +198,7 @@
         shifted = jnp.where(diagonal, gram - mean, gram)
         signs.append(shifted / jnp.sqrt(jnp.sum(shifted * shifted, keepdims=True) + 1e-6))
     for _ in range(SIGN_STEPS):
-        halves = [split(y) for y in signs]
-        squares = [split(dot_parts(y, y)) for y in halves]
-        cubes = [dot_parts(s, y) for y, s in zip(halves, squares)]
-        signs = [1.5 * y - 0.5 * c for y, c in zip(signs, cubes)]
+        signs = [next_sign(y) for y in signs]
     half = order // 2
     combines = []
     for y in signs:
@@ -228,7 +228,7 @@
         else:
             per = len(weights) // len(combines)
             weights = [
-                exact_dot(w, combines[i // per][(i % per) * cols:(i % per + 1) * cols, :])
+                split_dot(w, combines[i // per][(i % per) * cols:(i % per + 1) * cols, :])
                 for i, w in enumerate(weights)
             ]
             weights = [jnp.concatenate(weights[i:i + per], axis=0) for i in range(0, len(weights), per)]
@@ -243,15 +243,15 @@
                             jnp.concatenate([blocks[2 * p + i, 2 * q], blocks[2 * p + i, 2 * q + 1]], axis=1)
                             for i in range(2)
                         ], axis=0)
-                    right = exact_dot(cross, combines[q])
-                    merged[p, q] = exact_dot(combines[p], right, ((0,), (0,)))
+                    right = split_dot(cross, combines[q])
+                    merged[p, q] = split_dot(combines[p], right, ((0,), (0,)))
         blocks, count = merged, count // 2
     weight[...] = weights[0]
     total = dot_parts(split(wide_ref[...]), split(weight[...]))
     width = cols // parts
     rows = total.shape[0]
     turned[:, :rows] = total.T
-    turned[:, rows:] = exact_dot(weight[...], flat[-parts * cols:, :], ((0,), (0,)))
+    turned[:, rows:] = split_dot(weight[...], flat[-parts * cols:, :], ((0,), (0,)))
     for k in range(parts):
         outs[k][...] = turned[pl.ds(pl.multiple_of((me ^ k) * width, 8), width), :rows]
     coef_ref[...] = turned[pl.ds(pl.multiple_of(me * width, 8), width), rows:]
@@ -281,6 +281,7 @@
     position, patch = lax.axis_index("tm"), lax.axis_index("space")
     me = jnp.stack([position, position + parts * (patch % span)]).astype(jnp.int32)
 
+    held = snapshots
     snapshots, land_mask, taps_rows, taps_cols = (
         pltpu.with_memory_space_constraint(x, pltpu.HBM) for x in (snapshots, land_mask, taps_rows, taps_cols)
     )
@@ -298,7 +299,7 @@
             pl.BlockSpec(mask_block, lambda i: (rows // CHUNK - 1, 0)),
         ],
         out_specs=[pl.BlockSpec((half_cols, cols), lambda i: (0, 0))] * 2,
-        scratch_shapes=[pltpu.VMEM((grid_cols, CHUNK), F32), pltpu.VMEM((grid_cols, cols), F32)],
+        scratch_shapes=[pltpu.VMEM((grid_cols, CHUNK), F32)],
         compiler_params=params(),
         name="edge",
     )(taps_rows, taps_cols, snapshots, snapshots, land_mask, land_mask)
@@ -307,25 +308,22 @@
     below = lax.ppermute(to_above, "space", [(j, i) for i, j in up])
 
     count = parts // 2
-    chunks = (rows // 2 + 2 + CHUNK - 1) // CHUNK
 
     def half_of_rows(other, after):
         halves = pl.pallas_call(
             functools.partial(filter_kernel, parts, other),
             out_shape=[shape(piece, cols)] * count,
-            in_specs=[scalars(), scalars(), scalars(), pl.BlockSpec(memory_space=pltpu.HBM), whole()],
+            in_specs=[scalars(), scalars(), scalars(), whole(), whole()],
             out_specs=[whole()] * count,
             scratch_shapes=[
-                pltpu.VMEM((rows + 4, grid_cols, cols), F32),
-                pltpu.SemaphoreType.DMA((chunks,)),
                 pltpu.VMEM((grid_cols, CHUNK), F32),
-                pltpu.VMEM((2, grid_cols, cols), F32),
+                pltpu.VMEM((rows + 4, half_cols, cols), F32),
                 pltpu.VMEM((cells // 2, cols), F32),
             ],
             compiler_params=params(),
             cost_estimate=pl.CostEstimate(flops=0, bytes_accessed=4 * snapshots.size, transcendentals=0),
             name="filter",
-        )(after, taps_rows, taps_cols, snapshots, land_mask)
+        )(after, taps_rows, taps_cols, held, land_mask)
         return pl.pallas_call(
             functools.partial(halo_kernel, parts, count if other else 0),
             out_shape=[shape(piece, cols)] * count,

time: 83.9 us -> 81.7 us (0.974)
  Pallas kernels: 30 us -> 23.9 us
  local copies, waits for them, and re-layouts: 0.01 us -> 2.2 us
  waiting for transfers between devices: 27.4 us -> 29.2 us
    pallas_call x2, Pallas kernels: 8.73 us -> 5.59 us  [half_of_rows(): pl.pallas_call(functools.partial(filter_kernel, parts, other), out_shape=...]
    pallas_call x1, Pallas kernels: 15 us -> 12.3 us  [local(): pl.pallas_call(functools.partial(merge_kernel, parts, span), out_shape=[s...]
    unnamed x2 -> x6, local copies, waits for them, and re-layouts: 0.01 us -> 2.2 us
    ppermute x10, waiting for transfers between devices: 17.3 us -> 19.1 us  [swap(): return lax.ppermute(x, axis, [(i, i ^ mask) for i in range(count)])]
  transfers between devices with their start and end apart: 18 -> 18, of which waited for: 13 -> 13; matrix products, arithmetic and copies ran while one was open for 0% -> 0% of each run, Pallas kernels for 11% -> 8%
where the time goes in v7:
time: 81.7 us; the launch traced here: 81 us
  waiting for transfers between devices  29.2 us (36%)
  starting transfers between devices  24.8 us (30%)
  Pallas kernels  23.9 us (29%)
  local copies, waits for them, and re-layouts  2.2 us (3%)
    ppermute x10, waiting for transfers between devices, swap(): return lax.ppermute(x, axis, [(i, i ^ mask) for i in range(count)])  19.1 us
    pallas_call x1, Pallas kernels, local(): pl.pallas_call(functools.partial(merge_kernel, parts, span), out_shape=[s...  12.3 us
    ppermute x10, starting transfers between devices, swap(): return lax.ppermute(x, axis, [(i, i ^ mask) for i in range(count)])  10.9 us
    ppermute x6, waiting for transfers between devices, swap_both(): return lax.ppermute(x, ('tm', 'space'), route)  10 us
    ppermute x6, starting transfers between devices, swap_both(): return lax.ppermute(x, ('tm', 'space'), route)  7.8 us
    pallas_call x2, Pallas kernels, half_of_rows(): pl.pallas_call(functools.partial(filter_kernel, parts, other), out_shape=...  5.59 us
    ppermute x1, starting transfers between devices, local(): above = lax.ppermute(to_below, 'space', up)  4.84 us
    unnamed x6, local copies, waits for them, and re-layouts  2.2 us
  transfers between devices with their start and end apart: 18, of which 13 were waited for; matrix products, arithmetic and copies ran while one was open for 0% of the time, Pallas kernels for 8%

profile of v7, /device:TPU:0, one launch (start us, length us, event | category | flops | bytes accessed | tf_op | source)
XLA Modules:
  0.0 81.0 jit_solution(460926686468605186)
XLA Ops:
  1.9 4.8 %collective-permute-start = (f32[64,128]{1,0:T(8,128)S(1)}, f32[64,128]{1,0:T(8,128)S(1)}, u32[]{:S(2)}, u32[]{:S(2)}) collective-permute-start(f32[64,128]{1,0:T(8,128)S(1)} %get-tuple-element.21), channel_id=1, source_target_pairs={{0,1},{1,2},{2,3},{3,4},{4,5},{5,6},{6,7},{8,9},{9,10},{10,11},{11... | collective-permute-start | bytes 98312 | tf_op jit(solution)/shard_map/ppermute | solution.py:307
  8.1 2.2 %copy-done = f32[64,128,128]{2,1,0:T(8,128)S(1)} copy-done((f32[64,128,128]{2,1,0:T(8,128)S(1)}, f32[64,128,128]{2,1,0:T(8,128)}, u32[]{:S(2)}) %copy-start) | copy-done | bytes 4194328
  10.3 2.9 %filter.2 = (f32[512,128]{1,0:T(8,128)S(1)}, f32[512,128]{1,0:T(8,128)S(1)}) custom-call(s32[2]{0:T(128)S(1)} %pad_add_fusion.me_ref, f32[6]{0:T(128)} %rtaps_ref.5, f32[6]{0:T(128)} %ctaps_ref.5, f32[64,128,128]{2,1,0:T(8,128)S(1)} %copy-done, s32[64,128]{1,0:T(8,128)} %mask_ref.3), custom_call_target="tpu_custom_call" | custom-call | bytes 4194304 | tf_op jit(solution)/shard_map/filter/pallas_call | solution.py:313
  13.8 1.6 %collective-permute-start.3 = (f32[512,128]{1,0:T(8,128)S(1)}, f32[512,128]{1,0:T(8,128)S(1)}, u32[]{:S(2)}, u32[]{:S(2)}) collective-permute-start(f32[512,128]{1,0:T(8,128)S(1)} %get-tuple-element.25), channel_id=1, source_target_pairs={{0,16},{8,24},{16,0},{24,8},{1,17},{9,25},{17,1},{25,9},{2,18},{10... | collective-permute-start | bytes 786440 | tf_op jit(solution)/shard_map/ppermute | solution.py:32
  15.4 2.7 %filter.3 = (f32[512,128]{1,0:T(8,128)S(1)}, f32[512,128]{1,0:T(8,128)S(1)}) custom-call(s32[2]{0:T(128)S(1)} %pad_add_fusion.me_ref, f32[6]{0:T(128)} %rtaps_ref.5, f32[6]{0:T(128)} %ctaps_ref.5, f32[64,128,128]{2,1,0:T(8,128)S(1)} %copy-done.1, s32[64,128]{1,0:T(8,128)} %mask_ref.3), custom_call_target="tpu_custom_call" | custom-call | bytes 4194304 | tf_op jit(solution)/shard_map/filter/pallas_call | solution.py:313
  19.5 3.7 %collective-permute-done.3.refs_2_ = f32[512,128]{1,0:T(8,128)S(1)} collective-permute-done((f32[512,128]{1,0:T(8,128)S(1)}, f32[512,128]{1,0:T(8,128)S(1)}, u32[]{:S(2)}, u32[]{:S(2)}) %collective-permute-start.3) | collective-permute-done | bytes 262176 | tf_op jit(solution)/shard_map/ppermute | solution.py:32
  23.1 3.2 %collective-permute-done.4.refs_3_ = f32[512,128]{1,0:T(8,128)S(1)} collective-permute-done((f32[512,128]{1,0:T(8,128)S(1)}, f32[512,128]{1,0:T(8,128)S(1)}, u32[]{:S(2)}, u32[]{:S(2)}) %collective-permute-start.4) | collective-permute-done | bytes 262176 | tf_op jit(solution)/shard_map/ppermute | solution.py:32
  26.3 2.0 %gram.1 = (f32[4,224,128]{2,1,0:T(8,128)S(1)}, f32[4,224,128]{2,1,0:T(8,128)S(1)}, f32[512,512]{1,0:T(8,128)S(1)}) custom-call(s32[2]{0:T(128)S(1)} %pad_add_fusion.me_ref, f32[2048,128]{1,0:T(8,128)S(1)} %bitcast.22, f32[512,128]{1,0:T(8,128)S(1)} %get-tuple-element.30.refs_0_, f32[512,128]{1,0:T(8,128)S(1)} %collective-permute-done.2.refs_1_, ...), custom_call_target="tpu_custom_call" | custom-call | tf_op jit(solution)/shard_map/gram/pallas_call | solution.py:346
  29.2 1.4 %collective-permute-done.5 = f32[4,224,128]{2,1,0:T(8,128)S(1)} collective-permute-done((f32[4,224,128]{2,1,0:T(8,128)S(1)}, f32[4,224,128]{2,1,0:T(8,128)S(1)}, u32[]{:S(2)}, u32[]{:S(2)}) %collective-permute-start.5) | collective-permute-done | bytes 458784 | tf_op jit(solution)/shard_map/ppermute | solution.py:32
  30.7 1.6 %collective-permute-start.6 = (f32[224,128]{1,0:T(8,128)S(1)}, f32[224,128]{1,0:T(8,128)S(1)}, u32[]{:S(2)}, u32[]{:S(2)}) collective-permute-start(f32[224,128]{1,0:T(8,128)S(1)} %get-tuple-element.40), channel_id=1, source_target_pairs={{0,16},{1,17},{2,18},{3,19},{4,20},{5,21},{6,22},{7,23},{8,24},{9,... | collective-permute-start | bytes 344072 | tf_op jit(solution)/shard_map/ppermute | solution.py:42
  32.3 2.3 %collective-permute-start.8 = (f32[224,128]{1,0:T(8,128)S(1)}, f32[224,128]{1,0:T(8,128)S(1)}, u32[]{:S(2)}, u32[]{:S(2)}) collective-permute-start(f32[224,128]{1,0:T(8,128)S(1)} %get-tuple-element.41), channel_id=1, source_target_pairs={{0,17},{1,16},{2,19},{3,18},{4,21},{5,20},{6,23},{7,22},{8,25},{9,... | collective-permute-start | bytes 344072 | tf_op jit(solution)/shard_map/ppermute | solution.py:42
  34.6 3.8 %collective-permute-done.6 = f32[224,128]{1,0:T(8,128)S(1)} collective-permute-done((f32[224,128]{1,0:T(8,128)S(1)}, f32[224,128]{1,0:T(8,128)S(1)}, u32[]{:S(2)}, u32[]{:S(2)}) %collective-permute-start.6) | collective-permute-done | bytes 114720 | tf_op jit(solution)/shard_map/ppermute | solution.py:42
  38.7 1.8 %collective-permute-done.7 = f32[224,128]{1,0:T(8,128)S(1)} collective-permute-done((f32[224,128]{1,0:T(8,128)S(1)}, f32[224,128]{1,0:T(8,128)S(1)}, u32[]{:S(2)}, u32[]{:S(2)}) %collective-permute-start.7) | collective-permute-done | bytes 114720 | tf_op jit(solution)/shard_map/ppermute | solution.py:42
  40.5 2.7 %collective-permute-start.9 = (f32[224,128]{1,0:T(8,128)S(1)}, f32[224,128]{1,0:T(8,128)S(1)}, u32[]{:S(2)}, u32[]{:S(2)}) collective-permute-start(f32[224,128]{1,0:T(8,128)S(1)} %fusion.6), channel_id=1, source_target_pairs={{0,2},{1,3},{2,0},{3,1},{4,6},{5,7},{6,4},{7,5},{8,10},{9,11},{10,... | collective-permute-start | bytes 344072 | tf_op jit(solution)/shard_map/ppermute | solution.py:32
  43.3 2.8 %collective-permute-done.9 = f32[224,128]{1,0:T(8,128)S(1)} collective-permute-done((f32[224,128]{1,0:T(8,128)S(1)}, f32[224,128]{1,0:T(8,128)S(1)}, u32[]{:S(2)}, u32[]{:S(2)}) %collective-permute-start.9) | collective-permute-done | bytes 114720 | tf_op jit(solution)/shard_map/ppermute | solution.py:32
  46.1 3.1 %collective-permute-start.10 = (f32[224,128]{1,0:T(8,128)S(1)}, f32[224,128]{1,0:T(8,128)S(1)}, u32[]{:S(2)}, u32[]{:S(2)}) collective-permute-start(f32[224,128]{1,0:T(8,128)S(1)} %add.59), channel_id=1, source_target_pairs={{0,4},{1,5},{2,6},{3,7},{4,0},{5,1},{6,2},{7,3},{8,12},{9,13},{10,... | collective-permute-start | bytes 344072 | tf_op jit(solution)/shard_map/ppermute | solution.py:32
  49.2 2.8 %collective-permute-done.10 = f32[224,128]{1,0:T(8,128)S(1)} collective-permute-done((f32[224,128]{1,0:T(8,128)S(1)}, f32[224,128]{1,0:T(8,128)S(1)}, u32[]{:S(2)}, u32[]{:S(2)}) %collective-permute-start.10) | collective-permute-done | bytes 114720 | tf_op jit(solution)/shard_map/ppermute | solution.py:32
  52.0 3.2 %collective-permute-start.13 = (f32[224,128]{1,0:T(8,128)S(1)}, f32[224,128]{1,0:T(8,128)S(1)}, u32[]{:S(2)}, u32[]{:S(2)}) collective-permute-start(f32[224,128]{1,0:T(8,128)S(1)} %add.60), channel_id=1, source_target_pairs={{0,17},{1,16},{2,19},{3,18},{4,21},{5,20},{6,23},{7,22},{8,25},{9,... | collective-permute-start | bytes 344072 | tf_op jit(solution)/shard_map/ppermute | solution.py:42
  55.8 2.2 %collective-permute-done.13 = f32[224,128]{1,0:T(8,128)S(1)} collective-permute-done((f32[224,128]{1,0:T(8,128)S(1)}, f32[224,128]{1,0:T(8,128)S(1)}, u32[]{:S(2)}, u32[]{:S(2)}) %collective-permute-start.13) | collective-permute-done | bytes 114720 | tf_op jit(solution)/shard_map/ppermute | solution.py:42
  57.9 2.0 %collective-permute-done.12 = f32[224,128]{1,0:T(8,128)S(1)} collective-permute-done((f32[224,128]{1,0:T(8,128)S(1)}, f32[224,128]{1,0:T(8,128)S(1)}, u32[]{:S(2)}, u32[]{:S(2)}) %collective-permute-start.12) | collective-permute-done | bytes 114720 | tf_op jit(solution)/shard_map/ppermute | solution.py:42
  60.0 1.8 %collective-permute-done.14.odd_ref = f32[4,224,128]{2,1,0:T(8,128)S(1)} collective-permute-done((f32[4,224,128]{2,1,0:T(8,128)S(1)}, f32[4,224,128]{2,1,0:T(8,128)S(1)}, u32[]{:S(2)}, u32[]{:S(2)}) %collective-permute-start.14) | collective-permute-done | bytes 458784 | tf_op jit(solution)/shard_map/ppermute | solution.py:32
  61.9 12.3 %merge.1 = (f32[32,512]{1,0:T(8,128)S(1)}, f32[32,512]{1,0:T(8,128)S(1)}, f32[32,512]{1,0:T(8,128)S(1)}, f32[32,512]{1,0:T(8,128)S(1)}, f32[32,128]{1,0:T(8,128)}) custom-call(s32[2]{0:T(128)S(1)} %pad_add_fusion.me_ref, f32[4,224,128]{2,1,0:T(8,128)S(1)} %pad_maximum_fusion.even_ref, f32[4,224,128]{2,1,0:T(8,128)S(1)} %collective-permute-done.14.odd_ref, ...), custom_call_target="tpu_custom_call" | custom-call | tf_op jit(solution)/shard_map/merge/pallas_call | solution.py:366
  76.1 3.2 %collective-permute-done.16.refs_2_ = f32[32,512]{1,0:T(8,128)S(1)} collective-permute-done((f32[32,512]{1,0:T(8,128)S(1)}, f32[32,512]{1,0:T(8,128)S(1)}, u32[]{:S(2)}, u32[]{:S(2)}) %collective-permute-start.16) | collective-permute-done | bytes 65568 | tf_op jit(solution)/shard_map/ppermute | solution.py:32
  79.5 1.5 %final.1 = f32[32,32,64]{2,1,0:T(8,128)} custom-call(s32[2]{0:T(128)S(1)} %pad_add_fusion.me_ref, f32[32,512]{1,0:T(8,128)S(1)} %get-tuple-element.35.refs_0_, f32[32,512]{1,0:T(8,128)S(1)} %collective-permute-done.15.refs_1_, f32[32,512]{1,0:T(8,128)S(1)} %collective-permute-done.16.refs_2_, f32[32,512]{1,0:T(8,128)S(1)} %collective-permute-done.17.refs_3_), custom_call_target="tpu_custom_call" | custom-call | tf_op jit(solution)/shard_map/final/pallas_call | solution.py:381
  (32 shorter events, 8.8 us)
Async XLA Ops:
  1.9 11.3 %collective-permute-start = (f32[64,128]{1,0:T(8,128)S(1)}, f32[64,128]{1,0:T(8,128)S(1)}, u32[]{:S(2)}, u32[]{:S(2)}) collective-permute-start(f32[64,128]{1,0:T(8,128)S(1)} %get-tuple-element.21), channel_id=1, source_target_pairs={{0,1},{1,2},{2,3},{3,4},{4,5},{5,6},{6,7},{8,9},{9,10},{10,11},{11... | collective-permute-start | bytes 98312 | tf_op jit(solution)/shard_map/ppermute | solution.py:307
  6.7 6.5 %collective-permute-start.1 = (f32[64,128]{1,0:T(8,128)S(1)}, f32[64,128]{1,0:T(8,128)S(1)}, u32[]{:S(2)}, u32[]{:S(2)}) collective-permute-start(f32[64,128]{1,0:T(8,128)S(1)} %get-tuple-element.22), channel_id=1, source_target_pairs={{1,0},{2,1},{3,2},{4,3},{5,4},{6,5},{7,6},{9,8},{10,9},{11,10},{12... | collective-permute-start | bytes 98312 | tf_op jit(solution)/shard_map/ppermute | solution.py:308
  8.1 2.2 %copy-start = (f32[64,128,128]{2,1,0:T(8,128)S(1)}, f32[64,128,128]{2,1,0:T(8,128)}, u32[]{:S(2)}) copy-start(f32[64,128,128]{2,1,0:T(8,128)} %snaps.3) | copy-start | bytes 12582916
  10.3 5.1 %copy-start.1 = (f32[64,128,128]{2,1,0:T(8,128)S(1)}, f32[64,128,128]{2,1,0:T(8,128)}, u32[]{:S(2)}) copy-start(f32[64,128,128]{2,1,0:T(8,128)} %snaps.3) | copy-start | bytes 12582916
  10.3 16.0 %copy-start.2 = (f32[32,64,128]{2,1,0:T(8,128)S(1)}, f32[32,64,128]{2,1,0:T(8,128)}, u32[]{:S(2)}) copy-start(f32[32,64,128]{2,1,0:T(8,128)} %param.9) | copy-start | bytes 3145732
  13.8 9.3 %collective-permute-start.3 = (f32[512,128]{1,0:T(8,128)S(1)}, f32[512,128]{1,0:T(8,128)S(1)}, u32[]{:S(2)}, u32[]{:S(2)}) collective-permute-start(f32[512,128]{1,0:T(8,128)S(1)} %get-tuple-element.25), channel_id=1, source_target_pairs={{0,16},{8,24},{16,0},{24,8},{1,17},{9,25},{17,1},{25,9},{2,18},{10... | collective-permute-start | bytes 786440 | tf_op jit(solution)/shard_map/ppermute | solution.py:32
  15.4 10.9 %collective-permute-start.4 = (f32[512,128]{1,0:T(8,128)S(1)}, f32[512,128]{1,0:T(8,128)S(1)}, u32[]{:S(2)}, u32[]{:S(2)}) collective-permute-start(f32[512,128]{1,0:T(8,128)S(1)} %get-tuple-element.26), channel_id=1, source_target_pairs={{0,24},{8,16},{16,8},{24,0},{1,25},{9,17},{17,9},{25,1},{2,26},{10... | collective-permute-start | bytes 786440 | tf_op jit(solution)/shard_map/ppermute | solution.py:32
  18.8 7.5 %collective-permute-start.2 = (f32[512,128]{1,0:T(8,128)S(1)}, f32[512,128]{1,0:T(8,128)S(1)}, u32[]{:S(2)}, u32[]{:S(2)}) collective-permute-start(f32[512,128]{1,0:T(8,128)S(1)} %get-tuple-element.31), channel_id=1, source_target_pairs={{0,8},{8,0},{16,24},{24,16},{1,9},{9,1},{17,25},{25,17},{2,10},{10... | collective-permute-start | bytes 786440 | tf_op jit(solution)/shard_map/ppermute | solution.py:32
  28.3 2.3 %collective-permute-start.5 = (f32[4,224,128]{2,1,0:T(8,128)S(1)}, f32[4,224,128]{2,1,0:T(8,128)S(1)}, u32[]{:S(2)}, u32[]{:S(2)}) collective-permute-start(f32[4,224,128]{2,1,0:T(8,128)S(1)} %get-tuple-element.33), channel_id=1, source_target_pairs={{0,8},{8,0},{16,24},{24,16},{1,9},{9,1},{17,25},{25,17},{2,10},{10... | collective-permute-start | bytes 1376264 | tf_op jit(solution)/shard_map/ppermute | solution.py:32
  30.7 7.8 %collective-permute-start.6 = (f32[224,128]{1,0:T(8,128)S(1)}, f32[224,128]{1,0:T(8,128)S(1)}, u32[]{:S(2)}, u32[]{:S(2)}) collective-permute-start(f32[224,128]{1,0:T(8,128)S(1)} %get-tuple-element.40), channel_id=1, source_target_pairs={{0,16},{1,17},{2,18},{3,19},{4,20},{5,21},{6,22},{7,23},{8,24},{9,... | collective-permute-start | bytes 344072 | tf_op jit(solution)/shard_map/ppermute | solution.py:42
  32.3 6.5 %collective-permute-start.8 = (f32[224,128]{1,0:T(8,128)S(1)}, f32[224,128]{1,0:T(8,128)S(1)}, u32[]{:S(2)}, u32[]{:S(2)}) collective-permute-start(f32[224,128]{1,0:T(8,128)S(1)} %get-tuple-element.41), channel_id=1, source_target_pairs={{0,17},{1,16},{2,19},{3,18},{4,21},{5,20},{6,23},{7,22},{8,25},{9,... | collective-permute-start | bytes 344072 | tf_op jit(solution)/shard_map/ppermute | solution.py:42
  34.6 6.0 %collective-permute-start.7 = (f32[224,128]{1,0:T(8,128)S(1)}, f32[224,128]{1,0:T(8,128)S(1)}, u32[]{:S(2)}, u32[]{:S(2)}) collective-permute-start(f32[224,128]{1,0:T(8,128)S(1)} %get-tuple-element.42), channel_id=1, source_target_pairs={{0,1},{1,0},{2,3},{3,2},{4,5},{5,4},{6,7},{7,6},{8,9},{9,8},{10,11... | collective-permute-start | bytes 344072 | tf_op jit(solution)/shard_map/ppermute | solution.py:42
  40.5 5.5 %collective-permute-start.9 = (f32[224,128]{1,0:T(8,128)S(1)}, f32[224,128]{1,0:T(8,128)S(1)}, u32[]{:S(2)}, u32[]{:S(2)}) collective-permute-start(f32[224,128]{1,0:T(8,128)S(1)} %fusion.6), channel_id=1, source_target_pairs={{0,2},{1,3},{2,0},{3,1},{4,6},{5,7},{6,4},{7,5},{8,10},{9,11},{10,... | collective-permute-start | bytes 344072 | tf_op jit(solution)/shard_map/ppermute | solution.py:32
  46.1 5.9 %collective-permute-start.10 = (f32[224,128]{1,0:T(8,128)S(1)}, f32[224,128]{1,0:T(8,128)S(1)}, u32[]{:S(2)}, u32[]{:S(2)}) collective-permute-start(f32[224,128]{1,0:T(8,128)S(1)} %add.59), channel_id=1, source_target_pairs={{0,4},{1,5},{2,6},{3,7},{4,0},{5,1},{6,2},{7,3},{8,12},{9,13},{10,... | collective-permute-start | bytes 344072 | tf_op jit(solution)/shard_map/ppermute | solution.py:32
  52.0 6.0 %collective-permute-start.13 = (f32[224,128]{1,0:T(8,128)S(1)}, f32[224,128]{1,0:T(8,128)S(1)}, u32[]{:S(2)}, u32[]{:S(2)}) collective-permute-start(f32[224,128]{1,0:T(8,128)S(1)} %add.60), channel_id=1, source_target_pairs={{0,17},{1,16},{2,19},{3,18},{4,21},{5,20},{6,23},{7,22},{8,25},{9,... | collective-permute-start | bytes 344072 | tf_op jit(solution)/shard_map/ppermute | solution.py:42
  55.1 4.8 %collective-permute-start.12 = (f32[224,128]{1,0:T(8,128)S(1)}, f32[224,128]{1,0:T(8,128)S(1)}, u32[]{:S(2)}, u32[]{:S(2)}) collective-permute-start(f32[224,128]{1,0:T(8,128)S(1)} %add.60), channel_id=1, source_target_pairs={{0,1},{1,0},{2,3},{3,2},{4,5},{5,4},{6,7},{7,6},{8,9},{9,8},{10,11... | collective-permute-start | bytes 344072 | tf_op jit(solution)/shard_map/ppermute | solution.py:42
  55.1 4.8 %collective-permute-start.11 = (f32[224,128]{1,0:T(8,128)S(1)}, f32[224,128]{1,0:T(8,128)S(1)}, u32[]{:S(2)}, u32[]{:S(2)}) collective-permute-start(f32[224,128]{1,0:T(8,128)S(1)} %add.60), channel_id=1, source_target_pairs={{0,16},{1,17},{2,18},{3,19},{4,20},{5,21},{6,22},{7,23},{8,24},{9,... | collective-permute-start | bytes 344072 | tf_op jit(solution)/shard_map/ppermute | solution.py:42
  60.0 1.9 %collective-permute-start.14 = (f32[4,224,128]{2,1,0:T(8,128)S(1)}, f32[4,224,128]{2,1,0:T(8,128)S(1)}, u32[]{:S(2)}, u32[]{:S(2)}) collective-permute-start(f32[4,224,128]{2,1,0:T(8,128)S(1)} %pad_maximum_fusion.even_ref), channel_id=1, source_target_pairs={{0,8},{8,0},{16,24},{24,16},{1,9},{9,1},{17,25},{25,17},{2,10},{10... | collective-permute-start | bytes 1376264 | tf_op jit(solution)/shard_map/ppermute | solution.py:32
  74.2 1.9 %collective-permute-start.15 = (f32[32,512]{1,0:T(8,128)S(1)}, f32[32,512]{1,0:T(8,128)S(1)}, u32[]{:S(2)}, u32[]{:S(2)}) collective-permute-start(f32[32,512]{1,0:T(8,128)S(1)} %get-tuple-element.36), channel_id=1, source_target_pairs={{0,8},{8,0},{16,24},{24,16},{1,9},{9,1},{17,25},{25,17},{2,10},{10... | collective-permute-start | bytes 196616 | tf_op jit(solution)/shard_map/ppermute | solution.py:32
  74.3 4.9 %collective-permute-start.16 = (f32[32,512]{1,0:T(8,128)S(1)}, f32[32,512]{1,0:T(8,128)S(1)}, u32[]{:S(2)}, u32[]{:S(2)}) collective-permute-start(f32[32,512]{1,0:T(8,128)S(1)} %get-tuple-element.37), channel_id=1, source_target_pairs={{0,16},{8,24},{16,0},{24,8},{1,17},{9,25},{17,1},{25,9},{2,18},{10... | collective-permute-start | bytes 196616 | tf_op jit(solution)/shard_map/ppermute | solution.py:32
  75.0 4.6 %collective-permute-start.17 = (f32[32,512]{1,0:T(8,128)S(1)}, f32[32,512]{1,0:T(8,128)S(1)}, u32[]{:S(2)}, u32[]{:S(2)}) collective-permute-start(f32[32,512]{1,0:T(8,128)S(1)} %get-tuple-element.38), channel_id=1, source_target_pairs={{0,24},{8,16},{16,8},{24,0},{1,25},{9,17},{17,9},{25,1},{2,26},{10... | collective-permute-start | bytes 196616 | tf_op jit(solution)/shard_map/ppermute | solution.py:32

commit v8 on v7

--- a/solution.py
+++ b/solution.py
@@ -10,7 +10,7 @@
 SIGN_STEPS = 8
 TAPS = 6
 CHUNK = 8
-ROW_BLOCKS = 2
+ROW_BLOCKS = 4
 F32 = jnp.float32
 VMEM_LIMIT = 48 * 1024 * 1024
 
@@ -76,16 +76,18 @@
         out[...] = taps[0] * rows[0] + taps[1] * rows[1]
 
 
-def filter_kernel(parts, other, me_ref, rtaps_ref, ctaps_ref, snaps, mask_ref, *rest):
-    count = parts // 2
-    pieces, (mask_t, narrowed, filtered) = rest[:count], rest[count:]
+def filter_kernel(parts, me_ref, rtaps_ref, ctaps_ref, snap_hbm, mask_ref, *rest):
+    pieces, (snaps, sems, mask_t, narrowed, filtered) = rest[:parts], rest[parts:]
     rows, cells = narrowed.shape[0] - 4, narrowed.shape[1]
     me = me_ref[0]
-    side = me // count
-    if other:
-        side = 1 - side
-    chunks = (rows // 2 + 2 + CHUNK - 1) // CHUNK
-    start = side * (rows - chunks * CHUNK)
+    chunks = rows // CHUNK
+
+    def fetch(c):
+        at = pl.ds(c * CHUNK, CHUNK)
+        return pltpu.make_async_copy(snap_hbm.at[at], snaps.at[at], sems.at[c])
+
+    for c in range(chunks):
+        fetch(c).start()
 
     rtaps = [rtaps_ref[k] for k in range(TAPS)]
     ctaps = [ctaps_ref[k] for k in range(TAPS)]
@@ -94,7 +96,8 @@
     narrowed[rows + 2:rows + 4] = edge
 
     def narrow(c, carry):
-        base = pl.multiple_of(start + c * CHUNK, CHUNK)
+        fetch(c).wait()
+        base = pl.multiple_of(c * CHUNK, CHUNK)
         masks = mask_columns(mask_ref[pl.ds(base, CHUNK), :], mask_t)
         for x in range(CHUNK):
             row = narrowed_row(snaps, base + x, [m[:, x:x + 1] for m in masks], ctaps)
@@ -102,60 +105,81 @@
         return carry
 
     lax.fori_loop(0, chunks, narrow, 0)
-    first = side * (rows // 2)
-    for i in range(rows // 4):
-        total = rtaps[0] * narrowed[first + 2 * i]
+    for i in range(rows // 2):
+        total = rtaps[0] * narrowed[2 * i]
         for k in range(1, TAPS):
-            total = total + rtaps[k] * narrowed[first + 2 * i + k]
+            total = total + rtaps[k] * narrowed[2 * i + k]
         filtered[i * cells:(i + 1) * cells, :] = total
-    size = filtered.shape[0] // count
-    for k in range(count):
-        at = ((me ^ k) % count) * size
-        pieces[k][...] = filtered[pl.ds(pl.multiple_of(at, 8), size), :]
-
-
-def halo_kernel(parts, offset, me_ref, above_ref, below_ref, *refs):
+    size = filtered.shape[0] // parts
+    for k in range(parts):
+        pieces[k][...] = filtered[pl.ds(pl.multiple_of((me ^ k) * size, 8), size), :]
+
+
+def halo_kernel(parts, me_ref, above_ref, below_ref, *refs):
     outs = refs[len(refs) // 2:]
     me = me_ref[0]
     cells = above_ref.shape[0]
     for k, out in enumerate(outs):
         out[...] = refs[k][...]
 
-        @pl.when((me ^ (k + offset)) == 0)
+        @pl.when((me ^ k) == 0)
         def _():
             out[:cells, :] = out[:cells, :] + above_ref[...]
 
-        @pl.when((me ^ (k + offset)) == parts - 1)
+        @pl.when((me ^ k) == parts - 1)
         def _():
             out[-cells:, :] = out[-cells:, :] + below_ref[...]
 
 
-def block_order(parts):
-    return [(a, b) for a in range(parts) for b in range(a, parts)] + [(a, parts) for a in range(parts)]
-
-
-def gram_kernel(parts, span, me_ref, probes_ref, *refs):
+def cross_order(parts):
+    return [(a, b) for p in range(0, parts, 2) for q in range(p + 2, parts, 2) for a in (p, p + 1) for b in (q, q + 1)]
+
+
+def pair_kernel(parts, span, me_ref, probes_ref, *refs):
+    half = parts // 2
+    mine, theirs, (send_ref, keep_ref, wide, there, flat) = refs[:half], refs[half:2 * half], refs[2 * half:]
+    me, owner = me_ref[0], me_ref[2]
+    size, cols = mine[0].shape
+    low = pl.ds(pl.multiple_of((me % 2) * cols, cols), cols)
+    high = pl.ds(pl.multiple_of((1 - me % 2) * cols, cols), cols)
+    for h in range(half):
+        at = pl.ds(h * size, size)
+        wide[at, low] = mine[h][...]
+        wide[at, high] = theirs[h][...]
+        there[at, :] = probes_ref[pl.ds(pl.multiple_of((me ^ 2 * h) * size, 8), size), :]
+    left = split(wide[...])
+    gram = dot_parts(left, left, ((0,), (0,)))
+    flat[:cols, :] = gram[:cols, :cols]
+    flat[cols:2 * cols, :] = gram[:cols, cols:]
+    flat[2 * cols:3 * cols, :] = gram[cols:, cols:]
+    flat[3 * cols:, :] = dot_parts(left, split(there[...]), ((0,), (0,)))
+    give(owner, flat, send_ref, keep_ref)
+
+
+def give(owner, flat, send_ref, keep_ref):
+    count = 2 * send_ref.shape[0]
+    share = flat.shape[0] // count
+    for k in range(count):
+        out = send_ref if k % 2 else keep_ref
+        out[k // 2] = flat[pl.ds(pl.multiple_of((owner ^ k) * share, 8), share), :]
+
+
+def cross_kernel(parts, me_ref, *refs):
     pieces, (send_ref, keep_ref, wide, flat) = refs[:parts], refs[parts:]
     me, owner = me_ref[0], me_ref[1]
-    size, cols = pieces[0].shape
+    cols = pieces[0].shape[1]
     for k in range(parts):
         wide[:, pl.ds(pl.multiple_of((me ^ k) * cols, cols), cols)] = pieces[k][...]
-    where = {ab: j for j, ab in enumerate(block_order(parts))}
     sides = [split(wide[:, a * cols:(a + 2) * cols]) for a in range(0, parts, 2)]
-    sides.append(split(probes_ref[pl.ds(pl.multiple_of(me * size, 8), size), :]))
+    where = {ab: j for j, ab in enumerate(cross_order(parts))}
     for a in range(0, parts, 2):
-        for b in range(a, parts + 2, 2):
-            right = sides[b // 2]
-            prod = dot_parts(sides[a // 2], right, ((0,), (0,)))
+        for b in range(a + 2, parts, 2):
+            prod = dot_parts(sides[a // 2], sides[b // 2], ((0,), (0,)))
             for i in range(2):
-                for j in range(right[0].shape[1] // cols):
-                    if (a + i, b + j) in where:
-                        at = where[a + i, b + j] * cols
-                        flat[at:at + cols, :] = prod[i * cols:(i + 1) * cols, j * cols:(j + 1) * cols]
-    share = flat.shape[0] // (parts * span)
-    for k in range(parts * span):
-        out = send_ref if k % 2 else keep_ref
-        out[k // 2] = flat[pl.ds(pl.multiple_of((owner ^ k) * share, 8), share), :]
+                for j in range(2):
+                    at = where[a + i, b + j] * cols
+                    flat[at:at + cols, :] = prod[i * cols:(i + 1) * cols, j * cols:(j + 1) * cols]
+    give(owner, flat, send_ref, keep_ref)
 
 
 def split(x):
@@ -208,13 +232,22 @@
 
 
 def merge_kernel(parts, span, me_ref, even_ref, odd_ref, wide_ref, *refs):
-    outs, (coef_ref, flat, weight, turned) = refs[:parts], refs[parts:]
+    outs, (coef_ref, pairs, cross, weight, turned) = refs[:parts], refs[parts:]
     me, owner = me_ref[0], me_ref[1]
-    size, cols = even_ref.shape[1:]
+    cols = even_ref.shape[2]
+    pair_share, cross_share = pairs.shape[1] // (2 * span), cross.shape[0] // (parts * span)
     for k in range(parts * span):
-        source = odd_ref if k % 2 else even_ref
-        flat[pl.ds(pl.multiple_of((owner ^ k) * size, 8), size), :] = source[k // 2]
-    blocks = {ab: flat[j * cols:(j + 1) * cols, :] for j, ab in enumerate(block_order(parts))}
+        source = (odd_ref if k % 2 else even_ref).at[k // 2]
+        there = owner ^ k
+        place = there % 2 + 2 * (there // parts)
+        at = pl.ds(pl.multiple_of(place * pair_share, 8), pair_share)
+        pairs[(there % parts) // 2, at, :] = source[:pair_share, :]
+        cross[pl.ds(pl.multiple_of(there * cross_share, 8), cross_share), :] = source[pair_share:, :]
+    blocks = {ab: cross[j * cols:(j + 1) * cols, :] for j, ab in enumerate(cross_order(parts))}
+    for p in range(parts // 2):
+        for j, ab in enumerate(((2 * p, 2 * p), (2 * p, 2 * p + 1), (2 * p + 1, 2 * p + 1))):
+            blocks[ab] = pairs[p, j * cols:(j + 1) * cols, :]
+    products = jnp.concatenate([pairs[p, 3 * cols:, :] for p in range(parts // 2)], axis=0)
     weights, count = None, parts
     while count > 1:
         grams = []
@@ -251,7 +284,7 @@
     width = cols // parts
     rows = total.shape[0]
     turned[:, :rows] = total.T
-    turned[:, rows:] = split_dot(weight[...], flat[-parts * cols:, :], ((0,), (0,)))
+    turned[:, rows:] = split_dot(weight[...], products, ((0,), (0,)))
     for k in range(parts):
         outs[k][...] = turned[pl.ds(pl.multiple_of((me ^ k) * width, 8), width), :rows]
     coef_ref[...] = turned[pl.ds(pl.multiple_of(me * width, 8), width), rows:]
@@ -279,9 +312,9 @@
     piece = cells // parts
     span = 2 if patches > 1 else 1
     position, patch = lax.axis_index("tm"), lax.axis_index("space")
-    me = jnp.stack([position, position + parts * (patch % span)]).astype(jnp.int32)
-
-    held = snapshots
+    here = patch % span
+    me = jnp.stack([position, position + parts * here, position % 2 + 2 * here]).astype(jnp.int32)
+
     snapshots, land_mask, taps_rows, taps_cols = (
         pltpu.with_memory_space_constraint(x, pltpu.HBM) for x in (snapshots, land_mask, taps_rows, taps_cols)
     )
@@ -307,55 +340,78 @@
     above = lax.ppermute(to_below, "space", up)
     below = lax.ppermute(to_above, "space", [(j, i) for i, j in up])
 
-    count = parts // 2
-
-    def half_of_rows(other, after):
-        halves = pl.pallas_call(
-            functools.partial(filter_kernel, parts, other),
-            out_shape=[shape(piece, cols)] * count,
-            in_specs=[scalars(), scalars(), scalars(), whole(), whole()],
-            out_specs=[whole()] * count,
-            scratch_shapes=[
-                pltpu.VMEM((grid_cols, CHUNK), F32),
-                pltpu.VMEM((rows + 4, half_cols, cols), F32),
-                pltpu.VMEM((cells // 2, cols), F32),
-            ],
-            compiler_params=params(),
-            cost_estimate=pl.CostEstimate(flops=0, bytes_accessed=4 * snapshots.size, transcendentals=0),
-            name="filter",
-        )(after, taps_rows, taps_cols, held, land_mask)
-        return pl.pallas_call(
-            functools.partial(halo_kernel, parts, count if other else 0),
-            out_shape=[shape(piece, cols)] * count,
-            in_specs=[scalars()] + [whole()] * (count + 2),
-            out_specs=[whole()] * count,
-            input_output_aliases={3 + k: k for k in range(count)},
-            compiler_params=params(),
-            name="halo",
-        )(me, above, below, *halves)
-
-    leaving = half_of_rows(True, me)
-    far = [swap(leaving[k], "tm", k + count) for k in range(count)]
-    after, *leaving = lax.optimization_barrier([me] + list(leaving))
-    staying = half_of_rows(False, after)
-    far = [staying[0]] + [swap(staying[k], "tm", k) for k in range(1, count)] + far
-
-    blocks = len(block_order(parts))
+    pieces = pl.pallas_call(
+        functools.partial(filter_kernel, parts),
+        out_shape=[shape(piece, cols)] * parts,
+        in_specs=[scalars(), scalars(), scalars(), pl.BlockSpec(memory_space=pltpu.HBM), whole()],
+        out_specs=[whole()] * parts,
+        scratch_shapes=[
+            pltpu.VMEM((rows, grid_cols, cols), F32),
+            pltpu.SemaphoreType.DMA((rows // CHUNK,)),
+            pltpu.VMEM((grid_cols, CHUNK), F32),
+            pltpu.VMEM((rows + 4, half_cols, cols), F32),
+            pltpu.VMEM((cells, cols), F32),
+        ],
+        compiler_params=params(),
+        cost_estimate=pl.CostEstimate(flops=0, bytes_accessed=4 * snapshots.size, transcendentals=0),
+        name="filter",
+    )(me, taps_rows, taps_cols, snapshots, land_mask)
+    kept = pl.pallas_call(
+        functools.partial(halo_kernel, parts),
+        out_shape=[shape(piece, cols)] * parts,
+        in_specs=[scalars()] + [whole()] * (parts + 2),
+        out_specs=[whole()] * parts,
+        input_output_aliases={3 + k: k for k in range(parts)},
+        compiler_params=params(),
+        name="halo",
+    )(me, above, below, *pieces)
+    theirs = {k: swap(kept[k + 1], "tm", 1) for k in range(0, parts, 2)}
+    far = {0: kept[0], 1: theirs[0]}
+    for k in range(2, parts, 2):
+        far[k] = swap(kept[k], "tm", k)
+        far[k + 1] = swap(theirs[k], "tm", k)
+
+    owners = 2 * span
+    size = 5 * cols // owners
+    send, keep = pl.pallas_call(
+        functools.partial(pair_kernel, parts, span),
+        out_shape=[shape(span, size, cols)] * 2,
+        in_specs=[scalars()] + [whole()] * (parts + 1),
+        out_specs=[whole()] * 2,
+        scratch_shapes=[
+            pltpu.VMEM((cells // 2, 2 * cols), F32),
+            pltpu.VMEM((cells // 2, cols), F32),
+            pltpu.VMEM((5 * cols, cols), F32),
+        ],
+        compiler_params=params(),
+        cost_estimate=pl.CostEstimate(flops=0, bytes_accessed=0, transcendentals=0),
+        name="pair",
+    )(me, probes.reshape(cells, cols), *[kept[k] for k in range(0, parts, 2)], *[theirs[k] for k in range(0, parts, 2)])
+    got = swap(send, "tm", 1)
+    got, *waited = lax.optimization_barrier([got] + [far[k] for k in range(2, parts)])
+    far.update(zip(range(2, parts), waited))
+    pair_share = keep[0] + got[0]
+    for h in range(1, span):
+        pair_share = pair_share + swap(keep[h] + got[h], "space", h)
+
+    blocks = len(cross_order(parts))
     owners = parts * span
     size = blocks * cols // owners
     send, keep, wide = pl.pallas_call(
-        functools.partial(gram_kernel, parts, span),
+        functools.partial(cross_kernel, parts),
         out_shape=[shape(owners // 2, size, cols)] * 2 + [shape(piece, parts * cols)],
-        in_specs=[scalars()] + [whole()] * (parts + 1),
+        in_specs=[scalars()] + [whole()] * parts,
         out_specs=[whole()] * 3,
         scratch_shapes=[pltpu.VMEM((blocks * cols, cols), F32)],
         compiler_params=params(),
-        name="gram",
-    )(me, probes.reshape(cells, cols), *far)
+        cost_estimate=pl.CostEstimate(flops=0, bytes_accessed=0, transcendentals=0),
+        name="cross",
+    )(me, *[far[k] for k in range(parts)])
     got = swap(send, "tm", 1)
     mine = keep[0] + got[0]
     for h in range(1, owners // 2):
         mine = mine + swap_both(keep[h] + got[h], 2 * h)
+    mine = jnp.concatenate([pair_share, mine], axis=0)
     bits = [1 << b for b in range(1, patches.bit_length() - 1)]
     for bit in bits:
         mine = mine + swap(mine, "space", bit)
@@ -369,6 +425,7 @@
         in_specs=[scalars()] + [whole()] * 3,
         out_specs=[whole()] * (parts + 1),
         scratch_shapes=[
+            pltpu.VMEM((parts // 2, 5 * cols, cols), F32),
             pltpu.VMEM((blocks * cols, cols), F32),
             pltpu.VMEM((parts * cols, cols), F32),
             pltpu.VMEM((cols, piece + cols), F32),

time: 81.7 us -> 80.6 us (0.987)
  local copies, waits for them, and re-layouts: 2.2 us -> 0.01 us
  starting transfers between devices: 24.8 us -> 26.3 us
  waiting for transfers between devices: 29.2 us -> 27.8 us
  Pallas kernels: 23.9 us -> 24.8 us
    ppermute x6, waiting for transfers between devices: 10 us -> 7.38 us  [swap_both(): return lax.ppermute(x, ('tm', 'space'), route)]
    unnamed x6 -> x2, local copies, waits for them, and re-layouts: 2.2 us -> 0.01 us
    ppermute x10 -> x13, starting transfers between devices: 10.9 us -> 13 us  [swap(): return lax.ppermute(x, axis, [(i, i ^ mask) for i in range(count)])]
    ppermute x10 -> x13, waiting for transfers between devices: 19.1 us -> 20.4 us  [swap(): return lax.ppermute(x, axis, [(i, i ^ mask) for i in range(count)])]
    pallas_call x1, Pallas kernels: 12.3 us -> 13.3 us  [local(): pl.pallas_call(functools.partial(merge_kernel, parts, span), out_shape=[s...]
    pallas_call x5 -> x4, Pallas kernels: 8.82 us -> 8.76 us  [the longest x1 5.1 us: local(): pl.pallas_call(functools.partial(filter_kernel, parts), out_shape=[shape(...]
  transfers between devices with their start and end apart: 18 -> 21, of which waited for: 13 -> 13; matrix products, arithmetic and copies ran while one was open for 0% -> 0% of each run, Pallas kernels for 8% -> 9%
where the time goes in v8:
time: 80.6 us; the launch traced here: 79.9 us
  waiting for transfers between devices  27.8 us (34%)
  starting transfers between devices  26.3 us (33%)
  Pallas kernels  24.8 us (31%)
  between operations  0.81 us (1%)
    ppermute x13, waiting for transfers between devices, swap(): return lax.ppermute(x, axis, [(i, i ^ mask) for i in range(count)])  20.4 us
    pallas_call x1, Pallas kernels, local(): pl.pallas_call(functools.partial(merge_kernel, parts, span), out_shape=[s...  13.3 us
    ppermute x13, starting transfers between devices, swap(): return lax.ppermute(x, axis, [(i, i ^ mask) for i in range(count)])  13 us
    ppermute x6, waiting for transfers between devices, swap_both(): return lax.ppermute(x, ('tm', 'space'), route)  7.38 us
    ppermute x6, starting transfers between devices, swap_both(): return lax.ppermute(x, ('tm', 'space'), route)  7.11 us
    pallas_call x1, Pallas kernels, local(): pl.pallas_call(functools.partial(filter_kernel, parts), out_shape=[shape(...  5.1 us
    ppermute x1, starting transfers between devices, local(): above = lax.ppermute(to_below, 'space', up)  4.98 us
    pallas_call x1, Pallas kernels, local(): pl.pallas_call(functools.partial(pair_kernel, parts, span), out_shape=[sh...  1.8 us
  transfers between devices with their start and end apart: 21, of which 13 were waited for; matrix products, arithmetic and copies ran while one was open for 0% of the time, Pallas kernels for 9%

profile of v8, /device:TPU:0, one launch (start us, length us, event | category | flops | bytes accessed | tf_op | source)
XLA Modules:
  0.0 79.9 jit_solution(11339832620326617744)
XLA Ops:
  0.6 1.2 %edge.1 = (f32[64,128]{1,0:T(8,128)S(1)}, f32[64,128]{1,0:T(8,128)S(1)}) custom-call(f32[6]{0:T(128)} %rtaps_ref.3, f32[6]{0:T(128)} %ctaps_ref.3, f32[64,128,128]{2,1,0:T(8,128)} %snap_hbm.1, f32[64,128,128]{2,1,0:T(8,128)} %snap_hbm.1, s32[64,128]{1,0:T(8,128)} %mask_ref.1, s32[64,128]{1,0:T(8,128)} %mask_ref.1), custom_call_target="tpu_custom_call" | custom-call | tf_op jit(solution)/shard_map/edge/pallas_call | solution.py:323
  1.9 5.0 %collective-permute-start = (f32[64,128]{1,0:T(8,128)S(1)}, f32[64,128]{1,0:T(8,128)S(1)}, u32[]{:S(2)}, u32[]{:S(2)}) collective-permute-start(f32[64,128]{1,0:T(8,128)S(1)} %get-tuple-element.25), channel_id=1, source_target_pairs={{0,1},{1,2},{2,3},{3,4},{4,5},{5,6},{6,7},{8,9},{9,10},{10,11},{11... | collective-permute-start | bytes 98312 | tf_op jit(solution)/shard_map/ppermute | solution.py:340
  6.9 1.3 %collective-permute-start.1 = (f32[64,128]{1,0:T(8,128)S(1)}, f32[64,128]{1,0:T(8,128)S(1)}, u32[]{:S(2)}, u32[]{:S(2)}) collective-permute-start(f32[64,128]{1,0:T(8,128)S(1)} %get-tuple-element.26), channel_id=1, source_target_pairs={{1,0},{2,1},{3,2},{4,3},{5,4},{6,5},{7,6},{9,8},{10,9},{11,10},{12... | collective-permute-start | bytes 98312 | tf_op jit(solution)/shard_map/ppermute | solution.py:341
  8.3 5.1 %filter.1 = (f32[512,128]{1,0:T(8,128)S(1)}, f32[512,128]{1,0:T(8,128)S(1)}, f32[512,128]{1,0:T(8,128)S(1)}, f32[512,128]{1,0:T(8,128)S(1)}) custom-call(s32[3]{0:T(128)S(1)} %pad_add_fusion.me_ref, f32[6]{0:T(128)} %rtaps_ref.3, f32[6]{0:T(128)} %ctaps_ref.3, f32[64,128,128]{2,1,0:T(8,128)} %snap_hbm.1, s32[64,128]{1,0:T(8,128)} %mask_ref.1), custom_call_target="tpu_custom_call" | custom-call | bytes 4194304 | tf_op jit(solution)/shard_map/filter/pallas_call | solution.py:343
  14.7 1.5 %collective-permute-start.5 = (f32[512,128]{1,0:T(8,128)S(1)}, f32[512,128]{1,0:T(8,128)S(1)}, u32[]{:S(2)}, u32[]{:S(2)}) collective-permute-start(f32[512,128]{1,0:T(8,128)S(1)} %get-tuple-element.32.refs_1_), channel_id=1, source_target_pairs={{0,16},{8,24},{16,0},{24,8},{1,17},{9,25},{17,1},{25,9},{2,18},{10... | collective-permute-start | bytes 786440 | tf_op jit(solution)/shard_map/ppermute | solution.py:32
  17.3 1.8 %pair.1 = (f32[2,160,128]{2,1,0:T(8,128)S(1)}, f32[2,160,128]{2,1,0:T(8,128)S(1)}) custom-call(s32[3]{0:T(128)S(1)} %pad_add_fusion.me_ref, f32[2048,128]{1,0:T(8,128)S(1)} %bitcast.27, f32[512,128]{1,0:T(8,128)S(1)} %get-tuple-element.31.refs_0_, f32[512,128]{1,0:T(8,128)S(1)} %get-tuple-element.32.refs_1_, ...), custom_call_target="tpu_custom_call" | custom-call | tf_op jit(solution)/shard_map/pair/pallas_call | solution.py:376
  19.1 4.7 %collective-permute-done.5.refs_2_ = f32[512,128]{1,0:T(8,128)S(1)} collective-permute-done((f32[512,128]{1,0:T(8,128)S(1)}, f32[512,128]{1,0:T(8,128)S(1)}, u32[]{:S(2)}, u32[]{:S(2)}) %collective-permute-start.5) | collective-permute-done | bytes 262176 | tf_op jit(solution)/shard_map/ppermute | solution.py:32
  23.9 4.7 %collective-permute-done.6.refs_3_ = f32[512,128]{1,0:T(8,128)S(1)} collective-permute-done((f32[512,128]{1,0:T(8,128)S(1)}, f32[512,128]{1,0:T(8,128)S(1)}, u32[]{:S(2)}, u32[]{:S(2)}) %collective-permute-start.6) | collective-permute-done | bytes 262176 | tf_op jit(solution)/shard_map/ppermute | solution.py:32
  28.6 1.1 %cross.1 = (f32[4,64,128]{2,1,0:T(8,128)S(1)}, f32[4,64,128]{2,1,0:T(8,128)S(1)}, f32[512,512]{1,0:T(8,128)S(1)}) custom-call(s32[3]{0:T(128)S(1)} %pad_add_fusion.me_ref, f32[512,128]{1,0:T(8,128)S(1)} %get-tuple-element.31.refs_0_, f32[512,128]{1,0:T(8,128)S(1)} %collective-permute-done.2.refs_2_.refs_1_, f32[512,128]{1,0:T(8,128)S(1)} %collective-permute-done.5.refs_2_, ...), custom_call_target="tpu_custom_call" | custom-call | tf_op jit(solution)/shard_map/cross/pallas_call | solution.py:400
  29.9 2.7 %collective-permute-start.7 = (f32[160,128]{1,0:T(8,128)S(1)}, f32[160,128]{1,0:T(8,128)S(1)}, u32[]{:S(2)}, u32[]{:S(2)}) collective-permute-start(f32[160,128]{1,0:T(8,128)S(1)} %add_bitcast_fusion), channel_id=1, source_target_pairs={{0,1},{1,0},{2,3},{3,2},{4,5},{5,4},{6,7},{7,6},{8,9},{9,8},{10,11... | collective-permute-start | bytes 245768 | tf_op jit(solution)/shard_map/ppermute | solution.py:32
  32.6 1.6 %collective-permute-start.9 = (f32[64,128]{1,0:T(8,128)S(1)}, f32[64,128]{1,0:T(8,128)S(1)}, u32[]{:S(2)}, u32[]{:S(2)}) collective-permute-start(f32[64,128]{1,0:T(8,128)S(1)} %get-tuple-element.48), channel_id=1, source_target_pairs={{0,16},{1,17},{2,18},{3,19},{4,20},{5,21},{6,22},{7,23},{8,24},{9,... | collective-permute-start | bytes 98312 | tf_op jit(solution)/shard_map/ppermute | solution.py:42
  34.2 1.2 %collective-permute-start.11 = (f32[64,128]{1,0:T(8,128)S(1)}, f32[64,128]{1,0:T(8,128)S(1)}, u32[]{:S(2)}, u32[]{:S(2)}) collective-permute-start(f32[64,128]{1,0:T(8,128)S(1)} %get-tuple-element.49), channel_id=1, source_target_pairs={{0,17},{1,16},{2,19},{3,18},{4,21},{5,20},{6,23},{7,22},{8,25},{9,... | collective-permute-start | bytes 98312 | tf_op jit(solution)/shard_map/ppermute | solution.py:42
  36.6 2.6 %collective-permute-done.11 = f32[64,128]{1,0:T(8,128)S(1)} collective-permute-done((f32[64,128]{1,0:T(8,128)S(1)}, f32[64,128]{1,0:T(8,128)S(1)}, u32[]{:S(2)}, u32[]{:S(2)}) %collective-permute-start.11) | collective-permute-done | bytes 32800 | tf_op jit(solution)/shard_map/ppermute | solution.py:42
  39.3 2.0 %collective-permute-start.12 = (f32[224,128]{1,0:T(8,128)S(1)}, f32[224,128]{1,0:T(8,128)S(1)}, u32[]{:S(2)}, u32[]{:S(2)}) collective-permute-start(f32[224,128]{1,0:T(8,128)S(1)} %pad_maximum_fusion.1), channel_id=1, source_target_pairs={{0,2},{1,3},{2,0},{3,1},{4,6},{5,7},{6,4},{7,5},{8,10},{9,11},{10,... | collective-permute-start | bytes 344072 | tf_op jit(solution)/shard_map/ppermute | solution.py:32
  41.3 2.8 %collective-permute-done.12 = f32[224,128]{1,0:T(8,128)S(1)} collective-permute-done((f32[224,128]{1,0:T(8,128)S(1)}, f32[224,128]{1,0:T(8,128)S(1)}, u32[]{:S(2)}, u32[]{:S(2)}) %collective-permute-start.12) | collective-permute-done | bytes 114720 | tf_op jit(solution)/shard_map/ppermute | solution.py:32
  44.2 3.0 %collective-permute-start.13 = (f32[224,128]{1,0:T(8,128)S(1)}, f32[224,128]{1,0:T(8,128)S(1)}, u32[]{:S(2)}, u32[]{:S(2)}) collective-permute-start(f32[224,128]{1,0:T(8,128)S(1)} %fusion.7), channel_id=1, source_target_pairs={{0,4},{1,5},{2,6},{3,7},{4,0},{5,1},{6,2},{7,3},{8,12},{9,13},{10,... | collective-permute-start | bytes 344072 | tf_op jit(solution)/shard_map/ppermute | solution.py:32
  47.2 2.8 %collective-permute-done.13 = f32[224,128]{1,0:T(8,128)S(1)} collective-permute-done((f32[224,128]{1,0:T(8,128)S(1)}, f32[224,128]{1,0:T(8,128)S(1)}, u32[]{:S(2)}, u32[]{:S(2)}) %collective-permute-start.13) | collective-permute-done | bytes 114720 | tf_op jit(solution)/shard_map/ppermute | solution.py:32
  50.0 2.1 %collective-permute-start.16 = (f32[224,128]{1,0:T(8,128)S(1)}, f32[224,128]{1,0:T(8,128)S(1)}, u32[]{:S(2)}, u32[]{:S(2)}) collective-permute-start(f32[224,128]{1,0:T(8,128)S(1)} %add.88), channel_id=1, source_target_pairs={{0,17},{1,16},{2,19},{3,18},{4,21},{5,20},{6,23},{7,22},{8,25},{9,... | collective-permute-start | bytes 344072 | tf_op jit(solution)/shard_map/ppermute | solution.py:42
  53.6 2.2 %collective-permute-done.16 = f32[224,128]{1,0:T(8,128)S(1)} collective-permute-done((f32[224,128]{1,0:T(8,128)S(1)}, f32[224,128]{1,0:T(8,128)S(1)}, u32[]{:S(2)}, u32[]{:S(2)}) %collective-permute-start.16) | collective-permute-done | bytes 114720 | tf_op jit(solution)/shard_map/ppermute | solution.py:42
  55.8 1.3 %collective-permute-done.15 = f32[224,128]{1,0:T(8,128)S(1)} collective-permute-done((f32[224,128]{1,0:T(8,128)S(1)}, f32[224,128]{1,0:T(8,128)S(1)}, u32[]{:S(2)}, u32[]{:S(2)}) %collective-permute-start.15) | collective-permute-done | bytes 114720 | tf_op jit(solution)/shard_map/ppermute | solution.py:42
  57.9 1.8 %collective-permute-done.17.odd_ref = f32[4,224,128]{2,1,0:T(8,128)S(1)} collective-permute-done((f32[4,224,128]{2,1,0:T(8,128)S(1)}, f32[4,224,128]{2,1,0:T(8,128)S(1)}, u32[]{:S(2)}, u32[]{:S(2)}) %collective-permute-start.17) | collective-permute-done | bytes 458784 | tf_op jit(solution)/shard_map/ppermute | solution.py:32
  59.7 13.3 %merge.1 = (f32[32,512]{1,0:T(8,128)S(1)}, f32[32,512]{1,0:T(8,128)S(1)}, f32[32,512]{1,0:T(8,128)S(1)}, f32[32,512]{1,0:T(8,128)S(1)}, f32[32,128]{1,0:T(8,128)}) custom-call(s32[3]{0:T(128)S(1)} %pad_add_fusion.me_ref, f32[4,224,128]{2,1,0:T(8,128)S(1)} %pad_maximum_fusion.even_ref, f32[4,224,128]{2,1,0:T(8,128)S(1)} %collective-permute-done.17.odd_ref, ...), custom_call_target="tpu_custom_call" | custom-call | tf_op jit(solution)/shard_map/merge/pallas_call | solution.py:422
  75.0 3.2 %collective-permute-done.19.refs_2_ = f32[32,512]{1,0:T(8,128)S(1)} collective-permute-done((f32[32,512]{1,0:T(8,128)S(1)}, f32[32,512]{1,0:T(8,128)S(1)}, u32[]{:S(2)}, u32[]{:S(2)}) %collective-permute-start.19) | collective-permute-done | bytes 65568 | tf_op jit(solution)/shard_map/ppermute | solution.py:32
  78.4 1.5 %final.1 = f32[32,32,64]{2,1,0:T(8,128)} custom-call(s32[3]{0:T(128)S(1)} %pad_add_fusion.me_ref, f32[32,512]{1,0:T(8,128)S(1)} %get-tuple-element.43.refs_0_, f32[32,512]{1,0:T(8,128)S(1)} %collective-permute-done.18.refs_1_, f32[32,512]{1,0:T(8,128)S(1)} %collective-permute-done.19.refs_2_, f32[32,512]{1,0:T(8,128)S(1)} %collective-permute-done.20.refs_3_), custom_call_target="tpu_custom_call" | custom-call | tf_op jit(solution)/shard_map/final/pallas_call | solution.py:438
  (36 shorter events, 8.4 us)
Async XLA Ops:
  1.9 15.4 %copy-start = (f32[32,64,128]{2,1,0:T(8,128)S(1)}, f32[32,64,128]{2,1,0:T(8,128)}, u32[]{:S(2)}) copy-start(f32[32,64,128]{2,1,0:T(8,128)} %param.9) | copy-start | bytes 3145732
  1.9 11.5 %collective-permute-start = (f32[64,128]{1,0:T(8,128)S(1)}, f32[64,128]{1,0:T(8,128)S(1)}, u32[]{:S(2)}, u32[]{:S(2)}) collective-permute-start(f32[64,128]{1,0:T(8,128)S(1)} %get-tuple-element.25), channel_id=1, source_target_pairs={{0,1},{1,2},{2,3},{3,4},{4,5},{5,6},{6,7},{8,9},{9,10},{10,11},{11... | collective-permute-start | bytes 98312 | tf_op jit(solution)/shard_map/ppermute | solution.py:340
  6.9 6.5 %collective-permute-start.1 = (f32[64,128]{1,0:T(8,128)S(1)}, f32[64,128]{1,0:T(8,128)S(1)}, u32[]{:S(2)}, u32[]{:S(2)}) collective-permute-start(f32[64,128]{1,0:T(8,128)S(1)} %get-tuple-element.26), channel_id=1, source_target_pairs={{1,0},{2,1},{3,2},{4,3},{5,4},{6,5},{7,6},{9,8},{10,9},{11,10},{12... | collective-permute-start | bytes 98312 | tf_op jit(solution)/shard_map/ppermute | solution.py:341
  14.1 2.1 %collective-permute-start.3 = (f32[512,128]{1,0:T(8,128)S(1)}, f32[512,128]{1,0:T(8,128)S(1)}, u32[]{:S(2)}, u32[]{:S(2)}) collective-permute-start(f32[512,128]{1,0:T(8,128)S(1)} %get-tuple-element.34), channel_id=1, source_target_pairs={{0,8},{8,0},{16,24},{24,16},{1,9},{9,1},{17,25},{25,17},{2,10},{10... | collective-permute-start | bytes 786440 | tf_op jit(solution)/shard_map/ppermute | solution.py:32
  14.2 3.0 %collective-permute-start.2 = (f32[512,128]{1,0:T(8,128)S(1)}, f32[512,128]{1,0:T(8,128)S(1)}, u32[]{:S(2)}, u32[]{:S(2)}) collective-permute-start(f32[512,128]{1,0:T(8,128)S(1)} %get-tuple-element.33), channel_id=1, source_target_pairs={{0,8},{8,0},{16,24},{24,16},{1,9},{9,1},{17,25},{25,17},{2,10},{10... | collective-permute-start | bytes 786440 | tf_op jit(solution)/shard_map/ppermute | solution.py:32
  14.7 9.2 %collective-permute-start.5 = (f32[512,128]{1,0:T(8,128)S(1)}, f32[512,128]{1,0:T(8,128)S(1)}, u32[]{:S(2)}, u32[]{:S(2)}) collective-permute-start(f32[512,128]{1,0:T(8,128)S(1)} %get-tuple-element.32.refs_1_), channel_id=1, source_target_pairs={{0,16},{8,24},{16,0},{24,8},{1,17},{9,25},{17,1},{25,9},{2,18},{10... | collective-permute-start | bytes 786440 | tf_op jit(solution)/shard_map/ppermute | solution.py:32
  16.2 12.4 %collective-permute-start.6 = (f32[512,128]{1,0:T(8,128)S(1)}, f32[512,128]{1,0:T(8,128)S(1)}, u32[]{:S(2)}, u32[]{:S(2)}) collective-permute-start(f32[512,128]{1,0:T(8,128)S(1)} %collective-permute-done.3.refs_3_), channel_id=1, source_target_pairs={{0,16},{8,24},{16,0},{24,8},{1,17},{9,25},{17,1},{25,9},{2,18},{10... | collective-permute-start | bytes 786440 | tf_op jit(solution)/shard_map/ppermute | solution.py:32
  19.1 4.8 %collective-permute-start.4 = (f32[2,160,128]{2,1,0:T(8,128)S(1)}, f32[2,160,128]{2,1,0:T(8,128)S(1)}, u32[]{:S(2)}, u32[]{:S(2)}) collective-permute-start(f32[2,160,128]{2,1,0:T(8,128)S(1)} %get-tuple-element.36), channel_id=1, source_target_pairs={{0,8},{8,0},{16,24},{24,16},{1,9},{9,1},{17,25},{25,17},{2,10},{10... | collective-permute-start | bytes 491528 | tf_op jit(solution)/shard_map/ppermute | solution.py:32
  29.8 2.8 %collective-permute-start.8 = (f32[4,64,128]{2,1,0:T(8,128)S(1)}, f32[4,64,128]{2,1,0:T(8,128)S(1)}, u32[]{:S(2)}, u32[]{:S(2)}) collective-permute-start(f32[4,64,128]{2,1,0:T(8,128)S(1)} %get-tuple-element.41), channel_id=1, source_target_pairs={{0,8},{8,0},{16,24},{24,16},{1,9},{9,1},{17,25},{25,17},{2,10},{10... | collective-permute-start | bytes 393224 | tf_op jit(solution)/shard_map/ppermute | solution.py:32
  29.9 6.3 %collective-permute-start.7 = (f32[160,128]{1,0:T(8,128)S(1)}, f32[160,128]{1,0:T(8,128)S(1)}, u32[]{:S(2)}, u32[]{:S(2)}) collective-permute-start(f32[160,128]{1,0:T(8,128)S(1)} %add_bitcast_fusion), channel_id=1, source_target_pairs={{0,1},{1,0},{2,3},{3,2},{4,5},{5,4},{6,7},{7,6},{8,9},{9,8},{10,11... | collective-permute-start | bytes 245768 | tf_op jit(solution)/shard_map/ppermute | solution.py:32
  32.6 4.0 %collective-permute-start.9 = (f32[64,128]{1,0:T(8,128)S(1)}, f32[64,128]{1,0:T(8,128)S(1)}, u32[]{:S(2)}, u32[]{:S(2)}) collective-permute-start(f32[64,128]{1,0:T(8,128)S(1)} %get-tuple-element.48), channel_id=1, source_target_pairs={{0,16},{1,17},{2,18},{3,19},{4,20},{5,21},{6,22},{7,23},{8,24},{9,... | collective-permute-start | bytes 98312 | tf_op jit(solution)/shard_map/ppermute | solution.py:42
  34.2 5.0 %collective-permute-start.11 = (f32[64,128]{1,0:T(8,128)S(1)}, f32[64,128]{1,0:T(8,128)S(1)}, u32[]{:S(2)}, u32[]{:S(2)}) collective-permute-start(f32[64,128]{1,0:T(8,128)S(1)} %get-tuple-element.49), channel_id=1, source_target_pairs={{0,17},{1,16},{2,19},{3,18},{4,21},{5,20},{6,23},{7,22},{8,25},{9,... | collective-permute-start | bytes 98312 | tf_op jit(solution)/shard_map/ppermute | solution.py:42
  35.4 3.9 %collective-permute-start.10 = (f32[64,128]{1,0:T(8,128)S(1)}, f32[64,128]{1,0:T(8,128)S(1)}, u32[]{:S(2)}, u32[]{:S(2)}) collective-permute-start(f32[64,128]{1,0:T(8,128)S(1)} %get-tuple-element.50), channel_id=1, source_target_pairs={{0,1},{1,0},{2,3},{3,2},{4,5},{5,4},{6,7},{7,6},{8,9},{9,8},{10,11... | collective-permute-start | bytes 98312 | tf_op jit(solution)/shard_map/ppermute | solution.py:42
  39.3 4.9 %collective-permute-start.12 = (f32[224,128]{1,0:T(8,128)S(1)}, f32[224,128]{1,0:T(8,128)S(1)}, u32[]{:S(2)}, u32[]{:S(2)}) collective-permute-start(f32[224,128]{1,0:T(8,128)S(1)} %pad_maximum_fusion.1), channel_id=1, source_target_pairs={{0,2},{1,3},{2,0},{3,1},{4,6},{5,7},{6,4},{7,5},{8,10},{9,11},{10,... | collective-permute-start | bytes 344072 | tf_op jit(solution)/shard_map/ppermute | solution.py:32
  44.2 5.8 %collective-permute-start.13 = (f32[224,128]{1,0:T(8,128)S(1)}, f32[224,128]{1,0:T(8,128)S(1)}, u32[]{:S(2)}, u32[]{:S(2)}) collective-permute-start(f32[224,128]{1,0:T(8,128)S(1)} %fusion.7), channel_id=1, source_target_pairs={{0,4},{1,5},{2,6},{3,7},{4,0},{5,1},{6,2},{7,3},{8,12},{9,13},{10,... | collective-permute-start | bytes 344072 | tf_op jit(solution)/shard_map/ppermute | solution.py:32
  50.0 5.8 %collective-permute-start.16 = (f32[224,128]{1,0:T(8,128)S(1)}, f32[224,128]{1,0:T(8,128)S(1)}, u32[]{:S(2)}, u32[]{:S(2)}) collective-permute-start(f32[224,128]{1,0:T(8,128)S(1)} %add.88), channel_id=1, source_target_pairs={{0,17},{1,16},{2,19},{3,18},{4,21},{5,20},{6,23},{7,22},{8,25},{9,... | collective-permute-start | bytes 344072 | tf_op jit(solution)/shard_map/ppermute | solution.py:42
  52.1 4.9 %collective-permute-start.15 = (f32[224,128]{1,0:T(8,128)S(1)}, f32[224,128]{1,0:T(8,128)S(1)}, u32[]{:S(2)}, u32[]{:S(2)}) collective-permute-start(f32[224,128]{1,0:T(8,128)S(1)} %add.88), channel_id=1, source_target_pairs={{0,1},{1,0},{2,3},{3,2},{4,5},{5,4},{6,7},{7,6},{8,9},{9,8},{10,11... | collective-permute-start | bytes 344072 | tf_op jit(solution)/shard_map/ppermute | solution.py:42
  53.0 4.8 %collective-permute-start.14 = (f32[224,128]{1,0:T(8,128)S(1)}, f32[224,128]{1,0:T(8,128)S(1)}, u32[]{:S(2)}, u32[]{:S(2)}) collective-permute-start(f32[224,128]{1,0:T(8,128)S(1)} %add.88), channel_id=1, source_target_pairs={{0,16},{1,17},{2,18},{3,19},{4,20},{5,21},{6,22},{7,23},{8,24},{9,... | collective-permute-start | bytes 344072 | tf_op jit(solution)/shard_map/ppermute | solution.py:42
  57.9 1.9 %collective-permute-start.17 = (f32[4,224,128]{2,1,0:T(8,128)S(1)}, f32[4,224,128]{2,1,0:T(8,128)S(1)}, u32[]{:S(2)}, u32[]{:S(2)}) collective-permute-start(f32[4,224,128]{2,1,0:T(8,128)S(1)} %pad_maximum_fusion.even_ref), channel_id=1, source_target_pairs={{0,8},{8,0},{16,24},{24,16},{1,9},{9,1},{17,25},{25,17},{2,10},{10... | collective-permute-start | bytes 1376264 | tf_op jit(solution)/shard_map/ppermute | solution.py:32
  73.1 1.9 %collective-permute-start.18 = (f32[32,512]{1,0:T(8,128)S(1)}, f32[32,512]{1,0:T(8,128)S(1)}, u32[]{:S(2)}, u32[]{:S(2)}) collective-permute-start(f32[32,512]{1,0:T(8,128)S(1)} %get-tuple-element.44), channel_id=1, source_target_pairs={{0,8},{8,0},{16,24},{24,16},{1,9},{9,1},{17,25},{25,17},{2,10},{10... | collective-permute-start | bytes 196616 | tf_op jit(solution)/shard_map/ppermute | solution.py:32
  73.2 4.9 %collective-permute-start.19 = (f32[32,512]{1,0:T(8,128)S(1)}, f32[32,512]{1,0:T(8,128)S(1)}, u32[]{:S(2)}, u32[]{:S(2)}) collective-permute-start(f32[32,512]{1,0:T(8,128)S(1)} %get-tuple-element.45), channel_id=1, source_target_pairs={{0,16},{8,24},{16,0},{24,8},{1,17},{9,25},{17,1},{25,9},{2,18},{10... | collective-permute-start | bytes 196616 | tf_op jit(solution)/shard_map/ppermute | solution.py:32
  73.9 4.5 %collective-permute-start.20 = (f32[32,512]{1,0:T(8,128)S(1)}, f32[32,512]{1,0:T(8,128)S(1)}, u32[]{:S(2)}, u32[]{:S(2)}) collective-permute-start(f32[32,512]{1,0:T(8,128)S(1)} %get-tuple-element.46), channel_id=1, source_target_pairs={{0,24},{8,16},{16,8},{24,0},{1,25},{9,17},{17,9},{25,1},{2,26},{10... | collective-permute-start | bytes 196616 | tf_op jit(solution)/shard_map/ppermute | solution.py:32

commit v9 on v8

--- a/solution.py
+++ b/solution.py
@@ -10,7 +10,7 @@
 SIGN_STEPS = 8
 TAPS = 6
 CHUNK = 8
-ROW_BLOCKS = 4
+ROW_BLOCKS = 2
 F32 = jnp.float32
 VMEM_LIMIT = 48 * 1024 * 1024
 
@@ -76,10 +76,10 @@
         out[...] = taps[0] * rows[0] + taps[1] * rows[1]
 
 
-def filter_kernel(parts, me_ref, rtaps_ref, ctaps_ref, snap_hbm, mask_ref, *rest):
-    pieces, (snaps, sems, mask_t, narrowed, filtered) = rest[:parts], rest[parts:]
+def filter_kernel(parts, rtaps_ref, ctaps_ref, snap_hbm, mask_ref, *rest):
+    pieces, (snaps, sems, mask_t, spread, narrowed, filtered) = rest[:parts], rest[parts:]
     rows, cells = narrowed.shape[0] - 4, narrowed.shape[1]
-    me = me_ref[0]
+    me = lax.axis_index("tm")
     chunks = rows // CHUNK
 
     def fetch(c):
@@ -95,12 +95,16 @@
     narrowed[0:2] = edge
     narrowed[rows + 2:rows + 4] = edge
 
+    masks = mask_columns(mask_ref[...], mask_t)
+    for x in range(rows):
+        for j, mask in enumerate(masks):
+            spread[x, j] = jnp.broadcast_to(mask[:, x:x + 1], (cells, narrowed.shape[2]))
+
     def narrow(c, carry):
         fetch(c).wait()
         base = pl.multiple_of(c * CHUNK, CHUNK)
-        masks = mask_columns(mask_ref[pl.ds(base, CHUNK), :], mask_t)
         for x in range(CHUNK):
-            row = narrowed_row(snaps, base + x, [m[:, x:x + 1] for m in masks], ctaps)
+            row = narrowed_row(snaps, base + x, spread[base + x], ctaps)
             narrowed[base + 2 + x] = row
         return carry
 
@@ -115,9 +119,9 @@
         pieces[k][...] = filtered[pl.ds(pl.multiple_of((me ^ k) * size, 8), size), :]
 
 
-def halo_kernel(parts, me_ref, above_ref, below_ref, *refs):
+def halo_kernel(parts, above_ref, below_ref, *refs):
     outs = refs[len(refs) // 2:]
-    me = me_ref[0]
+    me = lax.axis_index("tm")
     cells = above_ref.shape[0]
     for k, out in enumerate(outs):
         out[...] = refs[k][...]
@@ -135,10 +139,12 @@
     return [(a, b) for p in range(0, parts, 2) for q in range(p + 2, parts, 2) for a in (p, p + 1) for b in (q, q + 1)]
 
 
-def pair_kernel(parts, span, me_ref, probes_ref, *refs):
+def pair_kernel(parts, span, probes_ref, *refs):
     half = parts // 2
-    mine, theirs, (send_ref, keep_ref, wide, there, flat) = refs[:half], refs[half:2 * half], refs[2 * half:]
-    me, owner = me_ref[0], me_ref[2]
+    owners = 2 * span
+    mine, theirs, refs = refs[:half], refs[half:2 * half], refs[2 * half:]
+    outs, (wide, there, flat) = refs[:owners], refs[owners:]
+    me, owner = positions(2, span)
     size, cols = mine[0].shape
     low = pl.ds(pl.multiple_of((me % 2) * cols, cols), cols)
     high = pl.ds(pl.multiple_of((1 - me % 2) * cols, cols), cols)
@@ -153,7 +159,14 @@
     flat[cols:2 * cols, :] = gram[:cols, cols:]
     flat[2 * cols:3 * cols, :] = gram[cols:, cols:]
     flat[3 * cols:, :] = dot_parts(left, split(there[...]), ((0,), (0,)))
-    give(owner, flat, send_ref, keep_ref)
+    share = flat.shape[0] // owners
+    for k, out in enumerate(outs):
+        out[...] = flat[pl.ds(pl.multiple_of((owner ^ k) * share, 8), share), :]
+
+
+def positions(count, span):
+    me = lax.axis_index("tm")
+    return me, me % count + count * (lax.axis_index("space") % span)
 
 
 def give(owner, flat, send_ref, keep_ref):
@@ -164,9 +177,9 @@
         out[k // 2] = flat[pl.ds(pl.multiple_of((owner ^ k) * share, 8), share), :]
 
 
-def cross_kernel(parts, me_ref, *refs):
+def cross_kernel(parts, span, *refs):
     pieces, (send_ref, keep_ref, wide, flat) = refs[:parts], refs[parts:]
-    me, owner = me_ref[0], me_ref[1]
+    me, owner = positions(parts, span)
     cols = pieces[0].shape[1]
     for k in range(parts):
         wide[:, pl.ds(pl.multiple_of((me ^ k) * cols, cols), cols)] = pieces[k][...]
@@ -193,10 +206,8 @@
 
 def dot_parts(a, b, dims=((1,), (0,))):
     (ah, al), (bh, bl) = a, b
-    free = 1 - dims[0][0]
-    rows = ah.shape[free]
-    both = dot(jnp.concatenate([ah, al], axis=free), bh, dims)
-    return both[:rows] + (dot(ah, bl, dims) + both[rows:])
+    left = jnp.concatenate([ah, ah, al], axis=dims[0][0])
+    return dot(left, jnp.concatenate([bh, bl, bh], axis=dims[1][0]), dims)
 
 
 def split_dot(a, b, dims=((1,), (0,))):
@@ -231,9 +242,9 @@
     return combines
 
 
-def merge_kernel(parts, span, me_ref, even_ref, odd_ref, wide_ref, *refs):
+def merge_kernel(parts, span, even_ref, odd_ref, wide_ref, *refs):
     outs, (coef_ref, pairs, cross, weight, turned) = refs[:parts], refs[parts:]
-    me, owner = me_ref[0], me_ref[1]
+    me, owner = positions(parts, span)
     cols = even_ref.shape[2]
     pair_share, cross_share = pairs.shape[1] // (2 * span), cross.shape[0] // (parts * span)
     for k in range(parts * span):
@@ -290,9 +301,9 @@
     coef_ref[...] = turned[pl.ds(pl.multiple_of(me * width, 8), width), rows:]
 
 
-def final_kernel(parts, me_ref, *refs):
+def final_kernel(parts, *refs):
     pieces, basis_ref = refs[:parts], refs[parts]
-    me = me_ref[0]
+    me = lax.axis_index("tm")
     per, cells = basis_ref.shape[0] // parts, basis_ref.shape[2]
     for k in range(parts):
         base = (me ^ k) * per
@@ -311,9 +322,6 @@
     cells = half_rows * half_cols
     piece = cells // parts
     span = 2 if patches > 1 else 1
-    position, patch = lax.axis_index("tm"), lax.axis_index("space")
-    here = patch % span
-    me = jnp.stack([position, position + parts * here, position % 2 + 2 * here]).astype(jnp.int32)
 
     snapshots, land_mask, taps_rows, taps_cols = (
         pltpu.with_memory_space_constraint(x, pltpu.HBM) for x in (snapshots, land_mask, taps_rows, taps_cols)
@@ -343,28 +351,29 @@
     pieces = pl.pallas_call(
         functools.partial(filter_kernel, parts),
         out_shape=[shape(piece, cols)] * parts,
-        in_specs=[scalars(), scalars(), scalars(), pl.BlockSpec(memory_space=pltpu.HBM), whole()],
+        in_specs=[scalars(), scalars(), pl.BlockSpec(memory_space=pltpu.HBM), whole()],
         out_specs=[whole()] * parts,
         scratch_shapes=[
             pltpu.VMEM((rows, grid_cols, cols), F32),
             pltpu.SemaphoreType.DMA((rows // CHUNK,)),
-            pltpu.VMEM((grid_cols, CHUNK), F32),
+            pltpu.VMEM((grid_cols, rows), F32),
+            pltpu.VMEM((rows, 2, half_cols, cols), F32),
             pltpu.VMEM((rows + 4, half_cols, cols), F32),
             pltpu.VMEM((cells, cols), F32),
         ],
         compiler_params=params(),
         cost_estimate=pl.CostEstimate(flops=0, bytes_accessed=4 * snapshots.size, transcendentals=0),
         name="filter",
-    )(me, taps_rows, taps_cols, snapshots, land_mask)
+    )(taps_rows, taps_cols, snapshots, land_mask)
     kept = pl.pallas_call(
         functools.partial(halo_kernel, parts),
         out_shape=[shape(piece, cols)] * parts,
-        in_specs=[scalars()] + [whole()] * (parts + 2),
+        in_specs=[whole()] * (parts + 2),
         out_specs=[whole()] * parts,
-        input_output_aliases={3 + k: k for k in range(parts)},
+        input_output_aliases={2 + k: k for k in range(parts)},
         compiler_params=params(),
         name="halo",
-    )(me, above, below, *pieces)
+    )(above, below, *pieces)
     theirs = {k: swap(kept[k + 1], "tm", 1) for k in range(0, parts, 2)}
     far = {0: kept[0], 1: theirs[0]}
     for k in range(2, parts, 2):
@@ -372,12 +381,11 @@
         far[k + 1] = swap(theirs[k], "tm", k)
 
     owners = 2 * span
-    size = 5 * cols // owners
-    send, keep = pl.pallas_call(
+    sums = pl.pallas_call(
         functools.partial(pair_kernel, parts, span),
-        out_shape=[shape(span, size, cols)] * 2,
-        in_specs=[scalars()] + [whole()] * (parts + 1),
-        out_specs=[whole()] * 2,
+        out_shape=[shape(5 * cols // owners, cols)] * owners,
+        in_specs=[whole()] * (parts + 1),
+        out_specs=[whole()] * owners,
         scratch_shapes=[
             pltpu.VMEM((cells // 2, 2 * cols), F32),
             pltpu.VMEM((cells // 2, cols), F32),
@@ -386,33 +394,34 @@
         compiler_params=params(),
         cost_estimate=pl.CostEstimate(flops=0, bytes_accessed=0, transcendentals=0),
         name="pair",
-    )(me, probes.reshape(cells, cols), *[kept[k] for k in range(0, parts, 2)], *[theirs[k] for k in range(0, parts, 2)])
-    got = swap(send, "tm", 1)
-    got, *waited = lax.optimization_barrier([got] + [far[k] for k in range(2, parts)])
-    far.update(zip(range(2, parts), waited))
-    pair_share = keep[0] + got[0]
-    for h in range(1, span):
-        pair_share = pair_share + swap(keep[h] + got[h], "space", h)
+    )(probes.reshape(cells, cols), *[kept[k] for k in range(0, parts, 2)], *[theirs[k] for k in range(0, parts, 2)])
+    got = [swap_both(sums[j], j % 2 + parts * (j // 2)) for j in range(1, owners)]
+    tied = lax.optimization_barrier(got + [far[k] for k in range(2, parts)])
+    got = tied[:owners - 1]
+    far.update(zip(range(2, parts), tied[owners - 1:]))
+    pair_share = sums[0]
+    for x in got:
+        pair_share = pair_share + x
+    bits = [1 << b for b in range(1, patches.bit_length() - 1)]
 
     blocks = len(cross_order(parts))
     owners = parts * span
     size = blocks * cols // owners
     send, keep, wide = pl.pallas_call(
-        functools.partial(cross_kernel, parts),
+        functools.partial(cross_kernel, parts, span),
         out_shape=[shape(owners // 2, size, cols)] * 2 + [shape(piece, parts * cols)],
-        in_specs=[scalars()] + [whole()] * parts,
+        in_specs=[whole()] * parts,
         out_specs=[whole()] * 3,
         scratch_shapes=[pltpu.VMEM((blocks * cols, cols), F32)],
         compiler_params=params(),
         cost_estimate=pl.CostEstimate(flops=0, bytes_accessed=0, transcendentals=0),
         name="cross",
-    )(me, *[far[k] for k in range(parts)])
+    )(*[far[k] for k in range(parts)])
     got = swap(send, "tm", 1)
     mine = keep[0] + got[0]
     for h in range(1, owners // 2):
         mine = mine + swap_both(keep[h] + got[h], 2 * h)
     mine = jnp.concatenate([pair_share, mine], axis=0)
-    bits = [1 << b for b in range(1, patches.bit_length() - 1)]
     for bit in bits:
         mine = mine + swap(mine, "space", bit)
     even = jnp.stack([mine] + [swap_both(mine, 2 * h) for h in range(1, owners // 2)])
@@ -422,7 +431,7 @@
     *sent, coefficients = pl.pallas_call(
         functools.partial(merge_kernel, parts, span),
         out_shape=[shape(width, piece)] * parts + [shape(width, cols)],
-        in_specs=[scalars()] + [whole()] * 3,
+        in_specs=[whole()] * 3,
         out_specs=[whole()] * (parts + 1),
         scratch_shapes=[
             pltpu.VMEM((parts // 2, 5 * cols, cols), F32),
@@ -432,17 +441,17 @@
         ],
         compiler_params=params(),
         name="merge",
-    )(me, even, odd, wide)
+    )(even, odd, wide)
     last = [sent[0]] + [swap(sent[k], "tm", k) for k in range(1, parts)]
 
     basis = pl.pallas_call(
         functools.partial(final_kernel, parts),
         out_shape=shape(half_rows, width, half_cols),
-        in_specs=[scalars()] + [whole()] * parts,
+        in_specs=[whole()] * parts,
         out_specs=whole(),
         compiler_params=params(),
         name="final",
-    )(me, *last)
+    )(*last)
     return basis.transpose(0, 2, 1), coefficients
 
 

time: 80.6 us -> 77.1 us (0.957)
  Pallas kernels: 24.8 us -> 19.6 us
  waiting for transfers between devices: 27.8 us -> 30.4 us
    ppermute x13 -> x11, starting transfers between devices: 13 us -> 9.41 us  [swap(): return lax.ppermute(x, axis, [(i, i ^ mask) for i in range(count)])]
    ppermute x6 -> x9, starting transfers between devices: 7.11 us -> 10.2 us  [swap_both(): return lax.ppermute(x, ('tm', 'space'), route)]
    ppermute x6 -> x9, waiting for transfers between devices: 7.38 us -> 9.82 us  [swap_both(): return lax.ppermute(x, ('tm', 'space'), route)]
    pallas_call x1, Pallas kernels: 13.3 us -> 11.6 us  [local(): pl.pallas_call(functools.partial(merge_kernel, parts, span), out_shape=[s...]
    pallas_call x1, Pallas kernels: 5.1 us -> 3.87 us  [local(): pl.pallas_call(functools.partial(filter_kernel, parts), out_shape=[shape(...]
    ppermute x13 -> x11, waiting for transfers between devices: 20.4 us -> 19.9 us  [swap(): return lax.ppermute(x, axis, [(i, i ^ mask) for i in range(count)])]
  transfers between devices with their start and end apart: 21 -> 22, of which waited for: 13 -> 16; matrix products, arithmetic and copies ran while one was open for 0% -> 0% of each run, Pallas kernels for 9% -> 7%
where the time goes in v9:
time: 77.1 us; the launch traced here: 76.8 us
  waiting for transfers between devices  30.4 us (39%)
  starting transfers between devices  25.9 us (34%)
  Pallas kernels  19.6 us (25%)
  between operations  0.79 us (1%)
    ppermute x11, waiting for transfers between devices, swap(): return lax.ppermute(x, axis, [(i, i ^ mask) for i in range(count)])  19.9 us
    pallas_call x1, Pallas kernels, local(): pl.pallas_call(functools.partial(merge_kernel, parts, span), out_shape=[s...  11.6 us
    ppermute x9, starting transfers between devices, swap_both(): return lax.ppermute(x, ('tm', 'space'), route)  10.2 us
    ppermute x9, waiting for transfers between devices, swap_both(): return lax.ppermute(x, ('tm', 'space'), route)  9.82 us
    ppermute x11, starting transfers between devices, swap(): return lax.ppermute(x, axis, [(i, i ^ mask) for i in range(count)])  9.41 us
    ppermute x1, starting transfers between devices, local(): above = lax.ppermute(to_below, 'space', up)  4.98 us
    pallas_call x1, Pallas kernels, local(): pl.pallas_call(functools.partial(filter_kernel, parts), out_shape=[shape(...  3.87 us
  transfers between devices with their start and end apart: 22, of which 16 were waited for; matrix products, arithmetic and copies ran while one was open for 0% of the time, Pallas kernels for 7%

profile of v9, /device:TPU:0, one launch (start us, length us, event | category | flops | bytes accessed | tf_op | source)
XLA Modules:
  0.0 76.8 jit_solution(5253884889406373456)
XLA Ops:
  0.6 1.2 %edge.1 = (f32[64,128]{1,0:T(8,128)S(1)}, f32[64,128]{1,0:T(8,128)S(1)}) custom-call(f32[6]{0:T(128)} %rtaps_ref.3, f32[6]{0:T(128)} %ctaps_ref.3, f32[64,128,128]{2,1,0:T(8,128)} %snap_hbm.1, f32[64,128,128]{2,1,0:T(8,128)} %snap_hbm.1, s32[64,128]{1,0:T(8,128)} %mask_ref.1, s32[64,128]{1,0:T(8,128)} %mask_ref.1), custom_call_target="tpu_custom_call" | custom-call | tf_op jit(solution)/shard_map/edge/pallas_call | solution.py:331
  1.9 5.0 %collective-permute-start = (f32[64,128]{1,0:T(8,128)S(1)}, f32[64,128]{1,0:T(8,128)S(1)}, u32[]{:S(2)}, u32[]{:S(2)}) collective-permute-start(f32[64,128]{1,0:T(8,128)S(1)} %get-tuple-element.29), channel_id=1, source_target_pairs={{0,1},{1,2},{2,3},{3,4},{4,5},{5,6},{6,7},{8,9},{9,10},{10,11},{11... | collective-permute-start | bytes 98312 | tf_op jit(solution)/shard_map/ppermute | solution.py:348
  6.9 1.3 %collective-permute-start.1 = (f32[64,128]{1,0:T(8,128)S(1)}, f32[64,128]{1,0:T(8,128)S(1)}, u32[]{:S(2)}, u32[]{:S(2)}) collective-permute-start(f32[64,128]{1,0:T(8,128)S(1)} %get-tuple-element.30), channel_id=1, source_target_pairs={{1,0},{2,1},{3,2},{4,3},{5,4},{6,5},{7,6},{9,8},{10,9},{11,10},{12... | collective-permute-start | bytes 98312 | tf_op jit(solution)/shard_map/ppermute | solution.py:349
  8.2 3.9 %filter.1 = (f32[512,128]{1,0:T(8,128)S(1)}, f32[512,128]{1,0:T(8,128)S(1)}, f32[512,128]{1,0:T(8,128)S(1)}, f32[512,128]{1,0:T(8,128)S(1)}) custom-call(f32[6]{0:T(128)} %rtaps_ref.3, f32[6]{0:T(128)} %ctaps_ref.3, f32[64,128,128]{2,1,0:T(8,128)} %snap_hbm.1, s32[64,128]{1,0:T(8,128)} %mask_ref.1), custom_call_target="tpu_custom_call" | custom-call | bytes 4194304 | tf_op jit(solution)/shard_map/filter/pallas_call | solution.py:351
  13.4 1.5 %collective-permute-start.7 = (f32[512,128]{1,0:T(8,128)S(1)}, f32[512,128]{1,0:T(8,128)S(1)}, u32[]{:S(2)}, u32[]{:S(2)}) collective-permute-start(f32[512,128]{1,0:T(8,128)S(1)} %get-tuple-element.36.refs_1_), channel_id=1, source_target_pairs={{0,16},{8,24},{16,0},{24,8},{1,17},{9,25},{17,1},{25,9},{2,18},{10... | collective-permute-start | bytes 786440 | tf_op jit(solution)/shard_map/ppermute | solution.py:32
  17.3 2.5 %collective-permute-start.5 = (f32[160,128]{1,0:T(8,128)S(1)}, f32[160,128]{1,0:T(8,128)S(1)}, u32[]{:S(2)}, u32[]{:S(2)}) collective-permute-start(f32[160,128]{1,0:T(8,128)S(1)} %get-tuple-element.41), channel_id=1, source_target_pairs={{0,1},{1,0},{2,3},{3,2},{4,5},{5,4},{6,7},{7,6},{8,9},{9,8},{10,11... | collective-permute-start | bytes 245768 | tf_op jit(solution)/shard_map/ppermute | solution.py:42
  19.9 2.7 %collective-permute-done.7.refs_2_ = f32[512,128]{1,0:T(8,128)S(1)} collective-permute-done((f32[512,128]{1,0:T(8,128)S(1)}, f32[512,128]{1,0:T(8,128)S(1)}, u32[]{:S(2)}, u32[]{:S(2)}) %collective-permute-start.7) | collective-permute-done | bytes 262176 | tf_op jit(solution)/shard_map/ppermute | solution.py:32
  22.9 1.5 %collective-permute-done.6 = f32[160,128]{1,0:T(8,128)S(1)} collective-permute-done((f32[160,128]{1,0:T(8,128)S(1)}, f32[160,128]{1,0:T(8,128)S(1)}, u32[]{:S(2)}, u32[]{:S(2)}) %collective-permute-start.6) | collective-permute-done | bytes 81952 | tf_op jit(solution)/shard_map/ppermute | solution.py:42
  24.3 3.0 %collective-permute-done.8.refs_3_ = f32[512,128]{1,0:T(8,128)S(1)} collective-permute-done((f32[512,128]{1,0:T(8,128)S(1)}, f32[512,128]{1,0:T(8,128)S(1)}, u32[]{:S(2)}, u32[]{:S(2)}) %collective-permute-start.8) | collective-permute-done | bytes 262176 | tf_op jit(solution)/shard_map/ppermute | solution.py:32
  28.1 1.3 %collective-permute-done.9 = f32[4,64,128]{2,1,0:T(8,128)S(1)} collective-permute-done((f32[4,64,128]{2,1,0:T(8,128)S(1)}, f32[4,64,128]{2,1,0:T(8,128)S(1)}, u32[]{:S(2)}, u32[]{:S(2)}) %collective-permute-start.9) | collective-permute-done | bytes 131104 | tf_op jit(solution)/shard_map/ppermute | solution.py:32
  29.4 1.6 %collective-permute-start.10 = (f32[64,128]{1,0:T(8,128)S(1)}, f32[64,128]{1,0:T(8,128)S(1)}, u32[]{:S(2)}, u32[]{:S(2)}) collective-permute-start(f32[64,128]{1,0:T(8,128)S(1)} %get-tuple-element.56), channel_id=1, source_target_pairs={{0,16},{1,17},{2,18},{3,19},{4,20},{5,21},{6,22},{7,23},{8,24},{9,... | collective-permute-start | bytes 98312 | tf_op jit(solution)/shard_map/ppermute | solution.py:42
  31.0 2.4 %collective-permute-start.12 = (f32[64,128]{1,0:T(8,128)S(1)}, f32[64,128]{1,0:T(8,128)S(1)}, u32[]{:S(2)}, u32[]{:S(2)}) collective-permute-start(f32[64,128]{1,0:T(8,128)S(1)} %get-tuple-element.57), channel_id=1, source_target_pairs={{0,17},{1,16},{2,19},{3,18},{4,21},{5,20},{6,23},{7,22},{8,25},{9,... | collective-permute-start | bytes 98312 | tf_op jit(solution)/shard_map/ppermute | solution.py:42
  33.5 2.3 %collective-permute-done.12 = f32[64,128]{1,0:T(8,128)S(1)} collective-permute-done((f32[64,128]{1,0:T(8,128)S(1)}, f32[64,128]{1,0:T(8,128)S(1)}, u32[]{:S(2)}, u32[]{:S(2)}) %collective-permute-start.12) | collective-permute-done | bytes 32800 | tf_op jit(solution)/shard_map/ppermute | solution.py:42
  35.8 1.5 %collective-permute-done.11 = f32[64,128]{1,0:T(8,128)S(1)} collective-permute-done((f32[64,128]{1,0:T(8,128)S(1)}, f32[64,128]{1,0:T(8,128)S(1)}, u32[]{:S(2)}, u32[]{:S(2)}) %collective-permute-start.11) | collective-permute-done | bytes 32800 | tf_op jit(solution)/shard_map/ppermute | solution.py:42
  37.3 1.6 %collective-permute-start.13 = (f32[224,128]{1,0:T(8,128)S(1)}, f32[224,128]{1,0:T(8,128)S(1)}, u32[]{:S(2)}, u32[]{:S(2)}) collective-permute-start(f32[224,128]{1,0:T(8,128)S(1)} %pad_maximum_fusion.1), channel_id=1, source_target_pairs={{0,2},{1,3},{2,0},{3,1},{4,6},{5,7},{6,4},{7,5},{8,10},{9,11},{10,... | collective-permute-start | bytes 344072 | tf_op jit(solution)/shard_map/ppermute | solution.py:32
  39.0 3.2 %collective-permute-done.13 = f32[224,128]{1,0:T(8,128)S(1)} collective-permute-done((f32[224,128]{1,0:T(8,128)S(1)}, f32[224,128]{1,0:T(8,128)S(1)}, u32[]{:S(2)}, u32[]{:S(2)}) %collective-permute-start.13) | collective-permute-done | bytes 114720 | tf_op jit(solution)/shard_map/ppermute | solution.py:32
  42.2 2.7 %collective-permute-start.14 = (f32[224,128]{1,0:T(8,128)S(1)}, f32[224,128]{1,0:T(8,128)S(1)}, u32[]{:S(2)}, u32[]{:S(2)}) collective-permute-start(f32[224,128]{1,0:T(8,128)S(1)} %fusion.7), channel_id=1, source_target_pairs={{0,4},{1,5},{2,6},{3,7},{4,0},{5,1},{6,2},{7,3},{8,12},{9,13},{10,... | collective-permute-start | bytes 344072 | tf_op jit(solution)/shard_map/ppermute | solution.py:32
  44.9 4.3 %collective-permute-done.14 = f32[224,128]{1,0:T(8,128)S(1)} collective-permute-done((f32[224,128]{1,0:T(8,128)S(1)}, f32[224,128]{1,0:T(8,128)S(1)}, u32[]{:S(2)}, u32[]{:S(2)}) %collective-permute-start.14) | collective-permute-done | bytes 114720 | tf_op jit(solution)/shard_map/ppermute | solution.py:32
  49.7 2.6 %collective-permute-start.16 = (f32[224,128]{1,0:T(8,128)S(1)}, f32[224,128]{1,0:T(8,128)S(1)}, u32[]{:S(2)}, u32[]{:S(2)}) collective-permute-start(f32[224,128]{1,0:T(8,128)S(1)} %add.63), channel_id=1, source_target_pairs={{0,1},{1,0},{2,3},{3,2},{4,5},{5,4},{6,7},{7,6},{8,9},{9,8},{10,11... | collective-permute-start | bytes 344072 | tf_op jit(solution)/shard_map/ppermute | solution.py:42
  52.8 2.2 %collective-permute-done.17 = f32[224,128]{1,0:T(8,128)S(1)} collective-permute-done((f32[224,128]{1,0:T(8,128)S(1)}, f32[224,128]{1,0:T(8,128)S(1)}, u32[]{:S(2)}, u32[]{:S(2)}) %collective-permute-start.17) | collective-permute-done | bytes 114720 | tf_op jit(solution)/shard_map/ppermute | solution.py:42
  55.0 1.3 %collective-permute-done.16 = f32[224,128]{1,0:T(8,128)S(1)} collective-permute-done((f32[224,128]{1,0:T(8,128)S(1)}, f32[224,128]{1,0:T(8,128)S(1)}, u32[]{:S(2)}, u32[]{:S(2)}) %collective-permute-start.16) | collective-permute-done | bytes 114720 | tf_op jit(solution)/shard_map/ppermute | solution.py:42
  57.2 1.8 %collective-permute-done.18.odd_ref = f32[4,224,128]{2,1,0:T(8,128)S(1)} collective-permute-done((f32[4,224,128]{2,1,0:T(8,128)S(1)}, f32[4,224,128]{2,1,0:T(8,128)S(1)}, u32[]{:S(2)}, u32[]{:S(2)}) %collective-permute-start.18) | collective-permute-done | bytes 458784 | tf_op jit(solution)/shard_map/ppermute | solution.py:32
  59.0 11.6 %merge.1 = (f32[32,512]{1,0:T(8,128)S(1)}, f32[32,512]{1,0:T(8,128)S(1)}, f32[32,512]{1,0:T(8,128)S(1)}, f32[32,512]{1,0:T(8,128)S(1)}, f32[32,128]{1,0:T(8,128)}) custom-call(f32[4,224,128]{2,1,0:T(8,128)S(1)} %pad_maximum_fusion.even_ref, f32[4,224,128]{2,1,0:T(8,128)S(1)} %collective-permute-done.18.odd_ref, f32[512,512]{1,0:T(8,128)S(1)} %get-tuple-element.50.wide_ref), custom_call_target="tpu_custom_call" | custom-call | tf_op jit(solution)/shard_map/merge/pallas_call | solution.py:431
  72.4 3.2 %collective-permute-done.20.refs_2_ = f32[32,512]{1,0:T(8,128)S(1)} collective-permute-done((f32[32,512]{1,0:T(8,128)S(1)}, f32[32,512]{1,0:T(8,128)S(1)}, u32[]{:S(2)}, u32[]{:S(2)}) %collective-permute-start.20) | collective-permute-done | bytes 65568 | tf_op jit(solution)/shard_map/ppermute | solution.py:32
  (36 shorter events, 9.9 us)
Async XLA Ops:
  1.9 14.1 %copy-start = (f32[32,64,128]{2,1,0:T(8,128)S(1)}, f32[32,64,128]{2,1,0:T(8,128)}, u32[]{:S(2)}) copy-start(f32[32,64,128]{2,1,0:T(8,128)} %param.9) | copy-start | bytes 3145732
  1.9 10.2 %collective-permute-start = (f32[64,128]{1,0:T(8,128)S(1)}, f32[64,128]{1,0:T(8,128)S(1)}, u32[]{:S(2)}, u32[]{:S(2)}) collective-permute-start(f32[64,128]{1,0:T(8,128)S(1)} %get-tuple-element.29), channel_id=1, source_target_pairs={{0,1},{1,2},{2,3},{3,4},{4,5},{5,6},{6,7},{8,9},{9,10},{10,11},{11... | collective-permute-start | bytes 98312 | tf_op jit(solution)/shard_map/ppermute | solution.py:348
  6.9 5.8 %collective-permute-start.1 = (f32[64,128]{1,0:T(8,128)S(1)}, f32[64,128]{1,0:T(8,128)S(1)}, u32[]{:S(2)}, u32[]{:S(2)}) collective-permute-start(f32[64,128]{1,0:T(8,128)S(1)} %get-tuple-element.30), channel_id=1, source_target_pairs={{1,0},{2,1},{3,2},{4,3},{5,4},{6,5},{7,6},{9,8},{10,9},{11,10},{12... | collective-permute-start | bytes 98312 | tf_op jit(solution)/shard_map/ppermute | solution.py:349
  12.9 2.1 %collective-permute-start.3 = (f32[512,128]{1,0:T(8,128)S(1)}, f32[512,128]{1,0:T(8,128)S(1)}, u32[]{:S(2)}, u32[]{:S(2)}) collective-permute-start(f32[512,128]{1,0:T(8,128)S(1)} %get-tuple-element.38), channel_id=1, source_target_pairs={{0,8},{8,0},{16,24},{24,16},{1,9},{9,1},{17,25},{25,17},{2,10},{10... | collective-permute-start | bytes 786440 | tf_op jit(solution)/shard_map/ppermute | solution.py:32
  12.9 3.0 %collective-permute-start.2 = (f32[512,128]{1,0:T(8,128)S(1)}, f32[512,128]{1,0:T(8,128)S(1)}, u32[]{:S(2)}, u32[]{:S(2)}) collective-permute-start(f32[512,128]{1,0:T(8,128)S(1)} %get-tuple-element.37), channel_id=1, source_target_pairs={{0,8},{8,0},{16,24},{24,16},{1,9},{9,1},{17,25},{25,17},{2,10},{10... | collective-permute-start | bytes 786440 | tf_op jit(solution)/shard_map/ppermute | solution.py:32
  13.4 9.2 %collective-permute-start.7 = (f32[512,128]{1,0:T(8,128)S(1)}, f32[512,128]{1,0:T(8,128)S(1)}, u32[]{:S(2)}, u32[]{:S(2)}) collective-permute-start(f32[512,128]{1,0:T(8,128)S(1)} %get-tuple-element.36.refs_1_), channel_id=1, source_target_pairs={{0,16},{8,24},{16,0},{24,8},{1,17},{9,25},{17,1},{25,9},{2,18},{10... | collective-permute-start | bytes 786440 | tf_op jit(solution)/shard_map/ppermute | solution.py:32
  15.0 12.4 %collective-permute-start.8 = (f32[512,128]{1,0:T(8,128)S(1)}, f32[512,128]{1,0:T(8,128)S(1)}, u32[]{:S(2)}, u32[]{:S(2)}) collective-permute-start(f32[512,128]{1,0:T(8,128)S(1)} %collective-permute-done.3.refs_3_), channel_id=1, source_target_pairs={{0,16},{8,24},{16,0},{24,8},{1,17},{9,25},{17,1},{25,9},{2,18},{10... | collective-permute-start | bytes 786440 | tf_op jit(solution)/shard_map/ppermute | solution.py:32
  17.2 5.4 %collective-permute-start.4 = (f32[160,128]{1,0:T(8,128)S(1)}, f32[160,128]{1,0:T(8,128)S(1)}, u32[]{:S(2)}, u32[]{:S(2)}) collective-permute-start(f32[160,128]{1,0:T(8,128)S(1)} %get-tuple-element.40), channel_id=1, source_target_pairs={{0,8},{1,9},{2,10},{3,11},{4,12},{5,13},{6,14},{7,15},{8,0},{9,1},... | collective-permute-start | bytes 245768 | tf_op jit(solution)/shard_map/ppermute | solution.py:42
  17.3 5.6 %collective-permute-start.5 = (f32[160,128]{1,0:T(8,128)S(1)}, f32[160,128]{1,0:T(8,128)S(1)}, u32[]{:S(2)}, u32[]{:S(2)}) collective-permute-start(f32[160,128]{1,0:T(8,128)S(1)} %get-tuple-element.41), channel_id=1, source_target_pairs={{0,1},{1,0},{2,3},{3,2},{4,5},{5,4},{6,7},{7,6},{8,9},{9,8},{10,11... | collective-permute-start | bytes 245768 | tf_op jit(solution)/shard_map/ppermute | solution.py:42
  19.8 4.5 %collective-permute-start.6 = (f32[160,128]{1,0:T(8,128)S(1)}, f32[160,128]{1,0:T(8,128)S(1)}, u32[]{:S(2)}, u32[]{:S(2)}) collective-permute-start(f32[160,128]{1,0:T(8,128)S(1)} %get-tuple-element.42), channel_id=1, source_target_pairs={{0,9},{1,8},{2,11},{3,10},{4,13},{5,12},{6,15},{7,14},{8,1},{9,0},... | collective-permute-start | bytes 245768 | tf_op jit(solution)/shard_map/ppermute | solution.py:42
  28.0 1.4 %collective-permute-start.9 = (f32[4,64,128]{2,1,0:T(8,128)S(1)}, f32[4,64,128]{2,1,0:T(8,128)S(1)}, u32[]{:S(2)}, u32[]{:S(2)}) collective-permute-start(f32[4,64,128]{2,1,0:T(8,128)S(1)} %get-tuple-element.49), channel_id=1, source_target_pairs={{0,8},{8,0},{16,24},{24,16},{1,9},{9,1},{17,25},{25,17},{2,10},{10... | collective-permute-start | bytes 393224 | tf_op jit(solution)/shard_map/ppermute | solution.py:32
  29.4 4.1 %collective-permute-start.10 = (f32[64,128]{1,0:T(8,128)S(1)}, f32[64,128]{1,0:T(8,128)S(1)}, u32[]{:S(2)}, u32[]{:S(2)}) collective-permute-start(f32[64,128]{1,0:T(8,128)S(1)} %get-tuple-element.56), channel_id=1, source_target_pairs={{0,16},{1,17},{2,18},{3,19},{4,20},{5,21},{6,22},{7,23},{8,24},{9,... | collective-permute-start | bytes 98312 | tf_op jit(solution)/shard_map/ppermute | solution.py:42
  31.0 4.8 %collective-permute-start.12 = (f32[64,128]{1,0:T(8,128)S(1)}, f32[64,128]{1,0:T(8,128)S(1)}, u32[]{:S(2)}, u32[]{:S(2)}) collective-permute-start(f32[64,128]{1,0:T(8,128)S(1)} %get-tuple-element.57), channel_id=1, source_target_pairs={{0,17},{1,16},{2,19},{3,18},{4,21},{5,20},{6,23},{7,22},{8,25},{9,... | collective-permute-start | bytes 98312 | tf_op jit(solution)/shard_map/ppermute | solution.py:42
  33.4 3.9 %collective-permute-start.11 = (f32[64,128]{1,0:T(8,128)S(1)}, f32[64,128]{1,0:T(8,128)S(1)}, u32[]{:S(2)}, u32[]{:S(2)}) collective-permute-start(f32[64,128]{1,0:T(8,128)S(1)} %get-tuple-element.58), channel_id=1, source_target_pairs={{0,1},{1,0},{2,3},{3,2},{4,5},{5,4},{6,7},{7,6},{8,9},{9,8},{10,11... | collective-permute-start | bytes 98312 | tf_op jit(solution)/shard_map/ppermute | solution.py:42
  37.3 4.9 %collective-permute-start.13 = (f32[224,128]{1,0:T(8,128)S(1)}, f32[224,128]{1,0:T(8,128)S(1)}, u32[]{:S(2)}, u32[]{:S(2)}) collective-permute-start(f32[224,128]{1,0:T(8,128)S(1)} %pad_maximum_fusion.1), channel_id=1, source_target_pairs={{0,2},{1,3},{2,0},{3,1},{4,6},{5,7},{6,4},{7,5},{8,10},{9,11},{10,... | collective-permute-start | bytes 344072 | tf_op jit(solution)/shard_map/ppermute | solution.py:32
  42.2 7.0 %collective-permute-start.14 = (f32[224,128]{1,0:T(8,128)S(1)}, f32[224,128]{1,0:T(8,128)S(1)}, u32[]{:S(2)}, u32[]{:S(2)}) collective-permute-start(f32[224,128]{1,0:T(8,128)S(1)} %fusion.7), channel_id=1, source_target_pairs={{0,4},{1,5},{2,6},{3,7},{4,0},{5,1},{6,2},{7,3},{8,12},{9,13},{10,... | collective-permute-start | bytes 344072 | tf_op jit(solution)/shard_map/ppermute | solution.py:32
  49.2 5.8 %collective-permute-start.17 = (f32[224,128]{1,0:T(8,128)S(1)}, f32[224,128]{1,0:T(8,128)S(1)}, u32[]{:S(2)}, u32[]{:S(2)}) collective-permute-start(f32[224,128]{1,0:T(8,128)S(1)} %add.63), channel_id=1, source_target_pairs={{0,17},{1,16},{2,19},{3,18},{4,21},{5,20},{6,23},{7,22},{8,25},{9,... | collective-permute-start | bytes 344072 | tf_op jit(solution)/shard_map/ppermute | solution.py:42
  49.7 6.6 %collective-permute-start.16 = (f32[224,128]{1,0:T(8,128)S(1)}, f32[224,128]{1,0:T(8,128)S(1)}, u32[]{:S(2)}, u32[]{:S(2)}) collective-permute-start(f32[224,128]{1,0:T(8,128)S(1)} %add.63), channel_id=1, source_target_pairs={{0,1},{1,0},{2,3},{3,2},{4,5},{5,4},{6,7},{7,6},{8,9},{9,8},{10,11... | collective-permute-start | bytes 344072 | tf_op jit(solution)/shard_map/ppermute | solution.py:42
  52.3 4.8 %collective-permute-start.15 = (f32[224,128]{1,0:T(8,128)S(1)}, f32[224,128]{1,0:T(8,128)S(1)}, u32[]{:S(2)}, u32[]{:S(2)}) collective-permute-start(f32[224,128]{1,0:T(8,128)S(1)} %add.63), channel_id=1, source_target_pairs={{0,16},{1,17},{2,18},{3,19},{4,20},{5,21},{6,22},{7,23},{8,24},{9,... | collective-permute-start | bytes 344072 | tf_op jit(solution)/shard_map/ppermute | solution.py:42
  57.1 1.9 %collective-permute-start.18 = (f32[4,224,128]{2,1,0:T(8,128)S(1)}, f32[4,224,128]{2,1,0:T(8,128)S(1)}, u32[]{:S(2)}, u32[]{:S(2)}) collective-permute-start(f32[4,224,128]{2,1,0:T(8,128)S(1)} %pad_maximum_fusion.even_ref), channel_id=1, source_target_pairs={{0,8},{8,0},{16,24},{24,16},{1,9},{9,1},{17,25},{25,17},{2,10},{10... | collective-permute-start | bytes 1376264 | tf_op jit(solution)/shard_map/ppermute | solution.py:32
  70.6 1.9 %collective-permute-start.19 = (f32[32,512]{1,0:T(8,128)S(1)}, f32[32,512]{1,0:T(8,128)S(1)}, u32[]{:S(2)}, u32[]{:S(2)}) collective-permute-start(f32[32,512]{1,0:T(8,128)S(1)} %get-tuple-element.52), channel_id=1, source_target_pairs={{0,8},{8,0},{16,24},{24,16},{1,9},{9,1},{17,25},{25,17},{2,10},{10... | collective-permute-start | bytes 196616 | tf_op jit(solution)/shard_map/ppermute | solution.py:32
  70.7 4.9 %collective-permute-start.20 = (f32[32,512]{1,0:T(8,128)S(1)}, f32[32,512]{1,0:T(8,128)S(1)}, u32[]{:S(2)}, u32[]{:S(2)}) collective-permute-start(f32[32,512]{1,0:T(8,128)S(1)} %get-tuple-element.53), channel_id=1, source_target_pairs={{0,16},{8,24},{16,0},{24,8},{1,17},{9,25},{17,1},{25,9},{2,18},{10... | collective-permute-start | bytes 196616 | tf_op jit(solution)/shard_map/ppermute | solution.py:32
  71.4 4.5 %collective-permute-start.21 = (f32[32,512]{1,0:T(8,128)S(1)}, f32[32,512]{1,0:T(8,128)S(1)}, u32[]{:S(2)}, u32[]{:S(2)}) collective-permute-start(f32[32,512]{1,0:T(8,128)S(1)} %get-tuple-element.54), channel_id=1, source_target_pairs={{0,24},{8,16},{16,8},{24,0},{1,25},{9,17},{17,9},{25,1},{2,26},{10... | collective-permute-start | bytes 196616 | tf_op jit(solution)/shard_map/ppermute | solution.py:32

commit v10 on v9

--- a/solution.py
+++ b/solution.py
@@ -10,7 +10,7 @@
 SIGN_STEPS = 8
 TAPS = 6
 CHUNK = 8
-ROW_BLOCKS = 2
+ROW_BLOCKS = 1
 F32 = jnp.float32
 VMEM_LIMIT = 48 * 1024 * 1024
 
@@ -65,15 +65,20 @@
     return shift_rows(before, 1) + here + shift_rows(after, -1)
 
 
-def edge_kernel(rtaps_ref, ctaps_ref, first_ref, last_ref, mask_first_ref, mask_last_ref, up_ref, down_ref, mask_t):
+def edge_kernel(rtaps_ref, ctaps_ref, first_ref, last_ref, mask_first_ref, mask_last_ref, near_ref, far_ref, mask_t):
     ctaps = [ctaps_ref[k] for k in range(TAPS)]
-    for out, snaps, mask_ref, taps, at in (
-        (up_ref, first_ref, mask_first_ref, (rtaps_ref[4], rtaps_ref[5]), 0),
-        (down_ref, last_ref, mask_last_ref, (rtaps_ref[0], rtaps_ref[1]), CHUNK - 2),
+    even = lax.axis_index("space") % 2 == 0
+    shares = []
+    for snaps, mask_ref, taps, at in (
+        (first_ref, mask_first_ref, (rtaps_ref[4], rtaps_ref[5]), 0),
+        (last_ref, mask_last_ref, (rtaps_ref[0], rtaps_ref[1]), CHUNK - 2),
     ):
         masks = mask_columns(mask_ref[...], mask_t)
         rows = [narrowed_row(snaps, x, [m[:, at + x:at + x + 1] for m in masks], ctaps) for x in range(2)]
-        out[...] = taps[0] * rows[0] + taps[1] * rows[1]
+        shares.append(taps[0] * rows[0] + taps[1] * rows[1])
+    up, down = shares
+    near_ref[...] = jnp.where(even, down, up)
+    far_ref[...] = jnp.where(even, up, down)
 
 
 def filter_kernel(parts, rtaps_ref, ctaps_ref, snap_hbm, mask_ref, *rest):
@@ -119,20 +124,23 @@
         pieces[k][...] = filtered[pl.ds(pl.multiple_of((me ^ k) * size, 8), size), :]
 
 
-def halo_kernel(parts, above_ref, below_ref, *refs):
+def halo_kernel(parts, near_ref, far_ref, *refs):
     outs = refs[len(refs) // 2:]
     me = lax.axis_index("tm")
-    cells = above_ref.shape[0]
+    cells = near_ref.shape[0]
+    even = lax.axis_index("space") % 2 == 0
+    above = jnp.where(even, far_ref[...], near_ref[...])
+    below = jnp.where(even, near_ref[...], far_ref[...])
     for k, out in enumerate(outs):
         out[...] = refs[k][...]
 
         @pl.when((me ^ k) == 0)
         def _():
-            out[:cells, :] = out[:cells, :] + above_ref[...]
+            out[:cells, :] = out[:cells, :] + above
 
         @pl.when((me ^ k) == parts - 1)
         def _():
-            out[-cells:, :] = out[-cells:, :] + below_ref[...]
+            out[-cells:, :] = out[-cells:, :] + below
 
 
 def cross_order(parts):
@@ -178,12 +186,15 @@
 
 
 def cross_kernel(parts, span, *refs):
-    pieces, (send_ref, keep_ref, wide, flat) = refs[:parts], refs[parts:]
+    pieces, (send_ref, keep_ref, high_ref, low_ref, wide, flat) = refs[:parts], refs[parts:]
     me, owner = positions(parts, span)
     cols = pieces[0].shape[1]
     for k in range(parts):
         wide[:, pl.ds(pl.multiple_of((me ^ k) * cols, cols), cols)] = pieces[k][...]
     sides = [split(wide[:, a * cols:(a + 2) * cols]) for a in range(0, parts, 2)]
+    for at, (high, low) in enumerate(sides):
+        high_ref[:, 2 * at * cols:2 * (at + 1) * cols] = high
+        low_ref[:, 2 * at * cols:2 * (at + 1) * cols] = low
     where = {ab: j for j, ab in enumerate(cross_order(parts))}
     for a in range(0, parts, 2):
         for b in range(a + 2, parts, 2):
@@ -242,8 +253,8 @@
     return combines
 
 
-def merge_kernel(parts, span, even_ref, odd_ref, wide_ref, *refs):
-    outs, (coef_ref, pairs, cross, weight, turned) = refs[:parts], refs[parts:]
+def merge_kernel(parts, span, even_ref, odd_ref, high_ref, low_ref, *refs):
+    outs, (weight_ref, product_ref, pairs, cross, turned) = refs[:parts], refs[parts:]
     me, owner = positions(parts, span)
     cols = even_ref.shape[2]
     pair_share, cross_share = pairs.shape[1] // (2 * span), cross.shape[0] // (parts * span)
@@ -258,7 +269,7 @@
     for p in range(parts // 2):
         for j, ab in enumerate(((2 * p, 2 * p), (2 * p, 2 * p + 1), (2 * p + 1, 2 * p + 1))):
             blocks[ab] = pairs[p, j * cols:(j + 1) * cols, :]
-    products = jnp.concatenate([pairs[p, 3 * cols:, :] for p in range(parts // 2)], axis=0)
+        product_ref[2 * p * cols:2 * (p + 1) * cols, :] = pairs[p, 3 * cols:, :]
     weights, count = None, parts
     while count > 1:
         grams = []
@@ -290,15 +301,17 @@
                     right = split_dot(cross, combines[q])
                     merged[p, q] = split_dot(combines[p], right, ((0,), (0,)))
         blocks, count = merged, count // 2
-    weight[...] = weights[0]
-    total = dot_parts(split(wide_ref[...]), split(weight[...]))
+    weight_ref[...] = weights[0]
     width = cols // parts
-    rows = total.shape[0]
-    turned[:, :rows] = total.T
-    turned[:, rows:] = split_dot(weight[...], products, ((0,), (0,)))
+    turned[...] = dot_parts((high_ref[...], low_ref[...]), split(weights[0])).T
     for k in range(parts):
-        outs[k][...] = turned[pl.ds(pl.multiple_of((me ^ k) * width, 8), width), :rows]
-    coef_ref[...] = turned[pl.ds(pl.multiple_of(me * width, 8), width), rows:]
+        outs[k][...] = turned[pl.ds(pl.multiple_of((me ^ k) * width, 8), width), :]
+
+
+def coefficient_kernel(parts, weight_ref, product_ref, coef_ref, held):
+    held[...] = split_dot(weight_ref[...], product_ref[...], ((0,), (0,)))
+    width = coef_ref.shape[0]
+    coef_ref[...] = held[pl.ds(pl.multiple_of(lax.axis_index("tm") * width, 8), width), :]
 
 
 def final_kernel(parts, *refs):
@@ -328,7 +341,7 @@
     )
 
     row_block, mask_block = (2, grid_cols, cols), (CHUNK, grid_cols)
-    to_above, to_below = pl.pallas_call(
+    to_near, to_far = pl.pallas_call(
         edge_kernel,
         out_shape=[shape(half_cols, cols)] * 2,
         grid=(1,),
@@ -344,9 +357,9 @@
         compiler_params=params(),
         name="edge",
     )(taps_rows, taps_cols, snapshots, snapshots, land_mask, land_mask)
-    up = [(i, i + 1) for i in range(patches - 1)]
-    above = lax.ppermute(to_below, "space", up)
-    below = lax.ppermute(to_above, "space", [(j, i) for i, j in up])
+    near = lax.ppermute(to_near, "space", [(i, i ^ 1) for i in range(patches) if i ^ 1 < patches])
+    pairs = [(i, i + 1) for i in range(1, patches - 1, 2)]
+    other = lax.ppermute(to_far, "space", pairs + [(j, i) for i, j in pairs])
 
     pieces = pl.pallas_call(
         functools.partial(filter_kernel, parts),
@@ -373,7 +386,7 @@
         input_output_aliases={2 + k: k for k in range(parts)},
         compiler_params=params(),
         name="halo",
-    )(above, below, *pieces)
+    )(near, other, *pieces)
     theirs = {k: swap(kept[k + 1], "tm", 1) for k in range(0, parts, 2)}
     far = {0: kept[0], 1: theirs[0]}
     for k in range(2, parts, 2):
@@ -407,12 +420,13 @@
     blocks = len(cross_order(parts))
     owners = parts * span
     size = blocks * cols // owners
-    send, keep, wide = pl.pallas_call(
+    factors = jax.ShapeDtypeStruct((piece, parts * cols), jnp.bfloat16)
+    send, keep, high, low = pl.pallas_call(
         functools.partial(cross_kernel, parts, span),
-        out_shape=[shape(owners // 2, size, cols)] * 2 + [shape(piece, parts * cols)],
+        out_shape=[shape(owners // 2, size, cols)] * 2 + [factors] * 2,
         in_specs=[whole()] * parts,
-        out_specs=[whole()] * 3,
-        scratch_shapes=[pltpu.VMEM((blocks * cols, cols), F32)],
+        out_specs=[whole()] * 4,
+        scratch_shapes=[pltpu.VMEM((piece, parts * cols), F32), pltpu.VMEM((blocks * cols, cols), F32)],
         compiler_params=params(),
         cost_estimate=pl.CostEstimate(flops=0, bytes_accessed=0, transcendentals=0),
         name="cross",
@@ -421,27 +435,40 @@
     mine = keep[0] + got[0]
     for h in range(1, owners // 2):
         mine = mine + swap_both(keep[h] + got[h], 2 * h)
+    for bit in bits[:1]:
+        pair_share = pair_share + swap(pair_share, "space", bit)
+    mine, pair_share = lax.optimization_barrier((mine, pair_share))
+    for bit in bits[:1]:
+        mine = mine + swap(mine, "space", bit)
     mine = jnp.concatenate([pair_share, mine], axis=0)
-    for bit in bits:
+    for bit in bits[1:]:
         mine = mine + swap(mine, "space", bit)
     even = jnp.stack([mine] + [swap_both(mine, 2 * h) for h in range(1, owners // 2)])
     odd = swap(even, "tm", 1)
 
     width = cols // parts
-    *sent, coefficients = pl.pallas_call(
+    *sent, weight, products = pl.pallas_call(
         functools.partial(merge_kernel, parts, span),
-        out_shape=[shape(width, piece)] * parts + [shape(width, cols)],
-        in_specs=[whole()] * 3,
-        out_specs=[whole()] * (parts + 1),
+        out_shape=[shape(width, piece)] * parts + [shape(parts * cols, cols)] * 2,
+        in_specs=[whole()] * 4,
+        out_specs=[whole()] * (parts + 2),
         scratch_shapes=[
             pltpu.VMEM((parts // 2, 5 * cols, cols), F32),
             pltpu.VMEM((blocks * cols, cols), F32),
-            pltpu.VMEM((parts * cols, cols), F32),
-            pltpu.VMEM((cols, piece + cols), F32),
+            pltpu.VMEM((cols, piece), F32),
         ],
         compiler_params=params(),
         name="merge",
-    )(even, odd, wide)
+    )(even, odd, high, low)
+    coefficients = pl.pallas_call(
+        functools.partial(coefficient_kernel, parts),
+        out_shape=shape(width, cols),
+        in_specs=[whole()] * 2,
+        out_specs=whole(),
+        scratch_shapes=[pltpu.VMEM((cols, cols), F32)],
+        compiler_params=params(),
+        name="coefficients",
+    )(weight, products)
     last = [sent[0]] + [swap(sent[k], "tm", k) for k in range(1, parts)]
 
     basis = pl.pallas_call(

time: 77.1 us -> 75.7 us (0.982)
  waiting for transfers between devices: 30.4 us -> 25.5 us
  starting transfers between devices: 25.9 us -> 28 us
  Pallas kernels: 19.6 us -> 21.1 us
    ppermute x11 -> x12, waiting for transfers between devices: 19.9 us -> 13.8 us  [swap(): return lax.ppermute(x, axis, [(i, i ^ mask) for i in range(count)])]
    ppermute x11 -> x12, starting transfers between devices: 9.41 us -> 12.6 us  [swap(): return lax.ppermute(x, axis, [(i, i ^ mask) for i in range(count)])]
    ppermute x2, starting transfers between devices: 6.27 us -> 3.65 us  [the longest x1 3 us: local(): lax.ppermute(to_near, 'space', [(i, i ^ 1) for i in range(patches) if i ^...]
    ppermute x9, waiting for transfers between devices: 9.82 us -> 11.7 us  [swap_both(): return lax.ppermute(x, ('tm', 'space'), route)]
    ppermute x9, starting transfers between devices: 10.2 us -> 11.8 us  [swap_both(): return lax.ppermute(x, ('tm', 'space'), route)]
    pallas_call x0 -> x1, Pallas kernels: none -> 0.92 us  [local(): pl.pallas_call(functools.partial(coefficient_kernel, parts), out_shape=sh...]
  transfers between devices with their start and end apart: 22 -> 23, of which waited for: 16 -> 15; matrix products, arithmetic and copies ran while one was open for 0% -> 0% of each run, Pallas kernels for 7% -> 8%
where the time goes in v10:
time: 75.7 us; the launch traced here: 75.5 us
  starting transfers between devices  28 us (37%)
  waiting for transfers between devices  25.5 us (34%)
  Pallas kernels  21.1 us (28%)
  between operations  0.79 us (1%)
    ppermute x12, waiting for transfers between devices, swap(): return lax.ppermute(x, axis, [(i, i ^ mask) for i in range(count)])  13.8 us
    ppermute x12, starting transfers between devices, swap(): return lax.ppermute(x, axis, [(i, i ^ mask) for i in range(count)])  12.6 us
    pallas_call x1, Pallas kernels, local(): pl.pallas_call(functools.partial(merge_kernel, parts, span), out_shape=[s...  12.1 us
    ppermute x9, starting transfers between devices, swap_both(): return lax.ppermute(x, ('tm', 'space'), route)  11.8 us
    ppermute x9, waiting for transfers between devices, swap_both(): return lax.ppermute(x, ('tm', 'space'), route)  11.7 us
    pallas_call x1, Pallas kernels, local(): pl.pallas_call(functools.partial(filter_kernel, parts), out_shape=[shape(...  3.87 us
    ppermute x1, starting transfers between devices, local(): lax.ppermute(to_near, 'space', [(i, i ^ 1) for i in range(patches) if i ^...  3 us
  transfers between devices with their start and end apart: 23, of which 15 were waited for; matrix products, arithmetic and copies ran while one was open for 0% of the time, Pallas kernels for 8%

profile of v10, /device:TPU:0, one launch (start us, length us, event | category | flops | bytes accessed | tf_op | source)
XLA Modules:
  0.0 75.5 jit_solution(3513162264002383963)
XLA Ops:
  0.6 1.2 %edge.1 = (f32[64,128]{1,0:T(8,128)S(1)}, f32[64,128]{1,0:T(8,128)S(1)}) custom-call(f32[6]{0:T(128)} %rtaps_ref.3, f32[6]{0:T(128)} %ctaps_ref.3, f32[64,128,128]{2,1,0:T(8,128)} %snap_hbm.1, f32[64,128,128]{2,1,0:T(8,128)} %snap_hbm.1, s32[64,128]{1,0:T(8,128)} %mask_ref.1, s32[64,128]{1,0:T(8,128)} %mask_ref.1), custom_call_target="tpu_custom_call" | custom-call | tf_op jit(solution)/shard_map/edge/pallas_call | solution.py:344
  1.9 3.0 %collective-permute-start = (f32[64,128]{1,0:T(8,128)S(1)}, f32[64,128]{1,0:T(8,128)S(1)}, u32[]{:S(2)}, u32[]{:S(2)}) collective-permute-start(f32[64,128]{1,0:T(8,128)S(1)} %get-tuple-element.33), channel_id=1, source_target_pairs={{0,1},{1,0},{2,3},{3,2},{4,5},{5,4},{6,7},{7,6},{8,9},{9,8},{10,11... | collective-permute-start | bytes 98312 | tf_op jit(solution)/shard_map/ppermute | solution.py:360
  5.6 3.9 %filter.1 = (f32[512,128]{1,0:T(8,128)S(1)}, f32[512,128]{1,0:T(8,128)S(1)}, f32[512,128]{1,0:T(8,128)S(1)}, f32[512,128]{1,0:T(8,128)S(1)}) custom-call(f32[6]{0:T(128)} %rtaps_ref.3, f32[6]{0:T(128)} %ctaps_ref.3, f32[64,128,128]{2,1,0:T(8,128)} %snap_hbm.1, s32[64,128]{1,0:T(8,128)} %mask_ref.1), custom_call_target="tpu_custom_call" | custom-call | bytes 4194304 | tf_op jit(solution)/shard_map/filter/pallas_call | solution.py:364
  10.2 1.5 %collective-permute-start.7 = (f32[512,128]{1,0:T(8,128)S(1)}, f32[512,128]{1,0:T(8,128)S(1)}, u32[]{:S(2)}, u32[]{:S(2)}) collective-permute-start(f32[512,128]{1,0:T(8,128)S(1)} %get-tuple-element.41.refs_1_), channel_id=1, source_target_pairs={{0,16},{8,24},{16,0},{24,8},{1,17},{9,25},{17,1},{25,9},{2,18},{10... | collective-permute-start | bytes 786440 | tf_op jit(solution)/shard_map/ppermute | solution.py:32
  12.8 1.2 %pair.1 = (f32[160,128]{1,0:T(8,128)S(1)}, f32[160,128]{1,0:T(8,128)S(1)}, f32[160,128]{1,0:T(8,128)S(1)}, f32[160,128]{1,0:T(8,128)S(1)}) custom-call(f32[2048,128]{1,0:T(8,128)S(1)} %bitcast.20, f32[512,128]{1,0:T(8,128)S(1)} %get-tuple-element.39.refs_0_, f32[512,128]{1,0:T(8,128)S(1)} %get-tuple-element.41.refs_1_, ...), custom_call_target="tpu_custom_call" | custom-call | tf_op jit(solution)/shard_map/pair/pallas_call | solution.py:397
  14.1 4.3 %collective-permute-start.5 = (f32[160,128]{1,0:T(8,128)S(1)}, f32[160,128]{1,0:T(8,128)S(1)}, u32[]{:S(2)}, u32[]{:S(2)}) collective-permute-start(f32[160,128]{1,0:T(8,128)S(1)} %get-tuple-element.44), channel_id=1, source_target_pairs={{0,1},{1,0},{2,3},{3,2},{4,5},{5,4},{6,7},{7,6},{8,9},{9,8},{10,11... | collective-permute-start | bytes 245768 | tf_op jit(solution)/shard_map/ppermute | solution.py:42
  19.4 2.1 %collective-permute-done.5 = f32[160,128]{1,0:T(8,128)S(1)} collective-permute-done((f32[160,128]{1,0:T(8,128)S(1)}, f32[160,128]{1,0:T(8,128)S(1)}, u32[]{:S(2)}, u32[]{:S(2)}) %collective-permute-start.5) | collective-permute-done | bytes 81952 | tf_op jit(solution)/shard_map/ppermute | solution.py:42
  21.5 1.5 %collective-permute-done.6 = f32[160,128]{1,0:T(8,128)S(1)} collective-permute-done((f32[160,128]{1,0:T(8,128)S(1)}, f32[160,128]{1,0:T(8,128)S(1)}, u32[]{:S(2)}, u32[]{:S(2)}) %collective-permute-start.6) | collective-permute-done | bytes 81952 | tf_op jit(solution)/shard_map/ppermute | solution.py:42
  22.9 1.2 %collective-permute-done.8.refs_3_ = f32[512,128]{1,0:T(8,128)S(1)} collective-permute-done((f32[512,128]{1,0:T(8,128)S(1)}, f32[512,128]{1,0:T(8,128)S(1)}, u32[]{:S(2)}, u32[]{:S(2)}) %collective-permute-start.8) | collective-permute-done | bytes 262176 | tf_op jit(solution)/shard_map/ppermute | solution.py:32
  24.9 3.8 %collective-permute-start.13 = (f32[160,128]{1,0:T(8,128)S(1)}, f32[160,128]{1,0:T(8,128)S(1)}, u32[]{:S(2)}, u32[]{:S(2)}) collective-permute-start(f32[160,128]{1,0:T(8,128)S(1)} %add_add_fusion), channel_id=1, source_target_pairs={{0,2},{1,3},{2,0},{3,1},{4,6},{5,7},{6,4},{7,5},{8,10},{9,11},{10,... | collective-permute-start | bytes 245768 | tf_op jit(solution)/shard_map/ppermute | solution.py:32
  28.7 1.6 %collective-permute-start.10 = (f32[64,128]{1,0:T(8,128)S(1)}, f32[64,128]{1,0:T(8,128)S(1)}, u32[]{:S(2)}, u32[]{:S(2)}) collective-permute-start(f32[64,128]{1,0:T(8,128)S(1)} %get-tuple-element.64), channel_id=1, source_target_pairs={{0,16},{1,17},{2,18},{3,19},{4,20},{5,21},{6,22},{7,23},{8,24},{9,... | collective-permute-start | bytes 98312 | tf_op jit(solution)/shard_map/ppermute | solution.py:42
  30.3 2.1 %collective-permute-start.12 = (f32[64,128]{1,0:T(8,128)S(1)}, f32[64,128]{1,0:T(8,128)S(1)}, u32[]{:S(2)}, u32[]{:S(2)}) collective-permute-start(f32[64,128]{1,0:T(8,128)S(1)} %get-tuple-element.65), channel_id=1, source_target_pairs={{0,17},{1,16},{2,19},{3,18},{4,21},{5,20},{6,23},{7,22},{8,25},{9,... | collective-permute-start | bytes 98312 | tf_op jit(solution)/shard_map/ppermute | solution.py:42
  32.7 2.4 %collective-permute-done.12 = f32[64,128]{1,0:T(8,128)S(1)} collective-permute-done((f32[64,128]{1,0:T(8,128)S(1)}, f32[64,128]{1,0:T(8,128)S(1)}, u32[]{:S(2)}, u32[]{:S(2)}) %collective-permute-start.12) | collective-permute-done | bytes 32800 | tf_op jit(solution)/shard_map/ppermute | solution.py:42
  36.3 1.3 %collective-permute-start.14 = (f32[64,128]{1,0:T(8,128)S(1)}, f32[64,128]{1,0:T(8,128)S(1)}, u32[]{:S(2)}, u32[]{:S(2)}) collective-permute-start(f32[64,128]{1,0:T(8,128)S(1)} %fusion.6), channel_id=1, source_target_pairs={{0,2},{1,3},{2,0},{3,1},{4,6},{5,7},{6,4},{7,5},{8,10},{9,11},{10,... | collective-permute-start | bytes 98312 | tf_op jit(solution)/shard_map/ppermute | solution.py:32
  37.6 2.7 %collective-permute-done.14 = f32[64,128]{1,0:T(8,128)S(1)} collective-permute-done((f32[64,128]{1,0:T(8,128)S(1)}, f32[64,128]{1,0:T(8,128)S(1)}, u32[]{:S(2)}, u32[]{:S(2)}) %collective-permute-start.14) | collective-permute-done | bytes 32800 | tf_op jit(solution)/shard_map/ppermute | solution.py:32
  40.3 2.3 %collective-permute-start.15 = (f32[224,128]{1,0:T(8,128)S(1)}, f32[224,128]{1,0:T(8,128)S(1)}, u32[]{:S(2)}, u32[]{:S(2)}) collective-permute-start(f32[224,128]{1,0:T(8,128)S(1)} %pad_maximum_fusion.1), channel_id=1, source_target_pairs={{0,4},{1,5},{2,6},{3,7},{4,0},{5,1},{6,2},{7,3},{8,12},{9,13},{10,... | collective-permute-start | bytes 344072 | tf_op jit(solution)/shard_map/ppermute | solution.py:32
  42.6 4.7 %collective-permute-done.15 = f32[224,128]{1,0:T(8,128)S(1)} collective-permute-done((f32[224,128]{1,0:T(8,128)S(1)}, f32[224,128]{1,0:T(8,128)S(1)}, u32[]{:S(2)}, u32[]{:S(2)}) %collective-permute-start.15) | collective-permute-done | bytes 114720 | tf_op jit(solution)/shard_map/ppermute | solution.py:32
  47.3 1.4 %collective-permute-start.18 = (f32[224,128]{1,0:T(8,128)S(1)}, f32[224,128]{1,0:T(8,128)S(1)}, u32[]{:S(2)}, u32[]{:S(2)}) collective-permute-start(f32[224,128]{1,0:T(8,128)S(1)} %fusion.7), channel_id=1, source_target_pairs={{0,17},{1,16},{2,19},{3,18},{4,21},{5,20},{6,23},{7,22},{8,25},{9,... | collective-permute-start | bytes 344072 | tf_op jit(solution)/shard_map/ppermute | solution.py:42
  48.7 1.7 %collective-permute-start.17 = (f32[224,128]{1,0:T(8,128)S(1)}, f32[224,128]{1,0:T(8,128)S(1)}, u32[]{:S(2)}, u32[]{:S(2)}) collective-permute-start(f32[224,128]{1,0:T(8,128)S(1)} %fusion.7), channel_id=1, source_target_pairs={{0,1},{1,0},{2,3},{3,2},{4,5},{5,4},{6,7},{7,6},{8,9},{9,8},{10,11... | collective-permute-start | bytes 344072 | tf_op jit(solution)/shard_map/ppermute | solution.py:42
  50.9 2.2 %collective-permute-done.18 = f32[224,128]{1,0:T(8,128)S(1)} collective-permute-done((f32[224,128]{1,0:T(8,128)S(1)}, f32[224,128]{1,0:T(8,128)S(1)}, u32[]{:S(2)}, u32[]{:S(2)}) %collective-permute-start.18) | collective-permute-done | bytes 114720 | tf_op jit(solution)/shard_map/ppermute | solution.py:42
  53.1 1.3 %collective-permute-done.17 = f32[224,128]{1,0:T(8,128)S(1)} collective-permute-done((f32[224,128]{1,0:T(8,128)S(1)}, f32[224,128]{1,0:T(8,128)S(1)}, u32[]{:S(2)}, u32[]{:S(2)}) %collective-permute-start.17) | collective-permute-done | bytes 114720 | tf_op jit(solution)/shard_map/ppermute | solution.py:42
  55.3 1.8 %collective-permute-done.19.odd_ref = f32[4,224,128]{2,1,0:T(8,128)S(1)} collective-permute-done((f32[4,224,128]{2,1,0:T(8,128)S(1)}, f32[4,224,128]{2,1,0:T(8,128)S(1)}, u32[]{:S(2)}, u32[]{:S(2)}) %collective-permute-start.19) | collective-permute-done | bytes 458784 | tf_op jit(solution)/shard_map/ppermute | solution.py:32
  57.1 12.1 %merge.1 = (f32[32,512]{1,0:T(8,128)S(1)}, f32[32,512]{1,0:T(8,128)S(1)}, f32[32,512]{1,0:T(8,128)S(1)}, f32[32,512]{1,0:T(8,128)S(1)}, f32[512,128]{1,0:T(8,128)S(1)}, /*index=5*/f32[512,128]{1,0:T(8,128)S(1)}) custom-call(f32[4,224,128]{2,1,0:T(8,128)S(1)} %pad_maximum_fusion.even_ref, f32[4,224,128]{2,1,0:T(8,128)S(1)} %collective-permute-done.19.odd_ref, ...), custom_call_target="tpu_custom_call" | custom-call | tf_op jit(solution)/shard_map/merge/pallas_call | solution.py:450
  72.0 2.3 %collective-permute-done.21.refs_2_ = f32[32,512]{1,0:T(8,128)S(1)} collective-permute-done((f32[32,512]{1,0:T(8,128)S(1)}, f32[32,512]{1,0:T(8,128)S(1)}, u32[]{:S(2)}, u32[]{:S(2)}) %collective-permute-start.21) | collective-permute-done | bytes 65568 | tf_op jit(solution)/shard_map/ppermute | solution.py:32
  (40 shorter events, 11.2 us)
Async XLA Ops:
  1.9 10.9 %copy-start = (f32[32,64,128]{2,1,0:T(8,128)S(1)}, f32[32,64,128]{2,1,0:T(8,128)}, u32[]{:S(2)}) copy-start(f32[32,64,128]{2,1,0:T(8,128)} %param.9) | copy-start | bytes 3145732
  1.9 7.5 %collective-permute-start = (f32[64,128]{1,0:T(8,128)S(1)}, f32[64,128]{1,0:T(8,128)S(1)}, u32[]{:S(2)}, u32[]{:S(2)}) collective-permute-start(f32[64,128]{1,0:T(8,128)S(1)} %get-tuple-element.33), channel_id=1, source_target_pairs={{0,1},{1,0},{2,3},{3,2},{4,5},{5,4},{6,7},{7,6},{8,9},{9,8},{10,11... | collective-permute-start | bytes 98312 | tf_op jit(solution)/shard_map/ppermute | solution.py:360
  4.9 4.5 %collective-permute-start.1 = (f32[64,128]{1,0:T(8,128)S(1)}, f32[64,128]{1,0:T(8,128)S(1)}, u32[]{:S(2)}, u32[]{:S(2)}) collective-permute-start(f32[64,128]{1,0:T(8,128)S(1)} %get-tuple-element.34), channel_id=1, source_target_pairs={{1,2},{3,4},{5,6},{2,1},{4,3},{6,5},{9,10},{11,12},{13,14},{10,9},... | collective-permute-start | bytes 98312 | tf_op jit(solution)/shard_map/ppermute | solution.py:362
  9.6 2.1 %collective-permute-start.3 = (f32[512,128]{1,0:T(8,128)S(1)}, f32[512,128]{1,0:T(8,128)S(1)}, u32[]{:S(2)}, u32[]{:S(2)}) collective-permute-start(f32[512,128]{1,0:T(8,128)S(1)} %get-tuple-element.42), channel_id=1, source_target_pairs={{0,8},{8,0},{16,24},{24,16},{1,9},{9,1},{17,25},{25,17},{2,10},{10... | collective-permute-start | bytes 786440 | tf_op jit(solution)/shard_map/ppermute | solution.py:32
  9.7 3.0 %collective-permute-start.2 = (f32[512,128]{1,0:T(8,128)S(1)}, f32[512,128]{1,0:T(8,128)S(1)}, u32[]{:S(2)}, u32[]{:S(2)}) collective-permute-start(f32[512,128]{1,0:T(8,128)S(1)} %get-tuple-element.40), channel_id=1, source_target_pairs={{0,8},{8,0},{16,24},{24,16},{1,9},{9,1},{17,25},{25,17},{2,10},{10... | collective-permute-start | bytes 786440 | tf_op jit(solution)/shard_map/ppermute | solution.py:32
  10.2 9.2 %collective-permute-start.7 = (f32[512,128]{1,0:T(8,128)S(1)}, f32[512,128]{1,0:T(8,128)S(1)}, u32[]{:S(2)}, u32[]{:S(2)}) collective-permute-start(f32[512,128]{1,0:T(8,128)S(1)} %get-tuple-element.41.refs_1_), channel_id=1, source_target_pairs={{0,16},{8,24},{16,0},{24,8},{1,17},{9,25},{17,1},{25,9},{2,18},{10... | collective-permute-start | bytes 786440 | tf_op jit(solution)/shard_map/ppermute | solution.py:32
  11.7 12.4 %collective-permute-start.8 = (f32[512,128]{1,0:T(8,128)S(1)}, f32[512,128]{1,0:T(8,128)S(1)}, u32[]{:S(2)}, u32[]{:S(2)}) collective-permute-start(f32[512,128]{1,0:T(8,128)S(1)} %collective-permute-done.3.refs_3_), channel_id=1, source_target_pairs={{0,16},{8,24},{16,0},{24,8},{1,17},{9,25},{17,1},{25,9},{2,18},{10... | collective-permute-start | bytes 786440 | tf_op jit(solution)/shard_map/ppermute | solution.py:32
  14.0 5.4 %collective-permute-start.4 = (f32[160,128]{1,0:T(8,128)S(1)}, f32[160,128]{1,0:T(8,128)S(1)}, u32[]{:S(2)}, u32[]{:S(2)}) collective-permute-start(f32[160,128]{1,0:T(8,128)S(1)} %get-tuple-element.43), channel_id=1, source_target_pairs={{0,8},{1,9},{2,10},{3,11},{4,12},{5,13},{6,14},{7,15},{8,0},{9,1},... | collective-permute-start | bytes 245768 | tf_op jit(solution)/shard_map/ppermute | solution.py:42
  14.1 7.4 %collective-permute-start.5 = (f32[160,128]{1,0:T(8,128)S(1)}, f32[160,128]{1,0:T(8,128)S(1)}, u32[]{:S(2)}, u32[]{:S(2)}) collective-permute-start(f32[160,128]{1,0:T(8,128)S(1)} %get-tuple-element.44), channel_id=1, source_target_pairs={{0,1},{1,0},{2,3},{3,2},{4,5},{5,4},{6,7},{7,6},{8,9},{9,8},{10,11... | collective-permute-start | bytes 245768 | tf_op jit(solution)/shard_map/ppermute | solution.py:42
  18.4 4.5 %collective-permute-start.6 = (f32[160,128]{1,0:T(8,128)S(1)}, f32[160,128]{1,0:T(8,128)S(1)}, u32[]{:S(2)}, u32[]{:S(2)}) collective-permute-start(f32[160,128]{1,0:T(8,128)S(1)} %get-tuple-element.45), channel_id=1, source_target_pairs={{0,9},{1,8},{2,11},{3,10},{4,13},{5,12},{6,15},{7,14},{8,1},{9,0},... | collective-permute-start | bytes 245768 | tf_op jit(solution)/shard_map/ppermute | solution.py:42
  24.8 3.9 %collective-permute-start.9 = (f32[4,64,128]{2,1,0:T(8,128)S(1)}, f32[4,64,128]{2,1,0:T(8,128)S(1)}, u32[]{:S(2)}, u32[]{:S(2)}) collective-permute-start(f32[4,64,128]{2,1,0:T(8,128)S(1)} %get-tuple-element.49), channel_id=1, source_target_pairs={{0,8},{8,0},{16,24},{24,16},{1,9},{9,1},{17,25},{25,17},{2,10},{10... | collective-permute-start | bytes 393224 | tf_op jit(solution)/shard_map/ppermute | solution.py:32
  24.9 7.5 %collective-permute-start.13 = (f32[160,128]{1,0:T(8,128)S(1)}, f32[160,128]{1,0:T(8,128)S(1)}, u32[]{:S(2)}, u32[]{:S(2)}) collective-permute-start(f32[160,128]{1,0:T(8,128)S(1)} %add_add_fusion), channel_id=1, source_target_pairs={{0,2},{1,3},{2,0},{3,1},{4,6},{5,7},{6,4},{7,5},{8,10},{9,11},{10,... | collective-permute-start | bytes 245768 | tf_op jit(solution)/shard_map/ppermute | solution.py:32
  28.7 4.0 %collective-permute-start.10 = (f32[64,128]{1,0:T(8,128)S(1)}, f32[64,128]{1,0:T(8,128)S(1)}, u32[]{:S(2)}, u32[]{:S(2)}) collective-permute-start(f32[64,128]{1,0:T(8,128)S(1)} %get-tuple-element.64), channel_id=1, source_target_pairs={{0,16},{1,17},{2,18},{3,19},{4,20},{5,21},{6,22},{7,23},{8,24},{9,... | collective-permute-start | bytes 98312 | tf_op jit(solution)/shard_map/ppermute | solution.py:42
  30.3 4.8 %collective-permute-start.12 = (f32[64,128]{1,0:T(8,128)S(1)}, f32[64,128]{1,0:T(8,128)S(1)}, u32[]{:S(2)}, u32[]{:S(2)}) collective-permute-start(f32[64,128]{1,0:T(8,128)S(1)} %get-tuple-element.65), channel_id=1, source_target_pairs={{0,17},{1,16},{2,19},{3,18},{4,21},{5,20},{6,23},{7,22},{8,25},{9,... | collective-permute-start | bytes 98312 | tf_op jit(solution)/shard_map/ppermute | solution.py:42
  32.4 3.9 %collective-permute-start.11 = (f32[64,128]{1,0:T(8,128)S(1)}, f32[64,128]{1,0:T(8,128)S(1)}, u32[]{:S(2)}, u32[]{:S(2)}) collective-permute-start(f32[64,128]{1,0:T(8,128)S(1)} %get-tuple-element.66), channel_id=1, source_target_pairs={{0,1},{1,0},{2,3},{3,2},{4,5},{5,4},{6,7},{7,6},{8,9},{9,8},{10,11... | collective-permute-start | bytes 98312 | tf_op jit(solution)/shard_map/ppermute | solution.py:42
  36.3 4.0 %collective-permute-start.14 = (f32[64,128]{1,0:T(8,128)S(1)}, f32[64,128]{1,0:T(8,128)S(1)}, u32[]{:S(2)}, u32[]{:S(2)}) collective-permute-start(f32[64,128]{1,0:T(8,128)S(1)} %fusion.6), channel_id=1, source_target_pairs={{0,2},{1,3},{2,0},{3,1},{4,6},{5,7},{6,4},{7,5},{8,10},{9,11},{10,... | collective-permute-start | bytes 98312 | tf_op jit(solution)/shard_map/ppermute | solution.py:32
  40.3 7.0 %collective-permute-start.15 = (f32[224,128]{1,0:T(8,128)S(1)}, f32[224,128]{1,0:T(8,128)S(1)}, u32[]{:S(2)}, u32[]{:S(2)}) collective-permute-start(f32[224,128]{1,0:T(8,128)S(1)} %pad_maximum_fusion.1), channel_id=1, source_target_pairs={{0,4},{1,5},{2,6},{3,7},{4,0},{5,1},{6,2},{7,3},{8,12},{9,13},{10,... | collective-permute-start | bytes 344072 | tf_op jit(solution)/shard_map/ppermute | solution.py:32
  47.3 5.8 %collective-permute-start.18 = (f32[224,128]{1,0:T(8,128)S(1)}, f32[224,128]{1,0:T(8,128)S(1)}, u32[]{:S(2)}, u32[]{:S(2)}) collective-permute-start(f32[224,128]{1,0:T(8,128)S(1)} %fusion.7), channel_id=1, source_target_pairs={{0,17},{1,16},{2,19},{3,18},{4,21},{5,20},{6,23},{7,22},{8,25},{9,... | collective-permute-start | bytes 344072 | tf_op jit(solution)/shard_map/ppermute | solution.py:42
  48.7 5.7 %collective-permute-start.17 = (f32[224,128]{1,0:T(8,128)S(1)}, f32[224,128]{1,0:T(8,128)S(1)}, u32[]{:S(2)}, u32[]{:S(2)}) collective-permute-start(f32[224,128]{1,0:T(8,128)S(1)} %fusion.7), channel_id=1, source_target_pairs={{0,1},{1,0},{2,3},{3,2},{4,5},{5,4},{6,7},{7,6},{8,9},{9,8},{10,11... | collective-permute-start | bytes 344072 | tf_op jit(solution)/shard_map/ppermute | solution.py:42
  50.4 4.8 %collective-permute-start.16 = (f32[224,128]{1,0:T(8,128)S(1)}, f32[224,128]{1,0:T(8,128)S(1)}, u32[]{:S(2)}, u32[]{:S(2)}) collective-permute-start(f32[224,128]{1,0:T(8,128)S(1)} %fusion.7), channel_id=1, source_target_pairs={{0,16},{1,17},{2,18},{3,19},{4,20},{5,21},{6,22},{7,23},{8,24},{9,... | collective-permute-start | bytes 344072 | tf_op jit(solution)/shard_map/ppermute | solution.py:42
  55.2 1.9 %collective-permute-start.19 = (f32[4,224,128]{2,1,0:T(8,128)S(1)}, f32[4,224,128]{2,1,0:T(8,128)S(1)}, u32[]{:S(2)}, u32[]{:S(2)}) collective-permute-start(f32[4,224,128]{2,1,0:T(8,128)S(1)} %pad_maximum_fusion.even_ref), channel_id=1, source_target_pairs={{0,8},{8,0},{16,24},{24,16},{1,9},{9,1},{17,25},{25,17},{2,10},{10... | collective-permute-start | bytes 1376264 | tf_op jit(solution)/shard_map/ppermute | solution.py:32
  69.2 2.8 %collective-permute-start.20 = (f32[32,512]{1,0:T(8,128)S(1)}, f32[32,512]{1,0:T(8,128)S(1)}, u32[]{:S(2)}, u32[]{:S(2)}) collective-permute-start(f32[32,512]{1,0:T(8,128)S(1)} %get-tuple-element.59), channel_id=1, source_target_pairs={{0,8},{8,0},{16,24},{24,16},{1,9},{9,1},{17,25},{25,17},{2,10},{10... | collective-permute-start | bytes 196616 | tf_op jit(solution)/shard_map/ppermute | solution.py:32
  69.4 4.9 %collective-permute-start.21 = (f32[32,512]{1,0:T(8,128)S(1)}, f32[32,512]{1,0:T(8,128)S(1)}, u32[]{:S(2)}, u32[]{:S(2)}) collective-permute-start(f32[32,512]{1,0:T(8,128)S(1)} %get-tuple-element.60), channel_id=1, source_target_pairs={{0,16},{8,24},{16,0},{24,8},{1,17},{9,25},{17,1},{25,9},{2,18},{10... | collective-permute-start | bytes 196616 | tf_op jit(solution)/shard_map/ppermute | solution.py:32
  70.1 4.5 %collective-permute-start.22 = (f32[32,512]{1,0:T(8,128)S(1)}, f32[32,512]{1,0:T(8,128)S(1)}, u32[]{:S(2)}, u32[]{:S(2)}) collective-permute-start(f32[32,512]{1,0:T(8,128)S(1)} %get-tuple-element.61), channel_id=1, source_target_pairs={{0,24},{8,16},{16,8},{24,0},{1,25},{9,17},{17,9},{25,1},{2,26},{10... | collective-permute-start | bytes 196616 | tf_op jit(solution)/shard_map/ppermute | solution.py:32

commit v11 on v10

--- a/solution.py
+++ b/solution.py
@@ -10,7 +10,7 @@
 SIGN_STEPS = 8
 TAPS = 6
 CHUNK = 8
-ROW_BLOCKS = 1
+ROW_BLOCKS = 2
 F32 = jnp.float32
 VMEM_LIMIT = 48 * 1024 * 1024
 
@@ -145,6 +145,14 @@
 
 def cross_order(parts):
     return [(a, b) for p in range(0, parts, 2) for q in range(p + 2, parts, 2) for a in (p, p + 1) for b in (q, q + 1)]
+
+
+def triangle(size):
+    return tuple(lax.broadcasted_iota(jnp.int32, (size, size), axis) for axis in range(2))
+
+
+def pair_rows(cols, owners):
+    return 4 * cols + 8 * owners
 
 
 def pair_kernel(parts, span, probes_ref, *refs):
@@ -163,10 +171,13 @@
         there[at, :] = probes_ref[pl.ds(pl.multiple_of((me ^ 2 * h) * size, 8), size), :]
     left = split(wide[...])
     gram = dot_parts(left, left, ((0,), (0,)))
-    flat[:cols, :] = gram[:cols, :cols]
-    flat[cols:2 * cols, :] = gram[:cols, cols:]
-    flat[2 * cols:3 * cols, :] = gram[cols:, cols:]
-    flat[3 * cols:, :] = dot_parts(left, split(there[...]), ((0,), (0,)))
+    first, second = gram[:cols, :cols], gram[cols:, cols:]
+    row, col = triangle(cols)
+    flat[:cols, :] = gram[:cols, cols:]
+    flat[cols:2 * cols, :] = jnp.where(row <= col, first, second)
+    flat[2 * cols:4 * cols, :] = dot_parts(left, split(there[...]), ((0,), (0,)))
+    diagonal = jnp.sum(jnp.where(row == col, second, 0.0), axis=0, keepdims=True)
+    flat[4 * cols:, :] = jnp.broadcast_to(diagonal, (flat.shape[0] - 4 * cols, cols))
     share = flat.shape[0] // owners
     for k, out in enumerate(outs):
         out[...] = flat[pl.ds(pl.multiple_of((owner ^ k) * share, 8), share), :]
@@ -266,10 +277,15 @@
         pairs[(there % parts) // 2, at, :] = source[:pair_share, :]
         cross[pl.ds(pl.multiple_of(there * cross_share, 8), cross_share), :] = source[pair_share:, :]
     blocks = {ab: cross[j * cols:(j + 1) * cols, :] for j, ab in enumerate(cross_order(parts))}
+    row, col = triangle(cols)
     for p in range(parts // 2):
-        for j, ab in enumerate(((2 * p, 2 * p), (2 * p, 2 * p + 1), (2 * p + 1, 2 * p + 1))):
-            blocks[ab] = pairs[p, j * cols:(j + 1) * cols, :]
-        product_ref[2 * p * cols:2 * (p + 1) * cols, :] = pairs[p, 3 * cols:, :]
+        packed = pairs[p, cols:2 * cols, :]
+        turned_back = packed.T
+        blocks[2 * p, 2 * p] = jnp.where(row <= col, packed, turned_back)
+        blocks[2 * p, 2 * p + 1] = pairs[p, :cols, :]
+        second = jnp.where(row > col, packed, turned_back)
+        blocks[2 * p + 1, 2 * p + 1] = jnp.where(row == col, pairs[p, 4 * cols:4 * cols + 1, :], second)
+        product_ref[2 * p * cols:2 * (p + 1) * cols, :] = pairs[p, 2 * cols:4 * cols, :]
     weights, count = None, parts
     while count > 1:
         grams = []
@@ -396,13 +412,13 @@
     owners = 2 * span
     sums = pl.pallas_call(
         functools.partial(pair_kernel, parts, span),
-        out_shape=[shape(5 * cols // owners, cols)] * owners,
+        out_shape=[shape(pair_rows(cols, owners) // owners, cols)] * owners,
         in_specs=[whole()] * (parts + 1),
         out_specs=[whole()] * owners,
         scratch_shapes=[
             pltpu.VMEM((cells // 2, 2 * cols), F32),
             pltpu.VMEM((cells // 2, cols), F32),
-            pltpu.VMEM((5 * cols, cols), F32),
+            pltpu.VMEM((pair_rows(cols, owners), cols), F32),
         ],
         compiler_params=params(),
         cost_estimate=pl.CostEstimate(flops=0, bytes_accessed=0, transcendentals=0),
@@ -453,7 +469,7 @@
         in_specs=[whole()] * 4,
         out_specs=[whole()] * (parts + 2),
         scratch_shapes=[
-            pltpu.VMEM((parts // 2, 5 * cols, cols), F32),
+            pltpu.VMEM((parts // 2, pair_rows(cols, 2 * span), cols), F32),
             pltpu.VMEM((blocks * cols, cols), F32),
             pltpu.VMEM((cols, piece), F32),
         ],

time: 75.7 us -> 74.4 us (0.983)
  Pallas kernels: 21.1 us -> 20.3 us
    pallas_call x1, Pallas kernels: 12.1 us -> 11.3 us  [local(): pl.pallas_call(functools.partial(merge_kernel, parts, span), out_shape=[s...]
where the time goes in v11:
time: 74.4 us; the launch traced here: 74.2 us
  starting transfers between devices  28 us (38%)
  waiting for transfers between devices  25 us (34%)
  Pallas kernels  20.3 us (27%)
  between operations  0.77 us (1%)
    ppermute x12, waiting for transfers between devices, swap(): return lax.ppermute(x, axis, [(i, i ^ mask) for i in range(count)])  13.9 us
    ppermute x12, starting transfers between devices, swap(): return lax.ppermute(x, axis, [(i, i ^ mask) for i in range(count)])  12.6 us
    ppermute x9, starting transfers between devices, swap_both(): return lax.ppermute(x, ('tm', 'space'), route)  11.8 us
    pallas_call x1, Pallas kernels, local(): pl.pallas_call(functools.partial(merge_kernel, parts, span), out_shape=[s...  11.3 us
    ppermute x9, waiting for transfers between devices, swap_both(): return lax.ppermute(x, ('tm', 'space'), route)  11.2 us
    pallas_call x1, Pallas kernels, local(): pl.pallas_call(functools.partial(filter_kernel, parts), out_shape=[shape(...  3.87 us
    ppermute x1, starting transfers between devices, local(): lax.ppermute(to_near, 'space', [(i, i ^ 1) for i in range(patches) if i ^...  3 us
  transfers between devices with their start and end apart: 23, of which 15 were waited for; matrix products, arithmetic and copies ran while one was open for 0% of the time, Pallas kernels for 8%

profile of v11, /device:TPU:0, one launch (start us, length us, event | category | flops | bytes accessed | tf_op | source)
XLA Modules:
  0.0 74.2 jit_solution(5062780845174062097)
XLA Ops:
  0.6 1.2 %edge.1 = (f32[64,128]{1,0:T(8,128)S(1)}, f32[64,128]{1,0:T(8,128)S(1)}) custom-call(f32[6]{0:T(128)} %rtaps_ref.3, f32[6]{0:T(128)} %ctaps_ref.3, f32[64,128,128]{2,1,0:T(8,128)} %snap_hbm.1, f32[64,128,128]{2,1,0:T(8,128)} %snap_hbm.1, s32[64,128]{1,0:T(8,128)} %mask_ref.1, s32[64,128]{1,0:T(8,128)} %mask_ref.1), custom_call_target="tpu_custom_call" | custom-call | tf_op jit(solution)/shard_map/edge/pallas_call | solution.py:360
  1.9 3.0 %collective-permute-start = (f32[64,128]{1,0:T(8,128)S(1)}, f32[64,128]{1,0:T(8,128)S(1)}, u32[]{:S(2)}, u32[]{:S(2)}) collective-permute-start(f32[64,128]{1,0:T(8,128)S(1)} %get-tuple-element.33), channel_id=1, source_target_pairs={{0,1},{1,0},{2,3},{3,2},{4,5},{5,4},{6,7},{7,6},{8,9},{9,8},{10,11... | collective-permute-start | bytes 98312 | tf_op jit(solution)/shard_map/ppermute | solution.py:376
  5.6 3.9 %filter.1 = (f32[512,128]{1,0:T(8,128)S(1)}, f32[512,128]{1,0:T(8,128)S(1)}, f32[512,128]{1,0:T(8,128)S(1)}, f32[512,128]{1,0:T(8,128)S(1)}) custom-call(f32[6]{0:T(128)} %rtaps_ref.3, f32[6]{0:T(128)} %ctaps_ref.3, f32[64,128,128]{2,1,0:T(8,128)} %snap_hbm.1, s32[64,128]{1,0:T(8,128)} %mask_ref.1), custom_call_target="tpu_custom_call" | custom-call | bytes 4194304 | tf_op jit(solution)/shard_map/filter/pallas_call | solution.py:380
  10.2 1.5 %collective-permute-start.7 = (f32[512,128]{1,0:T(8,128)S(1)}, f32[512,128]{1,0:T(8,128)S(1)}, u32[]{:S(2)}, u32[]{:S(2)}) collective-permute-start(f32[512,128]{1,0:T(8,128)S(1)} %get-tuple-element.41.refs_1_), channel_id=1, source_target_pairs={{0,16},{8,24},{16,0},{24,8},{1,17},{9,25},{17,1},{25,9},{2,18},{10... | collective-permute-start | bytes 786440 | tf_op jit(solution)/shard_map/ppermute | solution.py:32
  12.8 1.2 %pair.1 = (f32[136,128]{1,0:T(8,128)S(1)}, f32[136,128]{1,0:T(8,128)S(1)}, f32[136,128]{1,0:T(8,128)S(1)}, f32[136,128]{1,0:T(8,128)S(1)}) custom-call(f32[2048,128]{1,0:T(8,128)S(1)} %bitcast.20, f32[512,128]{1,0:T(8,128)S(1)} %get-tuple-element.39.refs_0_, f32[512,128]{1,0:T(8,128)S(1)} %get-tuple-element.41.refs_1_, ...), custom_call_target="tpu_custom_call" | custom-call | tf_op jit(solution)/shard_map/pair/pallas_call | solution.py:413
  14.1 4.3 %collective-permute-start.5 = (f32[136,128]{1,0:T(8,128)S(1)}, f32[136,128]{1,0:T(8,128)S(1)}, u32[]{:S(2)}, u32[]{:S(2)}) collective-permute-start(f32[136,128]{1,0:T(8,128)S(1)} %get-tuple-element.44), channel_id=1, source_target_pairs={{0,1},{1,0},{2,3},{3,2},{4,5},{5,4},{6,7},{7,6},{8,9},{9,8},{10,11... | collective-permute-start | bytes 208904 | tf_op jit(solution)/shard_map/ppermute | solution.py:42
  19.4 1.8 %collective-permute-done.5 = f32[136,128]{1,0:T(8,128)S(1)} collective-permute-done((f32[136,128]{1,0:T(8,128)S(1)}, f32[136,128]{1,0:T(8,128)S(1)}, u32[]{:S(2)}, u32[]{:S(2)}) %collective-permute-start.5) | collective-permute-done | bytes 69664 | tf_op jit(solution)/shard_map/ppermute | solution.py:42
  21.2 1.4 %collective-permute-done.6 = f32[136,128]{1,0:T(8,128)S(1)} collective-permute-done((f32[136,128]{1,0:T(8,128)S(1)}, f32[136,128]{1,0:T(8,128)S(1)}, u32[]{:S(2)}, u32[]{:S(2)}) %collective-permute-start.6) | collective-permute-done | bytes 69664 | tf_op jit(solution)/shard_map/ppermute | solution.py:42
  22.6 1.6 %collective-permute-done.8.refs_3_ = f32[512,128]{1,0:T(8,128)S(1)} collective-permute-done((f32[512,128]{1,0:T(8,128)S(1)}, f32[512,128]{1,0:T(8,128)S(1)}, u32[]{:S(2)}, u32[]{:S(2)}) %collective-permute-start.8) | collective-permute-done | bytes 262176 | tf_op jit(solution)/shard_map/ppermute | solution.py:32
  24.9 3.8 %collective-permute-start.13 = (f32[136,128]{1,0:T(8,128)S(1)}, f32[136,128]{1,0:T(8,128)S(1)}, u32[]{:S(2)}, u32[]{:S(2)}) collective-permute-start(f32[136,128]{1,0:T(8,128)S(1)} %add_add_fusion), channel_id=1, source_target_pairs={{0,2},{1,3},{2,0},{3,1},{4,6},{5,7},{6,4},{7,5},{8,10},{9,11},{10,... | collective-permute-start | bytes 208904 | tf_op jit(solution)/shard_map/ppermute | solution.py:32
  28.7 1.6 %collective-permute-start.10 = (f32[64,128]{1,0:T(8,128)S(1)}, f32[64,128]{1,0:T(8,128)S(1)}, u32[]{:S(2)}, u32[]{:S(2)}) collective-permute-start(f32[64,128]{1,0:T(8,128)S(1)} %get-tuple-element.64), channel_id=1, source_target_pairs={{0,16},{1,17},{2,18},{3,19},{4,20},{5,21},{6,22},{7,23},{8,24},{9,... | collective-permute-start | bytes 98312 | tf_op jit(solution)/shard_map/ppermute | solution.py:42
  30.3 2.1 %collective-permute-start.12 = (f32[64,128]{1,0:T(8,128)S(1)}, f32[64,128]{1,0:T(8,128)S(1)}, u32[]{:S(2)}, u32[]{:S(2)}) collective-permute-start(f32[64,128]{1,0:T(8,128)S(1)} %get-tuple-element.65), channel_id=1, source_target_pairs={{0,17},{1,16},{2,19},{3,18},{4,21},{5,20},{6,23},{7,22},{8,25},{9,... | collective-permute-start | bytes 98312 | tf_op jit(solution)/shard_map/ppermute | solution.py:42
  32.7 2.4 %collective-permute-done.12 = f32[64,128]{1,0:T(8,128)S(1)} collective-permute-done((f32[64,128]{1,0:T(8,128)S(1)}, f32[64,128]{1,0:T(8,128)S(1)}, u32[]{:S(2)}, u32[]{:S(2)}) %collective-permute-start.12) | collective-permute-done | bytes 32800 | tf_op jit(solution)/shard_map/ppermute | solution.py:42
  35.1 1.2 %collective-permute-done.11 = f32[64,128]{1,0:T(8,128)S(1)} collective-permute-done((f32[64,128]{1,0:T(8,128)S(1)}, f32[64,128]{1,0:T(8,128)S(1)}, u32[]{:S(2)}, u32[]{:S(2)}) %collective-permute-start.11) | collective-permute-done | bytes 32800 | tf_op jit(solution)/shard_map/ppermute | solution.py:42
  36.3 1.3 %collective-permute-start.14 = (f32[64,128]{1,0:T(8,128)S(1)}, f32[64,128]{1,0:T(8,128)S(1)}, u32[]{:S(2)}, u32[]{:S(2)}) collective-permute-start(f32[64,128]{1,0:T(8,128)S(1)} %fusion.6), channel_id=1, source_target_pairs={{0,2},{1,3},{2,0},{3,1},{4,6},{5,7},{6,4},{7,5},{8,10},{9,11},{10,... | collective-permute-start | bytes 98312 | tf_op jit(solution)/shard_map/ppermute | solution.py:32
  37.6 2.7 %collective-permute-done.14 = f32[64,128]{1,0:T(8,128)S(1)} collective-permute-done((f32[64,128]{1,0:T(8,128)S(1)}, f32[64,128]{1,0:T(8,128)S(1)}, u32[]{:S(2)}, u32[]{:S(2)}) %collective-permute-start.14) | collective-permute-done | bytes 32800 | tf_op jit(solution)/shard_map/ppermute | solution.py:32
  40.3 2.3 %collective-permute-start.15 = (f32[200,128]{1,0:T(8,128)S(1)}, f32[200,128]{1,0:T(8,128)S(1)}, u32[]{:S(2)}, u32[]{:S(2)}) collective-permute-start(f32[200,128]{1,0:T(8,128)S(1)} %pad_maximum_fusion.1), channel_id=1, source_target_pairs={{0,4},{1,5},{2,6},{3,7},{4,0},{5,1},{6,2},{7,3},{8,12},{9,13},{10,... | collective-permute-start | bytes 307208 | tf_op jit(solution)/shard_map/ppermute | solution.py:32
  42.6 4.4 %collective-permute-done.15 = f32[200,128]{1,0:T(8,128)S(1)} collective-permute-done((f32[200,128]{1,0:T(8,128)S(1)}, f32[200,128]{1,0:T(8,128)S(1)}, u32[]{:S(2)}, u32[]{:S(2)}) %collective-permute-start.15) | collective-permute-done | bytes 102432 | tf_op jit(solution)/shard_map/ppermute | solution.py:32
  47.0 1.4 %collective-permute-start.18 = (f32[200,128]{1,0:T(8,128)S(1)}, f32[200,128]{1,0:T(8,128)S(1)}, u32[]{:S(2)}, u32[]{:S(2)}) collective-permute-start(f32[200,128]{1,0:T(8,128)S(1)} %fusion.7), channel_id=1, source_target_pairs={{0,17},{1,16},{2,19},{3,18},{4,21},{5,20},{6,23},{7,22},{8,25},{9,... | collective-permute-start | bytes 307208 | tf_op jit(solution)/shard_map/ppermute | solution.py:42
  48.4 1.7 %collective-permute-start.17 = (f32[200,128]{1,0:T(8,128)S(1)}, f32[200,128]{1,0:T(8,128)S(1)}, u32[]{:S(2)}, u32[]{:S(2)}) collective-permute-start(f32[200,128]{1,0:T(8,128)S(1)} %fusion.7), channel_id=1, source_target_pairs={{0,1},{1,0},{2,3},{3,2},{4,5},{5,4},{6,7},{7,6},{8,9},{9,8},{10,11... | collective-permute-start | bytes 307208 | tf_op jit(solution)/shard_map/ppermute | solution.py:42
  50.6 2.1 %collective-permute-done.18 = f32[200,128]{1,0:T(8,128)S(1)} collective-permute-done((f32[200,128]{1,0:T(8,128)S(1)}, f32[200,128]{1,0:T(8,128)S(1)}, u32[]{:S(2)}, u32[]{:S(2)}) %collective-permute-start.18) | collective-permute-done | bytes 102432 | tf_op jit(solution)/shard_map/ppermute | solution.py:42
  54.9 1.7 %collective-permute-done.19.odd_ref = f32[4,200,128]{2,1,0:T(8,128)S(1)} collective-permute-done((f32[4,200,128]{2,1,0:T(8,128)S(1)}, f32[4,200,128]{2,1,0:T(8,128)S(1)}, u32[]{:S(2)}, u32[]{:S(2)}) %collective-permute-start.19) | collective-permute-done | bytes 409632 | tf_op jit(solution)/shard_map/ppermute | solution.py:32
  56.6 11.3 %merge.1 = (f32[32,512]{1,0:T(8,128)S(1)}, f32[32,512]{1,0:T(8,128)S(1)}, f32[32,512]{1,0:T(8,128)S(1)}, f32[32,512]{1,0:T(8,128)S(1)}, f32[512,128]{1,0:T(8,128)S(1)}, /*index=5*/f32[512,128]{1,0:T(8,128)S(1)}) custom-call(f32[4,200,128]{2,1,0:T(8,128)S(1)} %pad_maximum_fusion.even_ref, f32[4,200,128]{2,1,0:T(8,128)S(1)} %collective-permute-done.19.odd_ref, ...), custom_call_target="tpu_custom_call" | custom-call | tf_op jit(solution)/shard_map/merge/pallas_call | solution.py:466
  70.7 2.3 %collective-permute-done.21.refs_2_ = f32[32,512]{1,0:T(8,128)S(1)} collective-permute-done((f32[32,512]{1,0:T(8,128)S(1)}, f32[32,512]{1,0:T(8,128)S(1)}, u32[]{:S(2)}, u32[]{:S(2)}) %collective-permute-start.21) | collective-permute-done | bytes 65568 | tf_op jit(solution)/shard_map/ppermute | solution.py:32
  (40 shorter events, 11.3 us)
Async XLA Ops:
  1.9 10.9 %copy-start = (f32[32,64,128]{2,1,0:T(8,128)S(1)}, f32[32,64,128]{2,1,0:T(8,128)}, u32[]{:S(2)}) copy-start(f32[32,64,128]{2,1,0:T(8,128)} %param.9) | copy-start | bytes 3145732
  1.9 7.5 %collective-permute-start = (f32[64,128]{1,0:T(8,128)S(1)}, f32[64,128]{1,0:T(8,128)S(1)}, u32[]{:S(2)}, u32[]{:S(2)}) collective-permute-start(f32[64,128]{1,0:T(8,128)S(1)} %get-tuple-element.33), channel_id=1, source_target_pairs={{0,1},{1,0},{2,3},{3,2},{4,5},{5,4},{6,7},{7,6},{8,9},{9,8},{10,11... | collective-permute-start | bytes 98312 | tf_op jit(solution)/shard_map/ppermute | solution.py:376
  4.9 4.5 %collective-permute-start.1 = (f32[64,128]{1,0:T(8,128)S(1)}, f32[64,128]{1,0:T(8,128)S(1)}, u32[]{:S(2)}, u32[]{:S(2)}) collective-permute-start(f32[64,128]{1,0:T(8,128)S(1)} %get-tuple-element.34), channel_id=1, source_target_pairs={{1,2},{3,4},{5,6},{2,1},{4,3},{6,5},{9,10},{11,12},{13,14},{10,9},... | collective-permute-start | bytes 98312 | tf_op jit(solution)/shard_map/ppermute | solution.py:378
  9.6 2.1 %collective-permute-start.3 = (f32[512,128]{1,0:T(8,128)S(1)}, f32[512,128]{1,0:T(8,128)S(1)}, u32[]{:S(2)}, u32[]{:S(2)}) collective-permute-start(f32[512,128]{1,0:T(8,128)S(1)} %get-tuple-element.42), channel_id=1, source_target_pairs={{0,8},{8,0},{16,24},{24,16},{1,9},{9,1},{17,25},{25,17},{2,10},{10... | collective-permute-start | bytes 786440 | tf_op jit(solution)/shard_map/ppermute | solution.py:32
  9.7 3.0 %collective-permute-start.2 = (f32[512,128]{1,0:T(8,128)S(1)}, f32[512,128]{1,0:T(8,128)S(1)}, u32[]{:S(2)}, u32[]{:S(2)}) collective-permute-start(f32[512,128]{1,0:T(8,128)S(1)} %get-tuple-element.40), channel_id=1, source_target_pairs={{0,8},{8,0},{16,24},{24,16},{1,9},{9,1},{17,25},{25,17},{2,10},{10... | collective-permute-start | bytes 786440 | tf_op jit(solution)/shard_map/ppermute | solution.py:32
  10.2 9.2 %collective-permute-start.7 = (f32[512,128]{1,0:T(8,128)S(1)}, f32[512,128]{1,0:T(8,128)S(1)}, u32[]{:S(2)}, u32[]{:S(2)}) collective-permute-start(f32[512,128]{1,0:T(8,128)S(1)} %get-tuple-element.41.refs_1_), channel_id=1, source_target_pairs={{0,16},{8,24},{16,0},{24,8},{1,17},{9,25},{17,1},{25,9},{2,18},{10... | collective-permute-start | bytes 786440 | tf_op jit(solution)/shard_map/ppermute | solution.py:32
  11.7 12.4 %collective-permute-start.8 = (f32[512,128]{1,0:T(8,128)S(1)}, f32[512,128]{1,0:T(8,128)S(1)}, u32[]{:S(2)}, u32[]{:S(2)}) collective-permute-start(f32[512,128]{1,0:T(8,128)S(1)} %collective-permute-done.3.refs_3_), channel_id=1, source_target_pairs={{0,16},{8,24},{16,0},{24,8},{1,17},{9,25},{17,1},{25,9},{2,18},{10... | collective-permute-start | bytes 786440 | tf_op jit(solution)/shard_map/ppermute | solution.py:32
  14.0 5.4 %collective-permute-start.4 = (f32[136,128]{1,0:T(8,128)S(1)}, f32[136,128]{1,0:T(8,128)S(1)}, u32[]{:S(2)}, u32[]{:S(2)}) collective-permute-start(f32[136,128]{1,0:T(8,128)S(1)} %get-tuple-element.43), channel_id=1, source_target_pairs={{0,8},{1,9},{2,10},{3,11},{4,12},{5,13},{6,14},{7,15},{8,0},{9,1},... | collective-permute-start | bytes 208904 | tf_op jit(solution)/shard_map/ppermute | solution.py:42
  14.1 7.1 %collective-permute-start.5 = (f32[136,128]{1,0:T(8,128)S(1)}, f32[136,128]{1,0:T(8,128)S(1)}, u32[]{:S(2)}, u32[]{:S(2)}) collective-permute-start(f32[136,128]{1,0:T(8,128)S(1)} %get-tuple-element.44), channel_id=1, source_target_pairs={{0,1},{1,0},{2,3},{3,2},{4,5},{5,4},{6,7},{7,6},{8,9},{9,8},{10,11... | collective-permute-start | bytes 208904 | tf_op jit(solution)/shard_map/ppermute | solution.py:42
  18.4 4.1 %collective-permute-start.6 = (f32[136,128]{1,0:T(8,128)S(1)}, f32[136,128]{1,0:T(8,128)S(1)}, u32[]{:S(2)}, u32[]{:S(2)}) collective-permute-start(f32[136,128]{1,0:T(8,128)S(1)} %get-tuple-element.45), channel_id=1, source_target_pairs={{0,9},{1,8},{2,11},{3,10},{4,13},{5,12},{6,15},{7,14},{8,1},{9,0},... | collective-permute-start | bytes 208904 | tf_op jit(solution)/shard_map/ppermute | solution.py:42
  24.8 3.9 %collective-permute-start.9 = (f32[4,64,128]{2,1,0:T(8,128)S(1)}, f32[4,64,128]{2,1,0:T(8,128)S(1)}, u32[]{:S(2)}, u32[]{:S(2)}) collective-permute-start(f32[4,64,128]{2,1,0:T(8,128)S(1)} %get-tuple-element.49), channel_id=1, source_target_pairs={{0,8},{8,0},{16,24},{24,16},{1,9},{9,1},{17,25},{25,17},{2,10},{10... | collective-permute-start | bytes 393224 | tf_op jit(solution)/shard_map/ppermute | solution.py:32
  24.9 7.5 %collective-permute-start.13 = (f32[136,128]{1,0:T(8,128)S(1)}, f32[136,128]{1,0:T(8,128)S(1)}, u32[]{:S(2)}, u32[]{:S(2)}) collective-permute-start(f32[136,128]{1,0:T(8,128)S(1)} %add_add_fusion), channel_id=1, source_target_pairs={{0,2},{1,3},{2,0},{3,1},{4,6},{5,7},{6,4},{7,5},{8,10},{9,11},{10,... | collective-permute-start | bytes 208904 | tf_op jit(solution)/shard_map/ppermute | solution.py:32
  28.7 4.0 %collective-permute-start.10 = (f32[64,128]{1,0:T(8,128)S(1)}, f32[64,128]{1,0:T(8,128)S(1)}, u32[]{:S(2)}, u32[]{:S(2)}) collective-permute-start(f32[64,128]{1,0:T(8,128)S(1)} %get-tuple-element.64), channel_id=1, source_target_pairs={{0,16},{1,17},{2,18},{3,19},{4,20},{5,21},{6,22},{7,23},{8,24},{9,... | collective-permute-start | bytes 98312 | tf_op jit(solution)/shard_map/ppermute | solution.py:42
  30.3 4.8 %collective-permute-start.12 = (f32[64,128]{1,0:T(8,128)S(1)}, f32[64,128]{1,0:T(8,128)S(1)}, u32[]{:S(2)}, u32[]{:S(2)}) collective-permute-start(f32[64,128]{1,0:T(8,128)S(1)} %get-tuple-element.65), channel_id=1, source_target_pairs={{0,17},{1,16},{2,19},{3,18},{4,21},{5,20},{6,23},{7,22},{8,25},{9,... | collective-permute-start | bytes 98312 | tf_op jit(solution)/shard_map/ppermute | solution.py:42
  32.4 3.9 %collective-permute-start.11 = (f32[64,128]{1,0:T(8,128)S(1)}, f32[64,128]{1,0:T(8,128)S(1)}, u32[]{:S(2)}, u32[]{:S(2)}) collective-permute-start(f32[64,128]{1,0:T(8,128)S(1)} %get-tuple-element.66), channel_id=1, source_target_pairs={{0,1},{1,0},{2,3},{3,2},{4,5},{5,4},{6,7},{7,6},{8,9},{9,8},{10,11... | collective-permute-start | bytes 98312 | tf_op jit(solution)/shard_map/ppermute | solution.py:42
  36.3 4.0 %collective-permute-start.14 = (f32[64,128]{1,0:T(8,128)S(1)}, f32[64,128]{1,0:T(8,128)S(1)}, u32[]{:S(2)}, u32[]{:S(2)}) collective-permute-start(f32[64,128]{1,0:T(8,128)S(1)} %fusion.6), channel_id=1, source_target_pairs={{0,2},{1,3},{2,0},{3,1},{4,6},{5,7},{6,4},{7,5},{8,10},{9,11},{10,... | collective-permute-start | bytes 98312 | tf_op jit(solution)/shard_map/ppermute | solution.py:32
  40.3 6.7 %collective-permute-start.15 = (f32[200,128]{1,0:T(8,128)S(1)}, f32[200,128]{1,0:T(8,128)S(1)}, u32[]{:S(2)}, u32[]{:S(2)}) collective-permute-start(f32[200,128]{1,0:T(8,128)S(1)} %pad_maximum_fusion.1), channel_id=1, source_target_pairs={{0,4},{1,5},{2,6},{3,7},{4,0},{5,1},{6,2},{7,3},{8,12},{9,13},{10,... | collective-permute-start | bytes 307208 | tf_op jit(solution)/shard_map/ppermute | solution.py:32
  47.0 5.6 %collective-permute-start.18 = (f32[200,128]{1,0:T(8,128)S(1)}, f32[200,128]{1,0:T(8,128)S(1)}, u32[]{:S(2)}, u32[]{:S(2)}) collective-permute-start(f32[200,128]{1,0:T(8,128)S(1)} %fusion.7), channel_id=1, source_target_pairs={{0,17},{1,16},{2,19},{3,18},{4,21},{5,20},{6,23},{7,22},{8,25},{9,... | collective-permute-start | bytes 307208 | tf_op jit(solution)/shard_map/ppermute | solution.py:42
  48.4 5.4 %collective-permute-start.17 = (f32[200,128]{1,0:T(8,128)S(1)}, f32[200,128]{1,0:T(8,128)S(1)}, u32[]{:S(2)}, u32[]{:S(2)}) collective-permute-start(f32[200,128]{1,0:T(8,128)S(1)} %fusion.7), channel_id=1, source_target_pairs={{0,1},{1,0},{2,3},{3,2},{4,5},{5,4},{6,7},{7,6},{8,9},{9,8},{10,11... | collective-permute-start | bytes 307208 | tf_op jit(solution)/shard_map/ppermute | solution.py:42
  50.1 4.7 %collective-permute-start.16 = (f32[200,128]{1,0:T(8,128)S(1)}, f32[200,128]{1,0:T(8,128)S(1)}, u32[]{:S(2)}, u32[]{:S(2)}) collective-permute-start(f32[200,128]{1,0:T(8,128)S(1)} %fusion.7), channel_id=1, source_target_pairs={{0,16},{1,17},{2,18},{3,19},{4,20},{5,21},{6,22},{7,23},{8,24},{9,... | collective-permute-start | bytes 307208 | tf_op jit(solution)/shard_map/ppermute | solution.py:42
  54.8 1.8 %collective-permute-start.19 = (f32[4,200,128]{2,1,0:T(8,128)S(1)}, f32[4,200,128]{2,1,0:T(8,128)S(1)}, u32[]{:S(2)}, u32[]{:S(2)}) collective-permute-start(f32[4,200,128]{2,1,0:T(8,128)S(1)} %pad_maximum_fusion.even_ref), channel_id=1, source_target_pairs={{0,8},{8,0},{16,24},{24,16},{1,9},{9,1},{17,25},{25,17},{2,10},{10... | collective-permute-start | bytes 1228808 | tf_op jit(solution)/shard_map/ppermute | solution.py:32
  67.9 2.8 %collective-permute-start.20 = (f32[32,512]{1,0:T(8,128)S(1)}, f32[32,512]{1,0:T(8,128)S(1)}, u32[]{:S(2)}, u32[]{:S(2)}) collective-permute-start(f32[32,512]{1,0:T(8,128)S(1)} %get-tuple-element.59), channel_id=1, source_target_pairs={{0,8},{8,0},{16,24},{24,16},{1,9},{9,1},{17,25},{25,17},{2,10},{10... | collective-permute-start | bytes 196616 | tf_op jit(solution)/shard_map/ppermute | solution.py:32
  68.1 4.9 %collective-permute-start.21 = (f32[32,512]{1,0:T(8,128)S(1)}, f32[32,512]{1,0:T(8,128)S(1)}, u32[]{:S(2)}, u32[]{:S(2)}) collective-permute-start(f32[32,512]{1,0:T(8,128)S(1)} %get-tuple-element.60), channel_id=1, source_target_pairs={{0,16},{8,24},{16,0},{24,8},{1,17},{9,25},{17,1},{25,9},{2,18},{10... | collective-permute-start | bytes 196616 | tf_op jit(solution)/shard_map/ppermute | solution.py:32
  68.6 4.7 %collective-permute-start.22 = (f32[32,512]{1,0:T(8,128)S(1)}, f32[32,512]{1,0:T(8,128)S(1)}, u32[]{:S(2)}, u32[]{:S(2)}) collective-permute-start(f32[32,512]{1,0:T(8,128)S(1)} %get-tuple-element.61), channel_id=1, source_target_pairs={{0,24},{8,16},{16,8},{24,0},{1,25},{9,17},{17,9},{25,1},{2,26},{10... | collective-permute-start | bytes 196616 | tf_op jit(solution)/shard_map/ppermute | solution.py:32

commit v12 on v11

--- a/solution.py
+++ b/solution.py
@@ -264,29 +264,60 @@
     return combines
 
 
-def merge_kernel(parts, span, even_ref, odd_ref, high_ref, low_ref, *refs):
-    outs, (weight_ref, product_ref, pairs, cross, turned) = refs[:parts], refs[parts:]
-    me, owner = positions(parts, span)
+def place_shares(parts, span, even_ref, odd_ref, put):
+    _, owner = positions(parts, span)
+    for k in range(parts * span):
+        put(owner ^ k, (odd_ref if k % 2 else even_ref)[k // 2])
+
+
+def level_kernel(parts, span, even_ref, odd_ref, combine_ref, square_ref, product_ref, pairs):
     cols = even_ref.shape[2]
-    pair_share, cross_share = pairs.shape[1] // (2 * span), cross.shape[0] // (parts * span)
-    for k in range(parts * span):
-        source = (odd_ref if k % 2 else even_ref).at[k // 2]
-        there = owner ^ k
+    share = pairs.shape[1] // (2 * span)
+
+    def put(there, rows):
         place = there % 2 + 2 * (there // parts)
-        at = pl.ds(pl.multiple_of(place * pair_share, 8), pair_share)
-        pairs[(there % parts) // 2, at, :] = source[:pair_share, :]
-        cross[pl.ds(pl.multiple_of(there * cross_share, 8), cross_share), :] = source[pair_share:, :]
-    blocks = {ab: cross[j * cols:(j + 1) * cols, :] for j, ab in enumerate(cross_order(parts))}
+        pairs[(there % parts) // 2, pl.ds(pl.multiple_of(place * share, 8), share), :] = rows
+
+    place_shares(parts, span, even_ref, odd_ref, put)
     row, col = triangle(cols)
+    grams = []
     for p in range(parts // 2):
         packed = pairs[p, cols:2 * cols, :]
         turned_back = packed.T
-        blocks[2 * p, 2 * p] = jnp.where(row <= col, packed, turned_back)
-        blocks[2 * p, 2 * p + 1] = pairs[p, :cols, :]
+        first = jnp.where(row <= col, packed, turned_back)
+        between = pairs[p, :cols, :]
         second = jnp.where(row > col, packed, turned_back)
-        blocks[2 * p + 1, 2 * p + 1] = jnp.where(row == col, pairs[p, 4 * cols:4 * cols + 1, :], second)
+        second = jnp.where(row == col, pairs[p, 4 * cols:4 * cols + 1, :], second)
+        grams.append(jnp.concatenate([
+            jnp.concatenate([first, between], axis=1), jnp.concatenate([between.T, second], axis=1)
+        ], axis=0))
         product_ref[2 * p * cols:2 * (p + 1) * cols, :] = pairs[p, 2 * cols:4 * cols, :]
-    weights, count = None, parts
+    for p, (gram, combine) in enumerate(zip(grams, combine_of(grams))):
+        combine_ref[p] = combine
+        square_ref[p] = split_dot(combine, split_dot(gram, combine), ((0,), (0,)))
+
+
+def merge_kernel(parts, span, even_ref, odd_ref, combine_ref, square_ref, high_ref, low_ref, *refs):
+    outs, (weight_ref, cross, turned) = refs[:parts], refs[parts:]
+    me = lax.axis_index("tm")
+    cols = even_ref.shape[2]
+    share = cross.shape[0] // (parts * span)
+
+    def put(there, rows):
+        cross[pl.ds(pl.multiple_of(there * share, 8), share), :] = rows
+
+    place_shares(parts, span, even_ref, odd_ref, put)
+    where = {ab: j * cols for j, ab in enumerate(cross_order(parts))}
+    weights = [combine_ref[p] for p in range(parts // 2)]
+    blocks = {(p, p): square_ref[p] for p in range(parts // 2)}
+    for p in range(parts // 2):
+        for q in range(p + 1, parts // 2):
+            between = jnp.concatenate([
+                jnp.concatenate([cross[where[a, b]:where[a, b] + cols, :] for b in (2 * q, 2 * q + 1)], axis=1)
+                for a in (2 * p, 2 * p + 1)
+            ], axis=0)
+            blocks[p, q] = split_dot(weights[p], split_dot(between, weights[q]), ((0,), (0,)))
+    count = parts // 2
     while count > 1:
         grams = []
         for p in range(0, count, 2):
@@ -294,27 +325,24 @@
             high = jnp.concatenate([blocks[p, p + 1].T, blocks[p + 1, p + 1]], axis=1)
             grams.append(jnp.concatenate([low, high], axis=0))
         combines = combine_of(grams)
-        if weights is None:
-            weights = combines
-        else:
-            per = len(weights) // len(combines)
-            weights = [
-                split_dot(w, combines[i // per][(i % per) * cols:(i % per + 1) * cols, :])
-                for i, w in enumerate(weights)
-            ]
-            weights = [jnp.concatenate(weights[i:i + per], axis=0) for i in range(0, len(weights), per)]
+        per = len(weights) // len(combines)
+        weights = [
+            split_dot(w, combines[i // per][(i % per) * cols:(i % per + 1) * cols, :])
+            for i, w in enumerate(weights)
+        ]
+        weights = [jnp.concatenate(weights[i:i + per], axis=0) for i in range(0, len(weights), per)]
         merged = {}
         if count > 2:
             for p in range(count // 2):
                 for q in range(p, count // 2):
                     if p == q:
-                        cross = grams[p]
+                        between = grams[p]
                     else:
-                        cross = jnp.concatenate([
+                        between = jnp.concatenate([
                             jnp.concatenate([blocks[2 * p + i, 2 * q], blocks[2 * p + i, 2 * q + 1]], axis=1)
                             for i in range(2)
                         ], axis=0)
-                    right = split_dot(cross, combines[q])
+                    right = split_dot(between, combines[q])
                     merged[p, q] = split_dot(combines[p], right, ((0,), (0,)))
         blocks, count = merged, count // 2
     weight_ref[...] = weights[0]
@@ -454,28 +482,45 @@
     for bit in bits[:1]:
         pair_share = pair_share + swap(pair_share, "space", bit)
     mine, pair_share = lax.optimization_barrier((mine, pair_share))
+    for bit in bits[1:]:
+        pair_share = pair_share + swap(pair_share, "space", bit)
     for bit in bits[:1]:
         mine = mine + swap(mine, "space", bit)
-    mine = jnp.concatenate([pair_share, mine], axis=0)
+    mine, pair_share = lax.optimization_barrier((mine, pair_share))
     for bit in bits[1:]:
         mine = mine + swap(mine, "space", bit)
-    even = jnp.stack([mine] + [swap_both(mine, 2 * h) for h in range(1, owners // 2)])
-    odd = swap(even, "tm", 1)
-
+
+    def spread(x):
+        return [x] + [swap_both(x, 2 * h) for h in range(1, owners // 2)]
+
+    def gathered(shares):
+        even = jnp.stack(shares)
+        return even, swap(even, "tm", 1)
+
+    mine, *pair_shares = lax.optimization_barrier([mine] + spread(pair_share))
+
+    combines, squares, products = pl.pallas_call(
+        functools.partial(level_kernel, parts, span),
+        out_shape=[shape(parts // 2, 2 * cols, cols), shape(parts // 2, cols, cols), shape(parts * cols, cols)],
+        in_specs=[whole()] * 2,
+        out_specs=[whole()] * 3,
+        scratch_shapes=[pltpu.VMEM((parts // 2, pair_rows(cols, 2 * span), cols), F32)],
+        compiler_params=params(),
+        cost_estimate=pl.CostEstimate(flops=parts * SIGN_STEPS * 6 * (2 * cols) ** 3, bytes_accessed=0, transcendentals=0),
+        name="level",
+    )(*gathered(pair_shares))
+
+    combines, *shares = lax.optimization_barrier([combines] + spread(mine))
     width = cols // parts
-    *sent, weight, products = pl.pallas_call(
+    *sent, weight = pl.pallas_call(
         functools.partial(merge_kernel, parts, span),
-        out_shape=[shape(width, piece)] * parts + [shape(parts * cols, cols)] * 2,
-        in_specs=[whole()] * 4,
-        out_specs=[whole()] * (parts + 2),
-        scratch_shapes=[
-            pltpu.VMEM((parts // 2, pair_rows(cols, 2 * span), cols), F32),
-            pltpu.VMEM((blocks * cols, cols), F32),
-            pltpu.VMEM((cols, piece), F32),
-        ],
+        out_shape=[shape(width, piece)] * parts + [shape(parts * cols, cols)],
+        in_specs=[whole()] * 6,
+        out_specs=[whole()] * (parts + 1),
+        scratch_shapes=[pltpu.VMEM((blocks * cols, cols), F32), pltpu.VMEM((cols, piece), F32)],
         compiler_params=params(),
         name="merge",
-    )(even, odd, high, low)
+    )(*gathered(shares), combines, squares, high, low)
     coefficients = pl.pallas_call(
         functools.partial(coefficient_kernel, parts),
         out_shape=shape(width, cols),

time: 74.4 us -> 74.8 us (level)
  starting transfers between devices: 28 us -> 32.5 us
  waiting for transfers between devices: 25 us -> 20.8 us
    pallas_call x0 -> x1, Pallas kernels: none -> 5.72 us  [local(): pl.pallas_call(functools.partial(level_kernel, parts, span), out_shape=[s...]
    pallas_call x1, Pallas kernels: 11.3 us -> 5.6 us  [local(): pl.pallas_call(functools.partial(merge_kernel, parts, span), out_shape=[s...]
    ppermute x9 -> x12, waiting for transfers between devices: 11.2 us -> 7.02 us  [swap_both(): return lax.ppermute(x, ('tm', 'space'), route)]
    ppermute x9 -> x12, starting transfers between devices: 11.8 us -> 15.3 us  [swap_both(): return lax.ppermute(x, ('tm', 'space'), route)]
    ppermute x12 -> x14, starting transfers between devices: 12.6 us -> 13.5 us  [swap(): return lax.ppermute(x, axis, [(i, i ^ mask) for i in range(count)])]
    ppermute x12 -> x14, waiting for transfers between devices: 13.9 us -> 13.8 us  [swap(): return lax.ppermute(x, axis, [(i, i ^ mask) for i in range(count)])]
  transfers between devices with their start and end apart: 23 -> 28, of which waited for: 15 -> 12; matrix products, arithmetic and copies ran while one was open for 0% -> 0% of each run, Pallas kernels for 8% -> 16%
where the time goes in v12:
time: 74.8 us; the launch traced here: 74.6 us
  starting transfers between devices  32.5 us (43%)
  waiting for transfers between devices  20.8 us (28%)
  Pallas kernels  20.3 us (27%)
  between operations  0.85 us (1%)
    ppermute x12, starting transfers between devices, swap_both(): return lax.ppermute(x, ('tm', 'space'), route)  15.3 us
    ppermute x14, waiting for transfers between devices, swap(): return lax.ppermute(x, axis, [(i, i ^ mask) for i in range(count)])  13.8 us
    ppermute x14, starting transfers between devices, swap(): return lax.ppermute(x, axis, [(i, i ^ mask) for i in range(count)])  13.5 us
    ppermute x12, waiting for transfers between devices, swap_both(): return lax.ppermute(x, ('tm', 'space'), route)  7.02 us
    pallas_call x1, Pallas kernels, local(): pl.pallas_call(functools.partial(level_kernel, parts, span), out_shape=[s...  5.72 us
    pallas_call x1, Pallas kernels, local(): pl.pallas_call(functools.partial(merge_kernel, parts, span), out_shape=[s...  5.6 us
    pallas_call x1, Pallas kernels, local(): pl.pallas_call(functools.partial(filter_kernel, parts), out_shape=[shape(...  3.87 us
    ppermute x1, starting transfers between devices, local(): lax.ppermute(to_near, 'space', [(i, i ^ 1) for i in range(patches) if i ^...  3 us
  transfers between devices with their start and end apart: 28, of which 12 were waited for; matrix products, arithmetic and copies ran while one was open for 0% of the time, Pallas kernels for 16%

profile of v12, /device:TPU:0, one launch (start us, length us, event | category | flops | bytes accessed | tf_op | source)
XLA Modules:
  0.0 74.6 jit_solution(5821268278294659325)
XLA Ops:
  1.9 3.0 %collective-permute-start = (f32[64,128]{1,0:T(8,128)S(1)}, f32[64,128]{1,0:T(8,128)S(1)}, u32[]{:S(2)}, u32[]{:S(2)}) collective-permute-start(f32[64,128]{1,0:T(8,128)S(1)} %get-tuple-element.47), channel_id=1, source_target_pairs={{0,1},{1,0},{2,3},{3,2},{4,5},{5,4},{6,7},{7,6},{8,9},{9,8},{10,11... | collective-permute-start | bytes 98312 | tf_op jit(solution)/shard_map/ppermute | solution.py:404
  5.6 3.9 %filter.1 = (f32[512,128]{1,0:T(8,128)S(1)}, f32[512,128]{1,0:T(8,128)S(1)}, f32[512,128]{1,0:T(8,128)S(1)}, f32[512,128]{1,0:T(8,128)S(1)}) custom-call(f32[6]{0:T(128)} %rtaps_ref.3, f32[6]{0:T(128)} %ctaps_ref.3, f32[64,128,128]{2,1,0:T(8,128)} %snap_hbm.1, s32[64,128]{1,0:T(8,128)} %mask_ref.1), custom_call_target="tpu_custom_call" | custom-call | bytes 4194304 | tf_op jit(solution)/shard_map/filter/pallas_call | solution.py:408
  10.2 1.5 %collective-permute-start.7 = (f32[512,128]{1,0:T(8,128)S(1)}, f32[512,128]{1,0:T(8,128)S(1)}, u32[]{:S(2)}, u32[]{:S(2)}) collective-permute-start(f32[512,128]{1,0:T(8,128)S(1)} %get-tuple-element.55.refs_1_), channel_id=1, source_target_pairs={{0,16},{8,24},{16,0},{24,8},{1,17},{9,25},{17,1},{25,9},{2,18},{10... | collective-permute-start | bytes 786440 | tf_op jit(solution)/shard_map/ppermute | solution.py:32
  14.1 4.3 %collective-permute-start.5 = (f32[136,128]{1,0:T(8,128)S(1)}, f32[136,128]{1,0:T(8,128)S(1)}, u32[]{:S(2)}, u32[]{:S(2)}) collective-permute-start(f32[136,128]{1,0:T(8,128)S(1)} %get-tuple-element.58), channel_id=1, source_target_pairs={{0,1},{1,0},{2,3},{3,2},{4,5},{5,4},{6,7},{7,6},{8,9},{9,8},{10,11... | collective-permute-start | bytes 208904 | tf_op jit(solution)/shard_map/ppermute | solution.py:42
  19.4 1.8 %collective-permute-done.5 = f32[136,128]{1,0:T(8,128)S(1)} collective-permute-done((f32[136,128]{1,0:T(8,128)S(1)}, f32[136,128]{1,0:T(8,128)S(1)}, u32[]{:S(2)}, u32[]{:S(2)}) %collective-permute-start.5) | collective-permute-done | bytes 69664 | tf_op jit(solution)/shard_map/ppermute | solution.py:42
  21.2 1.4 %collective-permute-done.6 = f32[136,128]{1,0:T(8,128)S(1)} collective-permute-done((f32[136,128]{1,0:T(8,128)S(1)}, f32[136,128]{1,0:T(8,128)S(1)}, u32[]{:S(2)}, u32[]{:S(2)}) %collective-permute-start.6) | collective-permute-done | bytes 69664 | tf_op jit(solution)/shard_map/ppermute | solution.py:42
  22.6 1.6 %collective-permute-done.8.refs_3_ = f32[512,128]{1,0:T(8,128)S(1)} collective-permute-done((f32[512,128]{1,0:T(8,128)S(1)}, f32[512,128]{1,0:T(8,128)S(1)}, u32[]{:S(2)}, u32[]{:S(2)}) %collective-permute-start.8) | collective-permute-done | bytes 262176 | tf_op jit(solution)/shard_map/ppermute | solution.py:32
  24.9 3.8 %collective-permute-start.13 = (f32[136,128]{1,0:T(8,128)S(1)}, f32[136,128]{1,0:T(8,128)S(1)}, u32[]{:S(2)}, u32[]{:S(2)}) collective-permute-start(f32[136,128]{1,0:T(8,128)S(1)} %add_add_fusion), channel_id=1, source_target_pairs={{0,2},{1,3},{2,0},{3,1},{4,6},{5,7},{6,4},{7,5},{8,10},{9,11},{10,... | collective-permute-start | bytes 208904 | tf_op jit(solution)/shard_map/ppermute | solution.py:32
  28.7 1.6 %collective-permute-start.10 = (f32[64,128]{1,0:T(8,128)S(1)}, f32[64,128]{1,0:T(8,128)S(1)}, u32[]{:S(2)}, u32[]{:S(2)}) collective-permute-start(f32[64,128]{1,0:T(8,128)S(1)} %get-tuple-element.92), channel_id=1, source_target_pairs={{0,16},{1,17},{2,18},{3,19},{4,20},{5,21},{6,22},{7,23},{8,24},{9,... | collective-permute-start | bytes 98312 | tf_op jit(solution)/shard_map/ppermute | solution.py:42
  30.3 2.1 %collective-permute-start.12 = (f32[64,128]{1,0:T(8,128)S(1)}, f32[64,128]{1,0:T(8,128)S(1)}, u32[]{:S(2)}, u32[]{:S(2)}) collective-permute-start(f32[64,128]{1,0:T(8,128)S(1)} %get-tuple-element.93), channel_id=1, source_target_pairs={{0,17},{1,16},{2,19},{3,18},{4,21},{5,20},{6,23},{7,22},{8,25},{9,... | collective-permute-start | bytes 98312 | tf_op jit(solution)/shard_map/ppermute | solution.py:42
  32.7 2.4 %collective-permute-done.12 = f32[64,128]{1,0:T(8,128)S(1)} collective-permute-done((f32[64,128]{1,0:T(8,128)S(1)}, f32[64,128]{1,0:T(8,128)S(1)}, u32[]{:S(2)}, u32[]{:S(2)}) %collective-permute-start.12) | collective-permute-done | bytes 32800 | tf_op jit(solution)/shard_map/ppermute | solution.py:42
  36.3 2.3 %collective-permute-start.15 = (f32[136,128]{1,0:T(8,128)S(1)}, f32[136,128]{1,0:T(8,128)S(1)}, u32[]{:S(2)}, u32[]{:S(2)}) collective-permute-start(f32[136,128]{1,0:T(8,128)S(1)} %add.68), channel_id=1, source_target_pairs={{0,4},{1,5},{2,6},{3,7},{4,0},{5,1},{6,2},{7,3},{8,12},{9,13},{10,... | collective-permute-start | bytes 208904 | tf_op jit(solution)/shard_map/ppermute | solution.py:32
  39.4 3.1 %collective-permute-done.14 = f32[64,128]{1,0:T(8,128)S(1)} collective-permute-done((f32[64,128]{1,0:T(8,128)S(1)}, f32[64,128]{1,0:T(8,128)S(1)}, u32[]{:S(2)}, u32[]{:S(2)}) %collective-permute-start.14) | collective-permute-done | bytes 32800 | tf_op jit(solution)/shard_map/ppermute | solution.py:32
  42.6 1.4 %collective-permute-start.19 = (f32[136,128]{1,0:T(8,128)S(1)}, f32[136,128]{1,0:T(8,128)S(1)}, u32[]{:S(2)}, u32[]{:S(2)}) collective-permute-start(f32[136,128]{1,0:T(8,128)S(1)} %add.70), channel_id=1, source_target_pairs={{0,17},{1,16},{2,19},{3,18},{4,21},{5,20},{6,23},{7,22},{8,25},{9,... | collective-permute-start | bytes 208904 | tf_op jit(solution)/shard_map/ppermute | solution.py:42
  43.9 1.7 %collective-permute-start.18 = (f32[136,128]{1,0:T(8,128)S(1)}, f32[136,128]{1,0:T(8,128)S(1)}, u32[]{:S(2)}, u32[]{:S(2)}) collective-permute-start(f32[136,128]{1,0:T(8,128)S(1)} %add.70), channel_id=1, source_target_pairs={{0,1},{1,0},{2,3},{3,2},{4,5},{5,4},{6,7},{7,6},{8,9},{9,8},{10,11... | collective-permute-start | bytes 208904 | tf_op jit(solution)/shard_map/ppermute | solution.py:42
  46.1 1.3 %collective-permute-start.16 = (f32[64,128]{1,0:T(8,128)S(1)}, f32[64,128]{1,0:T(8,128)S(1)}, u32[]{:S(2)}, u32[]{:S(2)}) collective-permute-start(f32[64,128]{1,0:T(8,128)S(1)} %add.69), channel_id=1, source_target_pairs={{0,4},{1,5},{2,6},{3,7},{4,0},{5,1},{6,2},{7,3},{8,12},{9,13},{10,... | collective-permute-start | bytes 98312 | tf_op jit(solution)/shard_map/ppermute | solution.py:32
  47.5 3.8 %collective-permute-done.16 = f32[64,128]{1,0:T(8,128)S(1)} collective-permute-done((f32[64,128]{1,0:T(8,128)S(1)}, f32[64,128]{1,0:T(8,128)S(1)}, u32[]{:S(2)}, u32[]{:S(2)}) %collective-permute-start.16) | collective-permute-done | bytes 32800 | tf_op jit(solution)/shard_map/ppermute | solution.py:32
  52.5 2.0 %collective-permute-start.22 = (f32[64,128]{1,0:T(8,128)S(1)}, f32[64,128]{1,0:T(8,128)S(1)}, u32[]{:S(2)}, u32[]{:S(2)}) collective-permute-start(f32[64,128]{1,0:T(8,128)S(1)} %add.71), channel_id=1, source_target_pairs={{0,1},{1,0},{2,3},{3,2},{4,5},{5,4},{6,7},{7,6},{8,9},{9,8},{10,11... | collective-permute-start | bytes 98312 | tf_op jit(solution)/shard_map/ppermute | solution.py:42
  55.0 5.7 %level.1 = (f32[2,256,128]{2,1,0:T(8,128)S(1)}, f32[2,128,128]{2,1,0:T(8,128)S(1)}, f32[512,128]{1,0:T(8,128)S(1)}) custom-call(f32[4,136,128]{2,1,0:T(8,128)S(1)} %pad_maximum_fusion.even_ref, f32[4,136,128]{2,1,0:T(8,128)S(1)} %collective-permute-done.20.odd_ref), custom_call_target="tpu_custom_call" | custom-call | flops 3221225472 | tf_op jit(solution)/shard_map/level/pallas_call | solution.py:502
  60.8 1.3 %collective-permute-done.24.odd_ref = f32[4,64,128]{2,1,0:T(8,128)S(1)} collective-permute-done((f32[4,64,128]{2,1,0:T(8,128)S(1)}, f32[4,64,128]{2,1,0:T(8,128)S(1)}, u32[]{:S(2)}, u32[]{:S(2)}) %collective-permute-start.24) | collective-permute-done | bytes 131104 | tf_op jit(solution)/shard_map/ppermute | solution.py:32
  62.2 5.6 %merge.1 = (f32[32,512]{1,0:T(8,128)S(1)}, f32[32,512]{1,0:T(8,128)S(1)}, f32[32,512]{1,0:T(8,128)S(1)}, f32[32,512]{1,0:T(8,128)S(1)}, f32[512,128]{1,0:T(8,128)S(1)}) custom-call(f32[4,64,128]{2,1,0:T(8,128)S(1)} %pad_maximum_fusion.1.even_ref, f32[4,64,128]{2,1,0:T(8,128)S(1)} %collective-permute-done.24.odd_ref, ...), custom_call_target="tpu_custom_call" | custom-call | tf_op jit(solution)/shard_map/merge/pallas_call | solution.py:515
  68.0 1.5 %collective-permute-start.26 = (f32[32,512]{1,0:T(8,128)S(1)}, f32[32,512]{1,0:T(8,128)S(1)}, u32[]{:S(2)}, u32[]{:S(2)}) collective-permute-start(f32[32,512]{1,0:T(8,128)S(1)} %get-tuple-element.88), channel_id=1, source_target_pairs={{0,16},{8,24},{16,0},{24,8},{1,17},{9,25},{17,1},{25,9},{2,18},{10... | collective-permute-start | bytes 196616 | tf_op jit(solution)/shard_map/ppermute | solution.py:32
  70.6 1.7 %collective-permute-done.26.refs_2_ = f32[32,512]{1,0:T(8,128)S(1)} collective-permute-done((f32[32,512]{1,0:T(8,128)S(1)}, f32[32,512]{1,0:T(8,128)S(1)}, u32[]{:S(2)}, u32[]{:S(2)}) %collective-permute-start.26) | collective-permute-done | bytes 65568 | tf_op jit(solution)/shard_map/ppermute | solution.py:32
  72.4 1.3 %collective-permute-done.27.refs_3_ = f32[32,512]{1,0:T(8,128)S(1)} collective-permute-done((f32[32,512]{1,0:T(8,128)S(1)}, f32[32,512]{1,0:T(8,128)S(1)}, u32[]{:S(2)}, u32[]{:S(2)}) %collective-permute-start.27) | collective-permute-done | bytes 65568 | tf_op jit(solution)/shard_map/ppermute | solution.py:32
  (52 shorter events, 13.5 us)
Async XLA Ops:
  1.9 7.5 %collective-permute-start = (f32[64,128]{1,0:T(8,128)S(1)}, f32[64,128]{1,0:T(8,128)S(1)}, u32[]{:S(2)}, u32[]{:S(2)}) collective-permute-start(f32[64,128]{1,0:T(8,128)S(1)} %get-tuple-element.47), channel_id=1, source_target_pairs={{0,1},{1,0},{2,3},{3,2},{4,5},{5,4},{6,7},{7,6},{8,9},{9,8},{10,11... | collective-permute-start | bytes 98312 | tf_op jit(solution)/shard_map/ppermute | solution.py:404
  4.9 4.5 %collective-permute-start.1 = (f32[64,128]{1,0:T(8,128)S(1)}, f32[64,128]{1,0:T(8,128)S(1)}, u32[]{:S(2)}, u32[]{:S(2)}) collective-permute-start(f32[64,128]{1,0:T(8,128)S(1)} %get-tuple-element.48), channel_id=1, source_target_pairs={{1,2},{3,4},{5,6},{2,1},{4,3},{6,5},{9,10},{11,12},{13,14},{10,9},... | collective-permute-start | bytes 98312 | tf_op jit(solution)/shard_map/ppermute | solution.py:406
  10.2 9.2 %collective-permute-start.7 = (f32[512,128]{1,0:T(8,128)S(1)}, f32[512,128]{1,0:T(8,128)S(1)}, u32[]{:S(2)}, u32[]{:S(2)}) collective-permute-start(f32[512,128]{1,0:T(8,128)S(1)} %get-tuple-element.55.refs_1_), channel_id=1, source_target_pairs={{0,16},{8,24},{16,0},{24,8},{1,17},{9,25},{17,1},{25,9},{2,18},{10... | collective-permute-start | bytes 786440 | tf_op jit(solution)/shard_map/ppermute | solution.py:32
  11.7 12.4 %collective-permute-start.8 = (f32[512,128]{1,0:T(8,128)S(1)}, f32[512,128]{1,0:T(8,128)S(1)}, u32[]{:S(2)}, u32[]{:S(2)}) collective-permute-start(f32[512,128]{1,0:T(8,128)S(1)} %collective-permute-done.3.refs_3_), channel_id=1, source_target_pairs={{0,16},{8,24},{16,0},{24,8},{1,17},{9,25},{17,1},{25,9},{2,18},{10... | collective-permute-start | bytes 786440 | tf_op jit(solution)/shard_map/ppermute | solution.py:32
  14.0 5.4 %collective-permute-start.4 = (f32[136,128]{1,0:T(8,128)S(1)}, f32[136,128]{1,0:T(8,128)S(1)}, u32[]{:S(2)}, u32[]{:S(2)}) collective-permute-start(f32[136,128]{1,0:T(8,128)S(1)} %get-tuple-element.57), channel_id=1, source_target_pairs={{0,8},{1,9},{2,10},{3,11},{4,12},{5,13},{6,14},{7,15},{8,0},{9,1},... | collective-permute-start | bytes 208904 | tf_op jit(solution)/shard_map/ppermute | solution.py:42
  14.1 7.1 %collective-permute-start.5 = (f32[136,128]{1,0:T(8,128)S(1)}, f32[136,128]{1,0:T(8,128)S(1)}, u32[]{:S(2)}, u32[]{:S(2)}) collective-permute-start(f32[136,128]{1,0:T(8,128)S(1)} %get-tuple-element.58), channel_id=1, source_target_pairs={{0,1},{1,0},{2,3},{3,2},{4,5},{5,4},{6,7},{7,6},{8,9},{9,8},{10,11... | collective-permute-start | bytes 208904 | tf_op jit(solution)/shard_map/ppermute | solution.py:42
  18.4 4.1 %collective-permute-start.6 = (f32[136,128]{1,0:T(8,128)S(1)}, f32[136,128]{1,0:T(8,128)S(1)}, u32[]{:S(2)}, u32[]{:S(2)}) collective-permute-start(f32[136,128]{1,0:T(8,128)S(1)} %get-tuple-element.59), channel_id=1, source_target_pairs={{0,9},{1,8},{2,11},{3,10},{4,13},{5,12},{6,15},{7,14},{8,1},{9,0},... | collective-permute-start | bytes 208904 | tf_op jit(solution)/shard_map/ppermute | solution.py:42
  24.8 3.9 %collective-permute-start.9 = (f32[4,64,128]{2,1,0:T(8,128)S(1)}, f32[4,64,128]{2,1,0:T(8,128)S(1)}, u32[]{:S(2)}, u32[]{:S(2)}) collective-permute-start(f32[4,64,128]{2,1,0:T(8,128)S(1)} %get-tuple-element.63), channel_id=1, source_target_pairs={{0,8},{8,0},{16,24},{24,16},{1,9},{9,1},{17,25},{25,17},{2,10},{10... | collective-permute-start | bytes 393224 | tf_op jit(solution)/shard_map/ppermute | solution.py:32
  24.9 7.5 %collective-permute-start.13 = (f32[136,128]{1,0:T(8,128)S(1)}, f32[136,128]{1,0:T(8,128)S(1)}, u32[]{:S(2)}, u32[]{:S(2)}) collective-permute-start(f32[136,128]{1,0:T(8,128)S(1)} %add_add_fusion), channel_id=1, source_target_pairs={{0,2},{1,3},{2,0},{3,1},{4,6},{5,7},{6,4},{7,5},{8,10},{9,11},{10,... | collective-permute-start | bytes 208904 | tf_op jit(solution)/shard_map/ppermute | solution.py:32
  28.7 4.0 %collective-permute-start.10 = (f32[64,128]{1,0:T(8,128)S(1)}, f32[64,128]{1,0:T(8,128)S(1)}, u32[]{:S(2)}, u32[]{:S(2)}) collective-permute-start(f32[64,128]{1,0:T(8,128)S(1)} %get-tuple-element.92), channel_id=1, source_target_pairs={{0,16},{1,17},{2,18},{3,19},{4,20},{5,21},{6,22},{7,23},{8,24},{9,... | collective-permute-start | bytes 98312 | tf_op jit(solution)/shard_map/ppermute | solution.py:42
  30.3 4.8 %collective-permute-start.12 = (f32[64,128]{1,0:T(8,128)S(1)}, f32[64,128]{1,0:T(8,128)S(1)}, u32[]{:S(2)}, u32[]{:S(2)}) collective-permute-start(f32[64,128]{1,0:T(8,128)S(1)} %get-tuple-element.93), channel_id=1, source_target_pairs={{0,17},{1,16},{2,19},{3,18},{4,21},{5,20},{6,23},{7,22},{8,25},{9,... | collective-permute-start | bytes 98312 | tf_op jit(solution)/shard_map/ppermute | solution.py:42
  32.4 3.9 %collective-permute-start.11 = (f32[64,128]{1,0:T(8,128)S(1)}, f32[64,128]{1,0:T(8,128)S(1)}, u32[]{:S(2)}, u32[]{:S(2)}) collective-permute-start(f32[64,128]{1,0:T(8,128)S(1)} %get-tuple-element.94), channel_id=1, source_target_pairs={{0,1},{1,0},{2,3},{3,2},{4,5},{5,4},{6,7},{7,6},{8,9},{9,8},{10,11... | collective-permute-start | bytes 98312 | tf_op jit(solution)/shard_map/ppermute | solution.py:42
  36.3 6.2 %collective-permute-start.15 = (f32[136,128]{1,0:T(8,128)S(1)}, f32[136,128]{1,0:T(8,128)S(1)}, u32[]{:S(2)}, u32[]{:S(2)}) collective-permute-start(f32[136,128]{1,0:T(8,128)S(1)} %add.68), channel_id=1, source_target_pairs={{0,4},{1,5},{2,6},{3,7},{4,0},{5,1},{6,2},{7,3},{8,12},{9,13},{10,... | collective-permute-start | bytes 208904 | tf_op jit(solution)/shard_map/ppermute | solution.py:32
  38.6 3.9 %collective-permute-start.14 = (f32[64,128]{1,0:T(8,128)S(1)}, f32[64,128]{1,0:T(8,128)S(1)}, u32[]{:S(2)}, u32[]{:S(2)}) collective-permute-start(f32[64,128]{1,0:T(8,128)S(1)} %fusion.6), channel_id=1, source_target_pairs={{0,2},{1,3},{2,0},{3,1},{4,6},{5,7},{6,4},{7,5},{8,10},{9,11},{10,... | collective-permute-start | bytes 98312 | tf_op jit(solution)/shard_map/ppermute | solution.py:32
  42.6 8.7 %collective-permute-start.19 = (f32[136,128]{1,0:T(8,128)S(1)}, f32[136,128]{1,0:T(8,128)S(1)}, u32[]{:S(2)}, u32[]{:S(2)}) collective-permute-start(f32[136,128]{1,0:T(8,128)S(1)} %add.70), channel_id=1, source_target_pairs={{0,17},{1,16},{2,19},{3,18},{4,21},{5,20},{6,23},{7,22},{8,25},{9,... | collective-permute-start | bytes 208904 | tf_op jit(solution)/shard_map/ppermute | solution.py:42
  43.9 7.4 %collective-permute-start.18 = (f32[136,128]{1,0:T(8,128)S(1)}, f32[136,128]{1,0:T(8,128)S(1)}, u32[]{:S(2)}, u32[]{:S(2)}) collective-permute-start(f32[136,128]{1,0:T(8,128)S(1)} %add.70), channel_id=1, source_target_pairs={{0,1},{1,0},{2,3},{3,2},{4,5},{5,4},{6,7},{7,6},{8,9},{9,8},{10,11... | collective-permute-start | bytes 208904 | tf_op jit(solution)/shard_map/ppermute | solution.py:42
  45.6 5.7 %collective-permute-start.17 = (f32[136,128]{1,0:T(8,128)S(1)}, f32[136,128]{1,0:T(8,128)S(1)}, u32[]{:S(2)}, u32[]{:S(2)}) collective-permute-start(f32[136,128]{1,0:T(8,128)S(1)} %add.70), channel_id=1, source_target_pairs={{0,16},{1,17},{2,18},{3,19},{4,20},{5,21},{6,22},{7,23},{8,24},{9,... | collective-permute-start | bytes 208904 | tf_op jit(solution)/shard_map/ppermute | solution.py:42
  46.1 5.2 %collective-permute-start.16 = (f32[64,128]{1,0:T(8,128)S(1)}, f32[64,128]{1,0:T(8,128)S(1)}, u32[]{:S(2)}, u32[]{:S(2)}) collective-permute-start(f32[64,128]{1,0:T(8,128)S(1)} %add.69), channel_id=1, source_target_pairs={{0,4},{1,5},{2,6},{3,7},{4,0},{5,1},{6,2},{7,3},{8,12},{9,13},{10,... | collective-permute-start | bytes 98312 | tf_op jit(solution)/shard_map/ppermute | solution.py:32
  51.4 3.6 %collective-permute-start.20 = (f32[4,136,128]{2,1,0:T(8,128)S(1)}, f32[4,136,128]{2,1,0:T(8,128)S(1)}, u32[]{:S(2)}, u32[]{:S(2)}) collective-permute-start(f32[4,136,128]{2,1,0:T(8,128)S(1)} %pad_maximum_fusion.even_ref), channel_id=1, source_target_pairs={{0,8},{8,0},{16,24},{24,16},{1,9},{9,1},{17,25},{25,17},{2,10},{10... | collective-permute-start | bytes 835592 | tf_op jit(solution)/shard_map/ppermute | solution.py:32
  51.4 9.3 %collective-permute-start.23 = (f32[64,128]{1,0:T(8,128)S(1)}, f32[64,128]{1,0:T(8,128)S(1)}, u32[]{:S(2)}, u32[]{:S(2)}) collective-permute-start(f32[64,128]{1,0:T(8,128)S(1)} %add.71), channel_id=1, source_target_pairs={{0,17},{1,16},{2,19},{3,18},{4,21},{5,20},{6,23},{7,22},{8,25},{9,... | collective-permute-start | bytes 98312 | tf_op jit(solution)/shard_map/ppermute | solution.py:42
  52.5 8.3 %collective-permute-start.22 = (f32[64,128]{1,0:T(8,128)S(1)}, f32[64,128]{1,0:T(8,128)S(1)}, u32[]{:S(2)}, u32[]{:S(2)}) collective-permute-start(f32[64,128]{1,0:T(8,128)S(1)} %add.71), channel_id=1, source_target_pairs={{0,1},{1,0},{2,3},{3,2},{4,5},{5,4},{6,7},{7,6},{8,9},{9,8},{10,11... | collective-permute-start | bytes 98312 | tf_op jit(solution)/shard_map/ppermute | solution.py:42
  54.5 6.3 %collective-permute-start.21 = (f32[64,128]{1,0:T(8,128)S(1)}, f32[64,128]{1,0:T(8,128)S(1)}, u32[]{:S(2)}, u32[]{:S(2)}) collective-permute-start(f32[64,128]{1,0:T(8,128)S(1)} %add.71), channel_id=1, source_target_pairs={{0,16},{1,17},{2,18},{3,19},{4,20},{5,21},{6,22},{7,23},{8,24},{9,... | collective-permute-start | bytes 98312 | tf_op jit(solution)/shard_map/ppermute | solution.py:42
  68.0 4.4 %collective-permute-start.26 = (f32[32,512]{1,0:T(8,128)S(1)}, f32[32,512]{1,0:T(8,128)S(1)}, u32[]{:S(2)}, u32[]{:S(2)}) collective-permute-start(f32[32,512]{1,0:T(8,128)S(1)} %get-tuple-element.88), channel_id=1, source_target_pairs={{0,16},{8,24},{16,0},{24,8},{1,17},{9,25},{17,1},{25,9},{2,18},{10... | collective-permute-start | bytes 196616 | tf_op jit(solution)/shard_map/ppermute | solution.py:32
  69.5 4.1 %collective-permute-start.27 = (f32[32,512]{1,0:T(8,128)S(1)}, f32[32,512]{1,0:T(8,128)S(1)}, u32[]{:S(2)}, u32[]{:S(2)}) collective-permute-start(f32[32,512]{1,0:T(8,128)S(1)} %get-tuple-element.89), channel_id=1, source_target_pairs={{0,24},{8,16},{16,8},{24,0},{1,25},{9,17},{17,9},{25,1},{2,26},{10... | collective-permute-start | bytes 196616 | tf_op jit(solution)/shard_map/ppermute | solution.py:32
  (5 other events, 20.3 us)

commit v13 on v12

--- a/solution.py
+++ b/solution.py
@@ -152,14 +152,14 @@
 
 
 def pair_rows(cols, owners):
-    return 4 * cols + 8 * owners
+    return 2 * cols + 8 * owners
 
 
 def pair_kernel(parts, span, probes_ref, *refs):
     half = parts // 2
     owners = 2 * span
     mine, theirs, refs = refs[:half], refs[half:2 * half], refs[2 * half:]
-    outs, (wide, there, flat) = refs[:owners], refs[owners:]
+    outs, (wide, there, flat, products) = refs[:owners], refs[owners:]
     me, owner = positions(2, span)
     size, cols = mine[0].shape
     low = pl.ds(pl.multiple_of((me % 2) * cols, cols), cols)
@@ -175,12 +175,13 @@
     row, col = triangle(cols)
     flat[:cols, :] = gram[:cols, cols:]
     flat[cols:2 * cols, :] = jnp.where(row <= col, first, second)
-    flat[2 * cols:4 * cols, :] = dot_parts(left, split(there[...]), ((0,), (0,)))
+    products[...] = dot_parts(left, split(there[...]), ((0,), (0,)))
     diagonal = jnp.sum(jnp.where(row == col, second, 0.0), axis=0, keepdims=True)
-    flat[4 * cols:, :] = jnp.broadcast_to(diagonal, (flat.shape[0] - 4 * cols, cols))
-    share = flat.shape[0] // owners
+    flat[2 * cols:, :] = jnp.broadcast_to(diagonal, (flat.shape[0] - 2 * cols, cols))
+    share, rest = flat.shape[0] // owners, 2 * cols // owners
     for k, out in enumerate(outs):
-        out[...] = flat[pl.ds(pl.multiple_of((owner ^ k) * share, 8), share), :]
+        out[:share, :] = flat[pl.ds(pl.multiple_of((owner ^ k) * share, 8), share), :]
+        out[share:, :] = products[pl.ds(pl.multiple_of((owner ^ k) * rest, 8), rest), :]
 
 
 def positions(count, span):
@@ -270,7 +271,11 @@
         put(owner ^ k, (odd_ref if k % 2 else even_ref)[k // 2])
 
 
-def level_kernel(parts, span, even_ref, odd_ref, combine_ref, square_ref, product_ref, pairs):
+def pair_at(parts, step, j, core):
+    return j if step == parts // 2 else 2 * j + core
+
+
+def level_kernel(parts, span, even_ref, odd_ref, out_ref, pairs):
     cols = even_ref.shape[2]
     share = pairs.shape[1] // (2 * span)
 
@@ -281,35 +286,44 @@
     place_shares(parts, span, even_ref, odd_ref, put)
     row, col = triangle(cols)
     grams = []
-    for p in range(parts // 2):
+    step = out_ref.shape[0]
+    for j in range(step):
+        p = pair_at(parts, step, j, lax.axis_index("tm") % 2)
         packed = pairs[p, cols:2 * cols, :]
         turned_back = packed.T
         first = jnp.where(row <= col, packed, turned_back)
         between = pairs[p, :cols, :]
         second = jnp.where(row > col, packed, turned_back)
-        second = jnp.where(row == col, pairs[p, 4 * cols:4 * cols + 1, :], second)
+        second = jnp.where(row == col, pairs[p, 2 * cols:2 * cols + 1, :], second)
         grams.append(jnp.concatenate([
             jnp.concatenate([first, between], axis=1), jnp.concatenate([between.T, second], axis=1)
         ], axis=0))
-        product_ref[2 * p * cols:2 * (p + 1) * cols, :] = pairs[p, 2 * cols:4 * cols, :]
-    for p, (gram, combine) in enumerate(zip(grams, combine_of(grams))):
-        combine_ref[p] = combine
-        square_ref[p] = split_dot(combine, split_dot(gram, combine), ((0,), (0,)))
-
-
-def merge_kernel(parts, span, even_ref, odd_ref, combine_ref, square_ref, high_ref, low_ref, *refs):
-    outs, (weight_ref, cross, turned) = refs[:parts], refs[parts:]
+    for j, (gram, combine) in enumerate(zip(grams, combine_of(grams))):
+        out_ref[j, :2 * cols, :] = combine
+        out_ref[j, 2 * cols:, :] = split_dot(combine, split_dot(gram, combine), ((0,), (0,)))
+
+
+def merge_kernel(parts, span, even_ref, odd_ref, mine_ref, theirs_ref, high_ref, low_ref, *refs):
+    outs, (weight_ref, product_ref, level, cross, turned) = refs[:parts], refs[parts:]
     me = lax.axis_index("tm")
     cols = even_ref.shape[2]
     share = cross.shape[0] // (parts * span)
 
+    rest = 2 * cols // (2 * span)
+
     def put(there, rows):
-        cross[pl.ds(pl.multiple_of(there * share, 8), share), :] = rows
+        cross[pl.ds(pl.multiple_of(there * share, 8), share), :] = rows[:share]
+        at = ((there % parts) // 2) * 2 * cols + (there % 2 + 2 * (there // parts)) * rest
+        product_ref[pl.ds(pl.multiple_of(at, 8), rest), :] = rows[share:]
 
     place_shares(parts, span, even_ref, odd_ref, put)
     where = {ab: j * cols for j, ab in enumerate(cross_order(parts))}
-    weights = [combine_ref[p] for p in range(parts // 2)]
-    blocks = {(p, p): square_ref[p] for p in range(parts // 2)}
+    step = mine_ref.shape[0]
+    for j in range(step):
+        level[pair_at(parts, step, j, 1 - me % 2)] = theirs_ref[j]
+        level[pair_at(parts, step, j, me % 2)] = mine_ref[j]
+    weights = [level[p, :2 * cols, :] for p in range(parts // 2)]
+    blocks = {(p, p): level[p, 2 * cols:, :] for p in range(parts // 2)}
     for p in range(parts // 2):
         for q in range(p + 1, parts // 2):
             between = jnp.concatenate([
@@ -438,15 +452,17 @@
         far[k + 1] = swap(theirs[k], "tm", k)
 
     owners = 2 * span
+    pair_size = pair_rows(cols, owners) // owners
     sums = pl.pallas_call(
         functools.partial(pair_kernel, parts, span),
-        out_shape=[shape(pair_rows(cols, owners) // owners, cols)] * owners,
+        out_shape=[shape(pair_size + 2 * cols // owners, cols)] * owners,
         in_specs=[whole()] * (parts + 1),
         out_specs=[whole()] * owners,
         scratch_shapes=[
             pltpu.VMEM((cells // 2, 2 * cols), F32),
             pltpu.VMEM((cells // 2, cols), F32),
             pltpu.VMEM((pair_rows(cols, owners), cols), F32),
+            pltpu.VMEM((2 * cols, cols), F32),
         ],
         compiler_params=params(),
         cost_estimate=pl.CostEstimate(flops=0, bytes_accessed=0, transcendentals=0),
@@ -482,11 +498,13 @@
     for bit in bits[:1]:
         pair_share = pair_share + swap(pair_share, "space", bit)
     mine, pair_share = lax.optimization_barrier((mine, pair_share))
+    pair_share, product_share = pair_share[:pair_size], pair_share[pair_size:]
     for bit in bits[1:]:
         pair_share = pair_share + swap(pair_share, "space", bit)
     for bit in bits[:1]:
         mine = mine + swap(mine, "space", bit)
     mine, pair_share = lax.optimization_barrier((mine, pair_share))
+    mine = jnp.concatenate([mine, product_share], axis=0)
     for bit in bits[1:]:
         mine = mine + swap(mine, "space", bit)
 
@@ -499,28 +517,33 @@
 
     mine, *pair_shares = lax.optimization_barrier([mine] + spread(pair_share))
 
-    combines, squares, products = pl.pallas_call(
+    half = parts // 2
+    level = pl.pallas_call(
         functools.partial(level_kernel, parts, span),
-        out_shape=[shape(parts // 2, 2 * cols, cols), shape(parts // 2, cols, cols), shape(parts * cols, cols)],
+        out_shape=shape(half // 2 if half % 2 == 0 else half, 3 * cols, cols),
         in_specs=[whole()] * 2,
-        out_specs=[whole()] * 3,
-        scratch_shapes=[pltpu.VMEM((parts // 2, pair_rows(cols, 2 * span), cols), F32)],
+        out_specs=whole(),
+        scratch_shapes=[pltpu.VMEM((half, pair_rows(cols, 2 * span), cols), F32)],
         compiler_params=params(),
         cost_estimate=pl.CostEstimate(flops=parts * SIGN_STEPS * 6 * (2 * cols) ** 3, bytes_accessed=0, transcendentals=0),
         name="level",
     )(*gathered(pair_shares))
-
-    combines, *shares = lax.optimization_barrier([combines] + spread(mine))
+    level, *shares = lax.optimization_barrier([level] + spread(mine))
+    other_level = swap(level, "tm", 1)
     width = cols // parts
-    *sent, weight = pl.pallas_call(
+    *sent, weight, products = pl.pallas_call(
         functools.partial(merge_kernel, parts, span),
-        out_shape=[shape(width, piece)] * parts + [shape(parts * cols, cols)],
+        out_shape=[shape(width, piece)] * parts + [shape(parts * cols, cols)] * 2,
         in_specs=[whole()] * 6,
-        out_specs=[whole()] * (parts + 1),
-        scratch_shapes=[pltpu.VMEM((blocks * cols, cols), F32), pltpu.VMEM((cols, piece), F32)],
+        out_specs=[whole()] * (parts + 2),
+        scratch_shapes=[
+            pltpu.VMEM((half, 3 * cols, cols), F32),
+            pltpu.VMEM((blocks * cols, cols), F32),
+            pltpu.VMEM((cols, piece), F32),
+        ],
         compiler_params=params(),
         name="merge",
-    )(*gathered(shares), combines, squares, high, low)
+    )(*gathered(shares), level, other_level, high, low)
     coefficients = pl.pallas_call(
         functools.partial(coefficient_kernel, parts),
         out_shape=shape(width, cols),

time: 74.8 us -> 73.5 us (0.983)
  waiting for transfers between devices: 20.8 us -> 19.9 us
    ppermute x14 -> x15, waiting for transfers between devices: 13.8 us -> 10.9 us  [swap(): return lax.ppermute(x, axis, [(i, i ^ mask) for i in range(count)])]
    ppermute x12, waiting for transfers between devices: 7.02 us -> 8.98 us  [swap_both(): return lax.ppermute(x, ('tm', 'space'), route)]
    ppermute x14 -> x15, starting transfers between devices: 13.5 us -> 13.6 us  [swap(): return lax.ppermute(x, axis, [(i, i ^ mask) for i in range(count)])]
  transfers between devices with their start and end apart: 28 -> 29, of which waited for: 12 -> 14; matrix products, arithmetic and copies ran while one was open for 0% -> 0% of each run, Pallas kernels for 16% -> 15%
where the time goes in v13:
time: 73.5 us; the launch traced here: 73.3 us
  starting transfers between devices  32.5 us (44%)
  Pallas kernels  19.9 us (27%)
  waiting for transfers between devices  19.9 us (27%)
  between operations  0.86 us (1%)
    ppermute x12, starting transfers between devices, swap_both(): return lax.ppermute(x, ('tm', 'space'), route)  15.3 us
    ppermute x15, starting transfers between devices, swap(): return lax.ppermute(x, axis, [(i, i ^ mask) for i in range(count)])  13.6 us
    ppermute x15, waiting for transfers between devices, swap(): return lax.ppermute(x, axis, [(i, i ^ mask) for i in range(count)])  10.9 us
    ppermute x12, waiting for transfers between devices, swap_both(): return lax.ppermute(x, ('tm', 'space'), route)  8.98 us
    pallas_call x1, Pallas kernels, local(): pl.pallas_call(functools.partial(merge_kernel, parts, span), out_shape=[s...  5.69 us
    pallas_call x1, Pallas kernels, local(): pl.pallas_call(functools.partial(level_kernel, parts, span), out_shape=sh...  5.15 us
    pallas_call x1, Pallas kernels, local(): pl.pallas_call(functools.partial(filter_kernel, parts), out_shape=[shape(...  3.87 us
    ppermute x1, starting transfers between devices, local(): lax.ppermute(to_near, 'space', [(i, i ^ 1) for i in range(patches) if i ^...  3 us
  transfers between devices with their start and end apart: 29, of which 14 were waited for; matrix products, arithmetic and copies ran while one was open for 0% of the time, Pallas kernels for 15%

profile of v13, /device:TPU:0, one launch (start us, length us, event | category | flops | bytes accessed | tf_op | source)
XLA Modules:
  0.0 73.3 jit_solution(13063661753752803077)
XLA Ops:
  0.6 1.2 %edge.1 = (f32[64,128]{1,0:T(8,128)S(1)}, f32[64,128]{1,0:T(8,128)S(1)}) custom-call(f32[6]{0:T(128)} %rtaps_ref.3, f32[6]{0:T(128)} %ctaps_ref.3, f32[64,128,128]{2,1,0:T(8,128)} %snap_hbm.1, f32[64,128,128]{2,1,0:T(8,128)} %snap_hbm.1, s32[64,128]{1,0:T(8,128)} %mask_ref.1, s32[64,128]{1,0:T(8,128)} %mask_ref.1), custom_call_target="tpu_custom_call" | custom-call | tf_op jit(solution)/shard_map/edge/pallas_call | solution.py:402
  1.9 3.0 %collective-permute-start = (f32[64,128]{1,0:T(8,128)S(1)}, f32[64,128]{1,0:T(8,128)S(1)}, u32[]{:S(2)}, u32[]{:S(2)}) collective-permute-start(f32[64,128]{1,0:T(8,128)S(1)} %get-tuple-element.45), channel_id=1, source_target_pairs={{0,1},{1,0},{2,3},{3,2},{4,5},{5,4},{6,7},{7,6},{8,9},{9,8},{10,11... | collective-permute-start | bytes 98312 | tf_op jit(solution)/shard_map/ppermute | solution.py:418
  5.6 3.9 %filter.1 = (f32[512,128]{1,0:T(8,128)S(1)}, f32[512,128]{1,0:T(8,128)S(1)}, f32[512,128]{1,0:T(8,128)S(1)}, f32[512,128]{1,0:T(8,128)S(1)}) custom-call(f32[6]{0:T(128)} %rtaps_ref.3, f32[6]{0:T(128)} %ctaps_ref.3, f32[64,128,128]{2,1,0:T(8,128)} %snap_hbm.1, s32[64,128]{1,0:T(8,128)} %mask_ref.1), custom_call_target="tpu_custom_call" | custom-call | bytes 4194304 | tf_op jit(solution)/shard_map/filter/pallas_call | solution.py:422
  10.2 1.5 %collective-permute-start.7 = (f32[512,128]{1,0:T(8,128)S(1)}, f32[512,128]{1,0:T(8,128)S(1)}, u32[]{:S(2)}, u32[]{:S(2)}) collective-permute-start(f32[512,128]{1,0:T(8,128)S(1)} %get-tuple-element.53.refs_1_), channel_id=1, source_target_pairs={{0,16},{8,24},{16,0},{24,8},{1,17},{9,25},{17,1},{25,9},{2,18},{10... | collective-permute-start | bytes 786440 | tf_op jit(solution)/shard_map/ppermute | solution.py:32
  12.8 1.2 %pair.1 = (f32[136,128]{1,0:T(8,128)S(1)}, f32[136,128]{1,0:T(8,128)S(1)}, f32[136,128]{1,0:T(8,128)S(1)}, f32[136,128]{1,0:T(8,128)S(1)}) custom-call(f32[2048,128]{1,0:T(8,128)S(1)} %bitcast.24, f32[512,128]{1,0:T(8,128)S(1)} %get-tuple-element.51.refs_0_, f32[512,128]{1,0:T(8,128)S(1)} %get-tuple-element.53.refs_1_, ...), custom_call_target="tpu_custom_call" | custom-call | tf_op jit(solution)/shard_map/pair/pallas_call | solution.py:456
  14.1 4.3 %collective-permute-start.5 = (f32[136,128]{1,0:T(8,128)S(1)}, f32[136,128]{1,0:T(8,128)S(1)}, u32[]{:S(2)}, u32[]{:S(2)}) collective-permute-start(f32[136,128]{1,0:T(8,128)S(1)} %get-tuple-element.56), channel_id=1, source_target_pairs={{0,1},{1,0},{2,3},{3,2},{4,5},{5,4},{6,7},{7,6},{8,9},{9,8},{10,11... | collective-permute-start | bytes 208904 | tf_op jit(solution)/shard_map/ppermute | solution.py:42
  19.4 1.8 %collective-permute-done.5 = f32[136,128]{1,0:T(8,128)S(1)} collective-permute-done((f32[136,128]{1,0:T(8,128)S(1)}, f32[136,128]{1,0:T(8,128)S(1)}, u32[]{:S(2)}, u32[]{:S(2)}) %collective-permute-start.5) | collective-permute-done | bytes 69664 | tf_op jit(solution)/shard_map/ppermute | solution.py:42
  21.2 1.4 %collective-permute-done.6 = f32[136,128]{1,0:T(8,128)S(1)} collective-permute-done((f32[136,128]{1,0:T(8,128)S(1)}, f32[136,128]{1,0:T(8,128)S(1)}, u32[]{:S(2)}, u32[]{:S(2)}) %collective-permute-start.6) | collective-permute-done | bytes 69664 | tf_op jit(solution)/shard_map/ppermute | solution.py:42
  22.6 1.6 %collective-permute-done.8.refs_3_ = f32[512,128]{1,0:T(8,128)S(1)} collective-permute-done((f32[512,128]{1,0:T(8,128)S(1)}, f32[512,128]{1,0:T(8,128)S(1)}, u32[]{:S(2)}, u32[]{:S(2)}) %collective-permute-start.8) | collective-permute-done | bytes 262176 | tf_op jit(solution)/shard_map/ppermute | solution.py:32
  24.9 3.8 %collective-permute-start.13 = (f32[136,128]{1,0:T(8,128)S(1)}, f32[136,128]{1,0:T(8,128)S(1)}, u32[]{:S(2)}, u32[]{:S(2)}) collective-permute-start(f32[136,128]{1,0:T(8,128)S(1)} %add_add_fusion), channel_id=1, source_target_pairs={{0,2},{1,3},{2,0},{3,1},{4,6},{5,7},{6,4},{7,5},{8,10},{9,11},{10,... | collective-permute-start | bytes 208904 | tf_op jit(solution)/shard_map/ppermute | solution.py:32
  28.7 1.6 %collective-permute-start.10 = (f32[64,128]{1,0:T(8,128)S(1)}, f32[64,128]{1,0:T(8,128)S(1)}, u32[]{:S(2)}, u32[]{:S(2)}) collective-permute-start(f32[64,128]{1,0:T(8,128)S(1)} %get-tuple-element.88), channel_id=1, source_target_pairs={{0,16},{1,17},{2,18},{3,19},{4,20},{5,21},{6,22},{7,23},{8,24},{9,... | collective-permute-start | bytes 98312 | tf_op jit(solution)/shard_map/ppermute | solution.py:42
  30.3 2.1 %collective-permute-start.12 = (f32[64,128]{1,0:T(8,128)S(1)}, f32[64,128]{1,0:T(8,128)S(1)}, u32[]{:S(2)}, u32[]{:S(2)}) collective-permute-start(f32[64,128]{1,0:T(8,128)S(1)} %get-tuple-element.89), channel_id=1, source_target_pairs={{0,17},{1,16},{2,19},{3,18},{4,21},{5,20},{6,23},{7,22},{8,25},{9,... | collective-permute-start | bytes 98312 | tf_op jit(solution)/shard_map/ppermute | solution.py:42
  32.7 2.4 %collective-permute-done.12 = f32[64,128]{1,0:T(8,128)S(1)} collective-permute-done((f32[64,128]{1,0:T(8,128)S(1)}, f32[64,128]{1,0:T(8,128)S(1)}, u32[]{:S(2)}, u32[]{:S(2)}) %collective-permute-start.12) | collective-permute-done | bytes 32800 | tf_op jit(solution)/shard_map/ppermute | solution.py:42
  36.3 2.3 %collective-permute-start.15 = (f32[72,128]{1,0:T(8,128)S(1)}, f32[72,128]{1,0:T(8,128)S(1)}, u32[]{:S(2)}, u32[]{:S(2)}) collective-permute-start(f32[72,128]{1,0:T(8,128)S(1)} %slice.38), channel_id=1, source_target_pairs={{0,4},{1,5},{2,6},{3,7},{4,0},{5,1},{6,2},{7,3},{8,12},{9,13},{10,... | collective-permute-start | bytes 110600 | tf_op jit(solution)/shard_map/ppermute | solution.py:32
  39.4 3.1 %collective-permute-done.14 = f32[64,128]{1,0:T(8,128)S(1)} collective-permute-done((f32[64,128]{1,0:T(8,128)S(1)}, f32[64,128]{1,0:T(8,128)S(1)}, u32[]{:S(2)}, u32[]{:S(2)}) %collective-permute-start.14) | collective-permute-done | bytes 32800 | tf_op jit(solution)/shard_map/ppermute | solution.py:32
  43.6 1.3 %collective-permute-start.19 = (f32[72,128]{1,0:T(8,128)S(1)}, f32[72,128]{1,0:T(8,128)S(1)}, u32[]{:S(2)}, u32[]{:S(2)}) collective-permute-start(f32[72,128]{1,0:T(8,128)S(1)} %slice_add_fusion.4), channel_id=1, source_target_pairs={{0,17},{1,16},{2,19},{3,18},{4,21},{5,20},{6,23},{7,22},{8,25},{9,... | collective-permute-start | bytes 110600 | tf_op jit(solution)/shard_map/ppermute | solution.py:42
  44.9 1.6 %collective-permute-start.18 = (f32[72,128]{1,0:T(8,128)S(1)}, f32[72,128]{1,0:T(8,128)S(1)}, u32[]{:S(2)}, u32[]{:S(2)}) collective-permute-start(f32[72,128]{1,0:T(8,128)S(1)} %slice_add_fusion.4), channel_id=1, source_target_pairs={{0,1},{1,0},{2,3},{3,2},{4,5},{5,4},{6,7},{7,6},{8,9},{9,8},{10,11... | collective-permute-start | bytes 110600 | tf_op jit(solution)/shard_map/ppermute | solution.py:42
  47.1 1.5 %collective-permute-done.16 = f32[128,128]{1,0:T(8,128)S(1)} collective-permute-done((f32[128,128]{1,0:T(8,128)S(1)}, f32[128,128]{1,0:T(8,128)S(1)}, u32[]{:S(2)}, u32[]{:S(2)}) %collective-permute-start.16) | collective-permute-done | bytes 65568 | tf_op jit(solution)/shard_map/ppermute | solution.py:32
  48.9 1.6 %collective-permute-done.17 = f32[72,128]{1,0:T(8,128)S(1)} collective-permute-done((f32[72,128]{1,0:T(8,128)S(1)}, f32[72,128]{1,0:T(8,128)S(1)}, u32[]{:S(2)}, u32[]{:S(2)}) %collective-permute-start.17) | collective-permute-done | bytes 36896 | tf_op jit(solution)/shard_map/ppermute | solution.py:42
  52.6 1.5 %collective-permute-start.21 = (f32[128,128]{1,0:T(8,128)S(1)}, f32[128,128]{1,0:T(8,128)S(1)}, u32[]{:S(2)}, u32[]{:S(2)}) collective-permute-start(f32[128,128]{1,0:T(8,128)S(1)} %fusion.7), channel_id=1, source_target_pairs={{0,16},{1,17},{2,18},{3,19},{4,20},{5,21},{6,22},{7,23},{8,24},{9,... | collective-permute-start | bytes 196616 | tf_op jit(solution)/shard_map/ppermute | solution.py:42
  54.2 5.1 %level.1.mine_ref = f32[1,384,128]{2,1,0:T(8,128)S(1)} custom-call(f32[4,72,128]{2,1,0:T(8,128)S(1)} %pad_maximum_fusion.1.even_ref, f32[4,72,128]{2,1,0:T(8,128)S(1)} %collective-permute-done.20.odd_ref), custom_call_target="tpu_custom_call" | custom-call | flops 3221225472 | tf_op jit(solution)/shard_map/level/pallas_call | solution.py:521
  60.0 1.3 %collective-permute-done.25.theirs_ref = f32[1,384,128]{2,1,0:T(8,128)S(1)} collective-permute-done((f32[1,384,128]{2,1,0:T(8,128)S(1)}, f32[1,384,128]{2,1,0:T(8,128)S(1)}, u32[]{:S(2)}, u32[]{:S(2)}) %collective-permute-start.25) | collective-permute-done | bytes 196640 | tf_op jit(solution)/shard_map/ppermute | solution.py:32
  61.3 5.7 %merge.1 = (f32[32,512]{1,0:T(8,128)S(1)}, f32[32,512]{1,0:T(8,128)S(1)}, f32[32,512]{1,0:T(8,128)S(1)}, f32[32,512]{1,0:T(8,128)S(1)}, f32[512,128]{1,0:T(8,128)S(1)}, /*index=5*/f32[512,128]{1,0:T(8,128)S(1)}) custom-call(f32[4,128,128]{2,1,0:T(8,128)S(1)} %pad_maximum_fusion.even_ref, f32[4,128,128]{2,1,0:T(8,128)S(1)} %collective-permute-done.24.odd_ref, ...), custom_call_target="tpu_custom_call" | custom-call | tf_op jit(solution)/shard_map/merge/pallas_call | solution.py:534
  69.8 2.3 %collective-permute-done.27.refs_2_ = f32[32,512]{1,0:T(8,128)S(1)} collective-permute-done((f32[32,512]{1,0:T(8,128)S(1)}, f32[32,512]{1,0:T(8,128)S(1)}, u32[]{:S(2)}, u32[]{:S(2)}) %collective-permute-start.27) | collective-permute-done | bytes 65568 | tf_op jit(solution)/shard_map/ppermute | solution.py:32
  (57 shorter events, 15.2 us)
Async XLA Ops:
  1.9 7.5 %collective-permute-start = (f32[64,128]{1,0:T(8,128)S(1)}, f32[64,128]{1,0:T(8,128)S(1)}, u32[]{:S(2)}, u32[]{:S(2)}) collective-permute-start(f32[64,128]{1,0:T(8,128)S(1)} %get-tuple-element.45), channel_id=1, source_target_pairs={{0,1},{1,0},{2,3},{3,2},{4,5},{5,4},{6,7},{7,6},{8,9},{9,8},{10,11... | collective-permute-start | bytes 98312 | tf_op jit(solution)/shard_map/ppermute | solution.py:418
  4.9 4.5 %collective-permute-start.1 = (f32[64,128]{1,0:T(8,128)S(1)}, f32[64,128]{1,0:T(8,128)S(1)}, u32[]{:S(2)}, u32[]{:S(2)}) collective-permute-start(f32[64,128]{1,0:T(8,128)S(1)} %get-tuple-element.46), channel_id=1, source_target_pairs={{1,2},{3,4},{5,6},{2,1},{4,3},{6,5},{9,10},{11,12},{13,14},{10,9},... | collective-permute-start | bytes 98312 | tf_op jit(solution)/shard_map/ppermute | solution.py:420
  10.2 9.2 %collective-permute-start.7 = (f32[512,128]{1,0:T(8,128)S(1)}, f32[512,128]{1,0:T(8,128)S(1)}, u32[]{:S(2)}, u32[]{:S(2)}) collective-permute-start(f32[512,128]{1,0:T(8,128)S(1)} %get-tuple-element.53.refs_1_), channel_id=1, source_target_pairs={{0,16},{8,24},{16,0},{24,8},{1,17},{9,25},{17,1},{25,9},{2,18},{10... | collective-permute-start | bytes 786440 | tf_op jit(solution)/shard_map/ppermute | solution.py:32
  11.7 12.4 %collective-permute-start.8 = (f32[512,128]{1,0:T(8,128)S(1)}, f32[512,128]{1,0:T(8,128)S(1)}, u32[]{:S(2)}, u32[]{:S(2)}) collective-permute-start(f32[512,128]{1,0:T(8,128)S(1)} %collective-permute-done.3.refs_3_), channel_id=1, source_target_pairs={{0,16},{8,24},{16,0},{24,8},{1,17},{9,25},{17,1},{25,9},{2,18},{10... | collective-permute-start | bytes 786440 | tf_op jit(solution)/shard_map/ppermute | solution.py:32
  14.0 5.4 %collective-permute-start.4 = (f32[136,128]{1,0:T(8,128)S(1)}, f32[136,128]{1,0:T(8,128)S(1)}, u32[]{:S(2)}, u32[]{:S(2)}) collective-permute-start(f32[136,128]{1,0:T(8,128)S(1)} %get-tuple-element.55), channel_id=1, source_target_pairs={{0,8},{1,9},{2,10},{3,11},{4,12},{5,13},{6,14},{7,15},{8,0},{9,1},... | collective-permute-start | bytes 208904 | tf_op jit(solution)/shard_map/ppermute | solution.py:42
  14.1 7.1 %collective-permute-start.5 = (f32[136,128]{1,0:T(8,128)S(1)}, f32[136,128]{1,0:T(8,128)S(1)}, u32[]{:S(2)}, u32[]{:S(2)}) collective-permute-start(f32[136,128]{1,0:T(8,128)S(1)} %get-tuple-element.56), channel_id=1, source_target_pairs={{0,1},{1,0},{2,3},{3,2},{4,5},{5,4},{6,7},{7,6},{8,9},{9,8},{10,11... | collective-permute-start | bytes 208904 | tf_op jit(solution)/shard_map/ppermute | solution.py:42
  18.4 4.1 %collective-permute-start.6 = (f32[136,128]{1,0:T(8,128)S(1)}, f32[136,128]{1,0:T(8,128)S(1)}, u32[]{:S(2)}, u32[]{:S(2)}) collective-permute-start(f32[136,128]{1,0:T(8,128)S(1)} %get-tuple-element.57), channel_id=1, source_target_pairs={{0,9},{1,8},{2,11},{3,10},{4,13},{5,12},{6,15},{7,14},{8,1},{9,0},... | collective-permute-start | bytes 208904 | tf_op jit(solution)/shard_map/ppermute | solution.py:42
  24.8 3.9 %collective-permute-start.9 = (f32[4,64,128]{2,1,0:T(8,128)S(1)}, f32[4,64,128]{2,1,0:T(8,128)S(1)}, u32[]{:S(2)}, u32[]{:S(2)}) collective-permute-start(f32[4,64,128]{2,1,0:T(8,128)S(1)} %get-tuple-element.61), channel_id=1, source_target_pairs={{0,8},{8,0},{16,24},{24,16},{1,9},{9,1},{17,25},{25,17},{2,10},{10... | collective-permute-start | bytes 393224 | tf_op jit(solution)/shard_map/ppermute | solution.py:32
  24.9 7.5 %collective-permute-start.13 = (f32[136,128]{1,0:T(8,128)S(1)}, f32[136,128]{1,0:T(8,128)S(1)}, u32[]{:S(2)}, u32[]{:S(2)}) collective-permute-start(f32[136,128]{1,0:T(8,128)S(1)} %add_add_fusion), channel_id=1, source_target_pairs={{0,2},{1,3},{2,0},{3,1},{4,6},{5,7},{6,4},{7,5},{8,10},{9,11},{10,... | collective-permute-start | bytes 208904 | tf_op jit(solution)/shard_map/ppermute | solution.py:32
  28.7 4.0 %collective-permute-start.10 = (f32[64,128]{1,0:T(8,128)S(1)}, f32[64,128]{1,0:T(8,128)S(1)}, u32[]{:S(2)}, u32[]{:S(2)}) collective-permute-start(f32[64,128]{1,0:T(8,128)S(1)} %get-tuple-element.88), channel_id=1, source_target_pairs={{0,16},{1,17},{2,18},{3,19},{4,20},{5,21},{6,22},{7,23},{8,24},{9,... | collective-permute-start | bytes 98312 | tf_op jit(solution)/shard_map/ppermute | solution.py:42
  30.3 4.8 %collective-permute-start.12 = (f32[64,128]{1,0:T(8,128)S(1)}, f32[64,128]{1,0:T(8,128)S(1)}, u32[]{:S(2)}, u32[]{:S(2)}) collective-permute-start(f32[64,128]{1,0:T(8,128)S(1)} %get-tuple-element.89), channel_id=1, source_target_pairs={{0,17},{1,16},{2,19},{3,18},{4,21},{5,20},{6,23},{7,22},{8,25},{9,... | collective-permute-start | bytes 98312 | tf_op jit(solution)/shard_map/ppermute | solution.py:42
  32.4 3.9 %collective-permute-start.11 = (f32[64,128]{1,0:T(8,128)S(1)}, f32[64,128]{1,0:T(8,128)S(1)}, u32[]{:S(2)}, u32[]{:S(2)}) collective-permute-start(f32[64,128]{1,0:T(8,128)S(1)} %get-tuple-element.90), channel_id=1, source_target_pairs={{0,1},{1,0},{2,3},{3,2},{4,5},{5,4},{6,7},{7,6},{8,9},{9,8},{10,11... | collective-permute-start | bytes 98312 | tf_op jit(solution)/shard_map/ppermute | solution.py:42
  36.3 6.2 %collective-permute-start.15 = (f32[72,128]{1,0:T(8,128)S(1)}, f32[72,128]{1,0:T(8,128)S(1)}, u32[]{:S(2)}, u32[]{:S(2)}) collective-permute-start(f32[72,128]{1,0:T(8,128)S(1)} %slice.38), channel_id=1, source_target_pairs={{0,4},{1,5},{2,6},{3,7},{4,0},{5,1},{6,2},{7,3},{8,12},{9,13},{10,... | collective-permute-start | bytes 110600 | tf_op jit(solution)/shard_map/ppermute | solution.py:32
  38.6 3.9 %collective-permute-start.14 = (f32[64,128]{1,0:T(8,128)S(1)}, f32[64,128]{1,0:T(8,128)S(1)}, u32[]{:S(2)}, u32[]{:S(2)}) collective-permute-start(f32[64,128]{1,0:T(8,128)S(1)} %fusion.6), channel_id=1, source_target_pairs={{0,2},{1,3},{2,0},{3,1},{4,6},{5,7},{6,4},{7,5},{8,10},{9,11},{10,... | collective-permute-start | bytes 98312 | tf_op jit(solution)/shard_map/ppermute | solution.py:32
  42.6 5.9 %collective-permute-start.16 = (f32[128,128]{1,0:T(8,128)S(1)}, f32[128,128]{1,0:T(8,128)S(1)}, u32[]{:S(2)}, u32[]{:S(2)}) collective-permute-start(f32[128,128]{1,0:T(8,128)S(1)} %pad_maximum_fusion.2), channel_id=1, source_target_pairs={{0,4},{1,5},{2,6},{3,7},{4,0},{5,1},{6,2},{7,3},{8,12},{9,13},{10,... | collective-permute-start | bytes 196616 | tf_op jit(solution)/shard_map/ppermute | solution.py:32
  43.6 5.0 %collective-permute-start.19 = (f32[72,128]{1,0:T(8,128)S(1)}, f32[72,128]{1,0:T(8,128)S(1)}, u32[]{:S(2)}, u32[]{:S(2)}) collective-permute-start(f32[72,128]{1,0:T(8,128)S(1)} %slice_add_fusion.4), channel_id=1, source_target_pairs={{0,17},{1,16},{2,19},{3,18},{4,21},{5,20},{6,23},{7,22},{8,25},{9,... | collective-permute-start | bytes 110600 | tf_op jit(solution)/shard_map/ppermute | solution.py:42
  44.9 4.0 %collective-permute-start.18 = (f32[72,128]{1,0:T(8,128)S(1)}, f32[72,128]{1,0:T(8,128)S(1)}, u32[]{:S(2)}, u32[]{:S(2)}) collective-permute-start(f32[72,128]{1,0:T(8,128)S(1)} %slice_add_fusion.4), channel_id=1, source_target_pairs={{0,1},{1,0},{2,3},{3,2},{4,5},{5,4},{6,7},{7,6},{8,9},{9,8},{10,11... | collective-permute-start | bytes 110600 | tf_op jit(solution)/shard_map/ppermute | solution.py:42
  46.6 4.0 %collective-permute-start.17 = (f32[72,128]{1,0:T(8,128)S(1)}, f32[72,128]{1,0:T(8,128)S(1)}, u32[]{:S(2)}, u32[]{:S(2)}) collective-permute-start(f32[72,128]{1,0:T(8,128)S(1)} %slice_add_fusion.4), channel_id=1, source_target_pairs={{0,16},{1,17},{2,18},{3,19},{4,20},{5,21},{6,22},{7,23},{8,24},{9,... | collective-permute-start | bytes 110600 | tf_op jit(solution)/shard_map/ppermute | solution.py:42
  50.5 3.6 %collective-permute-start.20 = (f32[4,72,128]{2,1,0:T(8,128)S(1)}, f32[4,72,128]{2,1,0:T(8,128)S(1)}, u32[]{:S(2)}, u32[]{:S(2)}) collective-permute-start(f32[4,72,128]{2,1,0:T(8,128)S(1)} %pad_maximum_fusion.1.even_ref), channel_id=1, source_target_pairs={{0,8},{8,0},{16,24},{24,16},{1,9},{9,1},{17,25},{25,17},{2,10},{10... | collective-permute-start | bytes 442376 | tf_op jit(solution)/shard_map/ppermute | solution.py:32
  50.6 8.7 %collective-permute-start.23 = (f32[128,128]{1,0:T(8,128)S(1)}, f32[128,128]{1,0:T(8,128)S(1)}, u32[]{:S(2)}, u32[]{:S(2)}) collective-permute-start(f32[128,128]{1,0:T(8,128)S(1)} %fusion.7), channel_id=1, source_target_pairs={{0,17},{1,16},{2,19},{3,18},{4,21},{5,20},{6,23},{7,22},{8,25},{9,... | collective-permute-start | bytes 196616 | tf_op jit(solution)/shard_map/ppermute | solution.py:42
  51.6 7.8 %collective-permute-start.22 = (f32[128,128]{1,0:T(8,128)S(1)}, f32[128,128]{1,0:T(8,128)S(1)}, u32[]{:S(2)}, u32[]{:S(2)}) collective-permute-start(f32[128,128]{1,0:T(8,128)S(1)} %fusion.7), channel_id=1, source_target_pairs={{0,1},{1,0},{2,3},{3,2},{4,5},{5,4},{6,7},{7,6},{8,9},{9,8},{10,11... | collective-permute-start | bytes 196616 | tf_op jit(solution)/shard_map/ppermute | solution.py:42
  52.6 6.7 %collective-permute-start.21 = (f32[128,128]{1,0:T(8,128)S(1)}, f32[128,128]{1,0:T(8,128)S(1)}, u32[]{:S(2)}, u32[]{:S(2)}) collective-permute-start(f32[128,128]{1,0:T(8,128)S(1)} %fusion.7), channel_id=1, source_target_pairs={{0,16},{1,17},{2,18},{3,19},{4,20},{5,21},{6,22},{7,23},{8,24},{9,... | collective-permute-start | bytes 196616 | tf_op jit(solution)/shard_map/ppermute | solution.py:42
  67.2 4.9 %collective-permute-start.27 = (f32[32,512]{1,0:T(8,128)S(1)}, f32[32,512]{1,0:T(8,128)S(1)}, u32[]{:S(2)}, u32[]{:S(2)}) collective-permute-start(f32[32,512]{1,0:T(8,128)S(1)} %get-tuple-element.84), channel_id=1, source_target_pairs={{0,16},{8,24},{16,0},{24,8},{1,17},{9,25},{17,1},{25,9},{2,18},{10... | collective-permute-start | bytes 196616 | tf_op jit(solution)/shard_map/ppermute | solution.py:32
  67.7 4.7 %collective-permute-start.28 = (f32[32,512]{1,0:T(8,128)S(1)}, f32[32,512]{1,0:T(8,128)S(1)}, u32[]{:S(2)}, u32[]{:S(2)}) collective-permute-start(f32[32,512]{1,0:T(8,128)S(1)} %get-tuple-element.85), channel_id=1, source_target_pairs={{0,24},{8,16},{16,8},{24,0},{1,25},{9,17},{17,9},{25,1},{2,26},{10... | collective-permute-start | bytes 196616 | tf_op jit(solution)/shard_map/ppermute | solution.py:32
  (6 other events, 22.6 us)

commit v14 on v13

--- a/solution.py
+++ b/solution.py
@@ -151,8 +151,8 @@
     return tuple(lax.broadcasted_iota(jnp.int32, (size, size), axis) for axis in range(2))
 
 
-def pair_rows(cols, owners):
-    return 2 * cols + 8 * owners
+def pair_rows(cols):
+    return 2 * cols + 16
 
 
 def pair_kernel(parts, span, probes_ref, *refs):
@@ -178,9 +178,9 @@
     products[...] = dot_parts(left, split(there[...]), ((0,), (0,)))
     diagonal = jnp.sum(jnp.where(row == col, second, 0.0), axis=0, keepdims=True)
     flat[2 * cols:, :] = jnp.broadcast_to(diagonal, (flat.shape[0] - 2 * cols, cols))
-    share, rest = flat.shape[0] // owners, 2 * cols // owners
+    share, rest = flat.shape[0] // 2, 2 * cols // owners
     for k, out in enumerate(outs):
-        out[:share, :] = flat[pl.ds(pl.multiple_of((owner ^ k) * share, 8), share), :]
+        out[:share, :] = flat[pl.ds(pl.multiple_of(((owner ^ k) % 2) * share, 8), share), :]
         out[share:, :] = products[pl.ds(pl.multiple_of((owner ^ k) * rest, 8), rest), :]
 
 
@@ -275,15 +275,14 @@
     return j if step == parts // 2 else 2 * j + core
 
 
-def level_kernel(parts, span, even_ref, odd_ref, out_ref, pairs):
+def level_kernel(parts, even_ref, odd_ref, out_ref, pairs):
     cols = even_ref.shape[2]
-    share = pairs.shape[1] // (2 * span)
+    share = pairs.shape[1] // 2
 
     def put(there, rows):
-        place = there % 2 + 2 * (there // parts)
-        pairs[(there % parts) // 2, pl.ds(pl.multiple_of(place * share, 8), share), :] = rows
-
-    place_shares(parts, span, even_ref, odd_ref, put)
+        pairs[there // 2, pl.ds(pl.multiple_of((there % 2) * share, 8), share), :] = rows
+
+    place_shares(parts, 1, even_ref, odd_ref, put)
     row, col = triangle(cols)
     grams = []
     step = out_ref.shape[0]
@@ -452,7 +451,7 @@
         far[k + 1] = swap(theirs[k], "tm", k)
 
     owners = 2 * span
-    pair_size = pair_rows(cols, owners) // owners
+    pair_size = pair_rows(cols) // 2
     sums = pl.pallas_call(
         functools.partial(pair_kernel, parts, span),
         out_shape=[shape(pair_size + 2 * cols // owners, cols)] * owners,
@@ -461,7 +460,7 @@
         scratch_shapes=[
             pltpu.VMEM((cells // 2, 2 * cols), F32),
             pltpu.VMEM((cells // 2, cols), F32),
-            pltpu.VMEM((pair_rows(cols, owners), cols), F32),
+            pltpu.VMEM((pair_rows(cols), cols), F32),
             pltpu.VMEM((2 * cols, cols), F32),
         ],
         compiler_params=params(),
@@ -472,9 +471,9 @@
     tied = lax.optimization_barrier(got + [far[k] for k in range(2, parts)])
     got = tied[:owners - 1]
     far.update(zip(range(2, parts), tied[owners - 1:]))
-    pair_share = sums[0]
-    for x in got:
-        pair_share = pair_share + x
+    pair_share = sums[0] + got[0]
+    if span > 1:
+        pair_share = pair_share + (got[1] + got[2])
     bits = [1 << b for b in range(1, patches.bit_length() - 1)]
 
     blocks = len(cross_order(parts))
@@ -508,27 +507,27 @@
     for bit in bits[1:]:
         mine = mine + swap(mine, "space", bit)
 
-    def spread(x):
-        return [x] + [swap_both(x, 2 * h) for h in range(1, owners // 2)]
+    def spread(x, count):
+        return [x] + [swap_both(x, 2 * h) for h in range(1, count // 2)]
 
     def gathered(shares):
         even = jnp.stack(shares)
         return even, swap(even, "tm", 1)
 
-    mine, *pair_shares = lax.optimization_barrier([mine] + spread(pair_share))
+    mine, *pair_shares = lax.optimization_barrier([mine] + spread(pair_share, parts))
 
     half = parts // 2
     level = pl.pallas_call(
-        functools.partial(level_kernel, parts, span),
+        functools.partial(level_kernel, parts),
         out_shape=shape(half // 2 if half % 2 == 0 else half, 3 * cols, cols),
         in_specs=[whole()] * 2,
         out_specs=whole(),
-        scratch_shapes=[pltpu.VMEM((half, pair_rows(cols, 2 * span), cols), F32)],
+        scratch_shapes=[pltpu.VMEM((half, pair_rows(cols), cols), F32)],
         compiler_params=params(),
         cost_estimate=pl.CostEstimate(flops=parts * SIGN_STEPS * 6 * (2 * cols) ** 3, bytes_accessed=0, transcendentals=0),
         name="level",
     )(*gathered(pair_shares))
-    level, *shares = lax.optimization_barrier([level] + spread(mine))
+    level, *shares = lax.optimization_barrier([level] + spread(mine, owners))
     other_level = swap(level, "tm", 1)
     width = cols // parts
     *sent, weight, products = pl.pallas_call(

time: 73.5 us -> 72 us (0.980)
  starting transfers between devices: 32.5 us -> 31 us
    ppermute x12 -> x10, starting transfers between devices: 15.3 us -> 13.3 us  [swap_both(): return lax.ppermute(x, ('tm', 'space'), route)]
    ppermute x12 -> x10, waiting for transfers between devices: 8.98 us -> 8.31 us  [swap_both(): return lax.ppermute(x, ('tm', 'space'), route)]
  transfers between devices with their start and end apart: 29 -> 27, of which waited for: 14 -> 12; matrix products, arithmetic and copies ran while one was open for 0% -> 0% of each run, Pallas kernels for 15% -> 15%
where the time goes in v14:
time: 72 us; the launch traced here: 71.8 us
  starting transfers between devices  31 us (43%)
  waiting for transfers between devices  19.9 us (28%)
  Pallas kernels  19.8 us (28%)
  between operations  0.84 us (1%)
    ppermute x15, starting transfers between devices, swap(): return lax.ppermute(x, axis, [(i, i ^ mask) for i in range(count)])  14 us
    ppermute x10, starting transfers between devices, swap_both(): return lax.ppermute(x, ('tm', 'space'), route)  13.3 us
    ppermute x15, waiting for transfers between devices, swap(): return lax.ppermute(x, axis, [(i, i ^ mask) for i in range(count)])  11.6 us
    ppermute x10, waiting for transfers between devices, swap_both(): return lax.ppermute(x, ('tm', 'space'), route)  8.31 us
    pallas_call x1, Pallas kernels, local(): pl.pallas_call(functools.partial(merge_kernel, parts, span), out_shape=[s...  5.69 us
    pallas_call x1, Pallas kernels, local(): pl.pallas_call(functools.partial(level_kernel, parts), out_shape=shape(ha...  5.07 us
    pallas_call x1, Pallas kernels, local(): pl.pallas_call(functools.partial(filter_kernel, parts), out_shape=[shape(...  3.87 us
    ppermute x1, starting transfers between devices, local(): lax.ppermute(to_near, 'space', [(i, i ^ 1) for i in range(patches) if i ^...  3 us
  transfers between devices with their start and end apart: 27, of which 12 were waited for; matrix products, arithmetic and copies ran while one was open for 0% of the time, Pallas kernels for 15%

profile of v14, /device:TPU:0, one launch (start us, length us, event | category | flops | bytes accessed | tf_op | source)
XLA Modules:
  0.0 71.8 jit_solution(7689022060147492607)
XLA Ops:
  0.6 1.2 %edge.1 = (f32[64,128]{1,0:T(8,128)S(1)}, f32[64,128]{1,0:T(8,128)S(1)}) custom-call(f32[6]{0:T(128)} %rtaps_ref.3, f32[6]{0:T(128)} %ctaps_ref.3, f32[64,128,128]{2,1,0:T(8,128)} %snap_hbm.1, f32[64,128,128]{2,1,0:T(8,128)} %snap_hbm.1, s32[64,128]{1,0:T(8,128)} %mask_ref.1, s32[64,128]{1,0:T(8,128)} %mask_ref.1), custom_call_target="tpu_custom_call" | custom-call | tf_op jit(solution)/shard_map/edge/pallas_call | solution.py:401
  1.9 3.0 %collective-permute-start = (f32[64,128]{1,0:T(8,128)S(1)}, f32[64,128]{1,0:T(8,128)S(1)}, u32[]{:S(2)}, u32[]{:S(2)}) collective-permute-start(f32[64,128]{1,0:T(8,128)S(1)} %get-tuple-element.43), channel_id=1, source_target_pairs={{0,1},{1,0},{2,3},{3,2},{4,5},{5,4},{6,7},{7,6},{8,9},{9,8},{10,11... | collective-permute-start | bytes 98312 | tf_op jit(solution)/shard_map/ppermute | solution.py:417
  5.6 3.9 %filter.1 = (f32[512,128]{1,0:T(8,128)S(1)}, f32[512,128]{1,0:T(8,128)S(1)}, f32[512,128]{1,0:T(8,128)S(1)}, f32[512,128]{1,0:T(8,128)S(1)}) custom-call(f32[6]{0:T(128)} %rtaps_ref.3, f32[6]{0:T(128)} %ctaps_ref.3, f32[64,128,128]{2,1,0:T(8,128)} %snap_hbm.1, s32[64,128]{1,0:T(8,128)} %mask_ref.1), custom_call_target="tpu_custom_call" | custom-call | bytes 4194304 | tf_op jit(solution)/shard_map/filter/pallas_call | solution.py:421
  10.2 1.5 %collective-permute-start.7 = (f32[512,128]{1,0:T(8,128)S(1)}, f32[512,128]{1,0:T(8,128)S(1)}, u32[]{:S(2)}, u32[]{:S(2)}) collective-permute-start(f32[512,128]{1,0:T(8,128)S(1)} %get-tuple-element.51.refs_1_), channel_id=1, source_target_pairs={{0,16},{8,24},{16,0},{24,8},{1,17},{9,25},{17,1},{25,9},{2,18},{10... | collective-permute-start | bytes 786440 | tf_op jit(solution)/shard_map/ppermute | solution.py:32
  14.1 4.3 %collective-permute-start.5 = (f32[200,128]{1,0:T(8,128)S(1)}, f32[200,128]{1,0:T(8,128)S(1)}, u32[]{:S(2)}, u32[]{:S(2)}) collective-permute-start(f32[200,128]{1,0:T(8,128)S(1)} %get-tuple-element.54), channel_id=1, source_target_pairs={{0,1},{1,0},{2,3},{3,2},{4,5},{5,4},{6,7},{7,6},{8,9},{9,8},{10,11... | collective-permute-start | bytes 307208 | tf_op jit(solution)/shard_map/ppermute | solution.py:42
  19.4 2.8 %collective-permute-done.5 = f32[200,128]{1,0:T(8,128)S(1)} collective-permute-done((f32[200,128]{1,0:T(8,128)S(1)}, f32[200,128]{1,0:T(8,128)S(1)}, u32[]{:S(2)}, u32[]{:S(2)}) %collective-permute-start.5) | collective-permute-done | bytes 102432 | tf_op jit(solution)/shard_map/ppermute | solution.py:42
  22.2 1.7 %collective-permute-done.6 = f32[200,128]{1,0:T(8,128)S(1)} collective-permute-done((f32[200,128]{1,0:T(8,128)S(1)}, f32[200,128]{1,0:T(8,128)S(1)}, u32[]{:S(2)}, u32[]{:S(2)}) %collective-permute-start.6) | collective-permute-done | bytes 102432 | tf_op jit(solution)/shard_map/ppermute | solution.py:42
  25.0 3.7 %collective-permute-start.13 = (f32[200,128]{1,0:T(8,128)S(1)}, f32[200,128]{1,0:T(8,128)S(1)}, u32[]{:S(2)}, u32[]{:S(2)}) collective-permute-start(f32[200,128]{1,0:T(8,128)S(1)} %add_add_fusion), channel_id=1, source_target_pairs={{0,2},{1,3},{2,0},{3,1},{4,6},{5,7},{6,4},{7,5},{8,10},{9,11},{10,... | collective-permute-start | bytes 307208 | tf_op jit(solution)/shard_map/ppermute | solution.py:32
  28.7 1.6 %collective-permute-start.10 = (f32[64,128]{1,0:T(8,128)S(1)}, f32[64,128]{1,0:T(8,128)S(1)}, u32[]{:S(2)}, u32[]{:S(2)}) collective-permute-start(f32[64,128]{1,0:T(8,128)S(1)} %get-tuple-element.84), channel_id=1, source_target_pairs={{0,16},{1,17},{2,18},{3,19},{4,20},{5,21},{6,22},{7,23},{8,24},{9,... | collective-permute-start | bytes 98312 | tf_op jit(solution)/shard_map/ppermute | solution.py:42
  30.3 2.1 %collective-permute-start.12 = (f32[64,128]{1,0:T(8,128)S(1)}, f32[64,128]{1,0:T(8,128)S(1)}, u32[]{:S(2)}, u32[]{:S(2)}) collective-permute-start(f32[64,128]{1,0:T(8,128)S(1)} %get-tuple-element.85), channel_id=1, source_target_pairs={{0,17},{1,16},{2,19},{3,18},{4,21},{5,20},{6,23},{7,22},{8,25},{9,... | collective-permute-start | bytes 98312 | tf_op jit(solution)/shard_map/ppermute | solution.py:42
  32.7 2.4 %collective-permute-done.12 = f32[64,128]{1,0:T(8,128)S(1)} collective-permute-done((f32[64,128]{1,0:T(8,128)S(1)}, f32[64,128]{1,0:T(8,128)S(1)}, u32[]{:S(2)}, u32[]{:S(2)}) %collective-permute-start.12) | collective-permute-done | bytes 32800 | tf_op jit(solution)/shard_map/ppermute | solution.py:42
  36.3 2.3 %collective-permute-start.15 = (f32[136,128]{1,0:T(8,128)S(1)}, f32[136,128]{1,0:T(8,128)S(1)}, u32[]{:S(2)}, u32[]{:S(2)}) collective-permute-start(f32[136,128]{1,0:T(8,128)S(1)} %slice.38), channel_id=1, source_target_pairs={{0,4},{1,5},{2,6},{3,7},{4,0},{5,1},{6,2},{7,3},{8,12},{9,13},{10,... | collective-permute-start | bytes 208904 | tf_op jit(solution)/shard_map/ppermute | solution.py:32
  39.4 3.1 %collective-permute-done.14 = f32[64,128]{1,0:T(8,128)S(1)} collective-permute-done((f32[64,128]{1,0:T(8,128)S(1)}, f32[64,128]{1,0:T(8,128)S(1)}, u32[]{:S(2)}, u32[]{:S(2)}) %collective-permute-start.14) | collective-permute-done | bytes 32800 | tf_op jit(solution)/shard_map/ppermute | solution.py:32
  42.6 1.4 %collective-permute-start.16 = (f32[128,128]{1,0:T(8,128)S(1)}, f32[128,128]{1,0:T(8,128)S(1)}, u32[]{:S(2)}, u32[]{:S(2)}) collective-permute-start(f32[128,128]{1,0:T(8,128)S(1)} %pad_maximum_fusion.2), channel_id=1, source_target_pairs={{0,4},{1,5},{2,6},{3,7},{4,0},{5,1},{6,2},{7,3},{8,12},{9,13},{10,... | collective-permute-start | bytes 196616 | tf_op jit(solution)/shard_map/ppermute | solution.py:32
  44.0 1.5 %collective-permute-start.17 = (f32[136,128]{1,0:T(8,128)S(1)}, f32[136,128]{1,0:T(8,128)S(1)}, u32[]{:S(2)}, u32[]{:S(2)}) collective-permute-start(f32[136,128]{1,0:T(8,128)S(1)} %slice_add_fusion.4), channel_id=1, source_target_pairs={{0,16},{1,17},{2,18},{3,19},{4,20},{5,21},{6,22},{7,23},{8,24},{9,... | collective-permute-start | bytes 208904 | tf_op jit(solution)/shard_map/ppermute | solution.py:42
  45.5 3.0 %collective-permute-done.16 = f32[128,128]{1,0:T(8,128)S(1)} collective-permute-done((f32[128,128]{1,0:T(8,128)S(1)}, f32[128,128]{1,0:T(8,128)S(1)}, u32[]{:S(2)}, u32[]{:S(2)}) %collective-permute-start.16) | collective-permute-done | bytes 65568 | tf_op jit(solution)/shard_map/ppermute | solution.py:32
  48.7 1.4 %collective-permute-start.21 = (f32[128,128]{1,0:T(8,128)S(1)}, f32[128,128]{1,0:T(8,128)S(1)}, u32[]{:S(2)}, u32[]{:S(2)}) collective-permute-start(f32[128,128]{1,0:T(8,128)S(1)} %fusion.7), channel_id=1, source_target_pairs={{0,17},{1,16},{2,19},{3,18},{4,21},{5,20},{6,23},{7,22},{8,25},{9,... | collective-permute-start | bytes 196616 | tf_op jit(solution)/shard_map/ppermute | solution.py:42
  50.0 1.7 %collective-permute-start.20 = (f32[128,128]{1,0:T(8,128)S(1)}, f32[128,128]{1,0:T(8,128)S(1)}, u32[]{:S(2)}, u32[]{:S(2)}) collective-permute-start(f32[128,128]{1,0:T(8,128)S(1)} %fusion.7), channel_id=1, source_target_pairs={{0,1},{1,0},{2,3},{3,2},{4,5},{5,4},{6,7},{7,6},{8,9},{9,8},{10,11... | collective-permute-start | bytes 196616 | tf_op jit(solution)/shard_map/ppermute | solution.py:42
  52.2 5.1 %level.1.mine_ref = f32[1,384,128]{2,1,0:T(8,128)S(1)} custom-call(f32[2,136,128]{2,1,0:T(8,128)S(1)} %pad_maximum_fusion.1.even_ref, f32[2,136,128]{2,1,0:T(8,128)S(1)} %collective-permute-done.18.odd_ref), custom_call_target="tpu_custom_call" | custom-call | flops 3221225472 | tf_op jit(solution)/shard_map/level/pallas_call | solution.py:520
  57.9 1.3 %collective-permute-done.23.theirs_ref = f32[1,384,128]{2,1,0:T(8,128)S(1)} collective-permute-done((f32[1,384,128]{2,1,0:T(8,128)S(1)}, f32[1,384,128]{2,1,0:T(8,128)S(1)}, u32[]{:S(2)}, u32[]{:S(2)}) %collective-permute-start.23) | collective-permute-done | bytes 196640 | tf_op jit(solution)/shard_map/ppermute | solution.py:32
  59.2 5.7 %merge.1 = (f32[32,512]{1,0:T(8,128)S(1)}, f32[32,512]{1,0:T(8,128)S(1)}, f32[32,512]{1,0:T(8,128)S(1)}, f32[32,512]{1,0:T(8,128)S(1)}, f32[512,128]{1,0:T(8,128)S(1)}, /*index=5*/f32[512,128]{1,0:T(8,128)S(1)}) custom-call(f32[4,128,128]{2,1,0:T(8,128)S(1)} %pad_maximum_fusion.even_ref, f32[4,128,128]{2,1,0:T(8,128)S(1)} %collective-permute-done.22.odd_ref, ...), custom_call_target="tpu_custom_call" | custom-call | tf_op jit(solution)/shard_map/merge/pallas_call | solution.py:533
  65.1 1.5 %collective-permute-start.25 = (f32[32,512]{1,0:T(8,128)S(1)}, f32[32,512]{1,0:T(8,128)S(1)}, u32[]{:S(2)}, u32[]{:S(2)}) collective-permute-start(f32[32,512]{1,0:T(8,128)S(1)} %get-tuple-element.80), channel_id=1, source_target_pairs={{0,16},{8,24},{16,0},{24,8},{1,17},{9,25},{17,1},{25,9},{2,18},{10... | collective-permute-start | bytes 196616 | tf_op jit(solution)/shard_map/ppermute | solution.py:32
  67.8 1.7 %collective-permute-done.25.refs_2_ = f32[32,512]{1,0:T(8,128)S(1)} collective-permute-done((f32[32,512]{1,0:T(8,128)S(1)}, f32[32,512]{1,0:T(8,128)S(1)}, u32[]{:S(2)}, u32[]{:S(2)}) %collective-permute-start.25) | collective-permute-done | bytes 65568 | tf_op jit(solution)/shard_map/ppermute | solution.py:32
  69.5 1.3 %collective-permute-done.26.refs_3_ = f32[32,512]{1,0:T(8,128)S(1)} collective-permute-done((f32[32,512]{1,0:T(8,128)S(1)}, f32[32,512]{1,0:T(8,128)S(1)}, u32[]{:S(2)}, u32[]{:S(2)}) %collective-permute-start.26) | collective-permute-done | bytes 65568 | tf_op jit(solution)/shard_map/ppermute | solution.py:32
  (53 shorter events, 11.6 us)
Async XLA Ops:
  1.9 7.5 %collective-permute-start = (f32[64,128]{1,0:T(8,128)S(1)}, f32[64,128]{1,0:T(8,128)S(1)}, u32[]{:S(2)}, u32[]{:S(2)}) collective-permute-start(f32[64,128]{1,0:T(8,128)S(1)} %get-tuple-element.43), channel_id=1, source_target_pairs={{0,1},{1,0},{2,3},{3,2},{4,5},{5,4},{6,7},{7,6},{8,9},{9,8},{10,11... | collective-permute-start | bytes 98312 | tf_op jit(solution)/shard_map/ppermute | solution.py:417
  4.9 4.5 %collective-permute-start.1 = (f32[64,128]{1,0:T(8,128)S(1)}, f32[64,128]{1,0:T(8,128)S(1)}, u32[]{:S(2)}, u32[]{:S(2)}) collective-permute-start(f32[64,128]{1,0:T(8,128)S(1)} %get-tuple-element.44), channel_id=1, source_target_pairs={{1,2},{3,4},{5,6},{2,1},{4,3},{6,5},{9,10},{11,12},{13,14},{10,9},... | collective-permute-start | bytes 98312 | tf_op jit(solution)/shard_map/ppermute | solution.py:419
  9.7 3.0 %collective-permute-start.2 = (f32[512,128]{1,0:T(8,128)S(1)}, f32[512,128]{1,0:T(8,128)S(1)}, u32[]{:S(2)}, u32[]{:S(2)}) collective-permute-start(f32[512,128]{1,0:T(8,128)S(1)} %get-tuple-element.50), channel_id=1, source_target_pairs={{0,8},{8,0},{16,24},{24,16},{1,9},{9,1},{17,25},{25,17},{2,10},{10... | collective-permute-start | bytes 786440 | tf_op jit(solution)/shard_map/ppermute | solution.py:32
  10.2 9.2 %collective-permute-start.7 = (f32[512,128]{1,0:T(8,128)S(1)}, f32[512,128]{1,0:T(8,128)S(1)}, u32[]{:S(2)}, u32[]{:S(2)}) collective-permute-start(f32[512,128]{1,0:T(8,128)S(1)} %get-tuple-element.51.refs_1_), channel_id=1, source_target_pairs={{0,16},{8,24},{16,0},{24,8},{1,17},{9,25},{17,1},{25,9},{2,18},{10... | collective-permute-start | bytes 786440 | tf_op jit(solution)/shard_map/ppermute | solution.py:32
  11.7 12.4 %collective-permute-start.8 = (f32[512,128]{1,0:T(8,128)S(1)}, f32[512,128]{1,0:T(8,128)S(1)}, u32[]{:S(2)}, u32[]{:S(2)}) collective-permute-start(f32[512,128]{1,0:T(8,128)S(1)} %collective-permute-done.3.refs_3_), channel_id=1, source_target_pairs={{0,16},{8,24},{16,0},{24,8},{1,17},{9,25},{17,1},{25,9},{2,18},{10... | collective-permute-start | bytes 786440 | tf_op jit(solution)/shard_map/ppermute | solution.py:32
  14.0 5.4 %collective-permute-start.4 = (f32[200,128]{1,0:T(8,128)S(1)}, f32[200,128]{1,0:T(8,128)S(1)}, u32[]{:S(2)}, u32[]{:S(2)}) collective-permute-start(f32[200,128]{1,0:T(8,128)S(1)} %get-tuple-element.53), channel_id=1, source_target_pairs={{0,8},{1,9},{2,10},{3,11},{4,12},{5,13},{6,14},{7,15},{8,0},{9,1},... | collective-permute-start | bytes 307208 | tf_op jit(solution)/shard_map/ppermute | solution.py:42
  14.1 8.1 %collective-permute-start.5 = (f32[200,128]{1,0:T(8,128)S(1)}, f32[200,128]{1,0:T(8,128)S(1)}, u32[]{:S(2)}, u32[]{:S(2)}) collective-permute-start(f32[200,128]{1,0:T(8,128)S(1)} %get-tuple-element.54), channel_id=1, source_target_pairs={{0,1},{1,0},{2,3},{3,2},{4,5},{5,4},{6,7},{7,6},{8,9},{9,8},{10,11... | collective-permute-start | bytes 307208 | tf_op jit(solution)/shard_map/ppermute | solution.py:42
  18.4 5.4 %collective-permute-start.6 = (f32[200,128]{1,0:T(8,128)S(1)}, f32[200,128]{1,0:T(8,128)S(1)}, u32[]{:S(2)}, u32[]{:S(2)}) collective-permute-start(f32[200,128]{1,0:T(8,128)S(1)} %get-tuple-element.55), channel_id=1, source_target_pairs={{0,9},{1,8},{2,11},{3,10},{4,13},{5,12},{6,15},{7,14},{8,1},{9,0},... | collective-permute-start | bytes 307208 | tf_op jit(solution)/shard_map/ppermute | solution.py:42
  24.8 3.9 %collective-permute-start.9 = (f32[4,64,128]{2,1,0:T(8,128)S(1)}, f32[4,64,128]{2,1,0:T(8,128)S(1)}, u32[]{:S(2)}, u32[]{:S(2)}) collective-permute-start(f32[4,64,128]{2,1,0:T(8,128)S(1)} %get-tuple-element.59), channel_id=1, source_target_pairs={{0,8},{8,0},{16,24},{24,16},{1,9},{9,1},{17,25},{25,17},{2,10},{10... | collective-permute-start | bytes 393224 | tf_op jit(solution)/shard_map/ppermute | solution.py:32
  25.0 7.5 %collective-permute-start.13 = (f32[200,128]{1,0:T(8,128)S(1)}, f32[200,128]{1,0:T(8,128)S(1)}, u32[]{:S(2)}, u32[]{:S(2)}) collective-permute-start(f32[200,128]{1,0:T(8,128)S(1)} %add_add_fusion), channel_id=1, source_target_pairs={{0,2},{1,3},{2,0},{3,1},{4,6},{5,7},{6,4},{7,5},{8,10},{9,11},{10,... | collective-permute-start | bytes 307208 | tf_op jit(solution)/shard_map/ppermute | solution.py:32
  28.7 4.0 %collective-permute-start.10 = (f32[64,128]{1,0:T(8,128)S(1)}, f32[64,128]{1,0:T(8,128)S(1)}, u32[]{:S(2)}, u32[]{:S(2)}) collective-permute-start(f32[64,128]{1,0:T(8,128)S(1)} %get-tuple-element.84), channel_id=1, source_target_pairs={{0,16},{1,17},{2,18},{3,19},{4,20},{5,21},{6,22},{7,23},{8,24},{9,... | collective-permute-start | bytes 98312 | tf_op jit(solution)/shard_map/ppermute | solution.py:42
  30.3 4.8 %collective-permute-start.12 = (f32[64,128]{1,0:T(8,128)S(1)}, f32[64,128]{1,0:T(8,128)S(1)}, u32[]{:S(2)}, u32[]{:S(2)}) collective-permute-start(f32[64,128]{1,0:T(8,128)S(1)} %get-tuple-element.85), channel_id=1, source_target_pairs={{0,17},{1,16},{2,19},{3,18},{4,21},{5,20},{6,23},{7,22},{8,25},{9,... | collective-permute-start | bytes 98312 | tf_op jit(solution)/shard_map/ppermute | solution.py:42
  32.4 3.9 %collective-permute-start.11 = (f32[64,128]{1,0:T(8,128)S(1)}, f32[64,128]{1,0:T(8,128)S(1)}, u32[]{:S(2)}, u32[]{:S(2)}) collective-permute-start(f32[64,128]{1,0:T(8,128)S(1)} %get-tuple-element.86), channel_id=1, source_target_pairs={{0,1},{1,0},{2,3},{3,2},{4,5},{5,4},{6,7},{7,6},{8,9},{9,8},{10,11... | collective-permute-start | bytes 98312 | tf_op jit(solution)/shard_map/ppermute | solution.py:42
  36.3 6.2 %collective-permute-start.15 = (f32[136,128]{1,0:T(8,128)S(1)}, f32[136,128]{1,0:T(8,128)S(1)}, u32[]{:S(2)}, u32[]{:S(2)}) collective-permute-start(f32[136,128]{1,0:T(8,128)S(1)} %slice.38), channel_id=1, source_target_pairs={{0,4},{1,5},{2,6},{3,7},{4,0},{5,1},{6,2},{7,3},{8,12},{9,13},{10,... | collective-permute-start | bytes 208904 | tf_op jit(solution)/shard_map/ppermute | solution.py:32
  38.6 3.9 %collective-permute-start.14 = (f32[64,128]{1,0:T(8,128)S(1)}, f32[64,128]{1,0:T(8,128)S(1)}, u32[]{:S(2)}, u32[]{:S(2)}) collective-permute-start(f32[64,128]{1,0:T(8,128)S(1)} %fusion.6), channel_id=1, source_target_pairs={{0,2},{1,3},{2,0},{3,1},{4,6},{5,7},{6,4},{7,5},{8,10},{9,11},{10,... | collective-permute-start | bytes 98312 | tf_op jit(solution)/shard_map/ppermute | solution.py:32
  42.6 5.9 %collective-permute-start.16 = (f32[128,128]{1,0:T(8,128)S(1)}, f32[128,128]{1,0:T(8,128)S(1)}, u32[]{:S(2)}, u32[]{:S(2)}) collective-permute-start(f32[128,128]{1,0:T(8,128)S(1)} %pad_maximum_fusion.2), channel_id=1, source_target_pairs={{0,4},{1,5},{2,6},{3,7},{4,0},{5,1},{6,2},{7,3},{8,12},{9,13},{10,... | collective-permute-start | bytes 196616 | tf_op jit(solution)/shard_map/ppermute | solution.py:32
  44.0 4.5 %collective-permute-start.17 = (f32[136,128]{1,0:T(8,128)S(1)}, f32[136,128]{1,0:T(8,128)S(1)}, u32[]{:S(2)}, u32[]{:S(2)}) collective-permute-start(f32[136,128]{1,0:T(8,128)S(1)} %slice_add_fusion.4), channel_id=1, source_target_pairs={{0,16},{1,17},{2,18},{3,19},{4,20},{5,21},{6,22},{7,23},{8,24},{9,... | collective-permute-start | bytes 208904 | tf_op jit(solution)/shard_map/ppermute | solution.py:42
  48.6 3.6 %collective-permute-start.18 = (f32[2,136,128]{2,1,0:T(8,128)S(1)}, f32[2,136,128]{2,1,0:T(8,128)S(1)}, u32[]{:S(2)}, u32[]{:S(2)}) collective-permute-start(f32[2,136,128]{2,1,0:T(8,128)S(1)} %pad_maximum_fusion.1.even_ref), channel_id=1, source_target_pairs={{0,8},{8,0},{16,24},{24,16},{1,9},{9,1},{17,25},{25,17},{2,10},{10... | collective-permute-start | bytes 417800 | tf_op jit(solution)/shard_map/ppermute | solution.py:32
  48.7 8.6 %collective-permute-start.21 = (f32[128,128]{1,0:T(8,128)S(1)}, f32[128,128]{1,0:T(8,128)S(1)}, u32[]{:S(2)}, u32[]{:S(2)}) collective-permute-start(f32[128,128]{1,0:T(8,128)S(1)} %fusion.7), channel_id=1, source_target_pairs={{0,17},{1,16},{2,19},{3,18},{4,21},{5,20},{6,23},{7,22},{8,25},{9,... | collective-permute-start | bytes 196616 | tf_op jit(solution)/shard_map/ppermute | solution.py:42
  50.0 7.3 %collective-permute-start.20 = (f32[128,128]{1,0:T(8,128)S(1)}, f32[128,128]{1,0:T(8,128)S(1)}, u32[]{:S(2)}, u32[]{:S(2)}) collective-permute-start(f32[128,128]{1,0:T(8,128)S(1)} %fusion.7), channel_id=1, source_target_pairs={{0,1},{1,0},{2,3},{3,2},{4,5},{5,4},{6,7},{7,6},{8,9},{9,8},{10,11... | collective-permute-start | bytes 196616 | tf_op jit(solution)/shard_map/ppermute | solution.py:42
  51.7 5.6 %collective-permute-start.19 = (f32[128,128]{1,0:T(8,128)S(1)}, f32[128,128]{1,0:T(8,128)S(1)}, u32[]{:S(2)}, u32[]{:S(2)}) collective-permute-start(f32[128,128]{1,0:T(8,128)S(1)} %fusion.7), channel_id=1, source_target_pairs={{0,16},{1,17},{2,18},{3,19},{4,20},{5,21},{6,22},{7,23},{8,24},{9,... | collective-permute-start | bytes 196616 | tf_op jit(solution)/shard_map/ppermute | solution.py:42
  64.9 2.8 %collective-permute-start.24 = (f32[32,512]{1,0:T(8,128)S(1)}, f32[32,512]{1,0:T(8,128)S(1)}, u32[]{:S(2)}, u32[]{:S(2)}) collective-permute-start(f32[32,512]{1,0:T(8,128)S(1)} %get-tuple-element.79), channel_id=1, source_target_pairs={{0,8},{8,0},{16,24},{24,16},{1,9},{9,1},{17,25},{25,17},{2,10},{10... | collective-permute-start | bytes 196616 | tf_op jit(solution)/shard_map/ppermute | solution.py:32
  65.1 4.4 %collective-permute-start.25 = (f32[32,512]{1,0:T(8,128)S(1)}, f32[32,512]{1,0:T(8,128)S(1)}, u32[]{:S(2)}, u32[]{:S(2)}) collective-permute-start(f32[32,512]{1,0:T(8,128)S(1)} %get-tuple-element.80), channel_id=1, source_target_pairs={{0,16},{8,24},{16,0},{24,8},{1,17},{9,25},{17,1},{25,9},{2,18},{10... | collective-permute-start | bytes 196616 | tf_op jit(solution)/shard_map/ppermute | solution.py:32
  66.7 4.1 %collective-permute-start.26 = (f32[32,512]{1,0:T(8,128)S(1)}, f32[32,512]{1,0:T(8,128)S(1)}, u32[]{:S(2)}, u32[]{:S(2)}) collective-permute-start(f32[32,512]{1,0:T(8,128)S(1)} %get-tuple-element.81), channel_id=1, source_target_pairs={{0,24},{8,16},{16,8},{24,0},{1,25},{9,17},{17,9},{25,1},{2,26},{10... | collective-permute-start | bytes 196616 | tf_op jit(solution)/shard_map/ppermute | solution.py:32
  (4 other events, 16.7 us)

commit v15 on v14

--- a/solution.py
+++ b/solution.py
@@ -255,13 +255,16 @@
         mean = jnp.sum(jnp.where(diagonal, gram, 0.0)) / order
         shifted = jnp.where(diagonal, gram - mean, gram)
         signs.append(shifted / jnp.sqrt(jnp.sum(shifted * shifted, keepdims=True) + 1e-6))
-    for _ in range(SIGN_STEPS):
+    for _ in range(SIGN_STEPS - 1):
         signs = [next_sign(y) for y in signs]
     half = order // 2
     combines = []
     for y in signs:
-        projector = 0.5 * (jnp.where(diagonal, 1.0, 0.0) + y)
-        combines.append(projector[:, :half] + projector[:, half:])
+        whole_y = split(y)
+        folded = y[:, :half] + y[:, half:]
+        cubed = dot_parts(whole_y, split(dot_parts(whole_y, split(folded))))
+        ones = jnp.where(diagonal[:, :half] | diagonal[:, half:], 1.0, 0.0)
+        combines.append(0.5 * (ones + (1.5 * folded - 0.5 * cubed)))
     return combines
 
 

time: 72 us -> 72.1 us (level)
  no operation moved by 1% of the time
where the time goes in v15:
time: 72.1 us; the launch traced here: 71.9 us
  starting transfers between devices  31 us (43%)
  Pallas kernels  19.9 us (28%)
  waiting for transfers between devices  19.9 us (28%)
  between operations  0.84 us (1%)
    ppermute x15, starting transfers between devices, swap(): return lax.ppermute(x, axis, [(i, i ^ mask) for i in range(count)])  14 us
    ppermute x10, starting transfers between devices, swap_both(): return lax.ppermute(x, ('tm', 'space'), route)  13.3 us
    ppermute x15, waiting for transfers between devices, swap(): return lax.ppermute(x, axis, [(i, i ^ mask) for i in range(count)])  11.6 us
    ppermute x10, waiting for transfers between devices, swap_both(): return lax.ppermute(x, ('tm', 'space'), route)  8.31 us
    pallas_call x1, Pallas kernels, local(): pl.pallas_call(functools.partial(merge_kernel, parts, span), out_shape=[s...  5.79 us
    pallas_call x1, Pallas kernels, local(): pl.pallas_call(functools.partial(level_kernel, parts), out_shape=shape(ha...  5.1 us
    pallas_call x1, Pallas kernels, local(): pl.pallas_call(functools.partial(filter_kernel, parts), out_shape=[shape(...  3.87 us
    ppermute x1, starting transfers between devices, local(): lax.ppermute(to_near, 'space', [(i, i ^ 1) for i in range(patches) if i ^...  3 us
  transfers between devices with their start and end apart: 27, of which 12 were waited for; matrix products, arithmetic and copies ran while one was open for 0% of the time, Pallas kernels for 15%

profile of v15, /device:TPU:0, one launch (start us, length us, event | category | flops | bytes accessed | tf_op | source)
XLA Modules:
  0.0 71.9 jit_solution(14405957739104768446)
XLA Ops:
  0.6 1.2 %edge.1 = (f32[64,128]{1,0:T(8,128)S(1)}, f32[64,128]{1,0:T(8,128)S(1)}) custom-call(f32[6]{0:T(128)} %rtaps_ref.3, f32[6]{0:T(128)} %ctaps_ref.3, f32[64,128,128]{2,1,0:T(8,128)} %snap_hbm.1, f32[64,128,128]{2,1,0:T(8,128)} %snap_hbm.1, s32[64,128]{1,0:T(8,128)} %mask_ref.1, s32[64,128]{1,0:T(8,128)} %mask_ref.1), custom_call_target="tpu_custom_call" | custom-call | tf_op jit(solution)/shard_map/edge/pallas_call | solution.py:404
  1.9 3.0 %collective-permute-start = (f32[64,128]{1,0:T(8,128)S(1)}, f32[64,128]{1,0:T(8,128)S(1)}, u32[]{:S(2)}, u32[]{:S(2)}) collective-permute-start(f32[64,128]{1,0:T(8,128)S(1)} %get-tuple-element.43), channel_id=1, source_target_pairs={{0,1},{1,0},{2,3},{3,2},{4,5},{5,4},{6,7},{7,6},{8,9},{9,8},{10,11... | collective-permute-start | bytes 98312 | tf_op jit(solution)/shard_map/ppermute | solution.py:420
  5.6 3.9 %filter.1 = (f32[512,128]{1,0:T(8,128)S(1)}, f32[512,128]{1,0:T(8,128)S(1)}, f32[512,128]{1,0:T(8,128)S(1)}, f32[512,128]{1,0:T(8,128)S(1)}) custom-call(f32[6]{0:T(128)} %rtaps_ref.3, f32[6]{0:T(128)} %ctaps_ref.3, f32[64,128,128]{2,1,0:T(8,128)} %snap_hbm.1, s32[64,128]{1,0:T(8,128)} %mask_ref.1), custom_call_target="tpu_custom_call" | custom-call | bytes 4194304 | tf_op jit(solution)/shard_map/filter/pallas_call | solution.py:424
  10.2 1.5 %collective-permute-start.7 = (f32[512,128]{1,0:T(8,128)S(1)}, f32[512,128]{1,0:T(8,128)S(1)}, u32[]{:S(2)}, u32[]{:S(2)}) collective-permute-start(f32[512,128]{1,0:T(8,128)S(1)} %get-tuple-element.51.refs_1_), channel_id=1, source_target_pairs={{0,16},{8,24},{16,0},{24,8},{1,17},{9,25},{17,1},{25,9},{2,18},{10... | collective-permute-start | bytes 786440 | tf_op jit(solution)/shard_map/ppermute | solution.py:32
  14.1 4.3 %collective-permute-start.5 = (f32[200,128]{1,0:T(8,128)S(1)}, f32[200,128]{1,0:T(8,128)S(1)}, u32[]{:S(2)}, u32[]{:S(2)}) collective-permute-start(f32[200,128]{1,0:T(8,128)S(1)} %get-tuple-element.54), channel_id=1, source_target_pairs={{0,1},{1,0},{2,3},{3,2},{4,5},{5,4},{6,7},{7,6},{8,9},{9,8},{10,11... | collective-permute-start | bytes 307208 | tf_op jit(solution)/shard_map/ppermute | solution.py:42
  19.4 2.8 %collective-permute-done.5 = f32[200,128]{1,0:T(8,128)S(1)} collective-permute-done((f32[200,128]{1,0:T(8,128)S(1)}, f32[200,128]{1,0:T(8,128)S(1)}, u32[]{:S(2)}, u32[]{:S(2)}) %collective-permute-start.5) | collective-permute-done | bytes 102432 | tf_op jit(solution)/shard_map/ppermute | solution.py:42
  22.2 1.7 %collective-permute-done.6 = f32[200,128]{1,0:T(8,128)S(1)} collective-permute-done((f32[200,128]{1,0:T(8,128)S(1)}, f32[200,128]{1,0:T(8,128)S(1)}, u32[]{:S(2)}, u32[]{:S(2)}) %collective-permute-start.6) | collective-permute-done | bytes 102432 | tf_op jit(solution)/shard_map/ppermute | solution.py:42
  25.0 3.7 %collective-permute-start.13 = (f32[200,128]{1,0:T(8,128)S(1)}, f32[200,128]{1,0:T(8,128)S(1)}, u32[]{:S(2)}, u32[]{:S(2)}) collective-permute-start(f32[200,128]{1,0:T(8,128)S(1)} %add_add_fusion), channel_id=1, source_target_pairs={{0,2},{1,3},{2,0},{3,1},{4,6},{5,7},{6,4},{7,5},{8,10},{9,11},{10,... | collective-permute-start | bytes 307208 | tf_op jit(solution)/shard_map/ppermute | solution.py:32
  28.7 1.6 %collective-permute-start.10 = (f32[64,128]{1,0:T(8,128)S(1)}, f32[64,128]{1,0:T(8,128)S(1)}, u32[]{:S(2)}, u32[]{:S(2)}) collective-permute-start(f32[64,128]{1,0:T(8,128)S(1)} %get-tuple-element.84), channel_id=1, source_target_pairs={{0,16},{1,17},{2,18},{3,19},{4,20},{5,21},{6,22},{7,23},{8,24},{9,... | collective-permute-start | bytes 98312 | tf_op jit(solution)/shard_map/ppermute | solution.py:42
  30.3 2.1 %collective-permute-start.12 = (f32[64,128]{1,0:T(8,128)S(1)}, f32[64,128]{1,0:T(8,128)S(1)}, u32[]{:S(2)}, u32[]{:S(2)}) collective-permute-start(f32[64,128]{1,0:T(8,128)S(1)} %get-tuple-element.85), channel_id=1, source_target_pairs={{0,17},{1,16},{2,19},{3,18},{4,21},{5,20},{6,23},{7,22},{8,25},{9,... | collective-permute-start | bytes 98312 | tf_op jit(solution)/shard_map/ppermute | solution.py:42
  32.7 2.4 %collective-permute-done.12 = f32[64,128]{1,0:T(8,128)S(1)} collective-permute-done((f32[64,128]{1,0:T(8,128)S(1)}, f32[64,128]{1,0:T(8,128)S(1)}, u32[]{:S(2)}, u32[]{:S(2)}) %collective-permute-start.12) | collective-permute-done | bytes 32800 | tf_op jit(solution)/shard_map/ppermute | solution.py:42
  36.3 2.3 %collective-permute-start.15 = (f32[136,128]{1,0:T(8,128)S(1)}, f32[136,128]{1,0:T(8,128)S(1)}, u32[]{:S(2)}, u32[]{:S(2)}) collective-permute-start(f32[136,128]{1,0:T(8,128)S(1)} %slice.38), channel_id=1, source_target_pairs={{0,4},{1,5},{2,6},{3,7},{4,0},{5,1},{6,2},{7,3},{8,12},{9,13},{10,... | collective-permute-start | bytes 208904 | tf_op jit(solution)/shard_map/ppermute | solution.py:32
  39.4 3.1 %collective-permute-done.14 = f32[64,128]{1,0:T(8,128)S(1)} collective-permute-done((f32[64,128]{1,0:T(8,128)S(1)}, f32[64,128]{1,0:T(8,128)S(1)}, u32[]{:S(2)}, u32[]{:S(2)}) %collective-permute-start.14) | collective-permute-done | bytes 32800 | tf_op jit(solution)/shard_map/ppermute | solution.py:32
  42.6 1.4 %collective-permute-start.16 = (f32[128,128]{1,0:T(8,128)S(1)}, f32[128,128]{1,0:T(8,128)S(1)}, u32[]{:S(2)}, u32[]{:S(2)}) collective-permute-start(f32[128,128]{1,0:T(8,128)S(1)} %pad_maximum_fusion.2), channel_id=1, source_target_pairs={{0,4},{1,5},{2,6},{3,7},{4,0},{5,1},{6,2},{7,3},{8,12},{9,13},{10,... | collective-permute-start | bytes 196616 | tf_op jit(solution)/shard_map/ppermute | solution.py:32
  44.0 1.5 %collective-permute-start.17 = (f32[136,128]{1,0:T(8,128)S(1)}, f32[136,128]{1,0:T(8,128)S(1)}, u32[]{:S(2)}, u32[]{:S(2)}) collective-permute-start(f32[136,128]{1,0:T(8,128)S(1)} %slice_add_fusion.4), channel_id=1, source_target_pairs={{0,16},{1,17},{2,18},{3,19},{4,20},{5,21},{6,22},{7,23},{8,24},{9,... | collective-permute-start | bytes 208904 | tf_op jit(solution)/shard_map/ppermute | solution.py:42
  45.5 3.0 %collective-permute-done.16 = f32[128,128]{1,0:T(8,128)S(1)} collective-permute-done((f32[128,128]{1,0:T(8,128)S(1)}, f32[128,128]{1,0:T(8,128)S(1)}, u32[]{:S(2)}, u32[]{:S(2)}) %collective-permute-start.16) | collective-permute-done | bytes 65568 | tf_op jit(solution)/shard_map/ppermute | solution.py:32
  48.7 1.4 %collective-permute-start.21 = (f32[128,128]{1,0:T(8,128)S(1)}, f32[128,128]{1,0:T(8,128)S(1)}, u32[]{:S(2)}, u32[]{:S(2)}) collective-permute-start(f32[128,128]{1,0:T(8,128)S(1)} %fusion.7), channel_id=1, source_target_pairs={{0,17},{1,16},{2,19},{3,18},{4,21},{5,20},{6,23},{7,22},{8,25},{9,... | collective-permute-start | bytes 196616 | tf_op jit(solution)/shard_map/ppermute | solution.py:42
  50.0 1.7 %collective-permute-start.20 = (f32[128,128]{1,0:T(8,128)S(1)}, f32[128,128]{1,0:T(8,128)S(1)}, u32[]{:S(2)}, u32[]{:S(2)}) collective-permute-start(f32[128,128]{1,0:T(8,128)S(1)} %fusion.7), channel_id=1, source_target_pairs={{0,1},{1,0},{2,3},{3,2},{4,5},{5,4},{6,7},{7,6},{8,9},{9,8},{10,11... | collective-permute-start | bytes 196616 | tf_op jit(solution)/shard_map/ppermute | solution.py:42
  52.2 5.1 %level.1.mine_ref = f32[1,384,128]{2,1,0:T(8,128)S(1)} custom-call(f32[2,136,128]{2,1,0:T(8,128)S(1)} %pad_maximum_fusion.1.even_ref, f32[2,136,128]{2,1,0:T(8,128)S(1)} %collective-permute-done.18.odd_ref), custom_call_target="tpu_custom_call" | custom-call | flops 3221225472 | tf_op jit(solution)/shard_map/level/pallas_call | solution.py:523
  58.0 1.3 %collective-permute-done.23.theirs_ref = f32[1,384,128]{2,1,0:T(8,128)S(1)} collective-permute-done((f32[1,384,128]{2,1,0:T(8,128)S(1)}, f32[1,384,128]{2,1,0:T(8,128)S(1)}, u32[]{:S(2)}, u32[]{:S(2)}) %collective-permute-start.23) | collective-permute-done | bytes 196640 | tf_op jit(solution)/shard_map/ppermute | solution.py:32
  59.3 5.8 %merge.1 = (f32[32,512]{1,0:T(8,128)S(1)}, f32[32,512]{1,0:T(8,128)S(1)}, f32[32,512]{1,0:T(8,128)S(1)}, f32[32,512]{1,0:T(8,128)S(1)}, f32[512,128]{1,0:T(8,128)S(1)}, /*index=5*/f32[512,128]{1,0:T(8,128)S(1)}) custom-call(f32[4,128,128]{2,1,0:T(8,128)S(1)} %pad_maximum_fusion.even_ref, f32[4,128,128]{2,1,0:T(8,128)S(1)} %collective-permute-done.22.odd_ref, ...), custom_call_target="tpu_custom_call" | custom-call | tf_op jit(solution)/shard_map/merge/pallas_call | solution.py:536
  65.3 1.5 %collective-permute-start.25 = (f32[32,512]{1,0:T(8,128)S(1)}, f32[32,512]{1,0:T(8,128)S(1)}, u32[]{:S(2)}, u32[]{:S(2)}) collective-permute-start(f32[32,512]{1,0:T(8,128)S(1)} %get-tuple-element.80), channel_id=1, source_target_pairs={{0,16},{8,24},{16,0},{24,8},{1,17},{9,25},{17,1},{25,9},{2,18},{10... | collective-permute-start | bytes 196616 | tf_op jit(solution)/shard_map/ppermute | solution.py:32
  67.9 1.7 %collective-permute-done.25.refs_2_ = f32[32,512]{1,0:T(8,128)S(1)} collective-permute-done((f32[32,512]{1,0:T(8,128)S(1)}, f32[32,512]{1,0:T(8,128)S(1)}, u32[]{:S(2)}, u32[]{:S(2)}) %collective-permute-start.25) | collective-permute-done | bytes 65568 | tf_op jit(solution)/shard_map/ppermute | solution.py:32
  69.6 1.3 %collective-permute-done.26.refs_3_ = f32[32,512]{1,0:T(8,128)S(1)} collective-permute-done((f32[32,512]{1,0:T(8,128)S(1)}, f32[32,512]{1,0:T(8,128)S(1)}, u32[]{:S(2)}, u32[]{:S(2)}) %collective-permute-start.26) | collective-permute-done | bytes 65568 | tf_op jit(solution)/shard_map/ppermute | solution.py:32
  (53 shorter events, 11.6 us)
Async XLA Ops:
  1.9 7.5 %collective-permute-start = (f32[64,128]{1,0:T(8,128)S(1)}, f32[64,128]{1,0:T(8,128)S(1)}, u32[]{:S(2)}, u32[]{:S(2)}) collective-permute-start(f32[64,128]{1,0:T(8,128)S(1)} %get-tuple-element.43), channel_id=1, source_target_pairs={{0,1},{1,0},{2,3},{3,2},{4,5},{5,4},{6,7},{7,6},{8,9},{9,8},{10,11... | collective-permute-start | bytes 98312 | tf_op jit(solution)/shard_map/ppermute | solution.py:420
  4.9 4.5 %collective-permute-start.1 = (f32[64,128]{1,0:T(8,128)S(1)}, f32[64,128]{1,0:T(8,128)S(1)}, u32[]{:S(2)}, u32[]{:S(2)}) collective-permute-start(f32[64,128]{1,0:T(8,128)S(1)} %get-tuple-element.44), channel_id=1, source_target_pairs={{1,2},{3,4},{5,6},{2,1},{4,3},{6,5},{9,10},{11,12},{13,14},{10,9},... | collective-permute-start | bytes 98312 | tf_op jit(solution)/shard_map/ppermute | solution.py:422
  9.7 3.0 %collective-permute-start.2 = (f32[512,128]{1,0:T(8,128)S(1)}, f32[512,128]{1,0:T(8,128)S(1)}, u32[]{:S(2)}, u32[]{:S(2)}) collective-permute-start(f32[512,128]{1,0:T(8,128)S(1)} %get-tuple-element.50), channel_id=1, source_target_pairs={{0,8},{8,0},{16,24},{24,16},{1,9},{9,1},{17,25},{25,17},{2,10},{10... | collective-permute-start | bytes 786440 | tf_op jit(solution)/shard_map/ppermute | solution.py:32
  10.2 9.2 %collective-permute-start.7 = (f32[512,128]{1,0:T(8,128)S(1)}, f32[512,128]{1,0:T(8,128)S(1)}, u32[]{:S(2)}, u32[]{:S(2)}) collective-permute-start(f32[512,128]{1,0:T(8,128)S(1)} %get-tuple-element.51.refs_1_), channel_id=1, source_target_pairs={{0,16},{8,24},{16,0},{24,8},{1,17},{9,25},{17,1},{25,9},{2,18},{10... | collective-permute-start | bytes 786440 | tf_op jit(solution)/shard_map/ppermute | solution.py:32
  11.7 12.4 %collective-permute-start.8 = (f32[512,128]{1,0:T(8,128)S(1)}, f32[512,128]{1,0:T(8,128)S(1)}, u32[]{:S(2)}, u32[]{:S(2)}) collective-permute-start(f32[512,128]{1,0:T(8,128)S(1)} %collective-permute-done.3.refs_3_), channel_id=1, source_target_pairs={{0,16},{8,24},{16,0},{24,8},{1,17},{9,25},{17,1},{25,9},{2,18},{10... | collective-permute-start | bytes 786440 | tf_op jit(solution)/shard_map/ppermute | solution.py:32
  14.0 5.4 %collective-permute-start.4 = (f32[200,128]{1,0:T(8,128)S(1)}, f32[200,128]{1,0:T(8,128)S(1)}, u32[]{:S(2)}, u32[]{:S(2)}) collective-permute-start(f32[200,128]{1,0:T(8,128)S(1)} %get-tuple-element.53), channel_id=1, source_target_pairs={{0,8},{1,9},{2,10},{3,11},{4,12},{5,13},{6,14},{7,15},{8,0},{9,1},... | collective-permute-start | bytes 307208 | tf_op jit(solution)/shard_map/ppermute | solution.py:42
  14.1 8.1 %collective-permute-start.5 = (f32[200,128]{1,0:T(8,128)S(1)}, f32[200,128]{1,0:T(8,128)S(1)}, u32[]{:S(2)}, u32[]{:S(2)}) collective-permute-start(f32[200,128]{1,0:T(8,128)S(1)} %get-tuple-element.54), channel_id=1, source_target_pairs={{0,1},{1,0},{2,3},{3,2},{4,5},{5,4},{6,7},{7,6},{8,9},{9,8},{10,11... | collective-permute-start | bytes 307208 | tf_op jit(solution)/shard_map/ppermute | solution.py:42
  18.4 5.4 %collective-permute-start.6 = (f32[200,128]{1,0:T(8,128)S(1)}, f32[200,128]{1,0:T(8,128)S(1)}, u32[]{:S(2)}, u32[]{:S(2)}) collective-permute-start(f32[200,128]{1,0:T(8,128)S(1)} %get-tuple-element.55), channel_id=1, source_target_pairs={{0,9},{1,8},{2,11},{3,10},{4,13},{5,12},{6,15},{7,14},{8,1},{9,0},... | collective-permute-start | bytes 307208 | tf_op jit(solution)/shard_map/ppermute | solution.py:42
  24.8 3.9 %collective-permute-start.9 = (f32[4,64,128]{2,1,0:T(8,128)S(1)}, f32[4,64,128]{2,1,0:T(8,128)S(1)}, u32[]{:S(2)}, u32[]{:S(2)}) collective-permute-start(f32[4,64,128]{2,1,0:T(8,128)S(1)} %get-tuple-element.59), channel_id=1, source_target_pairs={{0,8},{8,0},{16,24},{24,16},{1,9},{9,1},{17,25},{25,17},{2,10},{10... | collective-permute-start | bytes 393224 | tf_op jit(solution)/shard_map/ppermute | solution.py:32
  25.0 7.5 %collective-permute-start.13 = (f32[200,128]{1,0:T(8,128)S(1)}, f32[200,128]{1,0:T(8,128)S(1)}, u32[]{:S(2)}, u32[]{:S(2)}) collective-permute-start(f32[200,128]{1,0:T(8,128)S(1)} %add_add_fusion), channel_id=1, source_target_pairs={{0,2},{1,3},{2,0},{3,1},{4,6},{5,7},{6,4},{7,5},{8,10},{9,11},{10,... | collective-permute-start | bytes 307208 | tf_op jit(solution)/shard_map/ppermute | solution.py:32
  28.7 4.0 %collective-permute-start.10 = (f32[64,128]{1,0:T(8,128)S(1)}, f32[64,128]{1,0:T(8,128)S(1)}, u32[]{:S(2)}, u32[]{:S(2)}) collective-permute-start(f32[64,128]{1,0:T(8,128)S(1)} %get-tuple-element.84), channel_id=1, source_target_pairs={{0,16},{1,17},{2,18},{3,19},{4,20},{5,21},{6,22},{7,23},{8,24},{9,... | collective-permute-start | bytes 98312 | tf_op jit(solution)/shard_map/ppermute | solution.py:42
  30.3 4.8 %collective-permute-start.12 = (f32[64,128]{1,0:T(8,128)S(1)}, f32[64,128]{1,0:T(8,128)S(1)}, u32[]{:S(2)}, u32[]{:S(2)}) collective-permute-start(f32[64,128]{1,0:T(8,128)S(1)} %get-tuple-element.85), channel_id=1, source_target_pairs={{0,17},{1,16},{2,19},{3,18},{4,21},{5,20},{6,23},{7,22},{8,25},{9,... | collective-permute-start | bytes 98312 | tf_op jit(solution)/shard_map/ppermute | solution.py:42
  32.4 3.9 %collective-permute-start.11 = (f32[64,128]{1,0:T(8,128)S(1)}, f32[64,128]{1,0:T(8,128)S(1)}, u32[]{:S(2)}, u32[]{:S(2)}) collective-permute-start(f32[64,128]{1,0:T(8,128)S(1)} %get-tuple-element.86), channel_id=1, source_target_pairs={{0,1},{1,0},{2,3},{3,2},{4,5},{5,4},{6,7},{7,6},{8,9},{9,8},{10,11... | collective-permute-start | bytes 98312 | tf_op jit(solution)/shard_map/ppermute | solution.py:42
  36.3 6.2 %collective-permute-start.15 = (f32[136,128]{1,0:T(8,128)S(1)}, f32[136,128]{1,0:T(8,128)S(1)}, u32[]{:S(2)}, u32[]{:S(2)}) collective-permute-start(f32[136,128]{1,0:T(8,128)S(1)} %slice.38), channel_id=1, source_target_pairs={{0,4},{1,5},{2,6},{3,7},{4,0},{5,1},{6,2},{7,3},{8,12},{9,13},{10,... | collective-permute-start | bytes 208904 | tf_op jit(solution)/shard_map/ppermute | solution.py:32
  38.6 3.9 %collective-permute-start.14 = (f32[64,128]{1,0:T(8,128)S(1)}, f32[64,128]{1,0:T(8,128)S(1)}, u32[]{:S(2)}, u32[]{:S(2)}) collective-permute-start(f32[64,128]{1,0:T(8,128)S(1)} %fusion.6), channel_id=1, source_target_pairs={{0,2},{1,3},{2,0},{3,1},{4,6},{5,7},{6,4},{7,5},{8,10},{9,11},{10,... | collective-permute-start | bytes 98312 | tf_op jit(solution)/shard_map/ppermute | solution.py:32
  42.6 5.9 %collective-permute-start.16 = (f32[128,128]{1,0:T(8,128)S(1)}, f32[128,128]{1,0:T(8,128)S(1)}, u32[]{:S(2)}, u32[]{:S(2)}) collective-permute-start(f32[128,128]{1,0:T(8,128)S(1)} %pad_maximum_fusion.2), channel_id=1, source_target_pairs={{0,4},{1,5},{2,6},{3,7},{4,0},{5,1},{6,2},{7,3},{8,12},{9,13},{10,... | collective-permute-start | bytes 196616 | tf_op jit(solution)/shard_map/ppermute | solution.py:32
  44.0 4.5 %collective-permute-start.17 = (f32[136,128]{1,0:T(8,128)S(1)}, f32[136,128]{1,0:T(8,128)S(1)}, u32[]{:S(2)}, u32[]{:S(2)}) collective-permute-start(f32[136,128]{1,0:T(8,128)S(1)} %slice_add_fusion.4), channel_id=1, source_target_pairs={{0,16},{1,17},{2,18},{3,19},{4,20},{5,21},{6,22},{7,23},{8,24},{9,... | collective-permute-start | bytes 208904 | tf_op jit(solution)/shard_map/ppermute | solution.py:42
  48.6 3.6 %collective-permute-start.18 = (f32[2,136,128]{2,1,0:T(8,128)S(1)}, f32[2,136,128]{2,1,0:T(8,128)S(1)}, u32[]{:S(2)}, u32[]{:S(2)}) collective-permute-start(f32[2,136,128]{2,1,0:T(8,128)S(1)} %pad_maximum_fusion.1.even_ref), channel_id=1, source_target_pairs={{0,8},{8,0},{16,24},{24,16},{1,9},{9,1},{17,25},{25,17},{2,10},{10... | collective-permute-start | bytes 417800 | tf_op jit(solution)/shard_map/ppermute | solution.py:32
  48.7 8.7 %collective-permute-start.21 = (f32[128,128]{1,0:T(8,128)S(1)}, f32[128,128]{1,0:T(8,128)S(1)}, u32[]{:S(2)}, u32[]{:S(2)}) collective-permute-start(f32[128,128]{1,0:T(8,128)S(1)} %fusion.7), channel_id=1, source_target_pairs={{0,17},{1,16},{2,19},{3,18},{4,21},{5,20},{6,23},{7,22},{8,25},{9,... | collective-permute-start | bytes 196616 | tf_op jit(solution)/shard_map/ppermute | solution.py:42
  50.0 7.3 %collective-permute-start.20 = (f32[128,128]{1,0:T(8,128)S(1)}, f32[128,128]{1,0:T(8,128)S(1)}, u32[]{:S(2)}, u32[]{:S(2)}) collective-permute-start(f32[128,128]{1,0:T(8,128)S(1)} %fusion.7), channel_id=1, source_target_pairs={{0,1},{1,0},{2,3},{3,2},{4,5},{5,4},{6,7},{7,6},{8,9},{9,8},{10,11... | collective-permute-start | bytes 196616 | tf_op jit(solution)/shard_map/ppermute | solution.py:42
  51.7 5.6 %collective-permute-start.19 = (f32[128,128]{1,0:T(8,128)S(1)}, f32[128,128]{1,0:T(8,128)S(1)}, u32[]{:S(2)}, u32[]{:S(2)}) collective-permute-start(f32[128,128]{1,0:T(8,128)S(1)} %fusion.7), channel_id=1, source_target_pairs={{0,16},{1,17},{2,18},{3,19},{4,20},{5,21},{6,22},{7,23},{8,24},{9,... | collective-permute-start | bytes 196616 | tf_op jit(solution)/shard_map/ppermute | solution.py:42
  65.1 2.8 %collective-permute-start.24 = (f32[32,512]{1,0:T(8,128)S(1)}, f32[32,512]{1,0:T(8,128)S(1)}, u32[]{:S(2)}, u32[]{:S(2)}) collective-permute-start(f32[32,512]{1,0:T(8,128)S(1)} %get-tuple-element.79), channel_id=1, source_target_pairs={{0,8},{8,0},{16,24},{24,16},{1,9},{9,1},{17,25},{25,17},{2,10},{10... | collective-permute-start | bytes 196616 | tf_op jit(solution)/shard_map/ppermute | solution.py:32
  65.3 4.4 %collective-permute-start.25 = (f32[32,512]{1,0:T(8,128)S(1)}, f32[32,512]{1,0:T(8,128)S(1)}, u32[]{:S(2)}, u32[]{:S(2)}) collective-permute-start(f32[32,512]{1,0:T(8,128)S(1)} %get-tuple-element.80), channel_id=1, source_target_pairs={{0,16},{8,24},{16,0},{24,8},{1,17},{9,25},{17,1},{25,9},{2,18},{10... | collective-permute-start | bytes 196616 | tf_op jit(solution)/shard_map/ppermute | solution.py:32
  66.8 4.1 %collective-permute-start.26 = (f32[32,512]{1,0:T(8,128)S(1)}, f32[32,512]{1,0:T(8,128)S(1)}, u32[]{:S(2)}, u32[]{:S(2)}) collective-permute-start(f32[32,512]{1,0:T(8,128)S(1)} %get-tuple-element.81), channel_id=1, source_target_pairs={{0,24},{8,16},{16,8},{24,0},{1,25},{9,17},{17,9},{25,1},{2,26},{10... | collective-permute-start | bytes 196616 | tf_op jit(solution)/shard_map/ppermute | solution.py:32
  (4 other events, 16.7 us)

commit v16 on v14

--- a/solution.py
+++ b/solution.py
@@ -10,7 +10,7 @@
 SIGN_STEPS = 8
 TAPS = 6
 CHUNK = 8
-ROW_BLOCKS = 2
+ROW_BLOCKS = 1
 F32 = jnp.float32
 VMEM_LIMIT = 48 * 1024 * 1024
 

time: 72 us -> 73.1 us (1.015)
  Pallas kernels: 19.8 us -> 20.9 us
  transfers between devices with their start and end apart: 27 -> 27, of which waited for: 12 -> 12; matrix products, arithmetic and copies ran while one was open for 0% -> 0% of each run, Pallas kernels for 15% -> 16%
where the time goes in v16:
time: 73.1 us; the launch traced here: 72.9 us
  starting transfers between devices  31 us (42%)
  Pallas kernels  20.9 us (29%)
  waiting for transfers between devices  19.9 us (27%)
  between operations  0.84 us (1%)
    ppermute x15, starting transfers between devices, swap(): return lax.ppermute(x, axis, [(i, i ^ mask) for i in range(count)])  14 us
    ppermute x10, starting transfers between devices, swap_both(): return lax.ppermute(x, ('tm', 'space'), route)  13.3 us
    ppermute x15, waiting for transfers between devices, swap(): return lax.ppermute(x, axis, [(i, i ^ mask) for i in range(count)])  11.6 us
    ppermute x10, waiting for transfers between devices, swap_both(): return lax.ppermute(x, ('tm', 'space'), route)  8.31 us
    pallas_call x1, Pallas kernels, local(): pl.pallas_call(functools.partial(merge_kernel, parts, span), out_shape=[s...  6.29 us
    pallas_call x1, Pallas kernels, local(): pl.pallas_call(functools.partial(level_kernel, parts), out_shape=shape(ha...  5.58 us
    pallas_call x1, Pallas kernels, local(): pl.pallas_call(functools.partial(filter_kernel, parts), out_shape=[shape(...  3.87 us
    ppermute x1, starting transfers between devices, local(): lax.ppermute(to_near, 'space', [(i, i ^ 1) for i in range(patches) if i ^...  3 us
  transfers between devices with their start and end apart: 27, of which 12 were waited for; matrix products, arithmetic and copies ran while one was open for 0% of the time, Pallas kernels for 16%

profile of v16, /device:TPU:0, one launch (start us, length us, event | category | flops | bytes accessed | tf_op | source)
XLA Modules:
  0.0 72.9 jit_solution(9483602071337134045)
XLA Ops:
  0.6 1.2 %edge.1 = (f32[64,128]{1,0:T(8,128)S(1)}, f32[64,128]{1,0:T(8,128)S(1)}) custom-call(f32[6]{0:T(128)} %rtaps_ref.3, f32[6]{0:T(128)} %ctaps_ref.3, f32[64,128,128]{2,1,0:T(8,128)} %snap_hbm.1, f32[64,128,128]{2,1,0:T(8,128)} %snap_hbm.1, s32[64,128]{1,0:T(8,128)} %mask_ref.1, s32[64,128]{1,0:T(8,128)} %mask_ref.1), custom_call_target="tpu_custom_call" | custom-call | tf_op jit(solution)/shard_map/edge/pallas_call | solution.py:401
  1.9 3.0 %collective-permute-start = (f32[64,128]{1,0:T(8,128)S(1)}, f32[64,128]{1,0:T(8,128)S(1)}, u32[]{:S(2)}, u32[]{:S(2)}) collective-permute-start(f32[64,128]{1,0:T(8,128)S(1)} %get-tuple-element.43), channel_id=1, source_target_pairs={{0,1},{1,0},{2,3},{3,2},{4,5},{5,4},{6,7},{7,6},{8,9},{9,8},{10,11... | collective-permute-start | bytes 98312 | tf_op jit(solution)/shard_map/ppermute | solution.py:417
  5.6 3.9 %filter.1 = (f32[512,128]{1,0:T(8,128)S(1)}, f32[512,128]{1,0:T(8,128)S(1)}, f32[512,128]{1,0:T(8,128)S(1)}, f32[512,128]{1,0:T(8,128)S(1)}) custom-call(f32[6]{0:T(128)} %rtaps_ref.3, f32[6]{0:T(128)} %ctaps_ref.3, f32[64,128,128]{2,1,0:T(8,128)} %snap_hbm.1, s32[64,128]{1,0:T(8,128)} %mask_ref.1), custom_call_target="tpu_custom_call" | custom-call | bytes 4194304 | tf_op jit(solution)/shard_map/filter/pallas_call | solution.py:421
  10.2 1.5 %collective-permute-start.7 = (f32[512,128]{1,0:T(8,128)S(1)}, f32[512,128]{1,0:T(8,128)S(1)}, u32[]{:S(2)}, u32[]{:S(2)}) collective-permute-start(f32[512,128]{1,0:T(8,128)S(1)} %get-tuple-element.51.refs_1_), channel_id=1, source_target_pairs={{0,16},{8,24},{16,0},{24,8},{1,17},{9,25},{17,1},{25,9},{2,18},{10... | collective-permute-start | bytes 786440 | tf_op jit(solution)/shard_map/ppermute | solution.py:32
  14.1 4.3 %collective-permute-start.5 = (f32[200,128]{1,0:T(8,128)S(1)}, f32[200,128]{1,0:T(8,128)S(1)}, u32[]{:S(2)}, u32[]{:S(2)}) collective-permute-start(f32[200,128]{1,0:T(8,128)S(1)} %get-tuple-element.54), channel_id=1, source_target_pairs={{0,1},{1,0},{2,3},{3,2},{4,5},{5,4},{6,7},{7,6},{8,9},{9,8},{10,11... | collective-permute-start | bytes 307208 | tf_op jit(solution)/shard_map/ppermute | solution.py:42
  19.4 2.8 %collective-permute-done.5 = f32[200,128]{1,0:T(8,128)S(1)} collective-permute-done((f32[200,128]{1,0:T(8,128)S(1)}, f32[200,128]{1,0:T(8,128)S(1)}, u32[]{:S(2)}, u32[]{:S(2)}) %collective-permute-start.5) | collective-permute-done | bytes 102432 | tf_op jit(solution)/shard_map/ppermute | solution.py:42
  22.2 1.7 %collective-permute-done.6 = f32[200,128]{1,0:T(8,128)S(1)} collective-permute-done((f32[200,128]{1,0:T(8,128)S(1)}, f32[200,128]{1,0:T(8,128)S(1)}, u32[]{:S(2)}, u32[]{:S(2)}) %collective-permute-start.6) | collective-permute-done | bytes 102432 | tf_op jit(solution)/shard_map/ppermute | solution.py:42
  25.0 3.7 %collective-permute-start.13 = (f32[200,128]{1,0:T(8,128)S(1)}, f32[200,128]{1,0:T(8,128)S(1)}, u32[]{:S(2)}, u32[]{:S(2)}) collective-permute-start(f32[200,128]{1,0:T(8,128)S(1)} %add_add_fusion), channel_id=1, source_target_pairs={{0,2},{1,3},{2,0},{3,1},{4,6},{5,7},{6,4},{7,5},{8,10},{9,11},{10,... | collective-permute-start | bytes 307208 | tf_op jit(solution)/shard_map/ppermute | solution.py:32
  28.7 1.6 %collective-permute-start.10 = (f32[64,128]{1,0:T(8,128)S(1)}, f32[64,128]{1,0:T(8,128)S(1)}, u32[]{:S(2)}, u32[]{:S(2)}) collective-permute-start(f32[64,128]{1,0:T(8,128)S(1)} %get-tuple-element.84), channel_id=1, source_target_pairs={{0,16},{1,17},{2,18},{3,19},{4,20},{5,21},{6,22},{7,23},{8,24},{9,... | collective-permute-start | bytes 98312 | tf_op jit(solution)/shard_map/ppermute | solution.py:42
  30.3 2.1 %collective-permute-start.12 = (f32[64,128]{1,0:T(8,128)S(1)}, f32[64,128]{1,0:T(8,128)S(1)}, u32[]{:S(2)}, u32[]{:S(2)}) collective-permute-start(f32[64,128]{1,0:T(8,128)S(1)} %get-tuple-element.85), channel_id=1, source_target_pairs={{0,17},{1,16},{2,19},{3,18},{4,21},{5,20},{6,23},{7,22},{8,25},{9,... | collective-permute-start | bytes 98312 | tf_op jit(solution)/shard_map/ppermute | solution.py:42
  32.7 2.4 %collective-permute-done.12 = f32[64,128]{1,0:T(8,128)S(1)} collective-permute-done((f32[64,128]{1,0:T(8,128)S(1)}, f32[64,128]{1,0:T(8,128)S(1)}, u32[]{:S(2)}, u32[]{:S(2)}) %collective-permute-start.12) | collective-permute-done | bytes 32800 | tf_op jit(solution)/shard_map/ppermute | solution.py:42
  36.3 2.3 %collective-permute-start.15 = (f32[136,128]{1,0:T(8,128)S(1)}, f32[136,128]{1,0:T(8,128)S(1)}, u32[]{:S(2)}, u32[]{:S(2)}) collective-permute-start(f32[136,128]{1,0:T(8,128)S(1)} %slice.38), channel_id=1, source_target_pairs={{0,4},{1,5},{2,6},{3,7},{4,0},{5,1},{6,2},{7,3},{8,12},{9,13},{10,... | collective-permute-start | bytes 208904 | tf_op jit(solution)/shard_map/ppermute | solution.py:32
  39.4 3.1 %collective-permute-done.14 = f32[64,128]{1,0:T(8,128)S(1)} collective-permute-done((f32[64,128]{1,0:T(8,128)S(1)}, f32[64,128]{1,0:T(8,128)S(1)}, u32[]{:S(2)}, u32[]{:S(2)}) %collective-permute-start.14) | collective-permute-done | bytes 32800 | tf_op jit(solution)/shard_map/ppermute | solution.py:32
  42.6 1.4 %collective-permute-start.16 = (f32[128,128]{1,0:T(8,128)S(1)}, f32[128,128]{1,0:T(8,128)S(1)}, u32[]{:S(2)}, u32[]{:S(2)}) collective-permute-start(f32[128,128]{1,0:T(8,128)S(1)} %pad_maximum_fusion.2), channel_id=1, source_target_pairs={{0,4},{1,5},{2,6},{3,7},{4,0},{5,1},{6,2},{7,3},{8,12},{9,13},{10,... | collective-permute-start | bytes 196616 | tf_op jit(solution)/shard_map/ppermute | solution.py:32
  44.0 1.5 %collective-permute-start.17 = (f32[136,128]{1,0:T(8,128)S(1)}, f32[136,128]{1,0:T(8,128)S(1)}, u32[]{:S(2)}, u32[]{:S(2)}) collective-permute-start(f32[136,128]{1,0:T(8,128)S(1)} %slice_add_fusion.4), channel_id=1, source_target_pairs={{0,16},{1,17},{2,18},{3,19},{4,20},{5,21},{6,22},{7,23},{8,24},{9,... | collective-permute-start | bytes 208904 | tf_op jit(solution)/shard_map/ppermute | solution.py:42
  45.5 3.0 %collective-permute-done.16 = f32[128,128]{1,0:T(8,128)S(1)} collective-permute-done((f32[128,128]{1,0:T(8,128)S(1)}, f32[128,128]{1,0:T(8,128)S(1)}, u32[]{:S(2)}, u32[]{:S(2)}) %collective-permute-start.16) | collective-permute-done | bytes 65568 | tf_op jit(solution)/shard_map/ppermute | solution.py:32
  48.7 1.4 %collective-permute-start.21 = (f32[128,128]{1,0:T(8,128)S(1)}, f32[128,128]{1,0:T(8,128)S(1)}, u32[]{:S(2)}, u32[]{:S(2)}) collective-permute-start(f32[128,128]{1,0:T(8,128)S(1)} %fusion.7), channel_id=1, source_target_pairs={{0,17},{1,16},{2,19},{3,18},{4,21},{5,20},{6,23},{7,22},{8,25},{9,... | collective-permute-start | bytes 196616 | tf_op jit(solution)/shard_map/ppermute | solution.py:42
  50.0 1.7 %collective-permute-start.20 = (f32[128,128]{1,0:T(8,128)S(1)}, f32[128,128]{1,0:T(8,128)S(1)}, u32[]{:S(2)}, u32[]{:S(2)}) collective-permute-start(f32[128,128]{1,0:T(8,128)S(1)} %fusion.7), channel_id=1, source_target_pairs={{0,1},{1,0},{2,3},{3,2},{4,5},{5,4},{6,7},{7,6},{8,9},{9,8},{10,11... | collective-permute-start | bytes 196616 | tf_op jit(solution)/shard_map/ppermute | solution.py:42
  52.2 5.6 %level.1.mine_ref = f32[1,384,128]{2,1,0:T(8,128)S(1)} custom-call(f32[2,136,128]{2,1,0:T(8,128)S(1)} %pad_maximum_fusion.1.even_ref, f32[2,136,128]{2,1,0:T(8,128)S(1)} %collective-permute-done.18.odd_ref), custom_call_target="tpu_custom_call" | custom-call | flops 3221225472 | tf_op jit(solution)/shard_map/level/pallas_call | solution.py:520
  58.4 1.3 %collective-permute-done.23.theirs_ref = f32[1,384,128]{2,1,0:T(8,128)S(1)} collective-permute-done((f32[1,384,128]{2,1,0:T(8,128)S(1)}, f32[1,384,128]{2,1,0:T(8,128)S(1)}, u32[]{:S(2)}, u32[]{:S(2)}) %collective-permute-start.23) | collective-permute-done | bytes 196640 | tf_op jit(solution)/shard_map/ppermute | solution.py:32
  59.7 6.3 %merge.1 = (f32[32,512]{1,0:T(8,128)S(1)}, f32[32,512]{1,0:T(8,128)S(1)}, f32[32,512]{1,0:T(8,128)S(1)}, f32[32,512]{1,0:T(8,128)S(1)}, f32[512,128]{1,0:T(8,128)S(1)}, /*index=5*/f32[512,128]{1,0:T(8,128)S(1)}) custom-call(f32[4,128,128]{2,1,0:T(8,128)S(1)} %pad_maximum_fusion.even_ref, f32[4,128,128]{2,1,0:T(8,128)S(1)} %collective-permute-done.22.odd_ref, ...), custom_call_target="tpu_custom_call" | custom-call | tf_op jit(solution)/shard_map/merge/pallas_call | solution.py:533
  66.2 1.5 %collective-permute-start.25 = (f32[32,512]{1,0:T(8,128)S(1)}, f32[32,512]{1,0:T(8,128)S(1)}, u32[]{:S(2)}, u32[]{:S(2)}) collective-permute-start(f32[32,512]{1,0:T(8,128)S(1)} %get-tuple-element.80), channel_id=1, source_target_pairs={{0,16},{8,24},{16,0},{24,8},{1,17},{9,25},{17,1},{25,9},{2,18},{10... | collective-permute-start | bytes 196616 | tf_op jit(solution)/shard_map/ppermute | solution.py:32
  68.9 1.7 %collective-permute-done.25.refs_2_ = f32[32,512]{1,0:T(8,128)S(1)} collective-permute-done((f32[32,512]{1,0:T(8,128)S(1)}, f32[32,512]{1,0:T(8,128)S(1)}, u32[]{:S(2)}, u32[]{:S(2)}) %collective-permute-start.25) | collective-permute-done | bytes 65568 | tf_op jit(solution)/shard_map/ppermute | solution.py:32
  70.6 1.3 %collective-permute-done.26.refs_3_ = f32[32,512]{1,0:T(8,128)S(1)} collective-permute-done((f32[32,512]{1,0:T(8,128)S(1)}, f32[32,512]{1,0:T(8,128)S(1)}, u32[]{:S(2)}, u32[]{:S(2)}) %collective-permute-start.26) | collective-permute-done | bytes 65568 | tf_op jit(solution)/shard_map/ppermute | solution.py:32
  (53 shorter events, 11.6 us)
Async XLA Ops:
  1.9 7.5 %collective-permute-start = (f32[64,128]{1,0:T(8,128)S(1)}, f32[64,128]{1,0:T(8,128)S(1)}, u32[]{:S(2)}, u32[]{:S(2)}) collective-permute-start(f32[64,128]{1,0:T(8,128)S(1)} %get-tuple-element.43), channel_id=1, source_target_pairs={{0,1},{1,0},{2,3},{3,2},{4,5},{5,4},{6,7},{7,6},{8,9},{9,8},{10,11... | collective-permute-start | bytes 98312 | tf_op jit(solution)/shard_map/ppermute | solution.py:417
  4.9 4.5 %collective-permute-start.1 = (f32[64,128]{1,0:T(8,128)S(1)}, f32[64,128]{1,0:T(8,128)S(1)}, u32[]{:S(2)}, u32[]{:S(2)}) collective-permute-start(f32[64,128]{1,0:T(8,128)S(1)} %get-tuple-element.44), channel_id=1, source_target_pairs={{1,2},{3,4},{5,6},{2,1},{4,3},{6,5},{9,10},{11,12},{13,14},{10,9},... | collective-permute-start | bytes 98312 | tf_op jit(solution)/shard_map/ppermute | solution.py:419
  9.7 3.0 %collective-permute-start.2 = (f32[512,128]{1,0:T(8,128)S(1)}, f32[512,128]{1,0:T(8,128)S(1)}, u32[]{:S(2)}, u32[]{:S(2)}) collective-permute-start(f32[512,128]{1,0:T(8,128)S(1)} %get-tuple-element.50), channel_id=1, source_target_pairs={{0,8},{8,0},{16,24},{24,16},{1,9},{9,1},{17,25},{25,17},{2,10},{10... | collective-permute-start | bytes 786440 | tf_op jit(solution)/shard_map/ppermute | solution.py:32
  10.2 9.2 %collective-permute-start.7 = (f32[512,128]{1,0:T(8,128)S(1)}, f32[512,128]{1,0:T(8,128)S(1)}, u32[]{:S(2)}, u32[]{:S(2)}) collective-permute-start(f32[512,128]{1,0:T(8,128)S(1)} %get-tuple-element.51.refs_1_), channel_id=1, source_target_pairs={{0,16},{8,24},{16,0},{24,8},{1,17},{9,25},{17,1},{25,9},{2,18},{10... | collective-permute-start | bytes 786440 | tf_op jit(solution)/shard_map/ppermute | solution.py:32
  11.7 12.4 %collective-permute-start.8 = (f32[512,128]{1,0:T(8,128)S(1)}, f32[512,128]{1,0:T(8,128)S(1)}, u32[]{:S(2)}, u32[]{:S(2)}) collective-permute-start(f32[512,128]{1,0:T(8,128)S(1)} %collective-permute-done.3.refs_3_), channel_id=1, source_target_pairs={{0,16},{8,24},{16,0},{24,8},{1,17},{9,25},{17,1},{25,9},{2,18},{10... | collective-permute-start | bytes 786440 | tf_op jit(solution)/shard_map/ppermute | solution.py:32
  14.0 5.4 %collective-permute-start.4 = (f32[200,128]{1,0:T(8,128)S(1)}, f32[200,128]{1,0:T(8,128)S(1)}, u32[]{:S(2)}, u32[]{:S(2)}) collective-permute-start(f32[200,128]{1,0:T(8,128)S(1)} %get-tuple-element.53), channel_id=1, source_target_pairs={{0,8},{1,9},{2,10},{3,11},{4,12},{5,13},{6,14},{7,15},{8,0},{9,1},... | collective-permute-start | bytes 307208 | tf_op jit(solution)/shard_map/ppermute | solution.py:42
  14.1 8.1 %collective-permute-start.5 = (f32[200,128]{1,0:T(8,128)S(1)}, f32[200,128]{1,0:T(8,128)S(1)}, u32[]{:S(2)}, u32[]{:S(2)}) collective-permute-start(f32[200,128]{1,0:T(8,128)S(1)} %get-tuple-element.54), channel_id=1, source_target_pairs={{0,1},{1,0},{2,3},{3,2},{4,5},{5,4},{6,7},{7,6},{8,9},{9,8},{10,11... | collective-permute-start | bytes 307208 | tf_op jit(solution)/shard_map/ppermute | solution.py:42
  18.4 5.4 %collective-permute-start.6 = (f32[200,128]{1,0:T(8,128)S(1)}, f32[200,128]{1,0:T(8,128)S(1)}, u32[]{:S(2)}, u32[]{:S(2)}) collective-permute-start(f32[200,128]{1,0:T(8,128)S(1)} %get-tuple-element.55), channel_id=1, source_target_pairs={{0,9},{1,8},{2,11},{3,10},{4,13},{5,12},{6,15},{7,14},{8,1},{9,0},... | collective-permute-start | bytes 307208 | tf_op jit(solution)/shard_map/ppermute | solution.py:42
  24.8 3.9 %collective-permute-start.9 = (f32[4,64,128]{2,1,0:T(8,128)S(1)}, f32[4,64,128]{2,1,0:T(8,128)S(1)}, u32[]{:S(2)}, u32[]{:S(2)}) collective-permute-start(f32[4,64,128]{2,1,0:T(8,128)S(1)} %get-tuple-element.59), channel_id=1, source_target_pairs={{0,8},{8,0},{16,24},{24,16},{1,9},{9,1},{17,25},{25,17},{2,10},{10... | collective-permute-start | bytes 393224 | tf_op jit(solution)/shard_map/ppermute | solution.py:32
  25.0 7.5 %collective-permute-start.13 = (f32[200,128]{1,0:T(8,128)S(1)}, f32[200,128]{1,0:T(8,128)S(1)}, u32[]{:S(2)}, u32[]{:S(2)}) collective-permute-start(f32[200,128]{1,0:T(8,128)S(1)} %add_add_fusion), channel_id=1, source_target_pairs={{0,2},{1,3},{2,0},{3,1},{4,6},{5,7},{6,4},{7,5},{8,10},{9,11},{10,... | collective-permute-start | bytes 307208 | tf_op jit(solution)/shard_map/ppermute | solution.py:32
  28.7 4.0 %collective-permute-start.10 = (f32[64,128]{1,0:T(8,128)S(1)}, f32[64,128]{1,0:T(8,128)S(1)}, u32[]{:S(2)}, u32[]{:S(2)}) collective-permute-start(f32[64,128]{1,0:T(8,128)S(1)} %get-tuple-element.84), channel_id=1, source_target_pairs={{0,16},{1,17},{2,18},{3,19},{4,20},{5,21},{6,22},{7,23},{8,24},{9,... | collective-permute-start | bytes 98312 | tf_op jit(solution)/shard_map/ppermute | solution.py:42
  30.3 4.8 %collective-permute-start.12 = (f32[64,128]{1,0:T(8,128)S(1)}, f32[64,128]{1,0:T(8,128)S(1)}, u32[]{:S(2)}, u32[]{:S(2)}) collective-permute-start(f32[64,128]{1,0:T(8,128)S(1)} %get-tuple-element.85), channel_id=1, source_target_pairs={{0,17},{1,16},{2,19},{3,18},{4,21},{5,20},{6,23},{7,22},{8,25},{9,... | collective-permute-start | bytes 98312 | tf_op jit(solution)/shard_map/ppermute | solution.py:42
  32.4 3.9 %collective-permute-start.11 = (f32[64,128]{1,0:T(8,128)S(1)}, f32[64,128]{1,0:T(8,128)S(1)}, u32[]{:S(2)}, u32[]{:S(2)}) collective-permute-start(f32[64,128]{1,0:T(8,128)S(1)} %get-tuple-element.86), channel_id=1, source_target_pairs={{0,1},{1,0},{2,3},{3,2},{4,5},{5,4},{6,7},{7,6},{8,9},{9,8},{10,11... | collective-permute-start | bytes 98312 | tf_op jit(solution)/shard_map/ppermute | solution.py:42
  36.3 6.2 %collective-permute-start.15 = (f32[136,128]{1,0:T(8,128)S(1)}, f32[136,128]{1,0:T(8,128)S(1)}, u32[]{:S(2)}, u32[]{:S(2)}) collective-permute-start(f32[136,128]{1,0:T(8,128)S(1)} %slice.38), channel_id=1, source_target_pairs={{0,4},{1,5},{2,6},{3,7},{4,0},{5,1},{6,2},{7,3},{8,12},{9,13},{10,... | collective-permute-start | bytes 208904 | tf_op jit(solution)/shard_map/ppermute | solution.py:32
  38.6 3.9 %collective-permute-start.14 = (f32[64,128]{1,0:T(8,128)S(1)}, f32[64,128]{1,0:T(8,128)S(1)}, u32[]{:S(2)}, u32[]{:S(2)}) collective-permute-start(f32[64,128]{1,0:T(8,128)S(1)} %fusion.6), channel_id=1, source_target_pairs={{0,2},{1,3},{2,0},{3,1},{4,6},{5,7},{6,4},{7,5},{8,10},{9,11},{10,... | collective-permute-start | bytes 98312 | tf_op jit(solution)/shard_map/ppermute | solution.py:32
  42.6 5.9 %collective-permute-start.16 = (f32[128,128]{1,0:T(8,128)S(1)}, f32[128,128]{1,0:T(8,128)S(1)}, u32[]{:S(2)}, u32[]{:S(2)}) collective-permute-start(f32[128,128]{1,0:T(8,128)S(1)} %pad_maximum_fusion.2), channel_id=1, source_target_pairs={{0,4},{1,5},{2,6},{3,7},{4,0},{5,1},{6,2},{7,3},{8,12},{9,13},{10,... | collective-permute-start | bytes 196616 | tf_op jit(solution)/shard_map/ppermute | solution.py:32
  44.0 4.5 %collective-permute-start.17 = (f32[136,128]{1,0:T(8,128)S(1)}, f32[136,128]{1,0:T(8,128)S(1)}, u32[]{:S(2)}, u32[]{:S(2)}) collective-permute-start(f32[136,128]{1,0:T(8,128)S(1)} %slice_add_fusion.4), channel_id=1, source_target_pairs={{0,16},{1,17},{2,18},{3,19},{4,20},{5,21},{6,22},{7,23},{8,24},{9,... | collective-permute-start | bytes 208904 | tf_op jit(solution)/shard_map/ppermute | solution.py:42
  48.6 3.6 %collective-permute-start.18 = (f32[2,136,128]{2,1,0:T(8,128)S(1)}, f32[2,136,128]{2,1,0:T(8,128)S(1)}, u32[]{:S(2)}, u32[]{:S(2)}) collective-permute-start(f32[2,136,128]{2,1,0:T(8,128)S(1)} %pad_maximum_fusion.1.even_ref), channel_id=1, source_target_pairs={{0,8},{8,0},{16,24},{24,16},{1,9},{9,1},{17,25},{25,17},{2,10},{10... | collective-permute-start | bytes 417800 | tf_op jit(solution)/shard_map/ppermute | solution.py:32
  48.7 9.2 %collective-permute-start.21 = (f32[128,128]{1,0:T(8,128)S(1)}, f32[128,128]{1,0:T(8,128)S(1)}, u32[]{:S(2)}, u32[]{:S(2)}) collective-permute-start(f32[128,128]{1,0:T(8,128)S(1)} %fusion.7), channel_id=1, source_target_pairs={{0,17},{1,16},{2,19},{3,18},{4,21},{5,20},{6,23},{7,22},{8,25},{9,... | collective-permute-start | bytes 196616 | tf_op jit(solution)/shard_map/ppermute | solution.py:42
  50.0 7.8 %collective-permute-start.20 = (f32[128,128]{1,0:T(8,128)S(1)}, f32[128,128]{1,0:T(8,128)S(1)}, u32[]{:S(2)}, u32[]{:S(2)}) collective-permute-start(f32[128,128]{1,0:T(8,128)S(1)} %fusion.7), channel_id=1, source_target_pairs={{0,1},{1,0},{2,3},{3,2},{4,5},{5,4},{6,7},{7,6},{8,9},{9,8},{10,11... | collective-permute-start | bytes 196616 | tf_op jit(solution)/shard_map/ppermute | solution.py:42
  51.7 6.1 %collective-permute-start.19 = (f32[128,128]{1,0:T(8,128)S(1)}, f32[128,128]{1,0:T(8,128)S(1)}, u32[]{:S(2)}, u32[]{:S(2)}) collective-permute-start(f32[128,128]{1,0:T(8,128)S(1)} %fusion.7), channel_id=1, source_target_pairs={{0,16},{1,17},{2,18},{3,19},{4,20},{5,21},{6,22},{7,23},{8,24},{9,... | collective-permute-start | bytes 196616 | tf_op jit(solution)/shard_map/ppermute | solution.py:42
  66.0 2.8 %collective-permute-start.24 = (f32[32,512]{1,0:T(8,128)S(1)}, f32[32,512]{1,0:T(8,128)S(1)}, u32[]{:S(2)}, u32[]{:S(2)}) collective-permute-start(f32[32,512]{1,0:T(8,128)S(1)} %get-tuple-element.79), channel_id=1, source_target_pairs={{0,8},{8,0},{16,24},{24,16},{1,9},{9,1},{17,25},{25,17},{2,10},{10... | collective-permute-start | bytes 196616 | tf_op jit(solution)/shard_map/ppermute | solution.py:32
  66.2 4.4 %collective-permute-start.25 = (f32[32,512]{1,0:T(8,128)S(1)}, f32[32,512]{1,0:T(8,128)S(1)}, u32[]{:S(2)}, u32[]{:S(2)}) collective-permute-start(f32[32,512]{1,0:T(8,128)S(1)} %get-tuple-element.80), channel_id=1, source_target_pairs={{0,16},{8,24},{16,0},{24,8},{1,17},{9,25},{17,1},{25,9},{2,18},{10... | collective-permute-start | bytes 196616 | tf_op jit(solution)/shard_map/ppermute | solution.py:32
  67.8 4.1 %collective-permute-start.26 = (f32[32,512]{1,0:T(8,128)S(1)}, f32[32,512]{1,0:T(8,128)S(1)}, u32[]{:S(2)}, u32[]{:S(2)}) collective-permute-start(f32[32,512]{1,0:T(8,128)S(1)} %get-tuple-element.81), channel_id=1, source_target_pairs={{0,24},{8,16},{16,8},{24,0},{1,25},{9,17},{17,9},{25,1},{2,26},{10... | collective-permute-start | bytes 196616 | tf_op jit(solution)/shard_map/ppermute | solution.py:32
  (4 other events, 16.7 us)

commit v17 on v14

--- a/solution.py
+++ b/solution.py
@@ -496,10 +496,10 @@
         mine = mine + swap_both(keep[h] + got[h], 2 * h)
     for bit in bits[:1]:
         pair_share = pair_share + swap(pair_share, "space", bit)
-    mine, pair_share = lax.optimization_barrier((mine, pair_share))
     pair_share, product_share = pair_share[:pair_size], pair_share[pair_size:]
     for bit in bits[1:]:
         pair_share = pair_share + swap(pair_share, "space", bit)
+    mine, pair_share = lax.optimization_barrier((mine, pair_share))
     for bit in bits[:1]:
         mine = mine + swap(mine, "space", bit)
     mine, pair_share = lax.optimization_barrier((mine, pair_share))

time: 72 us -> 72.7 us (level)
    ppermute x15, waiting for transfers between devices: 11.6 us -> 14 us  [swap(): return lax.ppermute(x, axis, [(i, i ^ mask) for i in range(count)])]
    ppermute x10, waiting for transfers between devices: 8.31 us -> 5.9 us  [swap_both(): return lax.ppermute(x, ('tm', 'space'), route)]
where the time goes in v17:
time: 72.7 us; the launch traced here: 72.5 us
  starting transfers between devices  31.7 us (44%)
  waiting for transfers between devices  20 us (28%)
  Pallas kernels  19.8 us (27%)
  between operations  0.82 us (1%)
    ppermute x15, starting transfers between devices, swap(): return lax.ppermute(x, axis, [(i, i ^ mask) for i in range(count)])  14.4 us
    ppermute x15, waiting for transfers between devices, swap(): return lax.ppermute(x, axis, [(i, i ^ mask) for i in range(count)])  14 us
    ppermute x10, starting transfers between devices, swap_both(): return lax.ppermute(x, ('tm', 'space'), route)  13.7 us
    ppermute x10, waiting for transfers between devices, swap_both(): return lax.ppermute(x, ('tm', 'space'), route)  5.9 us
    pallas_call x1, Pallas kernels, local(): pl.pallas_call(functools.partial(merge_kernel, parts, span), out_shape=[s...  5.69 us
    pallas_call x1, Pallas kernels, local(): pl.pallas_call(functools.partial(level_kernel, parts), out_shape=shape(ha...  5.07 us
    pallas_call x1, Pallas kernels, local(): pl.pallas_call(functools.partial(filter_kernel, parts), out_shape=[shape(...  3.87 us
    ppermute x1, starting transfers between devices, local(): lax.ppermute(to_near, 'space', [(i, i ^ 1) for i in range(patches) if i ^...  3 us
  transfers between devices with their start and end apart: 27, of which 12 were waited for; matrix products, arithmetic and copies ran while one was open for 0% of the time, Pallas kernels for 15%

profile of v17, /device:TPU:0, one launch (start us, length us, event | category | flops | bytes accessed | tf_op | source)
XLA Modules:
  0.0 72.5 jit_solution(6940453204710807880)
XLA Ops:
  0.6 1.2 %edge.1 = (f32[64,128]{1,0:T(8,128)S(1)}, f32[64,128]{1,0:T(8,128)S(1)}) custom-call(f32[6]{0:T(128)} %rtaps_ref.3, f32[6]{0:T(128)} %ctaps_ref.3, f32[64,128,128]{2,1,0:T(8,128)} %snap_hbm.1, f32[64,128,128]{2,1,0:T(8,128)} %snap_hbm.1, s32[64,128]{1,0:T(8,128)} %mask_ref.1, s32[64,128]{1,0:T(8,128)} %mask_ref.1), custom_call_target="tpu_custom_call" | custom-call | tf_op jit(solution)/shard_map/edge/pallas_call | solution.py:401
  1.9 3.0 %collective-permute-start = (f32[64,128]{1,0:T(8,128)S(1)}, f32[64,128]{1,0:T(8,128)S(1)}, u32[]{:S(2)}, u32[]{:S(2)}) collective-permute-start(f32[64,128]{1,0:T(8,128)S(1)} %get-tuple-element.43), channel_id=1, source_target_pairs={{0,1},{1,0},{2,3},{3,2},{4,5},{5,4},{6,7},{7,6},{8,9},{9,8},{10,11... | collective-permute-start | bytes 98312 | tf_op jit(solution)/shard_map/ppermute | solution.py:417
  5.6 3.9 %filter.1 = (f32[512,128]{1,0:T(8,128)S(1)}, f32[512,128]{1,0:T(8,128)S(1)}, f32[512,128]{1,0:T(8,128)S(1)}, f32[512,128]{1,0:T(8,128)S(1)}) custom-call(f32[6]{0:T(128)} %rtaps_ref.3, f32[6]{0:T(128)} %ctaps_ref.3, f32[64,128,128]{2,1,0:T(8,128)} %snap_hbm.1, s32[64,128]{1,0:T(8,128)} %mask_ref.1), custom_call_target="tpu_custom_call" | custom-call | bytes 4194304 | tf_op jit(solution)/shard_map/filter/pallas_call | solution.py:421
  10.2 1.5 %collective-permute-start.7 = (f32[512,128]{1,0:T(8,128)S(1)}, f32[512,128]{1,0:T(8,128)S(1)}, u32[]{:S(2)}, u32[]{:S(2)}) collective-permute-start(f32[512,128]{1,0:T(8,128)S(1)} %get-tuple-element.51.refs_1_), channel_id=1, source_target_pairs={{0,16},{8,24},{16,0},{24,8},{1,17},{9,25},{17,1},{25,9},{2,18},{10... | collective-permute-start | bytes 786440 | tf_op jit(solution)/shard_map/ppermute | solution.py:32
  12.8 1.2 %pair.1 = (f32[200,128]{1,0:T(8,128)S(1)}, f32[200,128]{1,0:T(8,128)S(1)}, f32[200,128]{1,0:T(8,128)S(1)}, f32[200,128]{1,0:T(8,128)S(1)}) custom-call(f32[2048,128]{1,0:T(8,128)S(1)} %bitcast.22, f32[512,128]{1,0:T(8,128)S(1)} %get-tuple-element.49.refs_0_, f32[512,128]{1,0:T(8,128)S(1)} %get-tuple-element.51.refs_1_, ...), custom_call_target="tpu_custom_call" | custom-call | tf_op jit(solution)/shard_map/pair/pallas_call | solution.py:455
  14.1 4.3 %collective-permute-start.5 = (f32[200,128]{1,0:T(8,128)S(1)}, f32[200,128]{1,0:T(8,128)S(1)}, u32[]{:S(2)}, u32[]{:S(2)}) collective-permute-start(f32[200,128]{1,0:T(8,128)S(1)} %get-tuple-element.54), channel_id=1, source_target_pairs={{0,1},{1,0},{2,3},{3,2},{4,5},{5,4},{6,7},{7,6},{8,9},{9,8},{10,11... | collective-permute-start | bytes 307208 | tf_op jit(solution)/shard_map/ppermute | solution.py:42
  19.4 2.8 %collective-permute-done.5 = f32[200,128]{1,0:T(8,128)S(1)} collective-permute-done((f32[200,128]{1,0:T(8,128)S(1)}, f32[200,128]{1,0:T(8,128)S(1)}, u32[]{:S(2)}, u32[]{:S(2)}) %collective-permute-start.5) | collective-permute-done | bytes 102432 | tf_op jit(solution)/shard_map/ppermute | solution.py:42
  22.2 1.7 %collective-permute-done.6 = f32[200,128]{1,0:T(8,128)S(1)} collective-permute-done((f32[200,128]{1,0:T(8,128)S(1)}, f32[200,128]{1,0:T(8,128)S(1)}, u32[]{:S(2)}, u32[]{:S(2)}) %collective-permute-start.6) | collective-permute-done | bytes 102432 | tf_op jit(solution)/shard_map/ppermute | solution.py:42
  25.0 3.7 %collective-permute-start.13 = (f32[200,128]{1,0:T(8,128)S(1)}, f32[200,128]{1,0:T(8,128)S(1)}, u32[]{:S(2)}, u32[]{:S(2)}) collective-permute-start(f32[200,128]{1,0:T(8,128)S(1)} %add_add_fusion), channel_id=1, source_target_pairs={{0,2},{1,3},{2,0},{3,1},{4,6},{5,7},{6,4},{7,5},{8,10},{9,11},{10,... | collective-permute-start | bytes 307208 | tf_op jit(solution)/shard_map/ppermute | solution.py:32
  28.7 1.6 %collective-permute-start.10 = (f32[64,128]{1,0:T(8,128)S(1)}, f32[64,128]{1,0:T(8,128)S(1)}, u32[]{:S(2)}, u32[]{:S(2)}) collective-permute-start(f32[64,128]{1,0:T(8,128)S(1)} %get-tuple-element.84), channel_id=1, source_target_pairs={{0,16},{1,17},{2,18},{3,19},{4,20},{5,21},{6,22},{7,23},{8,24},{9,... | collective-permute-start | bytes 98312 | tf_op jit(solution)/shard_map/ppermute | solution.py:42
  30.3 2.1 %collective-permute-start.12 = (f32[64,128]{1,0:T(8,128)S(1)}, f32[64,128]{1,0:T(8,128)S(1)}, u32[]{:S(2)}, u32[]{:S(2)}) collective-permute-start(f32[64,128]{1,0:T(8,128)S(1)} %get-tuple-element.85), channel_id=1, source_target_pairs={{0,17},{1,16},{2,19},{3,18},{4,21},{5,20},{6,23},{7,22},{8,25},{9,... | collective-permute-start | bytes 98312 | tf_op jit(solution)/shard_map/ppermute | solution.py:42
  32.5 2.6 %collective-permute-start.14 = (f32[136,128]{1,0:T(8,128)S(1)}, f32[136,128]{1,0:T(8,128)S(1)}, u32[]{:S(2)}, u32[]{:S(2)}) collective-permute-start(f32[136,128]{1,0:T(8,128)S(1)} %slice.44), channel_id=1, source_target_pairs={{0,4},{1,5},{2,6},{3,7},{4,0},{5,1},{6,2},{7,3},{8,12},{9,13},{10,... | collective-permute-start | bytes 208904 | tf_op jit(solution)/shard_map/ppermute | solution.py:32
  35.1 1.2 %collective-permute-done.11 = f32[64,128]{1,0:T(8,128)S(1)} collective-permute-done((f32[64,128]{1,0:T(8,128)S(1)}, f32[64,128]{1,0:T(8,128)S(1)}, u32[]{:S(2)}, u32[]{:S(2)}) %collective-permute-start.11) | collective-permute-done | bytes 32800 | tf_op jit(solution)/shard_map/ppermute | solution.py:42
  36.3 2.6 %collective-permute-done.14 = f32[136,128]{1,0:T(8,128)S(1)} collective-permute-done((f32[136,128]{1,0:T(8,128)S(1)}, f32[136,128]{1,0:T(8,128)S(1)}, u32[]{:S(2)}, u32[]{:S(2)}) %collective-permute-start.14) | collective-permute-done | bytes 69664 | tf_op jit(solution)/shard_map/ppermute | solution.py:32
  39.4 3.5 %collective-permute-done.15 = f32[64,128]{1,0:T(8,128)S(1)} collective-permute-done((f32[64,128]{1,0:T(8,128)S(1)}, f32[64,128]{1,0:T(8,128)S(1)}, u32[]{:S(2)}, u32[]{:S(2)}) %collective-permute-start.15) | collective-permute-done | bytes 32800 | tf_op jit(solution)/shard_map/ppermute | solution.py:32
  42.9 1.8 %collective-permute-start.16 = (f32[128,128]{1,0:T(8,128)S(1)}, f32[128,128]{1,0:T(8,128)S(1)}, u32[]{:S(2)}, u32[]{:S(2)}) collective-permute-start(f32[128,128]{1,0:T(8,128)S(1)} %pad_maximum_fusion.2), channel_id=1, source_target_pairs={{0,4},{1,5},{2,6},{3,7},{4,0},{5,1},{6,2},{7,3},{8,12},{9,13},{10,... | collective-permute-start | bytes 196616 | tf_op jit(solution)/shard_map/ppermute | solution.py:32
  44.8 1.5 %collective-permute-start.17 = (f32[136,128]{1,0:T(8,128)S(1)}, f32[136,128]{1,0:T(8,128)S(1)}, u32[]{:S(2)}, u32[]{:S(2)}) collective-permute-start(f32[136,128]{1,0:T(8,128)S(1)} %slice_add_fusion.4), channel_id=1, source_target_pairs={{0,16},{1,17},{2,18},{3,19},{4,20},{5,21},{6,22},{7,23},{8,24},{9,... | collective-permute-start | bytes 208904 | tf_op jit(solution)/shard_map/ppermute | solution.py:42
  46.3 2.6 %collective-permute-done.16 = f32[128,128]{1,0:T(8,128)S(1)} collective-permute-done((f32[128,128]{1,0:T(8,128)S(1)}, f32[128,128]{1,0:T(8,128)S(1)}, u32[]{:S(2)}, u32[]{:S(2)}) %collective-permute-start.16) | collective-permute-done | bytes 65568 | tf_op jit(solution)/shard_map/ppermute | solution.py:32
  49.2 3.3 %collective-permute-start.21 = (f32[128,128]{1,0:T(8,128)S(1)}, f32[128,128]{1,0:T(8,128)S(1)}, u32[]{:S(2)}, u32[]{:S(2)}) collective-permute-start(f32[128,128]{1,0:T(8,128)S(1)} %fusion.7), channel_id=1, source_target_pairs={{0,17},{1,16},{2,19},{3,18},{4,21},{5,20},{6,23},{7,22},{8,25},{9,... | collective-permute-start | bytes 196616 | tf_op jit(solution)/shard_map/ppermute | solution.py:42
  53.1 5.1 %level.1.mine_ref = f32[1,384,128]{2,1,0:T(8,128)S(1)} custom-call(f32[2,136,128]{2,1,0:T(8,128)S(1)} %pad_maximum_fusion.1.even_ref, f32[2,136,128]{2,1,0:T(8,128)S(1)} %collective-permute-done.18.odd_ref), custom_call_target="tpu_custom_call" | custom-call | flops 3221225472 | tf_op jit(solution)/shard_map/level/pallas_call | solution.py:520
  58.8 1.3 %collective-permute-done.23.theirs_ref = f32[1,384,128]{2,1,0:T(8,128)S(1)} collective-permute-done((f32[1,384,128]{2,1,0:T(8,128)S(1)}, f32[1,384,128]{2,1,0:T(8,128)S(1)}, u32[]{:S(2)}, u32[]{:S(2)}) %collective-permute-start.23) | collective-permute-done | bytes 196640 | tf_op jit(solution)/shard_map/ppermute | solution.py:32
  60.1 5.7 %merge.1 = (f32[32,512]{1,0:T(8,128)S(1)}, f32[32,512]{1,0:T(8,128)S(1)}, f32[32,512]{1,0:T(8,128)S(1)}, f32[32,512]{1,0:T(8,128)S(1)}, f32[512,128]{1,0:T(8,128)S(1)}, /*index=5*/f32[512,128]{1,0:T(8,128)S(1)}) custom-call(f32[4,128,128]{2,1,0:T(8,128)S(1)} %pad_maximum_fusion.even_ref, f32[4,128,128]{2,1,0:T(8,128)S(1)} %collective-permute-done.22.odd_ref, ...), custom_call_target="tpu_custom_call" | custom-call | tf_op jit(solution)/shard_map/merge/pallas_call | solution.py:533
  66.0 1.4 %collective-permute-start.25 = (f32[32,512]{1,0:T(8,128)S(1)}, f32[32,512]{1,0:T(8,128)S(1)}, u32[]{:S(2)}, u32[]{:S(2)}) collective-permute-start(f32[32,512]{1,0:T(8,128)S(1)} %get-tuple-element.80), channel_id=1, source_target_pairs={{0,16},{8,24},{16,0},{24,8},{1,17},{9,25},{17,1},{25,9},{2,18},{10... | collective-permute-start | bytes 196616 | tf_op jit(solution)/shard_map/ppermute | solution.py:32
  68.7 1.7 %collective-permute-done.25.refs_2_ = f32[32,512]{1,0:T(8,128)S(1)} collective-permute-done((f32[32,512]{1,0:T(8,128)S(1)}, f32[32,512]{1,0:T(8,128)S(1)}, u32[]{:S(2)}, u32[]{:S(2)}) %collective-permute-start.25) | collective-permute-done | bytes 65568 | tf_op jit(solution)/shard_map/ppermute | solution.py:32
  (53 shorter events, 10.3 us)
Async XLA Ops:
  1.9 7.5 %collective-permute-start = (f32[64,128]{1,0:T(8,128)S(1)}, f32[64,128]{1,0:T(8,128)S(1)}, u32[]{:S(2)}, u32[]{:S(2)}) collective-permute-start(f32[64,128]{1,0:T(8,128)S(1)} %get-tuple-element.43), channel_id=1, source_target_pairs={{0,1},{1,0},{2,3},{3,2},{4,5},{5,4},{6,7},{7,6},{8,9},{9,8},{10,11... | collective-permute-start | bytes 98312 | tf_op jit(solution)/shard_map/ppermute | solution.py:417
  4.9 4.5 %collective-permute-start.1 = (f32[64,128]{1,0:T(8,128)S(1)}, f32[64,128]{1,0:T(8,128)S(1)}, u32[]{:S(2)}, u32[]{:S(2)}) collective-permute-start(f32[64,128]{1,0:T(8,128)S(1)} %get-tuple-element.44), channel_id=1, source_target_pairs={{1,2},{3,4},{5,6},{2,1},{4,3},{6,5},{9,10},{11,12},{13,14},{10,9},... | collective-permute-start | bytes 98312 | tf_op jit(solution)/shard_map/ppermute | solution.py:419
  9.7 3.0 %collective-permute-start.2 = (f32[512,128]{1,0:T(8,128)S(1)}, f32[512,128]{1,0:T(8,128)S(1)}, u32[]{:S(2)}, u32[]{:S(2)}) collective-permute-start(f32[512,128]{1,0:T(8,128)S(1)} %get-tuple-element.50), channel_id=1, source_target_pairs={{0,8},{8,0},{16,24},{24,16},{1,9},{9,1},{17,25},{25,17},{2,10},{10... | collective-permute-start | bytes 786440 | tf_op jit(solution)/shard_map/ppermute | solution.py:32
  10.2 9.2 %collective-permute-start.7 = (f32[512,128]{1,0:T(8,128)S(1)}, f32[512,128]{1,0:T(8,128)S(1)}, u32[]{:S(2)}, u32[]{:S(2)}) collective-permute-start(f32[512,128]{1,0:T(8,128)S(1)} %get-tuple-element.51.refs_1_), channel_id=1, source_target_pairs={{0,16},{8,24},{16,0},{24,8},{1,17},{9,25},{17,1},{25,9},{2,18},{10... | collective-permute-start | bytes 786440 | tf_op jit(solution)/shard_map/ppermute | solution.py:32
  11.7 12.4 %collective-permute-start.8 = (f32[512,128]{1,0:T(8,128)S(1)}, f32[512,128]{1,0:T(8,128)S(1)}, u32[]{:S(2)}, u32[]{:S(2)}) collective-permute-start(f32[512,128]{1,0:T(8,128)S(1)} %collective-permute-done.3.refs_3_), channel_id=1, source_target_pairs={{0,16},{8,24},{16,0},{24,8},{1,17},{9,25},{17,1},{25,9},{2,18},{10... | collective-permute-start | bytes 786440 | tf_op jit(solution)/shard_map/ppermute | solution.py:32
  14.0 5.4 %collective-permute-start.4 = (f32[200,128]{1,0:T(8,128)S(1)}, f32[200,128]{1,0:T(8,128)S(1)}, u32[]{:S(2)}, u32[]{:S(2)}) collective-permute-start(f32[200,128]{1,0:T(8,128)S(1)} %get-tuple-element.53), channel_id=1, source_target_pairs={{0,8},{1,9},{2,10},{3,11},{4,12},{5,13},{6,14},{7,15},{8,0},{9,1},... | collective-permute-start | bytes 307208 | tf_op jit(solution)/shard_map/ppermute | solution.py:42
  14.1 8.1 %collective-permute-start.5 = (f32[200,128]{1,0:T(8,128)S(1)}, f32[200,128]{1,0:T(8,128)S(1)}, u32[]{:S(2)}, u32[]{:S(2)}) collective-permute-start(f32[200,128]{1,0:T(8,128)S(1)} %get-tuple-element.54), channel_id=1, source_target_pairs={{0,1},{1,0},{2,3},{3,2},{4,5},{5,4},{6,7},{7,6},{8,9},{9,8},{10,11... | collective-permute-start | bytes 307208 | tf_op jit(solution)/shard_map/ppermute | solution.py:42
  18.4 5.4 %collective-permute-start.6 = (f32[200,128]{1,0:T(8,128)S(1)}, f32[200,128]{1,0:T(8,128)S(1)}, u32[]{:S(2)}, u32[]{:S(2)}) collective-permute-start(f32[200,128]{1,0:T(8,128)S(1)} %get-tuple-element.55), channel_id=1, source_target_pairs={{0,9},{1,8},{2,11},{3,10},{4,13},{5,12},{6,15},{7,14},{8,1},{9,0},... | collective-permute-start | bytes 307208 | tf_op jit(solution)/shard_map/ppermute | solution.py:42
  24.8 3.9 %collective-permute-start.9 = (f32[4,64,128]{2,1,0:T(8,128)S(1)}, f32[4,64,128]{2,1,0:T(8,128)S(1)}, u32[]{:S(2)}, u32[]{:S(2)}) collective-permute-start(f32[4,64,128]{2,1,0:T(8,128)S(1)} %get-tuple-element.59), channel_id=1, source_target_pairs={{0,8},{8,0},{16,24},{24,16},{1,9},{9,1},{17,25},{25,17},{2,10},{10... | collective-permute-start | bytes 393224 | tf_op jit(solution)/shard_map/ppermute | solution.py:32
  25.0 7.5 %collective-permute-start.13 = (f32[200,128]{1,0:T(8,128)S(1)}, f32[200,128]{1,0:T(8,128)S(1)}, u32[]{:S(2)}, u32[]{:S(2)}) collective-permute-start(f32[200,128]{1,0:T(8,128)S(1)} %add_add_fusion), channel_id=1, source_target_pairs={{0,2},{1,3},{2,0},{3,1},{4,6},{5,7},{6,4},{7,5},{8,10},{9,11},{10,... | collective-permute-start | bytes 307208 | tf_op jit(solution)/shard_map/ppermute | solution.py:32
  28.7 6.4 %collective-permute-start.10 = (f32[64,128]{1,0:T(8,128)S(1)}, f32[64,128]{1,0:T(8,128)S(1)}, u32[]{:S(2)}, u32[]{:S(2)}) collective-permute-start(f32[64,128]{1,0:T(8,128)S(1)} %get-tuple-element.84), channel_id=1, source_target_pairs={{0,16},{1,17},{2,18},{3,19},{4,20},{5,21},{6,22},{7,23},{8,24},{9,... | collective-permute-start | bytes 98312 | tf_op jit(solution)/shard_map/ppermute | solution.py:42
  30.3 4.8 %collective-permute-start.12 = (f32[64,128]{1,0:T(8,128)S(1)}, f32[64,128]{1,0:T(8,128)S(1)}, u32[]{:S(2)}, u32[]{:S(2)}) collective-permute-start(f32[64,128]{1,0:T(8,128)S(1)} %get-tuple-element.85), channel_id=1, source_target_pairs={{0,17},{1,16},{2,19},{3,18},{4,21},{5,20},{6,23},{7,22},{8,25},{9,... | collective-permute-start | bytes 98312 | tf_op jit(solution)/shard_map/ppermute | solution.py:42
  32.4 3.9 %collective-permute-start.11 = (f32[64,128]{1,0:T(8,128)S(1)}, f32[64,128]{1,0:T(8,128)S(1)}, u32[]{:S(2)}, u32[]{:S(2)}) collective-permute-start(f32[64,128]{1,0:T(8,128)S(1)} %get-tuple-element.86), channel_id=1, source_target_pairs={{0,1},{1,0},{2,3},{3,2},{4,5},{5,4},{6,7},{7,6},{8,9},{9,8},{10,11... | collective-permute-start | bytes 98312 | tf_op jit(solution)/shard_map/ppermute | solution.py:42
  32.5 6.4 %collective-permute-start.14 = (f32[136,128]{1,0:T(8,128)S(1)}, f32[136,128]{1,0:T(8,128)S(1)}, u32[]{:S(2)}, u32[]{:S(2)}) collective-permute-start(f32[136,128]{1,0:T(8,128)S(1)} %slice.44), channel_id=1, source_target_pairs={{0,4},{1,5},{2,6},{3,7},{4,0},{5,1},{6,2},{7,3},{8,12},{9,13},{10,... | collective-permute-start | bytes 208904 | tf_op jit(solution)/shard_map/ppermute | solution.py:32
  38.9 4.0 %collective-permute-start.15 = (f32[64,128]{1,0:T(8,128)S(1)}, f32[64,128]{1,0:T(8,128)S(1)}, u32[]{:S(2)}, u32[]{:S(2)}) collective-permute-start(f32[64,128]{1,0:T(8,128)S(1)} %fusion.6), channel_id=1, source_target_pairs={{0,2},{1,3},{2,0},{3,1},{4,6},{5,7},{6,4},{7,5},{8,10},{9,11},{10,... | collective-permute-start | bytes 98312 | tf_op jit(solution)/shard_map/ppermute | solution.py:32
  42.9 5.9 %collective-permute-start.16 = (f32[128,128]{1,0:T(8,128)S(1)}, f32[128,128]{1,0:T(8,128)S(1)}, u32[]{:S(2)}, u32[]{:S(2)}) collective-permute-start(f32[128,128]{1,0:T(8,128)S(1)} %pad_maximum_fusion.2), channel_id=1, source_target_pairs={{0,4},{1,5},{2,6},{3,7},{4,0},{5,1},{6,2},{7,3},{8,12},{9,13},{10,... | collective-permute-start | bytes 196616 | tf_op jit(solution)/shard_map/ppermute | solution.py:32
  44.8 4.3 %collective-permute-start.17 = (f32[136,128]{1,0:T(8,128)S(1)}, f32[136,128]{1,0:T(8,128)S(1)}, u32[]{:S(2)}, u32[]{:S(2)}) collective-permute-start(f32[136,128]{1,0:T(8,128)S(1)} %slice_add_fusion.4), channel_id=1, source_target_pairs={{0,16},{1,17},{2,18},{3,19},{4,20},{5,21},{6,22},{7,23},{8,24},{9,... | collective-permute-start | bytes 208904 | tf_op jit(solution)/shard_map/ppermute | solution.py:42
  49.1 4.0 %collective-permute-start.18 = (f32[2,136,128]{2,1,0:T(8,128)S(1)}, f32[2,136,128]{2,1,0:T(8,128)S(1)}, u32[]{:S(2)}, u32[]{:S(2)}) collective-permute-start(f32[2,136,128]{2,1,0:T(8,128)S(1)} %pad_maximum_fusion.1.even_ref), channel_id=1, source_target_pairs={{0,8},{8,0},{16,24},{24,16},{1,9},{9,1},{17,25},{25,17},{2,10},{10... | collective-permute-start | bytes 417800 | tf_op jit(solution)/shard_map/ppermute | solution.py:32
  49.2 9.0 %collective-permute-start.21 = (f32[128,128]{1,0:T(8,128)S(1)}, f32[128,128]{1,0:T(8,128)S(1)}, u32[]{:S(2)}, u32[]{:S(2)}) collective-permute-start(f32[128,128]{1,0:T(8,128)S(1)} %fusion.7), channel_id=1, source_target_pairs={{0,17},{1,16},{2,19},{3,18},{4,21},{5,20},{6,23},{7,22},{8,25},{9,... | collective-permute-start | bytes 196616 | tf_op jit(solution)/shard_map/ppermute | solution.py:42
  52.4 5.7 %collective-permute-start.20 = (f32[128,128]{1,0:T(8,128)S(1)}, f32[128,128]{1,0:T(8,128)S(1)}, u32[]{:S(2)}, u32[]{:S(2)}) collective-permute-start(f32[128,128]{1,0:T(8,128)S(1)} %fusion.7), channel_id=1, source_target_pairs={{0,1},{1,0},{2,3},{3,2},{4,5},{5,4},{6,7},{7,6},{8,9},{9,8},{10,11... | collective-permute-start | bytes 196616 | tf_op jit(solution)/shard_map/ppermute | solution.py:42
  52.4 5.7 %collective-permute-start.19 = (f32[128,128]{1,0:T(8,128)S(1)}, f32[128,128]{1,0:T(8,128)S(1)}, u32[]{:S(2)}, u32[]{:S(2)}) collective-permute-start(f32[128,128]{1,0:T(8,128)S(1)} %fusion.7), channel_id=1, source_target_pairs={{0,16},{1,17},{2,18},{3,19},{4,20},{5,21},{6,22},{7,23},{8,24},{9,... | collective-permute-start | bytes 196616 | tf_op jit(solution)/shard_map/ppermute | solution.py:42
  65.8 2.8 %collective-permute-start.24 = (f32[32,512]{1,0:T(8,128)S(1)}, f32[32,512]{1,0:T(8,128)S(1)}, u32[]{:S(2)}, u32[]{:S(2)}) collective-permute-start(f32[32,512]{1,0:T(8,128)S(1)} %get-tuple-element.79), channel_id=1, source_target_pairs={{0,8},{8,0},{16,24},{24,16},{1,9},{9,1},{17,25},{25,17},{2,10},{10... | collective-permute-start | bytes 196616 | tf_op jit(solution)/shard_map/ppermute | solution.py:32
  66.0 4.4 %collective-permute-start.25 = (f32[32,512]{1,0:T(8,128)S(1)}, f32[32,512]{1,0:T(8,128)S(1)}, u32[]{:S(2)}, u32[]{:S(2)}) collective-permute-start(f32[32,512]{1,0:T(8,128)S(1)} %get-tuple-element.80), channel_id=1, source_target_pairs={{0,16},{8,24},{16,0},{24,8},{1,17},{9,25},{17,1},{25,9},{2,18},{10... | collective-permute-start | bytes 196616 | tf_op jit(solution)/shard_map/ppermute | solution.py:32
  67.4 4.1 %collective-permute-start.26 = (f32[32,512]{1,0:T(8,128)S(1)}, f32[32,512]{1,0:T(8,128)S(1)}, u32[]{:S(2)}, u32[]{:S(2)}) collective-permute-start(f32[32,512]{1,0:T(8,128)S(1)} %get-tuple-element.81), channel_id=1, source_target_pairs={{0,24},{8,16},{16,8},{24,0},{1,25},{9,17},{17,9},{25,1},{2,26},{10... | collective-permute-start | bytes 196616 | tf_op jit(solution)/shard_map/ppermute | solution.py:32
  (4 other events, 16.7 us)

commit v18 on v14

--- a/solution.py
+++ b/solution.py
@@ -9,7 +9,7 @@
 
 SIGN_STEPS = 8
 TAPS = 6
-CHUNK = 8
+CHUNK = 16
 ROW_BLOCKS = 2
 F32 = jnp.float32
 VMEM_LIMIT = 48 * 1024 * 1024

time: 72 us -> 72.1 us (level)
  no operation moved by 1% of the time
where the time goes in v18:
time: 72.1 us; the launch traced here: 71.9 us
  starting transfers between devices  31 us (43%)
  Pallas kernels  19.9 us (28%)
  waiting for transfers between devices  19.9 us (28%)
  between operations  0.84 us (1%)
    ppermute x15, starting transfers between devices, swap(): return lax.ppermute(x, axis, [(i, i ^ mask) for i in range(count)])  14.1 us
    ppermute x10, starting transfers between devices, swap_both(): return lax.ppermute(x, ('tm', 'space'), route)  13.2 us
    ppermute x15, waiting for transfers between devices, swap(): return lax.ppermute(x, axis, [(i, i ^ mask) for i in range(count)])  11.6 us
    ppermute x10, waiting for transfers between devices, swap_both(): return lax.ppermute(x, ('tm', 'space'), route)  8.31 us
    pallas_call x1, Pallas kernels, local(): pl.pallas_call(functools.partial(merge_kernel, parts, span), out_shape=[s...  5.69 us
    pallas_call x1, Pallas kernels, local(): pl.pallas_call(functools.partial(level_kernel, parts), out_shape=shape(ha...  5.07 us
    pallas_call x1, Pallas kernels, local(): pl.pallas_call(functools.partial(filter_kernel, parts), out_shape=[shape(...  3.8 us
    ppermute x1, starting transfers between devices, local(): lax.ppermute(to_near, 'space', [(i, i ^ 1) for i in range(patches) if i ^...  3 us
  transfers between devices with their start and end apart: 27, of which 12 were waited for; matrix products, arithmetic and copies ran while one was open for 0% of the time, Pallas kernels for 15%

profile of v18, /device:TPU:0, one launch (start us, length us, event | category | flops | bytes accessed | tf_op | source)
XLA Modules:
  0.0 71.9 jit_solution(17510395214612910680)
XLA Ops:
  0.6 1.2 %edge.1 = (f32[64,128]{1,0:T(8,128)S(1)}, f32[64,128]{1,0:T(8,128)S(1)}) custom-call(f32[6]{0:T(128)} %rtaps_ref.3, f32[6]{0:T(128)} %ctaps_ref.3, f32[64,128,128]{2,1,0:T(8,128)} %snap_hbm.1, f32[64,128,128]{2,1,0:T(8,128)} %snap_hbm.1, s32[64,128]{1,0:T(8,128)} %mask_ref.1, s32[64,128]{1,0:T(8,128)} %mask_ref.1), custom_call_target="tpu_custom_call" | custom-call | tf_op jit(solution)/shard_map/edge/pallas_call | solution.py:401
  1.9 3.0 %collective-permute-start = (f32[64,128]{1,0:T(8,128)S(1)}, f32[64,128]{1,0:T(8,128)S(1)}, u32[]{:S(2)}, u32[]{:S(2)}) collective-permute-start(f32[64,128]{1,0:T(8,128)S(1)} %get-tuple-element.43), channel_id=1, source_target_pairs={{0,1},{1,0},{2,3},{3,2},{4,5},{5,4},{6,7},{7,6},{8,9},{9,8},{10,11... | collective-permute-start | bytes 98312 | tf_op jit(solution)/shard_map/ppermute | solution.py:417
  5.6 3.8 %filter.1 = (f32[512,128]{1,0:T(8,128)S(1)}, f32[512,128]{1,0:T(8,128)S(1)}, f32[512,128]{1,0:T(8,128)S(1)}, f32[512,128]{1,0:T(8,128)S(1)}) custom-call(f32[6]{0:T(128)} %rtaps_ref.3, f32[6]{0:T(128)} %ctaps_ref.3, f32[64,128,128]{2,1,0:T(8,128)} %snap_hbm.1, s32[64,128]{1,0:T(8,128)} %mask_ref.1), custom_call_target="tpu_custom_call" | custom-call | bytes 4194304 | tf_op jit(solution)/shard_map/filter/pallas_call | solution.py:421
  10.3 1.5 %collective-permute-start.7 = (f32[512,128]{1,0:T(8,128)S(1)}, f32[512,128]{1,0:T(8,128)S(1)}, u32[]{:S(2)}, u32[]{:S(2)}) collective-permute-start(f32[512,128]{1,0:T(8,128)S(1)} %get-tuple-element.51.refs_1_), channel_id=1, source_target_pairs={{0,16},{8,24},{16,0},{24,8},{1,17},{9,25},{17,1},{25,9},{2,18},{10... | collective-permute-start | bytes 786440 | tf_op jit(solution)/shard_map/ppermute | solution.py:32
  14.2 4.3 %collective-permute-start.5 = (f32[200,128]{1,0:T(8,128)S(1)}, f32[200,128]{1,0:T(8,128)S(1)}, u32[]{:S(2)}, u32[]{:S(2)}) collective-permute-start(f32[200,128]{1,0:T(8,128)S(1)} %get-tuple-element.54), channel_id=1, source_target_pairs={{0,1},{1,0},{2,3},{3,2},{4,5},{5,4},{6,7},{7,6},{8,9},{9,8},{10,11... | collective-permute-start | bytes 307208 | tf_op jit(solution)/shard_map/ppermute | solution.py:42
  19.5 2.8 %collective-permute-done.5 = f32[200,128]{1,0:T(8,128)S(1)} collective-permute-done((f32[200,128]{1,0:T(8,128)S(1)}, f32[200,128]{1,0:T(8,128)S(1)}, u32[]{:S(2)}, u32[]{:S(2)}) %collective-permute-start.5) | collective-permute-done | bytes 102432 | tf_op jit(solution)/shard_map/ppermute | solution.py:42
  22.3 1.7 %collective-permute-done.6 = f32[200,128]{1,0:T(8,128)S(1)} collective-permute-done((f32[200,128]{1,0:T(8,128)S(1)}, f32[200,128]{1,0:T(8,128)S(1)}, u32[]{:S(2)}, u32[]{:S(2)}) %collective-permute-start.6) | collective-permute-done | bytes 102432 | tf_op jit(solution)/shard_map/ppermute | solution.py:42
  25.1 3.7 %collective-permute-start.13 = (f32[200,128]{1,0:T(8,128)S(1)}, f32[200,128]{1,0:T(8,128)S(1)}, u32[]{:S(2)}, u32[]{:S(2)}) collective-permute-start(f32[200,128]{1,0:T(8,128)S(1)} %add_add_fusion), channel_id=1, source_target_pairs={{0,2},{1,3},{2,0},{3,1},{4,6},{5,7},{6,4},{7,5},{8,10},{9,11},{10,... | collective-permute-start | bytes 307208 | tf_op jit(solution)/shard_map/ppermute | solution.py:32
  28.9 1.6 %collective-permute-start.10 = (f32[64,128]{1,0:T(8,128)S(1)}, f32[64,128]{1,0:T(8,128)S(1)}, u32[]{:S(2)}, u32[]{:S(2)}) collective-permute-start(f32[64,128]{1,0:T(8,128)S(1)} %get-tuple-element.84), channel_id=1, source_target_pairs={{0,16},{1,17},{2,18},{3,19},{4,20},{5,21},{6,22},{7,23},{8,24},{9,... | collective-permute-start | bytes 98312 | tf_op jit(solution)/shard_map/ppermute | solution.py:42
  30.5 2.0 %collective-permute-start.12 = (f32[64,128]{1,0:T(8,128)S(1)}, f32[64,128]{1,0:T(8,128)S(1)}, u32[]{:S(2)}, u32[]{:S(2)}) collective-permute-start(f32[64,128]{1,0:T(8,128)S(1)} %get-tuple-element.85), channel_id=1, source_target_pairs={{0,17},{1,16},{2,19},{3,18},{4,21},{5,20},{6,23},{7,22},{8,25},{9,... | collective-permute-start | bytes 98312 | tf_op jit(solution)/shard_map/ppermute | solution.py:42
  32.9 2.4 %collective-permute-done.12 = f32[64,128]{1,0:T(8,128)S(1)} collective-permute-done((f32[64,128]{1,0:T(8,128)S(1)}, f32[64,128]{1,0:T(8,128)S(1)}, u32[]{:S(2)}, u32[]{:S(2)}) %collective-permute-start.12) | collective-permute-done | bytes 32800 | tf_op jit(solution)/shard_map/ppermute | solution.py:42
  36.4 2.3 %collective-permute-start.15 = (f32[136,128]{1,0:T(8,128)S(1)}, f32[136,128]{1,0:T(8,128)S(1)}, u32[]{:S(2)}, u32[]{:S(2)}) collective-permute-start(f32[136,128]{1,0:T(8,128)S(1)} %slice.38), channel_id=1, source_target_pairs={{0,4},{1,5},{2,6},{3,7},{4,0},{5,1},{6,2},{7,3},{8,12},{9,13},{10,... | collective-permute-start | bytes 208904 | tf_op jit(solution)/shard_map/ppermute | solution.py:32
  39.6 3.1 %collective-permute-done.14 = f32[64,128]{1,0:T(8,128)S(1)} collective-permute-done((f32[64,128]{1,0:T(8,128)S(1)}, f32[64,128]{1,0:T(8,128)S(1)}, u32[]{:S(2)}, u32[]{:S(2)}) %collective-permute-start.14) | collective-permute-done | bytes 32800 | tf_op jit(solution)/shard_map/ppermute | solution.py:32
  42.7 1.4 %collective-permute-start.16 = (f32[128,128]{1,0:T(8,128)S(1)}, f32[128,128]{1,0:T(8,128)S(1)}, u32[]{:S(2)}, u32[]{:S(2)}) collective-permute-start(f32[128,128]{1,0:T(8,128)S(1)} %pad_maximum_fusion.2), channel_id=1, source_target_pairs={{0,4},{1,5},{2,6},{3,7},{4,0},{5,1},{6,2},{7,3},{8,12},{9,13},{10,... | collective-permute-start | bytes 196616 | tf_op jit(solution)/shard_map/ppermute | solution.py:32
  44.1 1.5 %collective-permute-start.17 = (f32[136,128]{1,0:T(8,128)S(1)}, f32[136,128]{1,0:T(8,128)S(1)}, u32[]{:S(2)}, u32[]{:S(2)}) collective-permute-start(f32[136,128]{1,0:T(8,128)S(1)} %slice_add_fusion.4), channel_id=1, source_target_pairs={{0,16},{1,17},{2,18},{3,19},{4,20},{5,21},{6,22},{7,23},{8,24},{9,... | collective-permute-start | bytes 208904 | tf_op jit(solution)/shard_map/ppermute | solution.py:42
  45.7 3.0 %collective-permute-done.16 = f32[128,128]{1,0:T(8,128)S(1)} collective-permute-done((f32[128,128]{1,0:T(8,128)S(1)}, f32[128,128]{1,0:T(8,128)S(1)}, u32[]{:S(2)}, u32[]{:S(2)}) %collective-permute-start.16) | collective-permute-done | bytes 65568 | tf_op jit(solution)/shard_map/ppermute | solution.py:32
  48.8 1.4 %collective-permute-start.21 = (f32[128,128]{1,0:T(8,128)S(1)}, f32[128,128]{1,0:T(8,128)S(1)}, u32[]{:S(2)}, u32[]{:S(2)}) collective-permute-start(f32[128,128]{1,0:T(8,128)S(1)} %fusion.7), channel_id=1, source_target_pairs={{0,17},{1,16},{2,19},{3,18},{4,21},{5,20},{6,23},{7,22},{8,25},{9,... | collective-permute-start | bytes 196616 | tf_op jit(solution)/shard_map/ppermute | solution.py:42
  50.1 1.7 %collective-permute-start.20 = (f32[128,128]{1,0:T(8,128)S(1)}, f32[128,128]{1,0:T(8,128)S(1)}, u32[]{:S(2)}, u32[]{:S(2)}) collective-permute-start(f32[128,128]{1,0:T(8,128)S(1)} %fusion.7), channel_id=1, source_target_pairs={{0,1},{1,0},{2,3},{3,2},{4,5},{5,4},{6,7},{7,6},{8,9},{9,8},{10,11... | collective-permute-start | bytes 196616 | tf_op jit(solution)/shard_map/ppermute | solution.py:42
  52.3 5.1 %level.1.mine_ref = f32[1,384,128]{2,1,0:T(8,128)S(1)} custom-call(f32[2,136,128]{2,1,0:T(8,128)S(1)} %pad_maximum_fusion.1.even_ref, f32[2,136,128]{2,1,0:T(8,128)S(1)} %collective-permute-done.18.odd_ref), custom_call_target="tpu_custom_call" | custom-call | flops 3221225472 | tf_op jit(solution)/shard_map/level/pallas_call | solution.py:520
  58.0 1.3 %collective-permute-done.23.theirs_ref = f32[1,384,128]{2,1,0:T(8,128)S(1)} collective-permute-done((f32[1,384,128]{2,1,0:T(8,128)S(1)}, f32[1,384,128]{2,1,0:T(8,128)S(1)}, u32[]{:S(2)}, u32[]{:S(2)}) %collective-permute-start.23) | collective-permute-done | bytes 196640 | tf_op jit(solution)/shard_map/ppermute | solution.py:32
  59.3 5.7 %merge.1 = (f32[32,512]{1,0:T(8,128)S(1)}, f32[32,512]{1,0:T(8,128)S(1)}, f32[32,512]{1,0:T(8,128)S(1)}, f32[32,512]{1,0:T(8,128)S(1)}, f32[512,128]{1,0:T(8,128)S(1)}, /*index=5*/f32[512,128]{1,0:T(8,128)S(1)}) custom-call(f32[4,128,128]{2,1,0:T(8,128)S(1)} %pad_maximum_fusion.even_ref, f32[4,128,128]{2,1,0:T(8,128)S(1)} %collective-permute-done.22.odd_ref, ...), custom_call_target="tpu_custom_call" | custom-call | tf_op jit(solution)/shard_map/merge/pallas_call | solution.py:533
  65.3 1.5 %collective-permute-start.25 = (f32[32,512]{1,0:T(8,128)S(1)}, f32[32,512]{1,0:T(8,128)S(1)}, u32[]{:S(2)}, u32[]{:S(2)}) collective-permute-start(f32[32,512]{1,0:T(8,128)S(1)} %get-tuple-element.80), channel_id=1, source_target_pairs={{0,16},{8,24},{16,0},{24,8},{1,17},{9,25},{17,1},{25,9},{2,18},{10... | collective-permute-start | bytes 196616 | tf_op jit(solution)/shard_map/ppermute | solution.py:32
  67.9 1.7 %collective-permute-done.25.refs_2_ = f32[32,512]{1,0:T(8,128)S(1)} collective-permute-done((f32[32,512]{1,0:T(8,128)S(1)}, f32[32,512]{1,0:T(8,128)S(1)}, u32[]{:S(2)}, u32[]{:S(2)}) %collective-permute-start.25) | collective-permute-done | bytes 65568 | tf_op jit(solution)/shard_map/ppermute | solution.py:32
  69.6 1.3 %collective-permute-done.26.refs_3_ = f32[32,512]{1,0:T(8,128)S(1)} collective-permute-done((f32[32,512]{1,0:T(8,128)S(1)}, f32[32,512]{1,0:T(8,128)S(1)}, u32[]{:S(2)}, u32[]{:S(2)}) %collective-permute-start.26) | collective-permute-done | bytes 65568 | tf_op jit(solution)/shard_map/ppermute | solution.py:32
  (53 shorter events, 11.8 us)
Async XLA Ops:
  1.9 7.5 %collective-permute-start = (f32[64,128]{1,0:T(8,128)S(1)}, f32[64,128]{1,0:T(8,128)S(1)}, u32[]{:S(2)}, u32[]{:S(2)}) collective-permute-start(f32[64,128]{1,0:T(8,128)S(1)} %get-tuple-element.43), channel_id=1, source_target_pairs={{0,1},{1,0},{2,3},{3,2},{4,5},{5,4},{6,7},{7,6},{8,9},{9,8},{10,11... | collective-permute-start | bytes 98312 | tf_op jit(solution)/shard_map/ppermute | solution.py:417
  4.9 4.5 %collective-permute-start.1 = (f32[64,128]{1,0:T(8,128)S(1)}, f32[64,128]{1,0:T(8,128)S(1)}, u32[]{:S(2)}, u32[]{:S(2)}) collective-permute-start(f32[64,128]{1,0:T(8,128)S(1)} %get-tuple-element.44), channel_id=1, source_target_pairs={{1,2},{3,4},{5,6},{2,1},{4,3},{6,5},{9,10},{11,12},{13,14},{10,9},... | collective-permute-start | bytes 98312 | tf_op jit(solution)/shard_map/ppermute | solution.py:419
  9.8 3.0 %collective-permute-start.2 = (f32[512,128]{1,0:T(8,128)S(1)}, f32[512,128]{1,0:T(8,128)S(1)}, u32[]{:S(2)}, u32[]{:S(2)}) collective-permute-start(f32[512,128]{1,0:T(8,128)S(1)} %get-tuple-element.50), channel_id=1, source_target_pairs={{0,8},{8,0},{16,24},{24,16},{1,9},{9,1},{17,25},{25,17},{2,10},{10... | collective-permute-start | bytes 786440 | tf_op jit(solution)/shard_map/ppermute | solution.py:32
  10.3 9.2 %collective-permute-start.7 = (f32[512,128]{1,0:T(8,128)S(1)}, f32[512,128]{1,0:T(8,128)S(1)}, u32[]{:S(2)}, u32[]{:S(2)}) collective-permute-start(f32[512,128]{1,0:T(8,128)S(1)} %get-tuple-element.51.refs_1_), channel_id=1, source_target_pairs={{0,16},{8,24},{16,0},{24,8},{1,17},{9,25},{17,1},{25,9},{2,18},{10... | collective-permute-start | bytes 786440 | tf_op jit(solution)/shard_map/ppermute | solution.py:32
  11.9 12.4 %collective-permute-start.8 = (f32[512,128]{1,0:T(8,128)S(1)}, f32[512,128]{1,0:T(8,128)S(1)}, u32[]{:S(2)}, u32[]{:S(2)}) collective-permute-start(f32[512,128]{1,0:T(8,128)S(1)} %collective-permute-done.3.refs_3_), channel_id=1, source_target_pairs={{0,16},{8,24},{16,0},{24,8},{1,17},{9,25},{17,1},{25,9},{2,18},{10... | collective-permute-start | bytes 786440 | tf_op jit(solution)/shard_map/ppermute | solution.py:32
  14.1 5.4 %collective-permute-start.4 = (f32[200,128]{1,0:T(8,128)S(1)}, f32[200,128]{1,0:T(8,128)S(1)}, u32[]{:S(2)}, u32[]{:S(2)}) collective-permute-start(f32[200,128]{1,0:T(8,128)S(1)} %get-tuple-element.53), channel_id=1, source_target_pairs={{0,8},{1,9},{2,10},{3,11},{4,12},{5,13},{6,14},{7,15},{8,0},{9,1},... | collective-permute-start | bytes 307208 | tf_op jit(solution)/shard_map/ppermute | solution.py:42
  14.2 8.1 %collective-permute-start.5 = (f32[200,128]{1,0:T(8,128)S(1)}, f32[200,128]{1,0:T(8,128)S(1)}, u32[]{:S(2)}, u32[]{:S(2)}) collective-permute-start(f32[200,128]{1,0:T(8,128)S(1)} %get-tuple-element.54), channel_id=1, source_target_pairs={{0,1},{1,0},{2,3},{3,2},{4,5},{5,4},{6,7},{7,6},{8,9},{9,8},{10,11... | collective-permute-start | bytes 307208 | tf_op jit(solution)/shard_map/ppermute | solution.py:42
  18.6 5.4 %collective-permute-start.6 = (f32[200,128]{1,0:T(8,128)S(1)}, f32[200,128]{1,0:T(8,128)S(1)}, u32[]{:S(2)}, u32[]{:S(2)}) collective-permute-start(f32[200,128]{1,0:T(8,128)S(1)} %get-tuple-element.55), channel_id=1, source_target_pairs={{0,9},{1,8},{2,11},{3,10},{4,13},{5,12},{6,15},{7,14},{8,1},{9,0},... | collective-permute-start | bytes 307208 | tf_op jit(solution)/shard_map/ppermute | solution.py:42
  24.9 3.9 %collective-permute-start.9 = (f32[4,64,128]{2,1,0:T(8,128)S(1)}, f32[4,64,128]{2,1,0:T(8,128)S(1)}, u32[]{:S(2)}, u32[]{:S(2)}) collective-permute-start(f32[4,64,128]{2,1,0:T(8,128)S(1)} %get-tuple-element.59), channel_id=1, source_target_pairs={{0,8},{8,0},{16,24},{24,16},{1,9},{9,1},{17,25},{25,17},{2,10},{10... | collective-permute-start | bytes 393224 | tf_op jit(solution)/shard_map/ppermute | solution.py:32
  25.1 7.5 %collective-permute-start.13 = (f32[200,128]{1,0:T(8,128)S(1)}, f32[200,128]{1,0:T(8,128)S(1)}, u32[]{:S(2)}, u32[]{:S(2)}) collective-permute-start(f32[200,128]{1,0:T(8,128)S(1)} %add_add_fusion), channel_id=1, source_target_pairs={{0,2},{1,3},{2,0},{3,1},{4,6},{5,7},{6,4},{7,5},{8,10},{9,11},{10,... | collective-permute-start | bytes 307208 | tf_op jit(solution)/shard_map/ppermute | solution.py:32
  28.9 4.0 %collective-permute-start.10 = (f32[64,128]{1,0:T(8,128)S(1)}, f32[64,128]{1,0:T(8,128)S(1)}, u32[]{:S(2)}, u32[]{:S(2)}) collective-permute-start(f32[64,128]{1,0:T(8,128)S(1)} %get-tuple-element.84), channel_id=1, source_target_pairs={{0,16},{1,17},{2,18},{3,19},{4,20},{5,21},{6,22},{7,23},{8,24},{9,... | collective-permute-start | bytes 98312 | tf_op jit(solution)/shard_map/ppermute | solution.py:42
  30.5 4.8 %collective-permute-start.12 = (f32[64,128]{1,0:T(8,128)S(1)}, f32[64,128]{1,0:T(8,128)S(1)}, u32[]{:S(2)}, u32[]{:S(2)}) collective-permute-start(f32[64,128]{1,0:T(8,128)S(1)} %get-tuple-element.85), channel_id=1, source_target_pairs={{0,17},{1,16},{2,19},{3,18},{4,21},{5,20},{6,23},{7,22},{8,25},{9,... | collective-permute-start | bytes 98312 | tf_op jit(solution)/shard_map/ppermute | solution.py:42
  32.5 3.9 %collective-permute-start.11 = (f32[64,128]{1,0:T(8,128)S(1)}, f32[64,128]{1,0:T(8,128)S(1)}, u32[]{:S(2)}, u32[]{:S(2)}) collective-permute-start(f32[64,128]{1,0:T(8,128)S(1)} %get-tuple-element.86), channel_id=1, source_target_pairs={{0,1},{1,0},{2,3},{3,2},{4,5},{5,4},{6,7},{7,6},{8,9},{9,8},{10,11... | collective-permute-start | bytes 98312 | tf_op jit(solution)/shard_map/ppermute | solution.py:42
  36.4 6.2 %collective-permute-start.15 = (f32[136,128]{1,0:T(8,128)S(1)}, f32[136,128]{1,0:T(8,128)S(1)}, u32[]{:S(2)}, u32[]{:S(2)}) collective-permute-start(f32[136,128]{1,0:T(8,128)S(1)} %slice.38), channel_id=1, source_target_pairs={{0,4},{1,5},{2,6},{3,7},{4,0},{5,1},{6,2},{7,3},{8,12},{9,13},{10,... | collective-permute-start | bytes 208904 | tf_op jit(solution)/shard_map/ppermute | solution.py:32
  38.8 3.9 %collective-permute-start.14 = (f32[64,128]{1,0:T(8,128)S(1)}, f32[64,128]{1,0:T(8,128)S(1)}, u32[]{:S(2)}, u32[]{:S(2)}) collective-permute-start(f32[64,128]{1,0:T(8,128)S(1)} %fusion.6), channel_id=1, source_target_pairs={{0,2},{1,3},{2,0},{3,1},{4,6},{5,7},{6,4},{7,5},{8,10},{9,11},{10,... | collective-permute-start | bytes 98312 | tf_op jit(solution)/shard_map/ppermute | solution.py:32
  42.7 5.9 %collective-permute-start.16 = (f32[128,128]{1,0:T(8,128)S(1)}, f32[128,128]{1,0:T(8,128)S(1)}, u32[]{:S(2)}, u32[]{:S(2)}) collective-permute-start(f32[128,128]{1,0:T(8,128)S(1)} %pad_maximum_fusion.2), channel_id=1, source_target_pairs={{0,4},{1,5},{2,6},{3,7},{4,0},{5,1},{6,2},{7,3},{8,12},{9,13},{10,... | collective-permute-start | bytes 196616 | tf_op jit(solution)/shard_map/ppermute | solution.py:32
  44.1 4.5 %collective-permute-start.17 = (f32[136,128]{1,0:T(8,128)S(1)}, f32[136,128]{1,0:T(8,128)S(1)}, u32[]{:S(2)}, u32[]{:S(2)}) collective-permute-start(f32[136,128]{1,0:T(8,128)S(1)} %slice_add_fusion.4), channel_id=1, source_target_pairs={{0,16},{1,17},{2,18},{3,19},{4,20},{5,21},{6,22},{7,23},{8,24},{9,... | collective-permute-start | bytes 208904 | tf_op jit(solution)/shard_map/ppermute | solution.py:42
  48.7 3.6 %collective-permute-start.18 = (f32[2,136,128]{2,1,0:T(8,128)S(1)}, f32[2,136,128]{2,1,0:T(8,128)S(1)}, u32[]{:S(2)}, u32[]{:S(2)}) collective-permute-start(f32[2,136,128]{2,1,0:T(8,128)S(1)} %pad_maximum_fusion.1.even_ref), channel_id=1, source_target_pairs={{0,8},{8,0},{16,24},{24,16},{1,9},{9,1},{17,25},{25,17},{2,10},{10... | collective-permute-start | bytes 417800 | tf_op jit(solution)/shard_map/ppermute | solution.py:32
  48.8 8.6 %collective-permute-start.21 = (f32[128,128]{1,0:T(8,128)S(1)}, f32[128,128]{1,0:T(8,128)S(1)}, u32[]{:S(2)}, u32[]{:S(2)}) collective-permute-start(f32[128,128]{1,0:T(8,128)S(1)} %fusion.7), channel_id=1, source_target_pairs={{0,17},{1,16},{2,19},{3,18},{4,21},{5,20},{6,23},{7,22},{8,25},{9,... | collective-permute-start | bytes 196616 | tf_op jit(solution)/shard_map/ppermute | solution.py:42
  50.1 7.3 %collective-permute-start.20 = (f32[128,128]{1,0:T(8,128)S(1)}, f32[128,128]{1,0:T(8,128)S(1)}, u32[]{:S(2)}, u32[]{:S(2)}) collective-permute-start(f32[128,128]{1,0:T(8,128)S(1)} %fusion.7), channel_id=1, source_target_pairs={{0,1},{1,0},{2,3},{3,2},{4,5},{5,4},{6,7},{7,6},{8,9},{9,8},{10,11... | collective-permute-start | bytes 196616 | tf_op jit(solution)/shard_map/ppermute | solution.py:42
  51.8 5.6 %collective-permute-start.19 = (f32[128,128]{1,0:T(8,128)S(1)}, f32[128,128]{1,0:T(8,128)S(1)}, u32[]{:S(2)}, u32[]{:S(2)}) collective-permute-start(f32[128,128]{1,0:T(8,128)S(1)} %fusion.7), channel_id=1, source_target_pairs={{0,16},{1,17},{2,18},{3,19},{4,20},{5,21},{6,22},{7,23},{8,24},{9,... | collective-permute-start | bytes 196616 | tf_op jit(solution)/shard_map/ppermute | solution.py:42
  65.0 2.8 %collective-permute-start.24 = (f32[32,512]{1,0:T(8,128)S(1)}, f32[32,512]{1,0:T(8,128)S(1)}, u32[]{:S(2)}, u32[]{:S(2)}) collective-permute-start(f32[32,512]{1,0:T(8,128)S(1)} %get-tuple-element.79), channel_id=1, source_target_pairs={{0,8},{8,0},{16,24},{24,16},{1,9},{9,1},{17,25},{25,17},{2,10},{10... | collective-permute-start | bytes 196616 | tf_op jit(solution)/shard_map/ppermute | solution.py:32
  65.3 4.4 %collective-permute-start.25 = (f32[32,512]{1,0:T(8,128)S(1)}, f32[32,512]{1,0:T(8,128)S(1)}, u32[]{:S(2)}, u32[]{:S(2)}) collective-permute-start(f32[32,512]{1,0:T(8,128)S(1)} %get-tuple-element.80), channel_id=1, source_target_pairs={{0,16},{8,24},{16,0},{24,8},{1,17},{9,25},{17,1},{25,9},{2,18},{10... | collective-permute-start | bytes 196616 | tf_op jit(solution)/shard_map/ppermute | solution.py:32
  66.8 4.1 %collective-permute-start.26 = (f32[32,512]{1,0:T(8,128)S(1)}, f32[32,512]{1,0:T(8,128)S(1)}, u32[]{:S(2)}, u32[]{:S(2)}) collective-permute-start(f32[32,512]{1,0:T(8,128)S(1)} %get-tuple-element.81), channel_id=1, source_target_pairs={{0,24},{8,16},{16,8},{24,0},{1,25},{9,17},{17,9},{25,1},{2,26},{10... | collective-permute-start | bytes 196616 | tf_op jit(solution)/shard_map/ppermute | solution.py:32
  (4 other events, 16.8 us)
